TPU v7x, 32 devices: a whole 2x2x4 slice. The times are simulated.
32 devices in a mesh: parts: 2 (over y), patch: 4 (over z), level: 2 (over x), sub: 2 (over core).
Axes of the slice: x: 2, y: 2, z: 4, core: 2. Of those that a mesh axis runs over, the one named last changes fastest.
Arguments:
- adjoint_height: float32 [4, 1024, 1024], P(('parts', 'level'), ('patch', 'sub')), parts along dimension 0, may hold values from -6 to 6
- adjoint_momenta: float32 [2, 4, 1024, 1024], P(None, ('parts', 'level'), ('patch', 'sub')), parts along dimension 1, may hold values from -6 to 6
- depth: float32 [2, 1024, 1024], P('level', ('patch', 'sub')), may hold values from 0.2 to 1
- wet_mask: int32 [2, 1024, 1024], P('level', ('patch', 'sub')), may hold values 0 or 1
- adjacency: int32 [2, 4, 4], P('level'), may hold values from -1 to 3, as said below
- nest_gain: float32 [2, 8192], P(None, ('patch', 'sub')), may hold values from 0.75 to 1
- nest_index: int32 [2, 8192], P(None, ('patch', 'sub')), may hold values from 0 to 1023, as said below
Outputs:
- height_out: float32 [4, 1024, 1024], P(('parts', 'level'), ('patch', 'sub')), parts along dimension 0
- momenta_out: float32 [2, 4, 1024, 1024], P(None, ('parts', 'level'), ('patch', 'sub')), parts along dimension 1
There are 2 independent parts, one for each index of `parts`. A program takes and returns all parts, laid end to end along the dimension named above; an argument that names none is the same for every part. Nothing has to cross between parts.
Inputs may be any that keep to these rules, and one draw needn't show every extreme that they name: `adjacency`: the patches of a level sit on a grid of cells in an order drawn from the seed; each row of a patch lists its grid neighbours, -1 at the grid's edge, and neighbour links are symmetric. `nest_index`: entries index a cell of the same half patch's strip, 1024 cells long.
All inputs are finite; a program needn't handle non-finite values. No bound on the sum of `wet_mask` on one device may be relied on, other than what follows from the above.
Results may differ from a plain program's by a relative error of at most 0.00002.
Values sent between devices are 32-bit elements; how exact they have to be, the bound alone decides.
No kernel may reach another device: no remote copies, remote signals or barrier semaphores. Data moves between devices by JAX's collectives and lax.ppermute only.
A program may use at most 64 MiB of HBM per device.

v0:
```python
import jax
import jax.numpy as jnp
from jax import lax
from jax.sharding import PartitionSpec as P

STEPS = 2


courant = 0.45


def passed_along(value, axis, steps):
    count = lax.axis_size(axis)
    initial, last = (max(0, -steps), min(count, count - steps))
    return lax.ppermute(value, axis, [(source, source + steps) for source in range(initial, last)])


def pick_row(table, index):
    return lax.dynamic_index_in_dim(table, index, 0, keepdims=False)


def body(adjoint_height, adjoint_momenta, depth, wet_mask, adjacency, nest_gain, nest_index):
    eta = adjoint_height[0]
    mom_row = adjoint_momenta[0, 0]
    mom_col = adjoint_momenta[1, 0]
    height = depth[0]
    wet = wet_mask[0].astype(jnp.float32)
    level = lax.axis_index("level")
    patch = lax.axis_index("patch")
    half = lax.axis_index("sub")
    levels = lax.axis_size("level")
    subs = lax.axis_size("sub")
    segments = lax.axis_size("patch") * subs
    links = pick_row(adjacency[0], patch)
    north = links[0]
    south = links[1]
    west = links[2]
    east = links[3]
    has_north = (north >= 0).astype(jnp.float32)
    has_south = (south >= 0).astype(jnp.float32)
    has_west = (west >= 0).astype(jnp.float32)
    has_east = (east >= 0).astype(jnp.float32)
    own_gain = pick_row(nest_gain, level)
    own_table = pick_row(nest_index, level)
    for step in range(STEPS):
        strip = eta[0]
        flux = strip
        inflow = jnp.zeros_like(strip)
        for turn in range(levels - 1):
            received = passed_along(flux, "level", -1)
            inflow = own_gain * jnp.take(received, own_table)
            flux = inflow + strip
        eta = eta.at[0].add(inflow)
        first_col = eta[:, 0]
        first_row = eta[0, :]
        east_cols = lax.all_gather(first_col[None], ("patch", "sub"), axis=0, tiled=True)
        east_rows = lax.all_gather(first_row[None], ("patch", "sub"), axis=0, tiled=True)
        east_col = jnp.take(east_cols, jnp.maximum(east, 0) * subs + half, axis=0) * has_east
        east_inside = jnp.take(
            east_rows, jnp.minimum(patch * subs + half + 1, segments - 1), axis=0
        )
        east_across = jnp.take(east_rows, jnp.maximum(south, 0) * subs, axis=0) * has_south
        south_row = jnp.where(half == subs - 1, east_across, east_inside)
        east_col, south_row = (east_col, south_row)
        east_eta = jnp.concatenate([eta[:, 1:], east_col[:, None]], axis=1)
        south_eta = jnp.concatenate([eta[1:], south_row[None]], axis=0)
        mom_row = wet * (mom_row - courant * (east_eta - eta))
        mom_col = wet * (mom_col - courant * (south_eta - eta))
        last_col = mom_row[:, -1]
        last_row = mom_col[-1, :]
        cols = lax.all_gather(last_col[None], ("patch", "sub"), axis=0, tiled=True)
        rows = lax.all_gather(last_row[None], ("patch", "sub"), axis=0, tiled=True)
        west_col = jnp.take(cols, jnp.maximum(west, 0) * subs + half, axis=0) * has_west
        inside = jnp.take(rows, jnp.maximum(patch * subs + half - 1, 0), axis=0)
        across = jnp.take(rows, jnp.maximum(north, 0) * subs + subs - 1, axis=0) * has_north
        north_row = jnp.where(half == 0, across, inside)
        west_col, north_row = (west_col, north_row)
        west_row = jnp.concatenate([west_col[:, None], mom_row[:, :-1]], axis=1)
        north_col = jnp.concatenate([north_row[None], mom_col[:-1]], axis=0)
        eta = wet * (eta - courant * height * (mom_row - west_row + (mom_col - north_col)))
    return (eta[None], jnp.stack([mom_row, mom_col])[:, None])


def solution(mesh):
    in_specs = (
        P(("parts", "level"), ("patch", "sub"), None),
        P(None, ("parts", "level"), ("patch", "sub"), None),
        P("level", ("patch", "sub"), None),
        P("level", ("patch", "sub"), None),
        P("level", None, None),
        P(None, ("patch", "sub")),
        P(None, ("patch", "sub")),
    )
    out_specs = (
        P(("parts", "level"), ("patch", "sub"), None),
        P(None, ("parts", "level"), ("patch", "sub"), None),
    )
    return jax.shard_map(body, mesh=mesh, in_specs=in_specs, out_specs=out_specs, check_vma=False)
```

profile of v0, /device:TPU:0, one launch (start us, length us, event | category | flops | bytes accessed | tf_op | source)
XLA Modules:
  0.0 152.6 jit_solution(2689515999720986161)
XLA Ops:
  0.6 0.0 copy-start
  0.6 1.0 copy.33
  1.7 1.3 collective-permute-start
  3.0 0.7 constant_dynamic-slice_fusion.4
  3.7 0.6 fusion.35
  4.3 0.0 copy-done
  4.3 0.0 copy-start.4
  4.3 0.7 copy-done.4
  10.1 0.0 collective-permute-done
  10.2 4.5 %gather_fusion = f32[1024]{0:T(1024)S(1)} fusion(f32[1024]{0:T(1024)S(1)} %collective-permute-done, s32[1024]{0:T(1024)S(1)} %fusion.22), kind=kCustom, calls=%fused_computation.clone | custom fusion | bytes 12288 | tf_op jit(solution)/shard_map/jit(_take)/gather | solution.py:51
  14.7 15.7 %all-gather.2 = f32[8192]{0:T(1024)S(1)} all-gather(f32[1024]{0:T(1024)S(1)} %get-tuple-element.51), channel_id=4, replica_groups=mesh['parts'=2,'patch'=4,'level'=2,'sub'=2] {'patch','sub'}, dimensions={0}, use_global_device_ids=true | all-gather | bytes 36864 | tf_op jit(solution)/shard_map/all_gather | solution.py:57
  30.4 0.1 scatter-add.6
  30.5 0.2 slice.143
  30.7 0.0 copy-start.1
  30.8 14.8 %all-gather = f32[1024,1]{1,0:T(8,128)S(1)} all-gather(f32[128,1]{1,0:T(8,128)S(1)} %slice.144), channel_id=2, replica_groups=mesh['parts'=2,'patch'=4,'level'=2,'sub'=2] {'patch','sub'}, dimensions={0}, use_global_device_ids=true | all-gather | bytes 4608 | tf_op jit(solution)/shard_map/all_gather | solution.py:56
  45.6 0.2 reduce.4
  45.8 0.1 copy.17
  46.0 0.0 copy-done.1
  46.0 1.6 %fusion.9 = (f32[128,1024]{1,0:T(8,128)S(1)}, f32[128,1024]{1,0:T(8,128)S(1)}) fusion(f32[128,1024]{1,0:T(8,128)S(1)} %scatter-add.6, f32[1,1024]{1,0:T(1,128)S(1)} %bitcast.119, f32[127,1024]{1,0:T(8,128)S(1)} %slice.147, f32[2,1,128,1024]{3,2,1,0:T(8,128)} %param.18, s32[1,128,1024]{2,1,0:T(8,128)S(1)} %copy-done.1, f32[128,1]{1,0:T(8,128)S(1)} %copy.17, ...), kind=kLoop, calls=%fused_computation.15 | loop fusion | flops 1441792 | bytes 4194304 | tf_op jit(solution)/shard_map/mul | solution.py:68
  47.6 14.2 %all-gather.5 = f32[8,1,1024]{2,1,0:T(1,128)S(1)} all-gather(f32[1,1,1024]{2,1,0:T(1,128)S(1)} %slice_bitcast_fusion.1), channel_id=1, replica_groups=mesh['parts'=2,'patch'=4,'level'=2,'sub'=2] {'patch','sub'}, dimensions={0}, use_global_device_ids=true | all-gather | bytes 36864 | tf_op jit(solution)/shard_map/all_gather | solution.py:72
  61.8 0.1 slice.145
  61.9 0.0 copy-start.2
  61.9 15.0 %all-gather.1 = f32[1024,1]{1,0:T(8,128)S(1)} all-gather(f32[128,1]{1,0:T(8,128)S(1)} %slice.145), channel_id=3, replica_groups=mesh['parts'=2,'patch'=4,'level'=2,'sub'=2] {'patch','sub'}, dimensions={0}, use_global_device_ids=true | all-gather | bytes 4608 | tf_op jit(solution)/shard_map/all_gather | solution.py:71
  76.9 0.2 reduce.5
  77.2 0.1 copy.18
  77.3 0.0 copy-done.2
  77.3 0.4 fusion.6
  77.7 1.3 collective-permute-start.1
  79.0 4.2 %collective-permute-done.1 = f32[1024]{0:T(1024)S(1)} collective-permute-done((f32[1024]{0:T(1024)S(1)}, f32[1024]{0:T(1024)S(1)}, u32[]{:S(2)}, u32[]{:S(2)}) %collective-permute-start.1) | collective-permute-done | bytes 4128 | tf_op jit(solution)/shard_map/ppermute | solution.py:15
  83.2 4.5 %gather_fusion.1 = f32[1024]{0:T(1024)S(1)} fusion(f32[1024]{0:T(1024)S(1)} %collective-permute-done.1, s32[1024]{0:T(1024)S(1)} %fusion.22), kind=kCustom, calls=%fused_computation.1.clone | custom fusion | bytes 12288 | tf_op jit(solution)/shard_map/jit(_take)/gather | solution.py:51
  87.8 0.1 scatter-add.9
  87.9 0.8 slice.155
  88.8 1.0 slice.151
  89.8 14.0 %all-gather.6 = f32[8,1,1024]{2,1,0:T(1,128)S(1)} all-gather(f32[1,1,1024]{2,1,0:T(1,128)S(1)} %bitcast.111), channel_id=1, replica_groups=mesh['parts'=2,'patch'=4,'level'=2,'sub'=2] {'patch','sub'}, dimensions={0}, use_global_device_ids=true | all-gather | bytes 36864 | tf_op jit(solution)/shard_map/all_gather | solution.py:57
  103.8 14.9 %all-gather.3 = f32[1024,1]{1,0:T(8,128)S(1)} all-gather(f32[128,1]{1,0:T(8,128)S(1)} %slice.152), channel_id=5, replica_groups=mesh['parts'=2,'patch'=4,'level'=2,'sub'=2] {'patch','sub'}, dimensions={0}, use_global_device_ids=true | all-gather | bytes 4608 | tf_op jit(solution)/shard_map/all_gather | solution.py:56
  118.7 0.2 reduce.6
  118.9 0.1 copy.19
  119.1 1.6 %fusion.20 = (f32[128,1024]{1,0:T(8,128)S(1)}, f32[128,1024]{1,0:T(8,128)S(1)}) fusion(f32[128,1024]{1,0:T(8,128)S(1)} %get-tuple-element.53, f32[128,1024]{1,0:T(8,128)S(1)} %scatter-add.9, f32[1,1024]{1,0:T(1,128)S(1)} %bitcast.117, f32[127,1024]{1,0:T(8,128)} %slice.155, s32[1,128,1024]{2,1,0:T(8,128)S(1)} %copy-done.1, ...), kind=kLoop, calls=%fused_computation.30 | loop fusion | flops 1441792 | bytes 4194304 | tf_op jit(solution)/shard_map/mul | solution.py:68
  120.6 14.3 %all-gather.7 = f32[8,1,1024]{2,1,0:T(1,128)S(1)} all-gather(f32[1,1,1024]{2,1,0:T(1,128)S(1)} %slice_bitcast_fusion), channel_id=1, replica_groups=mesh['parts'=2,'patch'=4,'level'=2,'sub'=2] {'patch','sub'}, dimensions={0}, use_global_device_ids=true | all-gather | bytes 36864 | tf_op jit(solution)/shard_map/all_gather | solution.py:72
  134.9 0.1 slice.153
  135.0 14.9 %all-gather.4 = f32[1024,1]{1,0:T(8,128)S(1)} all-gather(f32[128,1]{1,0:T(8,128)S(1)} %slice.153), channel_id=6, replica_groups=mesh['parts'=2,'patch'=4,'level'=2,'sub'=2] {'patch','sub'}, dimensions={0}, use_global_device_ids=true | all-gather | bytes 4608 | tf_op jit(solution)/shard_map/all_gather | solution.py:71
  149.9 0.2 reduce.7
  150.1 0.1 copy.20
  150.2 0.0 copy-start.3
  150.3 1.1 maximum_bitcast_fusion
  151.3 0.1 copy-done.3
  151.4 1.2 fusion.17
  (29 shorter events, 0.3 us)
Async XLA Ops:
  0.6 3.7 %copy-start = (s32[2,1024]{1,0:T(2,128)S(1)}, s32[2,1024]{1,0:T(2,128)}, u32[]{:S(2)}) copy-start(s32[2,1024]{1,0:T(2,128)} %param.23) | copy-start | bytes 24580
  1.7 8.4 %collective-permute-start = (f32[1024]{0:T(1024)S(1)}, f32[1024]{0:T(1024)S(1)}, u32[]{:S(2)}, u32[]{:S(2)}) collective-permute-start(f32[1024]{0:T(1024)S(1)} %bitcast.122), channel_id=1, source_target_pairs={{2,0},{3,1},{6,4},{7,5},{10,8},{11,9},{14,12},{15,13},{18,16},{19,... | collective-permute-start | bytes 12296 | tf_op jit(solution)/shard_map/ppermute | solution.py:15
  4.3 0.7 copy-start.4
  30.7 15.2 %copy-start.1 = (s32[1,128,1024]{2,1,0:T(8,128)S(1)}, s32[1,128,1024]{2,1,0:T(8,128)}, u32[]{:S(2)}) copy-start(s32[1,128,1024]{2,1,0:T(8,128)} %param.20) | copy-start | bytes 1572868
  61.9 15.4 %copy-start.2 = (f32[1,128,1024]{2,1,0:T(8,128)S(1)}, f32[1,128,1024]{2,1,0:T(8,128)}, u32[]{:S(2)}) copy-start(f32[1,128,1024]{2,1,0:T(8,128)} %param.19) | copy-start | bytes 1572868
  77.7 5.5 %collective-permute-start.1 = (f32[1024]{0:T(1024)S(1)}, f32[1024]{0:T(1024)S(1)}, u32[]{:S(2)}, u32[]{:S(2)}) collective-permute-start(f32[1024]{0:T(1024)S(1)} %bitcast.136), channel_id=1, source_target_pairs={{2,0},{3,1},{6,4},{7,5},{10,8},{11,9},{14,12},{15,13},{18,16},{19,... | collective-permute-start | bytes 12296 | tf_op jit(solution)/shard_map/ppermute | solution.py:15
  150.2 1.1 copy-start.3
where the time goes:
time: 153 us
  blocking collectives  118 us (77%)
  local copies, waits for them, and re-layouts  15.1 us (10%)
  other arithmetic  6.77 us (4%)
  between operations  6.05 us (4%)
  waiting for transfers between devices  4.2 us (3%)
  starting transfers between devices  2.57 us (2%)
    all_gather x2, blocking collectives, body(): cols = lax.all_gather(last_col[None], ('patch', 'sub'), axis=0, tiled=True)  29.9 us
    all_gather x2, blocking collectives, body(): lax.all_gather(first_col[None], ('patch', 'sub'), axis=0, tiled=True)  29.8 us
    all_gather x2, blocking collectives, body(): lax.all_gather(first_row[None], ('patch', 'sub'), axis=0, tiled=True)  29.7 us
    all_gather x2, blocking collectives, body(): rows = lax.all_gather(last_row[None], ('patch', 'sub'), axis=0, tiled=True)  28.5 us
    gather x2, local copies, waits for them, and re-layouts, body(): inflow = own_gain * jnp.take(received, own_table)  9.05 us
    ppermute x2, waiting for transfers between devices, passed_along(): lax.ppermute(value, axis, [(source, source + steps) for source in range(i...  4.2 us
    mul x2, other arithmetic, body(): mom_col = wet * (mom_col - courant * (south_eta - eta))  3.13 us
  transfers between devices with their start and end apart: 2, of which 1 were waited for; matrix products, arithmetic and copies ran while one was open for 1% of the time, Pallas kernels for 0%

commit v1 on v0

--- a/solution.py
+++ b/solution.py
@@ -15,6 +15,12 @@
     return lax.ppermute(value, axis, [(source, source + steps) for source in range(initial, last)])
 
 
+def from_all(value, axes):
+    count = lax.axis_size(axes)
+    others = [lax.ppermute(value, axes, [(source, source ^ turn) for source in range(count)]) for turn in range(1, count)]
+    return jnp.stack([value] + others)
+
+
 def pick_row(table, index):
     return lax.dynamic_index_in_dim(table, index, 0, keepdims=False)
 
@@ -30,7 +36,8 @@
     half = lax.axis_index("sub")
     levels = lax.axis_size("level")
     subs = lax.axis_size("sub")
-    segments = lax.axis_size("patch") * subs
+    own = patch * subs + half
+    cols = eta.shape[1]
     links = pick_row(adjacency[0], patch)
     north = links[0]
     south = links[1]
@@ -53,28 +60,22 @@
         eta = eta.at[0].add(inflow)
         first_col = eta[:, 0]
         first_row = eta[0, :]
-        east_cols = lax.all_gather(first_col[None], ("patch", "sub"), axis=0, tiled=True)
-        east_rows = lax.all_gather(first_row[None], ("patch", "sub"), axis=0, tiled=True)
-        east_col = jnp.take(east_cols, jnp.maximum(east, 0) * subs + half, axis=0) * has_east
-        east_inside = jnp.take(
-            east_rows, jnp.minimum(patch * subs + half + 1, segments - 1), axis=0
-        )
-        east_across = jnp.take(east_rows, jnp.maximum(south, 0) * subs, axis=0) * has_south
-        south_row = jnp.where(half == subs - 1, east_across, east_inside)
-        east_col, south_row = (east_col, south_row)
+        edges = from_all(jnp.concatenate([first_row, first_col]), ("patch", "sub"))
+        east_col = pick_row(edges, own ^ (jnp.maximum(east, 0) * subs + half))[cols:] * has_east
+        across = jnp.where(half == subs - 1, jnp.maximum(south, 0) * subs, own + 1)
+        keep = jnp.where(half == subs - 1, has_south, 1.0)
+        south_row = pick_row(edges, own ^ across)[:cols] * keep
         east_eta = jnp.concatenate([eta[:, 1:], east_col[:, None]], axis=1)
         south_eta = jnp.concatenate([eta[1:], south_row[None]], axis=0)
         mom_row = wet * (mom_row - courant * (east_eta - eta))
         mom_col = wet * (mom_col - courant * (south_eta - eta))
         last_col = mom_row[:, -1]
         last_row = mom_col[-1, :]
-        cols = lax.all_gather(last_col[None], ("patch", "sub"), axis=0, tiled=True)
-        rows = lax.all_gather(last_row[None], ("patch", "sub"), axis=0, tiled=True)
-        west_col = jnp.take(cols, jnp.maximum(west, 0) * subs + half, axis=0) * has_west
-        inside = jnp.take(rows, jnp.maximum(patch * subs + half - 1, 0), axis=0)
-        across = jnp.take(rows, jnp.maximum(north, 0) * subs + subs - 1, axis=0) * has_north
-        north_row = jnp.where(half == 0, across, inside)
-        west_col, north_row = (west_col, north_row)
+        edges = from_all(jnp.concatenate([last_row, last_col]), ("patch", "sub"))
+        west_col = pick_row(edges, own ^ (jnp.maximum(west, 0) * subs + half))[cols:] * has_west
+        across = jnp.where(half == 0, jnp.maximum(north, 0) * subs + subs - 1, own - 1)
+        keep = jnp.where(half == 0, has_north, 1.0)
+        north_row = pick_row(edges, own ^ across)[:cols] * keep
         west_row = jnp.concatenate([west_col[:, None], mom_row[:, :-1]], axis=1)
         north_col = jnp.concatenate([north_row[None], mom_col[:-1]], axis=0)
         eta = wet * (eta - courant * height * (mom_row - west_row + (mom_col - north_col)))

time: 153 us -> 76.1 us (0.50)
  blocking collectives: 118 us -> 0 us
  starting transfers between devices: 2.57 us -> 36.3 us
  waiting for transfers between devices: 4.2 us -> 9.76 us
  local copies, waits for them, and re-layouts: 15.1 us -> 16.7 us
    all_gather x8 -> x0, blocking collectives: 118 us -> none  [the longest x2 29.9 us: body(): cols = lax.all_gather(last_col[None], ('patch', 'sub'), axis=0, tiled=True)]
    ppermute x0 -> x28, starting transfers between devices: none -> 33.7 us  [from_all(): lax.ppermute(value, axes, [(source, source ^ turn) for source in range(co...]
    ppermute x2, waiting for transfers between devices: 4.2 us -> 7.97 us  [passed_along(): lax.ppermute(value, axis, [(source, source + steps) for source in range(i...]
    ppermute x0 -> x28, waiting for transfers between devices: none -> 1.79 us  [from_all(): lax.ppermute(value, axes, [(source, source ^ turn) for source in range(co...]
  transfers between devices with their start and end apart: 2 -> 30, of which waited for: 1 -> 7; matrix products, arithmetic and copies ran while one was open for 1% -> 7% of each run, Pallas kernels for 0% -> 0%
where the time goes in v1:
time: 76.1 us; the launch traced here: 75.8 us
  starting transfers between devices  36.3 us (48%)
  local copies, waits for them, and re-layouts  16.7 us (22%)
  waiting for transfers between devices  9.76 us (13%)
  between operations  6.61 us (9%)
  other arithmetic  6.44 us (8%)
    ppermute x28, starting transfers between devices, from_all(): lax.ppermute(value, axes, [(source, source ^ turn) for source in range(co...  33.7 us
    gather x2, local copies, waits for them, and re-layouts, body(): inflow = own_gain * jnp.take(received, own_table)  9.04 us
    ppermute x2, waiting for transfers between devices, passed_along(): lax.ppermute(value, axis, [(source, source + steps) for source in range(i...  7.97 us
    mul x2, other arithmetic, body(): mom_col = wet * (mom_col - courant * (south_eta - eta))  3.35 us
    ppermute x2, starting transfers between devices, passed_along(): lax.ppermute(value, axis, [(source, source + steps) for source in range(i...  2.57 us
    broadcast_in_dim x2, other arithmetic, body(): return (eta[None], jnp.stack([mom_row, mom_col])[:, None])  2.28 us
    slice x2, local copies, waits for them, and re-layouts, body(): east_eta = jnp.concatenate([eta[:, 1:], east_col[:, None]], axis=1)  1.99 us
    ppermute x28, waiting for transfers between devices, from_all(): lax.ppermute(value, axes, [(source, source ^ turn) for source in range(co...  1.79 us
  transfers between devices with their start and end apart: 30, of which 7 were waited for; matrix products, arithmetic and copies ran while one was open for 7% of the time, Pallas kernels for 0%

profile of v1, /device:TPU:0, one launch (start us, length us, event | category | flops | bytes accessed | tf_op | source)
XLA Modules:
  0.0 75.8 jit_solution(950755373141925280)
XLA Ops:
  0.6 1.0 %copy.20 = f32[1,128,1024]{2,1,0:T(8,128)S(1)} copy(f32[1,128,1024]{2,1,0:T(8,128)} %param.13) | data formatting | bytes 1048576
  1.7 1.3 %collective-permute-start = (f32[1024]{0:T(1024)S(1)}, f32[1024]{0:T(1024)S(1)}, u32[]{:S(2)}, u32[]{:S(2)}) collective-permute-start(f32[1024]{0:T(1024)S(1)} %bitcast.66), channel_id=1, source_target_pairs={{2,0},{3,1},{6,4},{7,5},{10,8},{11,9},{14,12},{15,13},{18,16},{19,... | collective-permute-start | bytes 12296 | tf_op jit(solution)/shard_map/ppermute | solution.py:15
  3.0 0.7 copy-done.4
  3.7 3.8 %collective-permute-done = f32[1024]{0:T(1024)S(1)} collective-permute-done((f32[1024]{0:T(1024)S(1)}, f32[1024]{0:T(1024)S(1)}, u32[]{:S(2)}, u32[]{:S(2)}) %collective-permute-start) | collective-permute-done | bytes 4128 | tf_op jit(solution)/shard_map/ppermute | solution.py:15
  7.5 4.5 %gather_fusion = f32[1024]{0:T(1024)S(1)} fusion(f32[1024]{0:T(1024)S(1)} %collective-permute-done, s32[1024]{0:T(1024)S(1)} %fusion.22), kind=kCustom, calls=%fused_computation.clone | custom fusion | bytes 12288 | tf_op jit(solution)/shard_map/jit(_take)/gather | solution.py:58
  12.0 0.1 scatter-add.6
  12.1 0.1 slice_reduce_fusion.3
  12.3 3.1 %collective-permute-start.7 = (f32[1152]{0:T(1024)S(1)}, f32[1152]{0:T(1024)S(1)}, u32[]{:S(2)}, u32[]{:S(2)}) collective-permute-start(f32[1152]{0:T(1024)S(1)} %pad_maximum_fusion), channel_id=1, source_target_pairs={{0,13},{1,12},{4,9},{5,8},{8,5},{9,4},{12,1},{13,0},{2,15},{3,14},... | collective-permute-start | bytes 13832 | tf_op jit(solution)/shard_map/ppermute | solution.py:20
  15.4 1.8 %collective-permute-start.6 = (f32[1152]{0:T(1024)S(1)}, f32[1152]{0:T(1024)S(1)}, u32[]{:S(2)}, u32[]{:S(2)}) collective-permute-start(f32[1152]{0:T(1024)S(1)} %pad_maximum_fusion), channel_id=1, source_target_pairs={{0,12},{1,13},{4,8},{5,9},{8,4},{9,5},{12,0},{13,1},{2,14},{3,15},... | collective-permute-start | bytes 13832 | tf_op jit(solution)/shard_map/ppermute | solution.py:20
  17.2 0.7 constant_dynamic-slice_fusion
  17.8 0.4 collective-permute-start.5
  18.2 2.2 %collective-permute-start.4 = (f32[1152]{0:T(1024)S(1)}, f32[1152]{0:T(1024)S(1)}, u32[]{:S(2)}, u32[]{:S(2)}) collective-permute-start(f32[1152]{0:T(1024)S(1)} %pad_maximum_fusion), channel_id=1, source_target_pairs={{0,8},{1,9},{4,12},{5,13},{8,0},{9,1},{12,4},{13,5},{2,10},{3,11},... | collective-permute-start | bytes 13832 | tf_op jit(solution)/shard_map/ppermute | solution.py:20
  20.4 0.9 %collective-permute-start.3 = (f32[1152]{0:T(1024)S(1)}, f32[1152]{0:T(1024)S(1)}, u32[]{:S(2)}, u32[]{:S(2)}) collective-permute-start(f32[1152]{0:T(1024)S(1)} %pad_maximum_fusion), channel_id=1, source_target_pairs={{0,5},{1,4},{4,1},{5,0},{8,13},{9,12},{12,9},{13,8},{2,7},{3,6},{6... | collective-permute-start | bytes 13832 | tf_op jit(solution)/shard_map/ppermute | solution.py:20
  21.4 0.9 %collective-permute-start.2 = (f32[1152]{0:T(1024)S(1)}, f32[1152]{0:T(1024)S(1)}, u32[]{:S(2)}, u32[]{:S(2)}) collective-permute-start(f32[1152]{0:T(1024)S(1)} %pad_maximum_fusion), channel_id=1, source_target_pairs={{0,4},{1,5},{4,0},{5,1},{8,12},{9,13},{12,8},{13,9},{2,6},{3,7},{6... | collective-permute-start | bytes 13832 | tf_op jit(solution)/shard_map/ppermute | solution.py:20
  22.3 0.7 fusion.27
  25.7 1.0 %slice.169 = f32[128,1023]{1,0:T(8,128)} slice(f32[128,1024]{1,0:T(8,128)S(1)} %scatter-add.6), slice={[0:128], [1:1024]} | slice | bytes 1047552 | tf_op jit(solution)/shard_map/slice | solution.py:68
  26.9 0.1 stack.125
  26.9 0.1 fusion.26
  27.0 0.1 copy.13
  27.2 1.8 %fusion.5 = (f32[128,1024]{1,0:T(8,128)S(1)}, f32[128,1024]{1,0:T(8,128)S(1)}) fusion(f32[128,1024]{1,0:T(8,128)S(1)} %scatter-add.6, f32[1,1024]{1,0:T(1,128)S(1)} %dynamic-slice_multiply_fusion.3, f32[127,1024]{1,0:T(8,128)S(1)} %slice.171, f32[2,1,128,1024]{3,2,1,0:T(8,128)} %param.14, s32[1,128,1024]{2,1,0:T(8,128)S(1)} %copy-done.1, ...), kind=kLoop, calls=%fused_computation.10 | loop fusion | flops 1441792 | bytes 4194304 | tf_op jit(solution)/shard_map/mul | solution.py:71
  29.0 0.2 slice_reduce_fusion.2
  29.2 3.2 %collective-permute-start.14 = (f32[1152]{0:T(1024)S(1)}, f32[1152]{0:T(1024)S(1)}, u32[]{:S(2)}, u32[]{:S(2)}) collective-permute-start(f32[1152]{0:T(1024)S(1)} %pad_maximum_fusion.1), channel_id=1, source_target_pairs={{0,13},{1,12},{4,9},{5,8},{8,5},{9,4},{12,1},{13,0},{2,15},{3,14},... | collective-permute-start | bytes 13832 | tf_op jit(solution)/shard_map/ppermute | solution.py:20
  32.4 0.7 collective-permute-start.13
  33.1 2.3 %collective-permute-start.11 = (f32[1152]{0:T(1024)S(1)}, f32[1152]{0:T(1024)S(1)}, u32[]{:S(2)}, u32[]{:S(2)}) collective-permute-start(f32[1152]{0:T(1024)S(1)} %pad_maximum_fusion.1), channel_id=1, source_target_pairs={{0,8},{1,9},{4,12},{5,13},{8,0},{9,1},{12,4},{13,5},{2,10},{3,11},... | collective-permute-start | bytes 13832 | tf_op jit(solution)/shard_map/ppermute | solution.py:20
  35.5 1.0 %collective-permute-start.10 = (f32[1152]{0:T(1024)S(1)}, f32[1152]{0:T(1024)S(1)}, u32[]{:S(2)}, u32[]{:S(2)}) collective-permute-start(f32[1152]{0:T(1024)S(1)} %pad_maximum_fusion.1), channel_id=1, source_target_pairs={{0,5},{1,4},{4,1},{5,0},{8,13},{9,12},{12,9},{13,8},{2,7},{3,6},{6... | collective-permute-start | bytes 13832 | tf_op jit(solution)/shard_map/ppermute | solution.py:20
  36.5 1.0 %collective-permute-start.9 = (f32[1152]{0:T(1024)S(1)}, f32[1152]{0:T(1024)S(1)}, u32[]{:S(2)}, u32[]{:S(2)}) collective-permute-start(f32[1152]{0:T(1024)S(1)} %pad_maximum_fusion.1), channel_id=1, source_target_pairs={{0,4},{1,5},{4,0},{5,1},{8,12},{9,13},{12,8},{13,9},{2,6},{3,7},{6... | collective-permute-start | bytes 13832 | tf_op jit(solution)/shard_map/ppermute | solution.py:20
  37.5 0.3 collective-permute-done.13
  40.7 0.1 fusion.25
  40.8 0.1 copy.14
  41.0 0.4 fusion.9
  41.4 1.3 %collective-permute-start.15 = (f32[1024]{0:T(1024)S(1)}, f32[1024]{0:T(1024)S(1)}, u32[]{:S(2)}, u32[]{:S(2)}) collective-permute-start(f32[1024]{0:T(1024)S(1)} %bitcast.68), channel_id=1, source_target_pairs={{2,0},{3,1},{6,4},{7,5},{10,8},{11,9},{14,12},{15,13},{18,16},{19,... | collective-permute-start | bytes 12296 | tf_op jit(solution)/shard_map/ppermute | solution.py:15
  42.7 4.2 %collective-permute-done.15 = f32[1024]{0:T(1024)S(1)} collective-permute-done((f32[1024]{0:T(1024)S(1)}, f32[1024]{0:T(1024)S(1)}, u32[]{:S(2)}, u32[]{:S(2)}) %collective-permute-start.15) | collective-permute-done | bytes 4128 | tf_op jit(solution)/shard_map/ppermute | solution.py:15
  46.9 4.5 %gather_fusion.1 = f32[1024]{0:T(1024)S(1)} fusion(f32[1024]{0:T(1024)S(1)} %collective-permute-done.15, s32[1024]{0:T(1024)S(1)} %fusion.22), kind=kCustom, calls=%fused_computation.1.clone | custom fusion | bytes 12288 | tf_op jit(solution)/shard_map/jit(_take)/gather | solution.py:58
  51.4 0.1 scatter-add.9
  51.5 0.1 slice_reduce_fusion.1
  51.7 1.8 %collective-permute-start.22 = (f32[1152]{0:T(1024)S(1)}, f32[1152]{0:T(1024)S(1)}, u32[]{:S(2)}, u32[]{:S(2)}) collective-permute-start(f32[1152]{0:T(1024)S(1)} %pad_maximum_fusion.2), channel_id=1, source_target_pairs={{0,13},{1,12},{4,9},{5,8},{8,5},{9,4},{12,1},{13,0},{2,15},{3,14},... | collective-permute-start | bytes 13832 | tf_op jit(solution)/shard_map/ppermute | solution.py:20
  53.5 1.3 %collective-permute-start.21 = (f32[1152]{0:T(1024)S(1)}, f32[1152]{0:T(1024)S(1)}, u32[]{:S(2)}, u32[]{:S(2)}) collective-permute-start(f32[1152]{0:T(1024)S(1)} %pad_maximum_fusion.2), channel_id=1, source_target_pairs={{0,12},{1,13},{4,8},{5,9},{8,4},{9,5},{12,0},{13,1},{2,14},{3,15},... | collective-permute-start | bytes 13832 | tf_op jit(solution)/shard_map/ppermute | solution.py:20
  54.8 0.5 collective-permute-start.20
  55.3 2.6 %collective-permute-start.19 = (f32[1152]{0:T(1024)S(1)}, f32[1152]{0:T(1024)S(1)}, u32[]{:S(2)}, u32[]{:S(2)}) collective-permute-start(f32[1152]{0:T(1024)S(1)} %pad_maximum_fusion.2), channel_id=1, source_target_pairs={{0,8},{1,9},{4,12},{5,13},{8,0},{9,1},{12,4},{13,5},{2,10},{3,11},... | collective-permute-start | bytes 13832 | tf_op jit(solution)/shard_map/ppermute | solution.py:20
  57.9 0.4 collective-permute-start.18
  58.3 0.9 %collective-permute-start.17 = (f32[1152]{0:T(1024)S(1)}, f32[1152]{0:T(1024)S(1)}, u32[]{:S(2)}, u32[]{:S(2)}) collective-permute-start(f32[1152]{0:T(1024)S(1)} %pad_maximum_fusion.2), channel_id=1, source_target_pairs={{0,4},{1,5},{4,0},{5,1},{8,12},{9,13},{12,8},{13,9},{2,6},{3,7},{6... | collective-permute-start | bytes 13832 | tf_op jit(solution)/shard_map/ppermute | solution.py:20
  59.2 0.6 collective-permute-start.16
  59.8 0.8 %slice.179 = f32[127,1024]{1,0:T(8,128)} slice(f32[128,1024]{1,0:T(8,128)S(1)} %scatter-add.9), slice={[1:128], [0:1024]} | slice | bytes 1040384 | tf_op jit(solution)/shard_map/slice | solution.py:69
  60.6 1.0 %slice.177 = f32[128,1023]{1,0:T(8,128)} slice(f32[128,1024]{1,0:T(8,128)S(1)} %scatter-add.9), slice={[0:128], [1:1024]} | slice | bytes 1047552 | tf_op jit(solution)/shard_map/slice | solution.py:68
  61.7 0.3 collective-permute-done.17
  62.0 0.1 stack.143
  62.1 0.1 fusion.24
  62.2 0.1 copy.15
  62.3 1.6 %fusion.15 = (f32[128,1024]{1,0:T(8,128)S(1)}, f32[128,1024]{1,0:T(8,128)S(1)}) fusion(f32[128,1024]{1,0:T(8,128)S(1)} %get-tuple-element.29, f32[128,1024]{1,0:T(8,128)S(1)} %scatter-add.9, f32[1,1024]{1,0:T(1,128)S(1)} %dynamic-slice_multiply_fusion.1, f32[127,1024]{1,0:T(8,128)} %slice.179, s32[1,128,1024]{2,1,0:T(8,128)S(1)} %copy-done.1, ...), kind=kLoop, calls=%fused_computation.24 | loop fusion | flops 1441792 | bytes 4194304 | tf_op jit(solution)/shard_map/mul | solution.py:71
  63.8 0.2 slice_reduce_fusion
  64.0 2.4 %collective-permute-start.29 = (f32[1152]{0:T(1024)S(1)}, f32[1152]{0:T(1024)S(1)}, u32[]{:S(2)}, u32[]{:S(2)}) collective-permute-start(f32[1152]{0:T(1024)S(1)} %pad_maximum_fusion.3), channel_id=1, source_target_pairs={{0,13},{1,12},{4,9},{5,8},{8,5},{9,4},{12,1},{13,0},{2,15},{3,14},... | collective-permute-start | bytes 13832 | tf_op jit(solution)/shard_map/ppermute | solution.py:20
  66.5 0.8 %collective-permute-start.28 = (f32[1152]{0:T(1024)S(1)}, f32[1152]{0:T(1024)S(1)}, u32[]{:S(2)}, u32[]{:S(2)}) collective-permute-start(f32[1152]{0:T(1024)S(1)} %pad_maximum_fusion.3), channel_id=1, source_target_pairs={{0,12},{1,13},{4,8},{5,9},{8,4},{9,5},{12,0},{13,1},{2,14},{3,15},... | collective-permute-start | bytes 13832 | tf_op jit(solution)/shard_map/ppermute | solution.py:20
  67.3 0.2 collective-permute-start.27
  67.5 2.8 %collective-permute-start.26 = (f32[1152]{0:T(1024)S(1)}, f32[1152]{0:T(1024)S(1)}, u32[]{:S(2)}, u32[]{:S(2)}) collective-permute-start(f32[1152]{0:T(1024)S(1)} %pad_maximum_fusion.3), channel_id=1, source_target_pairs={{0,8},{1,9},{4,12},{5,13},{8,0},{9,1},{12,4},{13,5},{2,10},{3,11},... | collective-permute-start | bytes 13832 | tf_op jit(solution)/shard_map/ppermute | solution.py:20
  70.3 0.3 collective-permute-start.25
  70.6 1.1 %collective-permute-start.24 = (f32[1152]{0:T(1024)S(1)}, f32[1152]{0:T(1024)S(1)}, u32[]{:S(2)}, u32[]{:S(2)}) collective-permute-start(f32[1152]{0:T(1024)S(1)} %pad_maximum_fusion.3), channel_id=1, source_target_pairs={{0,4},{1,5},{4,0},{5,1},{8,12},{9,13},{12,8},{13,9},{2,6},{3,7},{6... | collective-permute-start | bytes 13832 | tf_op jit(solution)/shard_map/ppermute | solution.py:20
  71.7 0.2 collective-permute-done.28
  71.9 0.2 collective-permute-start.23
  72.2 1.1 %maximum_bitcast_fusion = f32[2,1,128,1024]{3,2,1,0:T(8,128)} fusion(f32[1,128,1024]{2,1,0:T(8,128)S(1)} %bitcast.55, f32[1,128,1024]{2,1,0:T(8,128)S(1)} %bitcast.52), kind=kLoop, calls=%fused_computation.2 | loop fusion | flops 262144 | bytes 2097152 | tf_op jit(solution)/shard_map/broadcast_in_dim | solution.py:82
  73.3 0.1 collective-permute-done.25
  73.4 0.8 %collective-permute-done.24 = f32[1152]{0:T(1024)S(1)} collective-permute-done((f32[1152]{0:T(1024)S(1)}, f32[1152]{0:T(1024)S(1)}, u32[]{:S(2)}, u32[]{:S(2)}) %collective-permute-start.24) | collective-permute-done | bytes 4640 | tf_op jit(solution)/shard_map/ppermute | solution.py:20
  74.3 0.1 fusion.23
  74.4 0.1 copy.16
  74.5 1.2 %fusion.20 = f32[1,128,1024]{2,1,0:T(8,128)} fusion(f32[128,1024]{1,0:T(8,128)S(1)} %scatter-add.9, f32[128,1024]{1,0:T(8,128)S(1)} %get-tuple-element.32, f32[128,1023]{1,0:T(8,128)S(1)} %bitcast.53, f32[128,1]{1,0:T(8,128)S(1)} %copy.16, f32[128,1024]{1,0:T(8,128)S(1)} %get-tuple-element.31, f32[127,1024]{1,0:T(8,128)S(1)} %bitcast.56, ...), kind=kLoop, calls=%fused_computation.30 | loop fusion | flops 1310720 | bytes 4194304 | tf_op jit(solution)/shard_map/broadcast_in_dim | solution.py:82
  (88 shorter events, 0.6 us)
Async XLA Ops:
  0.6 2.4 %copy-start = (s32[2,1024]{1,0:T(2,128)S(1)}, s32[2,1024]{1,0:T(2,128)}, u32[]{:S(2)}) copy-start(s32[2,1024]{1,0:T(2,128)} %param.19) | copy-start | bytes 24580
  1.7 5.8 %collective-permute-start = (f32[1024]{0:T(1024)S(1)}, f32[1024]{0:T(1024)S(1)}, u32[]{:S(2)}, u32[]{:S(2)}) collective-permute-start(f32[1024]{0:T(1024)S(1)} %bitcast.66), channel_id=1, source_target_pairs={{2,0},{3,1},{6,4},{7,5},{10,8},{11,9},{14,12},{15,13},{18,16},{19,... | collective-permute-start | bytes 12296 | tf_op jit(solution)/shard_map/ppermute | solution.py:15
  3.0 0.7 copy-start.4
  12.3 9.1 %collective-permute-start.7 = (f32[1152]{0:T(1024)S(1)}, f32[1152]{0:T(1024)S(1)}, u32[]{:S(2)}, u32[]{:S(2)}) collective-permute-start(f32[1152]{0:T(1024)S(1)} %pad_maximum_fusion), channel_id=1, source_target_pairs={{0,13},{1,12},{4,9},{5,8},{8,5},{9,4},{12,1},{13,0},{2,15},{3,14},... | collective-permute-start | bytes 13832 | tf_op jit(solution)/shard_map/ppermute | solution.py:20
  15.4 6.9 %collective-permute-start.6 = (f32[1152]{0:T(1024)S(1)}, f32[1152]{0:T(1024)S(1)}, u32[]{:S(2)}, u32[]{:S(2)}) collective-permute-start(f32[1152]{0:T(1024)S(1)} %pad_maximum_fusion), channel_id=1, source_target_pairs={{0,12},{1,13},{4,8},{5,9},{8,4},{9,5},{12,0},{13,1},{2,14},{3,15},... | collective-permute-start | bytes 13832 | tf_op jit(solution)/shard_map/ppermute | solution.py:20
  17.8 8.9 %collective-permute-start.5 = (f32[1152]{0:T(1024)S(1)}, f32[1152]{0:T(1024)S(1)}, u32[]{:S(2)}, u32[]{:S(2)}) collective-permute-start(f32[1152]{0:T(1024)S(1)} %pad_maximum_fusion), channel_id=1, source_target_pairs={{0,9},{1,8},{4,13},{5,12},{8,1},{9,0},{12,5},{13,4},{2,11},{3,10},... | collective-permute-start | bytes 13832 | tf_op jit(solution)/shard_map/ppermute | solution.py:20
  18.2 8.5 %collective-permute-start.4 = (f32[1152]{0:T(1024)S(1)}, f32[1152]{0:T(1024)S(1)}, u32[]{:S(2)}, u32[]{:S(2)}) collective-permute-start(f32[1152]{0:T(1024)S(1)} %pad_maximum_fusion), channel_id=1, source_target_pairs={{0,8},{1,9},{4,12},{5,13},{8,0},{9,1},{12,4},{13,5},{2,10},{3,11},... | collective-permute-start | bytes 13832 | tf_op jit(solution)/shard_map/ppermute | solution.py:20
  20.4 6.4 %collective-permute-start.3 = (f32[1152]{0:T(1024)S(1)}, f32[1152]{0:T(1024)S(1)}, u32[]{:S(2)}, u32[]{:S(2)}) collective-permute-start(f32[1152]{0:T(1024)S(1)} %pad_maximum_fusion), channel_id=1, source_target_pairs={{0,5},{1,4},{4,1},{5,0},{8,13},{9,12},{12,9},{13,8},{2,7},{3,6},{6... | collective-permute-start | bytes 13832 | tf_op jit(solution)/shard_map/ppermute | solution.py:20
  21.4 5.5 %collective-permute-start.2 = (f32[1152]{0:T(1024)S(1)}, f32[1152]{0:T(1024)S(1)}, u32[]{:S(2)}, u32[]{:S(2)}) collective-permute-start(f32[1152]{0:T(1024)S(1)} %pad_maximum_fusion), channel_id=1, source_target_pairs={{0,4},{1,5},{4,0},{5,1},{8,12},{9,13},{12,8},{13,9},{2,6},{3,7},{6... | collective-permute-start | bytes 13832 | tf_op jit(solution)/shard_map/ppermute | solution.py:20
  22.2 4.6 %collective-permute-start.1 = (f32[1152]{0:T(1024)S(1)}, f32[1152]{0:T(1024)S(1)}, u32[]{:S(2)}, u32[]{:S(2)}) collective-permute-start(f32[1152]{0:T(1024)S(1)} %pad_maximum_fusion), channel_id=1, source_target_pairs={{0,1},{1,0},{4,5},{5,4},{8,9},{9,8},{12,13},{13,12},{2,3},{3,2},{6... | collective-permute-start | bytes 13832 | tf_op jit(solution)/shard_map/ppermute | solution.py:20
  25.7 1.4 %copy-start.1 = (s32[1,128,1024]{2,1,0:T(8,128)S(1)}, s32[1,128,1024]{2,1,0:T(8,128)}, u32[]{:S(2)}) copy-start(s32[1,128,1024]{2,1,0:T(8,128)} %param.16) | copy-start | bytes 1572868
  27.2 13.8 %copy-start.2 = (f32[1,128,1024]{2,1,0:T(8,128)S(1)}, f32[1,128,1024]{2,1,0:T(8,128)}, u32[]{:S(2)}) copy-start(f32[1,128,1024]{2,1,0:T(8,128)} %param.15) | copy-start | bytes 1572868
  29.2 7.3 %collective-permute-start.14 = (f32[1152]{0:T(1024)S(1)}, f32[1152]{0:T(1024)S(1)}, u32[]{:S(2)}, u32[]{:S(2)}) collective-permute-start(f32[1152]{0:T(1024)S(1)} %pad_maximum_fusion.1), channel_id=1, source_target_pairs={{0,13},{1,12},{4,9},{5,8},{8,5},{9,4},{12,1},{13,0},{2,15},{3,14},... | collective-permute-start | bytes 13832 | tf_op jit(solution)/shard_map/ppermute | solution.py:20
  32.4 5.4 %collective-permute-start.13 = (f32[1152]{0:T(1024)S(1)}, f32[1152]{0:T(1024)S(1)}, u32[]{:S(2)}, u32[]{:S(2)}) collective-permute-start(f32[1152]{0:T(1024)S(1)} %pad_maximum_fusion.1), channel_id=1, source_target_pairs={{0,12},{1,13},{4,8},{5,9},{8,4},{9,5},{12,0},{13,1},{2,14},{3,15},... | collective-permute-start | bytes 13832 | tf_op jit(solution)/shard_map/ppermute | solution.py:20
  33.1 7.4 %collective-permute-start.12 = (f32[1152]{0:T(1024)S(1)}, f32[1152]{0:T(1024)S(1)}, u32[]{:S(2)}, u32[]{:S(2)}) collective-permute-start(f32[1152]{0:T(1024)S(1)} %pad_maximum_fusion.1), channel_id=1, source_target_pairs={{0,9},{1,8},{4,13},{5,12},{8,1},{9,0},{12,5},{13,4},{2,11},{3,10},... | collective-permute-start | bytes 13832 | tf_op jit(solution)/shard_map/ppermute | solution.py:20
  33.1 7.4 %collective-permute-start.11 = (f32[1152]{0:T(1024)S(1)}, f32[1152]{0:T(1024)S(1)}, u32[]{:S(2)}, u32[]{:S(2)}) collective-permute-start(f32[1152]{0:T(1024)S(1)} %pad_maximum_fusion.1), channel_id=1, source_target_pairs={{0,8},{1,9},{4,12},{5,13},{8,0},{9,1},{12,4},{13,5},{2,10},{3,11},... | collective-permute-start | bytes 13832 | tf_op jit(solution)/shard_map/ppermute | solution.py:20
  35.5 5.1 %collective-permute-start.10 = (f32[1152]{0:T(1024)S(1)}, f32[1152]{0:T(1024)S(1)}, u32[]{:S(2)}, u32[]{:S(2)}) collective-permute-start(f32[1152]{0:T(1024)S(1)} %pad_maximum_fusion.1), channel_id=1, source_target_pairs={{0,5},{1,4},{4,1},{5,0},{8,13},{9,12},{12,9},{13,8},{2,7},{3,6},{6... | collective-permute-start | bytes 13832 | tf_op jit(solution)/shard_map/ppermute | solution.py:20
  36.5 4.1 %collective-permute-start.9 = (f32[1152]{0:T(1024)S(1)}, f32[1152]{0:T(1024)S(1)}, u32[]{:S(2)}, u32[]{:S(2)}) collective-permute-start(f32[1152]{0:T(1024)S(1)} %pad_maximum_fusion.1), channel_id=1, source_target_pairs={{0,4},{1,5},{4,0},{5,1},{8,12},{9,13},{12,8},{13,9},{2,6},{3,7},{6... | collective-permute-start | bytes 13832 | tf_op jit(solution)/shard_map/ppermute | solution.py:20
  37.8 2.8 %collective-permute-start.8 = (f32[1152]{0:T(1024)S(1)}, f32[1152]{0:T(1024)S(1)}, u32[]{:S(2)}, u32[]{:S(2)}) collective-permute-start(f32[1152]{0:T(1024)S(1)} %pad_maximum_fusion.1), channel_id=1, source_target_pairs={{0,1},{1,0},{4,5},{5,4},{8,9},{9,8},{12,13},{13,12},{2,3},{3,2},{6... | collective-permute-start | bytes 13832 | tf_op jit(solution)/shard_map/ppermute | solution.py:20
  41.4 5.5 %collective-permute-start.15 = (f32[1024]{0:T(1024)S(1)}, f32[1024]{0:T(1024)S(1)}, u32[]{:S(2)}, u32[]{:S(2)}) collective-permute-start(f32[1024]{0:T(1024)S(1)} %bitcast.68), channel_id=1, source_target_pairs={{2,0},{3,1},{6,4},{7,5},{10,8},{11,9},{14,12},{15,13},{18,16},{19,... | collective-permute-start | bytes 12296 | tf_op jit(solution)/shard_map/ppermute | solution.py:15
  51.7 6.6 %collective-permute-start.22 = (f32[1152]{0:T(1024)S(1)}, f32[1152]{0:T(1024)S(1)}, u32[]{:S(2)}, u32[]{:S(2)}) collective-permute-start(f32[1152]{0:T(1024)S(1)} %pad_maximum_fusion.2), channel_id=1, source_target_pairs={{0,13},{1,12},{4,9},{5,8},{8,5},{9,4},{12,1},{13,0},{2,15},{3,14},... | collective-permute-start | bytes 13832 | tf_op jit(solution)/shard_map/ppermute | solution.py:20
  53.5 5.7 %collective-permute-start.21 = (f32[1152]{0:T(1024)S(1)}, f32[1152]{0:T(1024)S(1)}, u32[]{:S(2)}, u32[]{:S(2)}) collective-permute-start(f32[1152]{0:T(1024)S(1)} %pad_maximum_fusion.2), channel_id=1, source_target_pairs={{0,12},{1,13},{4,8},{5,9},{8,4},{9,5},{12,0},{13,1},{2,14},{3,15},... | collective-permute-start | bytes 13832 | tf_op jit(solution)/shard_map/ppermute | solution.py:20
  54.8 6.8 %collective-permute-start.20 = (f32[1152]{0:T(1024)S(1)}, f32[1152]{0:T(1024)S(1)}, u32[]{:S(2)}, u32[]{:S(2)}) collective-permute-start(f32[1152]{0:T(1024)S(1)} %pad_maximum_fusion.2), channel_id=1, source_target_pairs={{0,9},{1,8},{4,13},{5,12},{8,1},{9,0},{12,5},{13,4},{2,11},{3,10},... | collective-permute-start | bytes 13832 | tf_op jit(solution)/shard_map/ppermute | solution.py:20
  55.3 6.3 %collective-permute-start.19 = (f32[1152]{0:T(1024)S(1)}, f32[1152]{0:T(1024)S(1)}, u32[]{:S(2)}, u32[]{:S(2)}) collective-permute-start(f32[1152]{0:T(1024)S(1)} %pad_maximum_fusion.2), channel_id=1, source_target_pairs={{0,8},{1,9},{4,12},{5,13},{8,0},{9,1},{12,4},{13,5},{2,10},{3,11},... | collective-permute-start | bytes 13832 | tf_op jit(solution)/shard_map/ppermute | solution.py:20
  57.9 3.8 %collective-permute-start.18 = (f32[1152]{0:T(1024)S(1)}, f32[1152]{0:T(1024)S(1)}, u32[]{:S(2)}, u32[]{:S(2)}) collective-permute-start(f32[1152]{0:T(1024)S(1)} %pad_maximum_fusion.2), channel_id=1, source_target_pairs={{0,5},{1,4},{4,1},{5,0},{8,13},{9,12},{12,9},{13,8},{2,7},{3,6},{6... | collective-permute-start | bytes 13832 | tf_op jit(solution)/shard_map/ppermute | solution.py:20
  58.3 3.7 %collective-permute-start.17 = (f32[1152]{0:T(1024)S(1)}, f32[1152]{0:T(1024)S(1)}, u32[]{:S(2)}, u32[]{:S(2)}) collective-permute-start(f32[1152]{0:T(1024)S(1)} %pad_maximum_fusion.2), channel_id=1, source_target_pairs={{0,4},{1,5},{4,0},{5,1},{8,12},{9,13},{12,8},{13,9},{2,6},{3,7},{6... | collective-permute-start | bytes 13832 | tf_op jit(solution)/shard_map/ppermute | solution.py:20
  59.2 2.8 %collective-permute-start.16 = (f32[1152]{0:T(1024)S(1)}, f32[1152]{0:T(1024)S(1)}, u32[]{:S(2)}, u32[]{:S(2)}) collective-permute-start(f32[1152]{0:T(1024)S(1)} %pad_maximum_fusion.2), channel_id=1, source_target_pairs={{0,1},{1,0},{4,5},{5,4},{8,9},{9,8},{12,13},{13,12},{2,3},{3,2},{6... | collective-permute-start | bytes 13832 | tf_op jit(solution)/shard_map/ppermute | solution.py:20
  64.0 6.5 %collective-permute-start.29 = (f32[1152]{0:T(1024)S(1)}, f32[1152]{0:T(1024)S(1)}, u32[]{:S(2)}, u32[]{:S(2)}) collective-permute-start(f32[1152]{0:T(1024)S(1)} %pad_maximum_fusion.3), channel_id=1, source_target_pairs={{0,13},{1,12},{4,9},{5,8},{8,5},{9,4},{12,1},{13,0},{2,15},{3,14},... | collective-permute-start | bytes 13832 | tf_op jit(solution)/shard_map/ppermute | solution.py:20
  66.5 5.5 %collective-permute-start.28 = (f32[1152]{0:T(1024)S(1)}, f32[1152]{0:T(1024)S(1)}, u32[]{:S(2)}, u32[]{:S(2)}) collective-permute-start(f32[1152]{0:T(1024)S(1)} %pad_maximum_fusion.3), channel_id=1, source_target_pairs={{0,12},{1,13},{4,8},{5,9},{8,4},{9,5},{12,0},{13,1},{2,14},{3,15},... | collective-permute-start | bytes 13832 | tf_op jit(solution)/shard_map/ppermute | solution.py:20
  67.3 6.0 %collective-permute-start.27 = (f32[1152]{0:T(1024)S(1)}, f32[1152]{0:T(1024)S(1)}, u32[]{:S(2)}, u32[]{:S(2)}) collective-permute-start(f32[1152]{0:T(1024)S(1)} %pad_maximum_fusion.3), channel_id=1, source_target_pairs={{0,9},{1,8},{4,13},{5,12},{8,1},{9,0},{12,5},{13,4},{2,11},{3,10},... | collective-permute-start | bytes 13832 | tf_op jit(solution)/shard_map/ppermute | solution.py:20
  67.5 5.8 %collective-permute-start.26 = (f32[1152]{0:T(1024)S(1)}, f32[1152]{0:T(1024)S(1)}, u32[]{:S(2)}, u32[]{:S(2)}) collective-permute-start(f32[1152]{0:T(1024)S(1)} %pad_maximum_fusion.3), channel_id=1, source_target_pairs={{0,8},{1,9},{4,12},{5,13},{8,0},{9,1},{12,4},{13,5},{2,10},{3,11},... | collective-permute-start | bytes 13832 | tf_op jit(solution)/shard_map/ppermute | solution.py:20
  70.3 3.1 %collective-permute-start.25 = (f32[1152]{0:T(1024)S(1)}, f32[1152]{0:T(1024)S(1)}, u32[]{:S(2)}, u32[]{:S(2)}) collective-permute-start(f32[1152]{0:T(1024)S(1)} %pad_maximum_fusion.3), channel_id=1, source_target_pairs={{0,5},{1,4},{4,1},{5,0},{8,13},{9,12},{12,9},{13,8},{2,7},{3,6},{6... | collective-permute-start | bytes 13832 | tf_op jit(solution)/shard_map/ppermute | solution.py:20
  70.6 3.7 %collective-permute-start.24 = (f32[1152]{0:T(1024)S(1)}, f32[1152]{0:T(1024)S(1)}, u32[]{:S(2)}, u32[]{:S(2)}) collective-permute-start(f32[1152]{0:T(1024)S(1)} %pad_maximum_fusion.3), channel_id=1, source_target_pairs={{0,4},{1,5},{4,0},{5,1},{8,12},{9,13},{12,8},{13,9},{2,6},{3,7},{6... | collective-permute-start | bytes 13832 | tf_op jit(solution)/shard_map/ppermute | solution.py:20
  71.9 2.3 %collective-permute-start.23 = (f32[1152]{0:T(1024)S(1)}, f32[1152]{0:T(1024)S(1)}, u32[]{:S(2)}, u32[]{:S(2)}) collective-permute-start(f32[1152]{0:T(1024)S(1)} %pad_maximum_fusion.3), channel_id=1, source_target_pairs={{0,1},{1,0},{4,5},{5,4},{8,9},{9,8},{12,13},{13,12},{2,3},{3,2},{6... | collective-permute-start | bytes 13832 | tf_op jit(solution)/shard_map/ppermute | solution.py:20
  72.2 2.4 %copy-start.3 = (f32[1,128,1024]{2,1,0:T(8,128)S(1)}, f32[1,128,1024]{2,1,0:T(8,128)}, u32[]{:S(2)}) copy-start(f32[1,128,1024]{2,1,0:T(8,128)} %param.15) | copy-start | bytes 1572868

commit v2 on v1

--- a/solution.py
+++ b/solution.py
@@ -16,9 +16,8 @@
 
 
 def from_all(value, axes):
-    count = lax.axis_size(axes)
-    others = [lax.ppermute(value, axes, [(source, source ^ turn) for source in range(count)]) for turn in range(1, count)]
-    return jnp.stack([value] + others)
+    copies = jnp.broadcast_to(value, (lax.axis_size(axes),) + value.shape)
+    return lax.all_to_all(copies, axes, 0, 0, tiled=True)
 
 
 def pick_row(table, index):
@@ -61,10 +60,10 @@
         first_col = eta[:, 0]
         first_row = eta[0, :]
         edges = from_all(jnp.concatenate([first_row, first_col]), ("patch", "sub"))
-        east_col = pick_row(edges, own ^ (jnp.maximum(east, 0) * subs + half))[cols:] * has_east
+        east_col = pick_row(edges, jnp.maximum(east, 0) * subs + half)[cols:] * has_east
         across = jnp.where(half == subs - 1, jnp.maximum(south, 0) * subs, own + 1)
         keep = jnp.where(half == subs - 1, has_south, 1.0)
-        south_row = pick_row(edges, own ^ across)[:cols] * keep
+        south_row = pick_row(edges, across)[:cols] * keep
         east_eta = jnp.concatenate([eta[:, 1:], east_col[:, None]], axis=1)
         south_eta = jnp.concatenate([eta[1:], south_row[None]], axis=0)
         mom_row = wet * (mom_row - courant * (east_eta - eta))
@@ -72,10 +71,10 @@
         last_col = mom_row[:, -1]
         last_row = mom_col[-1, :]
         edges = from_all(jnp.concatenate([last_row, last_col]), ("patch", "sub"))
-        west_col = pick_row(edges, own ^ (jnp.maximum(west, 0) * subs + half))[cols:] * has_west
+        west_col = pick_row(edges, jnp.maximum(west, 0) * subs + half)[cols:] * has_west
         across = jnp.where(half == 0, jnp.maximum(north, 0) * subs + subs - 1, own - 1)
         keep = jnp.where(half == 0, has_north, 1.0)
-        north_row = pick_row(edges, own ^ across)[:cols] * keep
+        north_row = pick_row(edges, across)[:cols] * keep
         west_row = jnp.concatenate([west_col[:, None], mom_row[:, :-1]], axis=1)
         north_col = jnp.concatenate([north_row[None], mom_col[:-1]], axis=0)
         eta = wet * (eta - courant * height * (mom_row - west_row + (mom_col - north_col)))

time: 76.1 us -> 70.9 us (0.932)
  starting transfers between devices: 36.3 us -> 18.7 us
  waiting for transfers between devices: 9.76 us -> 20.6 us
  local copies, waits for them, and re-layouts: 16.7 us -> 18.8 us
    ppermute x28 -> x0, starting transfers between devices: 33.7 us -> none  [from_all(): lax.ppermute(value, axes, [(source, source ^ turn) for source in range(co...]
    all_to_all x0 -> x4, starting transfers between devices: none -> 16.2 us  [from_all(): return lax.all_to_all(copies, axes, 0, 0, tiled=True)]
    all_to_all x0 -> x4, waiting for transfers between devices: none -> 13.3 us  [from_all(): return lax.all_to_all(copies, axes, 0, 0, tiled=True)]
    broadcast_in_dim x0 -> x4, local copies, waits for them, and re-layouts: none -> 2.54 us  [from_all(): copies = jnp.broadcast_to(value, (lax.axis_size(axes),) + value.shape)]
    ppermute x28 -> x0, waiting for transfers between devices: 1.79 us -> none  [from_all(): lax.ppermute(value, axes, [(source, source ^ turn) for source in range(co...]
  transfers between devices with their start and end apart: 30 -> 6, of which waited for: 7 -> 6; matrix products, arithmetic and copies ran while one was open for 7% -> 7% of each run, Pallas kernels for 0% -> 0%
where the time goes in v2:
time: 70.9 us; the launch traced here: 70.3 us
  waiting for transfers between devices  20.6 us (29%)
  local copies, waits for them, and re-layouts  18.8 us (27%)
  starting transfers between devices  18.7 us (26%)
  other arithmetic  6.2 us (9%)
  between operations  5.92 us (8%)
    all_to_all x4, starting transfers between devices, from_all(): return lax.all_to_all(copies, axes, 0, 0, tiled=True)  16.2 us
    all_to_all x4, waiting for transfers between devices, from_all(): return lax.all_to_all(copies, axes, 0, 0, tiled=True)  13.3 us
    gather x2, local copies, waits for them, and re-layouts, body(): inflow = own_gain * jnp.take(received, own_table)  9.04 us
    ppermute x2, waiting for transfers between devices, passed_along(): lax.ppermute(value, axis, [(source, source + steps) for source in range(i...  7.27 us
    mul x2, other arithmetic, body(): mom_col = wet * (mom_col - courant * (south_eta - eta))  3.43 us
    ppermute x2, starting transfers between devices, passed_along(): lax.ppermute(value, axis, [(source, source + steps) for source in range(i...  2.57 us
    broadcast_in_dim x4, local copies, waits for them, and re-layouts, from_all(): copies = jnp.broadcast_to(value, (lax.axis_size(axes),) + value.shape)  2.54 us
    broadcast_in_dim x2, other arithmetic, body(): return (eta[None], jnp.stack([mom_row, mom_col])[:, None])  2.28 us
  transfers between devices with their start and end apart: 6, of which 6 were waited for; matrix products, arithmetic and copies ran while one was open for 7% of the time, Pallas kernels for 0%

profile of v2, /device:TPU:0, one launch (start us, length us, event | category | flops | bytes accessed | tf_op | source)
XLA Modules:
  0.0 70.3 jit_solution(3261579913762230143)
XLA Ops:
  0.6 0.0 copy-start
  0.6 1.0 %copy.20 = f32[1,128,1024]{2,1,0:T(8,128)S(1)} copy(f32[1,128,1024]{2,1,0:T(8,128)} %param.13) | data formatting | bytes 1048576
  1.7 1.3 %collective-permute-start = (f32[1024]{0:T(1024)S(1)}, f32[1024]{0:T(1024)S(1)}, u32[]{:S(2)}, u32[]{:S(2)}) collective-permute-start(f32[1024]{0:T(1024)S(1)} %bitcast.82), channel_id=1, source_target_pairs={{2,0},{3,1},{6,4},{7,5},{10,8},{11,9},{14,12},{15,13},{18,16},{19,... | collective-permute-start | bytes 12296 | tf_op jit(solution)/shard_map/ppermute | solution.py:15
  3.0 0.0 copy-start.4
  3.0 0.0 copy-done
  3.0 0.7 copy-done.4
  3.7 0.7 constant_dynamic-slice_fusion
  4.4 3.1 %collective-permute-done = f32[1024]{0:T(1024)S(1)} collective-permute-done((f32[1024]{0:T(1024)S(1)}, f32[1024]{0:T(1024)S(1)}, u32[]{:S(2)}, u32[]{:S(2)}) %collective-permute-start) | collective-permute-done | bytes 4128 | tf_op jit(solution)/shard_map/ppermute | solution.py:15
  7.5 4.5 %gather_fusion = f32[1024]{0:T(1024)S(1)} fusion(f32[1024]{0:T(1024)S(1)} %collective-permute-done, s32[1024]{0:T(1024)S(1)} %fusion.22), kind=kCustom, calls=%fused_computation.clone | custom fusion | bytes 12288 | tf_op jit(solution)/shard_map/jit(_take)/gather | solution.py:57
  12.0 0.1 scatter-add.6
  12.1 0.1 slice_reduce_fusion.3
  12.3 0.6 broadcast_in_dim.32
  12.9 6.0 %all-to-all-start = ((f32[8,1,1152]{2,1,0:T(1,128)}), f32[8,1,1152]{2,1,0:T(1,128)S(1)}, u32[]{:S(2)}, u32[]{:S(2)}) async-start(f32[8,1,1152]{2,1,0:T(1,128)} %broadcast_in_dim.32), calls=%async_computation | async-start | bytes 73728 | tf_op jit(solution)/shard_map/all_to_all | solution.py:20
  18.9 0.6 fusion.27
  22.0 0.0 copy-start.1
  22.1 1.0 %slice.169 = f32[128,1023]{1,0:T(8,128)} slice(f32[128,1024]{1,0:T(8,128)S(1)} %scatter-add.6), slice={[0:128], [1:1024]} | slice | bytes 1047552 | tf_op jit(solution)/shard_map/slice | solution.py:67
  23.1 1.6 %all-to-all-done = f32[8,1,1152]{2,1,0:T(1,128)S(1)} async-done(((f32[8,1,1152]{2,1,0:T(1,128)}), f32[8,1,1152]{2,1,0:T(1,128)S(1)}, u32[]{:S(2)}, u32[]{:S(2)}) %all-to-all-start) | async-done | bytes 36896 | tf_op jit(solution)/shard_map/all_to_all | solution.py:20
  24.7 0.1 copy.13
  24.8 0.0 copy-done.1
  24.8 0.0 copy-start.2
  24.9 1.9 %fusion.5 = (f32[128,1024]{1,0:T(8,128)S(1)}, f32[128,1024]{1,0:T(8,128)S(1)}) fusion(f32[128,1024]{1,0:T(8,128)S(1)} %scatter-add.6, f32[1,1024]{1,0:T(1,128)S(1)} %slice_multiply_fusion.3, f32[127,1024]{1,0:T(8,128)S(1)} %slice.172, f32[2,1,128,1024]{3,2,1,0:T(8,128)} %param.14, s32[1,128,1024]{2,1,0:T(8,128)S(1)} %copy-done.1, f32[128,1]{1,0:T(8,128)S(1)} %copy.13, ...), kind=kLoop, calls=%fused_computation.10 | loop fusion | flops 1441792 | bytes 4194304 | tf_op jit(solution)/shard_map/mul | solution.py:70
  26.7 0.2 slice_reduce_fusion.2
  26.9 0.6 broadcast_in_dim.33
  27.6 3.5 %all-to-all-start.1 = ((f32[8,1,1152]{2,1,0:T(1,128)}), f32[8,1,1152]{2,1,0:T(1,128)S(1)}, u32[]{:S(2)}, u32[]{:S(2)}) async-start(f32[8,1,1152]{2,1,0:T(1,128)} %broadcast_in_dim.33), calls=%async_computation.1 | async-start | bytes 73728 | tf_op jit(solution)/shard_map/all_to_all | solution.py:20
  33.6 3.2 %all-to-all-done.1 = f32[8,1,1152]{2,1,0:T(1,128)S(1)} async-done(((f32[8,1,1152]{2,1,0:T(1,128)}), f32[8,1,1152]{2,1,0:T(1,128)S(1)}, u32[]{:S(2)}, u32[]{:S(2)}) %all-to-all-start.1) | async-done | bytes 36896 | tf_op jit(solution)/shard_map/all_to_all | solution.py:20
  36.8 0.1 copy.14
  36.9 0.0 copy-done.2
  36.9 0.4 fusion.9
  37.3 1.3 %collective-permute-start.1 = (f32[1024]{0:T(1024)S(1)}, f32[1024]{0:T(1024)S(1)}, u32[]{:S(2)}, u32[]{:S(2)}) collective-permute-start(f32[1024]{0:T(1024)S(1)} %bitcast.84), channel_id=1, source_target_pairs={{2,0},{3,1},{6,4},{7,5},{10,8},{11,9},{14,12},{15,13},{18,16},{19,... | collective-permute-start | bytes 12296 | tf_op jit(solution)/shard_map/ppermute | solution.py:15
  38.6 4.2 %collective-permute-done.1 = f32[1024]{0:T(1024)S(1)} collective-permute-done((f32[1024]{0:T(1024)S(1)}, f32[1024]{0:T(1024)S(1)}, u32[]{:S(2)}, u32[]{:S(2)}) %collective-permute-start.1) | collective-permute-done | bytes 4128 | tf_op jit(solution)/shard_map/ppermute | solution.py:15
  42.8 4.5 %gather_fusion.1 = f32[1024]{0:T(1024)S(1)} fusion(f32[1024]{0:T(1024)S(1)} %collective-permute-done.1, s32[1024]{0:T(1024)S(1)} %fusion.22), kind=kCustom, calls=%fused_computation.1.clone | custom fusion | bytes 12288 | tf_op jit(solution)/shard_map/jit(_take)/gather | solution.py:57
  47.4 0.1 scatter-add.9
  47.5 0.1 slice_reduce_fusion.1
  47.6 0.6 broadcast_in_dim.34
  48.3 3.3 %all-to-all-start.2 = ((f32[8,1,1152]{2,1,0:T(1,128)}), f32[8,1,1152]{2,1,0:T(1,128)S(1)}, u32[]{:S(2)}, u32[]{:S(2)}) async-start(f32[8,1,1152]{2,1,0:T(1,128)} %broadcast_in_dim.34), calls=%async_computation.2 | async-start | bytes 73728 | tf_op jit(solution)/shard_map/all_to_all | solution.py:20
  51.6 0.8 %slice.184 = f32[127,1024]{1,0:T(8,128)} slice(f32[128,1024]{1,0:T(8,128)S(1)} %scatter-add.9), slice={[1:128], [0:1024]} | slice | bytes 1040384 | tf_op jit(solution)/shard_map/slice | solution.py:68
  52.4 1.0 %slice.181 = f32[128,1023]{1,0:T(8,128)} slice(f32[128,1024]{1,0:T(8,128)S(1)} %scatter-add.9), slice={[0:128], [1:1024]} | slice | bytes 1047552 | tf_op jit(solution)/shard_map/slice | solution.py:67
  53.4 3.9 %all-to-all-done.2 = f32[8,1,1152]{2,1,0:T(1,128)S(1)} async-done(((f32[8,1,1152]{2,1,0:T(1,128)}), f32[8,1,1152]{2,1,0:T(1,128)S(1)}, u32[]{:S(2)}, u32[]{:S(2)}) %all-to-all-start.2) | async-done | bytes 36896 | tf_op jit(solution)/shard_map/all_to_all | solution.py:20
  57.3 0.1 copy.15
  57.4 1.6 %fusion.15 = (f32[128,1024]{1,0:T(8,128)S(1)}, f32[128,1024]{1,0:T(8,128)S(1)}) fusion(f32[128,1024]{1,0:T(8,128)S(1)} %get-tuple-element.29, f32[128,1024]{1,0:T(8,128)S(1)} %scatter-add.9, f32[1,1024]{1,0:T(1,128)S(1)} %slice_multiply_fusion.1, f32[127,1024]{1,0:T(8,128)} %slice.184, s32[1,128,1024]{2,1,0:T(8,128)S(1)} %copy-done.1, ...), kind=kLoop, calls=%fused_computation.24 | loop fusion | flops 1441792 | bytes 4194304 | tf_op jit(solution)/shard_map/mul | solution.py:70
  59.0 0.2 slice_reduce_fusion
  59.2 0.6 broadcast_in_dim.35
  59.9 3.3 %all-to-all-start.3 = ((f32[8,1,1152]{2,1,0:T(1,128)}), f32[8,1,1152]{2,1,0:T(1,128)S(1)}, u32[]{:S(2)}, u32[]{:S(2)}) async-start(f32[8,1,1152]{2,1,0:T(1,128)} %broadcast_in_dim.35), calls=%async_computation.3 | async-start | bytes 73728 | tf_op jit(solution)/shard_map/all_to_all | solution.py:20
  63.2 0.0 copy-start.3
  63.2 1.1 %maximum_bitcast_fusion = f32[2,1,128,1024]{3,2,1,0:T(8,128)} fusion(f32[1,128,1024]{2,1,0:T(8,128)S(1)} %bitcast.71, f32[1,128,1024]{2,1,0:T(8,128)S(1)} %bitcast.68), kind=kLoop, calls=%fused_computation.2 | loop fusion | flops 262144 | bytes 2097152 | tf_op jit(solution)/shard_map/broadcast_in_dim | solution.py:81
  64.3 4.6 %all-to-all-done.3 = f32[8,1,1152]{2,1,0:T(1,128)S(1)} async-done(((f32[8,1,1152]{2,1,0:T(1,128)}), f32[8,1,1152]{2,1,0:T(1,128)S(1)}, u32[]{:S(2)}, u32[]{:S(2)}) %all-to-all-start.3) | async-done | bytes 36896 | tf_op jit(solution)/shard_map/all_to_all | solution.py:20
  68.9 0.1 copy.16
  69.0 0.0 copy-done.3
  69.0 1.2 %fusion.20 = f32[1,128,1024]{2,1,0:T(8,128)} fusion(f32[128,1024]{1,0:T(8,128)S(1)} %scatter-add.9, f32[128,1024]{1,0:T(8,128)S(1)} %get-tuple-element.32, f32[128,1023]{1,0:T(8,128)S(1)} %bitcast.69, f32[128,1]{1,0:T(8,128)S(1)} %copy.16, f32[128,1024]{1,0:T(8,128)S(1)} %get-tuple-element.31, f32[127,1024]{1,0:T(8,128)S(1)} %bitcast.72, ...), kind=kLoop, calls=%fused_computation.30 | loop fusion | flops 1310720 | bytes 4194304 | tf_op jit(solution)/shard_map/broadcast_in_dim | solution.py:81
  (27 shorter events, 0.2 us)
Async XLA Ops:
  0.6 2.4 %copy-start = (f32[2,1024]{1,0:T(2,128)S(1)}, f32[2,1024]{1,0:T(2,128)}, u32[]{:S(2)}) copy-start(f32[2,1024]{1,0:T(2,128)} %param.18) | copy-start | bytes 24580
  1.7 5.8 %collective-permute-start = (f32[1024]{0:T(1024)S(1)}, f32[1024]{0:T(1024)S(1)}, u32[]{:S(2)}, u32[]{:S(2)}) collective-permute-start(f32[1024]{0:T(1024)S(1)} %bitcast.82), channel_id=1, source_target_pairs={{2,0},{3,1},{6,4},{7,5},{10,8},{11,9},{14,12},{15,13},{18,16},{19,... | collective-permute-start | bytes 12296 | tf_op jit(solution)/shard_map/ppermute | solution.py:15
  3.0 0.7 copy-start.4
  12.9 11.8 %all-to-all-start = ((f32[8,1,1152]{2,1,0:T(1,128)}), f32[8,1,1152]{2,1,0:T(1,128)S(1)}, u32[]{:S(2)}, u32[]{:S(2)}) async-start(f32[8,1,1152]{2,1,0:T(1,128)} %broadcast_in_dim.32), calls=%async_computation | async-start | bytes 73728 | tf_op jit(solution)/shard_map/all_to_all | solution.py:20
  22.0 2.8 %copy-start.1 = (s32[1,128,1024]{2,1,0:T(8,128)S(1)}, s32[1,128,1024]{2,1,0:T(8,128)}, u32[]{:S(2)}) copy-start(s32[1,128,1024]{2,1,0:T(8,128)} %param.16) | copy-start | bytes 1572868
  24.8 12.1 %copy-start.2 = (f32[1,128,1024]{2,1,0:T(8,128)S(1)}, f32[1,128,1024]{2,1,0:T(8,128)}, u32[]{:S(2)}) copy-start(f32[1,128,1024]{2,1,0:T(8,128)} %param.15) | copy-start | bytes 1572868
  27.6 9.2 %all-to-all-start.1 = ((f32[8,1,1152]{2,1,0:T(1,128)}), f32[8,1,1152]{2,1,0:T(1,128)S(1)}, u32[]{:S(2)}, u32[]{:S(2)}) async-start(f32[8,1,1152]{2,1,0:T(1,128)} %broadcast_in_dim.33), calls=%async_computation.1 | async-start | bytes 73728 | tf_op jit(solution)/shard_map/all_to_all | solution.py:20
  37.3 5.5 %collective-permute-start.1 = (f32[1024]{0:T(1024)S(1)}, f32[1024]{0:T(1024)S(1)}, u32[]{:S(2)}, u32[]{:S(2)}) collective-permute-start(f32[1024]{0:T(1024)S(1)} %bitcast.84), channel_id=1, source_target_pairs={{2,0},{3,1},{6,4},{7,5},{10,8},{11,9},{14,12},{15,13},{18,16},{19,... | collective-permute-start | bytes 12296 | tf_op jit(solution)/shard_map/ppermute | solution.py:15
  48.3 9.0 %all-to-all-start.2 = ((f32[8,1,1152]{2,1,0:T(1,128)}), f32[8,1,1152]{2,1,0:T(1,128)S(1)}, u32[]{:S(2)}, u32[]{:S(2)}) async-start(f32[8,1,1152]{2,1,0:T(1,128)} %broadcast_in_dim.34), calls=%async_computation.2 | async-start | bytes 73728 | tf_op jit(solution)/shard_map/all_to_all | solution.py:20
  59.9 9.0 %all-to-all-start.3 = ((f32[8,1,1152]{2,1,0:T(1,128)}), f32[8,1,1152]{2,1,0:T(1,128)S(1)}, u32[]{:S(2)}, u32[]{:S(2)}) async-start(f32[8,1,1152]{2,1,0:T(1,128)} %broadcast_in_dim.35), calls=%async_computation.3 | async-start | bytes 73728 | tf_op jit(solution)/shard_map/all_to_all | solution.py:20
  63.2 5.8 %copy-start.3 = (f32[1,128,1024]{2,1,0:T(8,128)S(1)}, f32[1,128,1024]{2,1,0:T(8,128)}, u32[]{:S(2)}) copy-start(f32[1,128,1024]{2,1,0:T(8,128)} %param.15) | copy-start | bytes 1572868

commit v3 on v2

v3 whole, which is shorter than its diff:
```python
import functools

import jax
import jax.numpy as jnp
from jax import lax
from jax.experimental import pallas as pl
from jax.experimental.pallas import tpu as pltpu
from jax.sharding import PartitionSpec as P

STEPS = 2
LANES = 128
TILE = 8
VMEM_LIMIT = 48 * 1024 * 1024

courant = 0.45

STRIP_SUM, STRIP, STRIP_DEPTH, GAIN, INDEX, EDGE_FLOW, EDGE_DEPTH, EDGE_SUM = range(8)
(FIRST_ETA, SECOND_ETA, FIRST_ROW, FIRST_COL, FIRST_DEPTH, NEXT_ETA, LAST_ETA, NEXT_ROW,
 LAST_ROW, LAST_COL, NEXT_DEPTH, LAST_DEPTH) = range(12)


def iota(shape, axis):
    return lax.broadcasted_iota(jnp.int32, shape, axis)


def rolled(value, shift, axis):
    return pltpu.roll(value, shift % value.shape[axis], axis)


def wet(depth):
    return (depth > 0).astype(jnp.float32)


def pack_kernel(*refs):
    (eta_top, eta_low, eta_left, eta_right, row_top, row_low, row_left, row_right,
     col_top, col_low, col_left, col_right, depth_top, depth_low, depth_left, depth_right,
     wet_top, wet_low, wet_left, wet_right, gain_ref, index_ref, out_ref) = refs
    count, _, width = out_ref.shape
    cols = width - 2 * LANES
    level = lax.axis_index("level")
    lane = iota((TILE, cols), 1)

    def loaded(eta, row, col, depth, mask):
        mask = mask[0].astype(jnp.float32)
        return eta[0], row[0, 0], col[0, 0], mask * depth[0], mask

    eta, row, col, depth, mask = loaded(eta_top, row_top, col_top, depth_top, wet_top)
    east = jnp.where(lane == cols - 1, 0.0, rolled(eta, -1, 1))
    row = mask * (row - courant * (east - eta))
    west = jnp.where(lane == 0, 0.0, rolled(row, 1, 1))
    col = mask * (col - courant * (rolled(eta, -1, 0) - eta))
    strip_sum = mask * eta - courant * depth * (row - west + col)
    out_ref[0, STRIP_SUM:STRIP_SUM + 1, :cols] = strip_sum[:1]
    out_ref[0, STRIP:STRIP + 1, :cols] = eta[:1]
    out_ref[0, STRIP_DEPTH:STRIP_DEPTH + 1, :cols] = depth[:1]
    out_ref[0, GAIN:GAIN + 1, :cols] = gain_ref[pl.ds(level, 1), :]
    out_ref[0, INDEX:INDEX + 1, :cols] = index_ref[pl.ds(level, 1), :].astype(jnp.float32)

    eta, row, col, depth, mask = loaded(eta_low, row_low, col_low, depth_low, wet_low)
    east = jnp.where(lane == cols - 1, 0.0, rolled(eta, -1, 1))
    row = mask * (row - courant * (east - eta))
    west = jnp.where(lane == 0, 0.0, rolled(row, 1, 1))
    flow = mask * (col + courant * eta)
    above = rolled(flow - courant * mask * rolled(eta, -1, 0), 1, 0)
    edge_sum = mask * eta - courant * depth * (row - west - above)
    out_ref[0, EDGE_FLOW:EDGE_FLOW + 1, :cols] = flow[TILE - 1:]
    out_ref[0, EDGE_DEPTH:EDGE_DEPTH + 1, :cols] = depth[TILE - 1:]
    out_ref[0, EDGE_SUM:EDGE_SUM + 1, :cols] = edge_sum[TILE - 1:]

    lane = iota(eta_left.shape[1:], 1)
    columns = jnp.zeros(eta_left.shape[1:], jnp.float32)
    depth_first = depth_left[0] * wet_left[0].astype(jnp.float32)
    depth_last = depth_right[0] * wet_right[0].astype(jnp.float32)
    for place, value, at in (
        (FIRST_ETA, eta_left[0], 0), (SECOND_ETA, eta_left[0], 1), (FIRST_ROW, row_left[0, 0], 0),
        (FIRST_COL, col_left[0, 0], 0), (FIRST_DEPTH, depth_first, 0),
        (NEXT_ETA, eta_right[0], LANES - 2), (LAST_ETA, eta_right[0], LANES - 1),
        (NEXT_ROW, row_right[0, 0], LANES - 2), (LAST_ROW, row_right[0, 0], LANES - 1),
        (LAST_COL, col_right[0, 0], LANES - 1),
        (NEXT_DEPTH, depth_last, LANES - 2), (LAST_DEPTH, depth_last, LANES - 1),
    ):
        moved = value if place == at else rolled(value, place - at, 1)
        columns = jnp.where(lane == place, moved, columns)
    columns = columns.T
    out_ref[0, :, cols:cols + LANES] = columns[:TILE]
    out_ref[0, :, cols + LANES:] = columns[TILE:2 * TILE]
    packet = out_ref[0]
    for turn in range(1, count):
        out_ref[turn] = packet


class Links:
    def __init__(self, links_ref, subs):
        self.links_ref, self.subs = links_ref, subs

    def across(self, segment, way):
        patch = self.links_ref[0, segment // self.subs, way]
        return jnp.maximum(patch, 0), jnp.where(patch >= 0, 1.0, 0.0)

    def north(self, segment):
        patch, there = self.across(segment, 0)
        inside = segment % self.subs > 0
        return jnp.where(inside, segment - 1, patch * self.subs + self.subs - 1), jnp.where(inside, 1.0, there)

    def south(self, segment):
        patch, there = self.across(segment, 1)
        inside = segment % self.subs < self.subs - 1
        return jnp.where(inside, segment + 1, patch * self.subs), jnp.where(inside, 1.0, there)

    def west(self, segment):
        patch, there = self.across(segment, 2)
        return patch * self.subs + segment % self.subs, there

    def east(self, segment):
        patch, there = self.across(segment, 3)
        return patch * self.subs + segment % self.subs, there


def nested(table, flux, index):
    segments, cols = index.shape
    del table
    rows = []
    for low in range(0, segments, TILE):
        tiles = []
        for left in range(0, cols, LANES):
            at = index[low:low + TILE, left:left + LANES]
            lane, tile = at % LANES, at // LANES
            taken = jnp.zeros(at.shape, jnp.float32)
            for source in range(cols // LANES):
                values = flux[low:low + TILE, source * LANES:(source + 1) * LANES]
                found = jnp.take_along_axis(values, lane, axis=1, mode="promise_in_bounds")
                taken = jnp.where(tile == source, found, taken)
            tiles.append(taken)
        rows.append(jnp.concatenate(tiles, axis=1))
    return jnp.concatenate(rows, axis=0) if len(rows) > 1 else rows[0]


def strips_of(links, got_ref, finer, picked_ref, narrow_ref):
    count, _, width = got_ref.shape
    cols = width - 2 * LANES
    lane = iota((count, LANES), 1)
    strip, depth = got_ref[:, STRIP, :cols], got_ref[:, STRIP_DEPTH, :cols]
    mask = wet(depth)
    if finer is None:
        inflow = jnp.zeros_like(strip)
    else:
        gain = got_ref[:, GAIN, :cols]
        index = got_ref[:, INDEX, :cols].astype(jnp.int32)
        inflow = gain * nested(None, finer[0], index)
    eta = strip + inflow

    narrow_ref[...] = eta[:, :LANES]
    for segment in range(count):
        east, there = links.east(segment)
        picked_ref[segment:segment + 1, :LANES] = narrow_ref[pl.ds(east, 1), :] * there
    east_eta = rolled(picked_ref[:, :LANES], -1, 1)
    after = rolled(inflow, -1, 1)
    after = jnp.concatenate(
        [after[:, :-LANES], jnp.where(lane == LANES - 1, east_eta, after[:, -LANES:])], axis=1)
    more_row = courant * mask * (inflow - after)

    last_eta = got_ref[:, LAST_ETA % TILE, cols:cols + LANES]
    last_row = got_ref[:, LAST_ROW % TILE, cols + LANES:]
    first_of_last = rolled(last_row + courant * last_eta, -1, 1)
    narrow_ref[...] = mask[:, -LANES:] * first_of_last + more_row[:, -LANES:]
    for segment in range(count):
        west, there = links.west(segment)
        picked_ref[segment:segment + 1, :LANES] = narrow_ref[pl.ds(west, 1), :] * there
    west_row = rolled(picked_ref[:, :LANES], 1, 1)
    before = rolled(more_row, 1, 1)
    before = jnp.concatenate([jnp.where(lane == 0, west_row, before[:, :LANES]), before[:, LANES:]], axis=1)

    for segment in range(count):
        north, there = links.north(segment)
        picked_ref[segment:segment + 1, :] = got_ref[pl.ds(north, 1), EDGE_FLOW, :cols] * there
    flow = picked_ref[...]
    for segment in range(count):
        north, there = links.north(segment)
        picked_ref[segment:segment + 1, :] = got_ref[pl.ds(north, 1), EDGE_DEPTH, :cols] * there
    north_col = flow - courant * wet(picked_ref[...]) * eta
    later = (got_ref[:, STRIP_SUM, :cols] + mask * inflow
             - courant * depth * (more_row - before + courant * mask * inflow - north_col))
    if finer is None:
        return inflow, eta, inflow, later
    later_inflow = gain * nested(None, finer[1], index)
    return inflow, eta, later_inflow, later + later_inflow


def strips_kernel(subs, *refs):
    links_ref, got_ref = refs[:2]
    out_ref, picked_ref, narrow_ref = refs[-3:]
    finer = (refs[2][0], refs[2][1]) if len(refs) == 6 else None
    _, eta, _, later = strips_of(Links(links_ref, subs), got_ref, finer, picked_ref, narrow_ref)
    out_ref[0] = eta
    out_ref[1] = later


def final_kernel(subs, links_ref, got_ref, finer_ref, eta_ref, momenta_ref, depth_ref, wet_ref,
                 eta_out, momenta_out, picked_ref, narrow_ref, strips_ref, eta_pad, col_pad):
    count, _, width = got_ref.shape
    rows, cols = eta_ref.shape[1:]
    links = Links(links_ref, subs)
    for place, value in enumerate(
            strips_of(links, got_ref, (finer_ref[0], finer_ref[1]), picked_ref, narrow_ref)):
        for segment in range(count):
            strips_ref[place * count + segment] = value[segment:segment + 1]
    own = lax.axis_index("patch") * subs + lax.axis_index("sub")
    lane = iota((1, LANES), 1)
    first, last = lane == 0, lane == LANES - 1

    def strip_tile(which, segment, left):
        return strips_ref[which * count + segment, :, left:left + LANES]

    def strip_row(which, segment):
        return strips_ref[which * count + segment]

    def packet_row(segment, row, left=0, size=cols):
        return got_ref[pl.ds(segment, 1), row, left:left + size]

    def packet_column(segment, column):
        left = cols + column // TILE * LANES
        return got_ref[pl.ds(segment, 1), column % TILE, left:left + LANES]

    def edge_col(segment, there, eta, left, turned):
        north, beyond = links.north(segment)
        flow = packet_row(north, EDGE_FLOW, left, LANES)
        mask = wet(packet_row(north, EDGE_DEPTH, left, LANES))
        return beyond * (rolled(flow, turned, 1) - courant * rolled(mask, turned, 1) * eta)

    end = cols - LANES
    west, there = links.west(own)
    eta = packet_column(west, LAST_ETA) + jnp.where(first, rolled(strip_tile(0, west, end), 1, 1), 0.0)
    next_eta = packet_column(west, NEXT_ETA) + jnp.where(first, rolled(strip_tile(0, west, end), 2, 1), 0.0)
    depth = packet_column(west, LAST_DEPTH) * there
    mask = wet(depth)
    next_row = wet(packet_column(west, NEXT_DEPTH)) * (
        packet_column(west, NEXT_ROW) - courant * (eta - next_eta))
    below, beyond = links.south(west)
    south_eta = jnp.where(last, strip_tile(1, below, end) * beyond, rolled(eta, -1, 1))
    col = mask * (packet_column(west, LAST_COL) - courant * (south_eta - eta))
    north_col = jnp.where(first, edge_col(west, there, eta, end, 1), rolled(col, 1, 1))
    west_flow = mask * (packet_column(west, LAST_ROW) + courant * eta)
    west_sum = (mask * eta - courant * depth * (col - next_row - north_col)
                + jnp.where(first, rolled(strip_tile(2, west, end), 1, 1), 0.0))
    west_depth = depth
    east, there = links.east(own)
    eta = there * (packet_column(east, FIRST_ETA) + jnp.where(first, strip_tile(0, east, 0), 0.0))
    second_eta = packet_column(east, SECOND_ETA) + jnp.where(first, rolled(strip_tile(0, east, 0), -1, 1), 0.0)
    depth = packet_column(east, FIRST_DEPTH) * there
    mask = wet(depth)
    row = mask * (packet_column(east, FIRST_ROW) - courant * (second_eta - eta))
    below, beyond = links.south(east)
    south_eta = jnp.where(last, rolled(strip_tile(1, below, 0), -1, 1) * beyond, rolled(eta, -1, 1))
    col = mask * (packet_column(east, FIRST_COL) - courant * (south_eta - eta))
    north_col = jnp.where(first, edge_col(east, there, eta, 0, 0), rolled(col, 1, 1))
    east_sum = (mask * eta - courant * depth * (row + col - north_col)
                + there * jnp.where(first, strip_tile(2, east, 0), 0.0))
    sides = jnp.concatenate(
        [west_flow, west_sum, west_depth, eta, east_sum, depth, jnp.zeros((2, LANES), jnp.float32)], axis=0).T
    west_flow, west_sum, west_depth, east_eta, east_sum, east_depth = [
        sides[:, place:place + 1] for place in range(6)]
    west_wet = wet(west_depth)
    north, there = links.north(own)
    north_depth = packet_row(north, EDGE_DEPTH) * there
    north_wet = wet(north_depth)
    north_col = packet_row(north, EDGE_FLOW) * there - courant * north_wet * strip_row(1, own)
    north_east, beyond = links.east(north)
    right_eta = beyond * packet_column(north_east, FIRST_ETA)
    north_west, beyond = links.west(north)
    left_row = beyond * wet(packet_column(north_west, LAST_DEPTH)) * (
        packet_column(north_west, LAST_ROW)
        - courant * (packet_column(north, FIRST_ETA) - packet_column(north_west, LAST_ETA)))
    nothing = jnp.zeros((1, cols - LANES), jnp.float32)
    corners = (jnp.concatenate([jnp.where(first, rolled(left_row, 1, 1), 0.0), nothing], axis=1)
               + jnp.concatenate([nothing, jnp.where(last, courant * right_eta, 0.0)], axis=1))
    north_eta = packet_row(north, EDGE_SUM) + courant * north_depth * (corners - north_col)
    south, there_south = links.south(own)

    lanes = iota((TILE, cols), 1)
    eta_pad[TILE:TILE + rows] = eta_ref[0]
    eta_pad[TILE:TILE + 1] = strip_row(1, own)
    eta_pad[TILE + rows:TILE + rows + 1] = strip_row(1, south) * there_south
    col_pad[TILE - 1:TILE] = north_col

    def step(number, east_of, west_of, last_step):
        for low in range(0, rows, TILE):
            chunk = slice(low, low + TILE)
            eta = eta_pad[TILE + low:2 * TILE + low]
            mask = wet_ref[0, chunk].astype(jnp.float32)
            depth = depth_ref[0, chunk]
            if number == 0:
                row, col = momenta_ref[0, 0, chunk], momenta_ref[1, 0, chunk]
            else:
                row, col = momenta_out[0, 0, chunk], col_pad[TILE + low:2 * TILE + low]
            east = jnp.where(lanes == cols - 1, east_of(low), rolled(eta, -1, 1))
            south = eta_pad[TILE + low + 1:2 * TILE + low + 1]
            row = mask * (row - courant * (east - eta))
            col = mask * (col - courant * (south - eta))
            momenta_out[0, 0, chunk] = row
            col_pad[TILE + low:2 * TILE + low] = col
            if last_step:
                momenta_out[1, 0, chunk] = col
            west = jnp.where(lanes == 0, west_of(low, eta), rolled(row, 1, 1))
            north = col_pad[TILE + low - 1:2 * TILE + low - 1]
            eta = mask * (eta - courant * depth * (row - west + (col - north)))
            if last_step:
                eta_out[0, chunk] = eta
            else:
                eta_pad[TILE + low:2 * TILE + low] = eta

    first_west = []

    def west_before(low, eta):
        value = west_flow[low:low + TILE] - courant * west_wet[low:low + TILE] * eta[:, :1]
        first_west.append(value)
        return value

    step(0, lambda low: east_eta[low:low + TILE], west_before, False)

    eta_pad[TILE:TILE + 1] += strip_row(2, own)
    eta_pad[TILE + rows:TILE + rows + 1] = strip_row(3, south) * there_south
    col_pad[TILE - 1:TILE] = north_col_after(north_col, north_wet, north_eta, eta_pad[TILE:TILE + 1])

    def east_after(low):
        chunk = slice(low, low + TILE)
        return east_sum[chunk] + courant * east_depth[chunk] * momenta_out[0, 0, chunk, cols - 1:]

    def west_after(low, eta):
        chunk = slice(low, low + TILE)
        row = first_west[low // TILE]
        west_eta = west_sum[chunk] - courant * west_depth[chunk] * row
        return west_wet[chunk] * (row - courant * (eta[:, :1] - west_eta))

    step(1, east_after, west_after, True)


def north_col_after(col, mask, eta, south_eta):
    return mask * (col - courant * (south_eta - eta))


def body(adjoint_height, adjoint_momenta, depth, wet_mask, adjacency, nest_gain, nest_index):
    rows, cols = adjoint_height.shape[1:]
    levels = lax.axis_size("level")
    subs = lax.axis_size("sub")
    count = lax.axis_size("patch") * subs
    params = pltpu.CompilerParams(vmem_limit_bytes=VMEM_LIMIT)
    whole = pl.BlockSpec(memory_space=pltpu.VMEM)
    scalars = pl.BlockSpec(memory_space=pltpu.SMEM)
    low, right = rows // TILE - 1, cols // LANES - 1

    def edges(leading):
        none = (0,) * len(leading)
        return [
            pl.BlockSpec(leading + shape, functools.partial(lambda place, step: none + place, place))
            for shape, place in (
                ((TILE, cols), (0, 0)), ((TILE, cols), (low, 0)),
                ((rows, LANES), (0, 0)), ((rows, LANES), (0, right)))
        ]

    def momentum(which):
        return [
            pl.BlockSpec((1, 1) + shape, functools.partial(lambda place, step: (which, 0) + place, place))
            for shape, place in (
                ((TILE, cols), (0, 0)), ((TILE, cols), (low, 0)),
                ((rows, LANES), (0, 0)), ((rows, LANES), (0, right)))
        ]

    table = pl.BlockSpec((levels, cols), lambda step: (0, 0))
    packet = (count, 8, cols + 2 * LANES)
    packed = pl.pallas_call(
        pack_kernel,
        grid=(1,),
        out_shape=jax.ShapeDtypeStruct(packet, jnp.float32),
        in_specs=edges((1,)) + momentum(0) + momentum(1) + edges((1,)) + edges((1,)) + [table, table],
        out_specs=pl.BlockSpec(packet, lambda step: (0, 0, 0)),
        compiler_params=params,
        name="pack",
    )(*[adjoint_height] * 4, *[adjoint_momenta] * 8, *[depth] * 4, *[wet_mask] * 4, nest_gain, nest_index)
    got = lax.all_to_all(packed, ("patch", "sub"), 0, 0, tiled=True)

    work = [pltpu.VMEM((count, cols), jnp.float32), pltpu.VMEM((count, LANES), jnp.float32)]
    flux = ()
    for turn in range(levels - 1):
        strips = pl.pallas_call(
            functools.partial(strips_kernel, subs),
            out_shape=jax.ShapeDtypeStruct((2, count, cols), jnp.float32),
            in_specs=[scalars, whole] + [whole] * len(flux),
            out_specs=whole,
            scratch_shapes=work,
            compiler_params=params,
            name="strips",
        )(adjacency, got, *flux)
        flux = (lax.ppermute(strips, "level", [(source, source - 1) for source in range(1, levels)]),)

    return pl.pallas_call(
        functools.partial(final_kernel, subs),
        out_shape=[
            jax.ShapeDtypeStruct(adjoint_height.shape, jnp.float32),
            jax.ShapeDtypeStruct(adjoint_momenta.shape, jnp.float32),
        ],
        in_specs=[scalars] + [whole] * 6,
        out_specs=[whole, whole],
        scratch_shapes=work + [
            pltpu.VMEM((4 * count, 1, cols), jnp.float32),
            pltpu.VMEM((rows + 2 * TILE, cols), jnp.float32),
            pltpu.VMEM((rows + 2 * TILE, cols), jnp.float32),
        ],
        compiler_params=params,
        name="final",
    )(adjacency, got, *flux, adjoint_height, adjoint_momenta, depth, wet_mask)


def solution(mesh):
    in_specs = (
        P(("parts", "level"), ("patch", "sub"), None),
        P(None, ("parts", "level"), ("patch", "sub"), None),
        P("level", ("patch", "sub"), None),
        P("level", ("patch", "sub"), None),
        P("level", None, None),
        P(None, ("patch", "sub")),
        P(None, ("patch", "sub")),
    )
    out_specs = (
        P(("parts", "level"), ("patch", "sub"), None),
        P(None, ("parts", "level"), ("patch", "sub"), None),
    )
    return jax.shard_map(body, mesh=mesh, in_specs=in_specs, out_specs=out_specs, check_vma=False)
```

time: 70.9 us -> 36.9 us (0.52)
  starting transfers between devices: 18.7 us -> 1.29 us
  blocking collectives: 0 us -> 17.4 us
  waiting for transfers between devices: 20.6 us -> 4.86 us
  local copies, waits for them, and re-layouts: 18.8 us -> 5.74 us
  Pallas kernels: 0 us -> 6.55 us
  other arithmetic: 6.2 us -> 0 us
  between operations: 5.92 us -> 0.66 us
    all_to_all x0 -> x1, blocking collectives: none -> 17.4 us  [body(): got = lax.all_to_all(packed, ('patch', 'sub'), 0, 0, tiled=True)]
    all_to_all x4 -> x0, starting transfers between devices: 16.2 us -> none  [from_all(): return lax.all_to_all(copies, axes, 0, 0, tiled=True)]
    all_to_all x4 -> x0, waiting for transfers between devices: 13.3 us -> none  [from_all(): return lax.all_to_all(copies, axes, 0, 0, tiled=True)]
    gather x2 -> x0, local copies, waits for them, and re-layouts: 9.04 us -> none  [body(): inflow = own_gain * jnp.take(received, own_table)]
    pallas_call x0 -> x3, Pallas kernels: none -> 6.55 us  [the longest x1 5.51 us: body(): pl.pallas_call(functools.partial(final_kernel, subs), out_shape=[jax.Shap...]
    slice x11 -> x0, local copies, waits for them, and re-layouts: 4.05 us -> none  [the longest x2 1.99 us: body(): east_eta = jnp.concatenate([eta[:, 1:], east_col[:, None]], axis=1)]
    unnamed x11 -> x16, local copies, waits for them, and re-layouts: 1.74 us -> 5.74 us
    mul x12 -> x0, other arithmetic: 3.87 us -> none  [the longest x2 3.43 us: body(): mom_col = wet * (mom_col - courant * (south_eta - eta))]
  transfers between devices with their start and end apart: 6 -> 1, of which waited for: 6 -> 1; matrix products, arithmetic and copies ran while one was open for 7% -> 0% of each run, Pallas kernels for 0% -> 0%
where the time goes in v3:
time: 36.9 us; the launch traced here: 36.5 us
  blocking collectives  17.4 us (47%)
  Pallas kernels  6.55 us (18%)
  local copies, waits for them, and re-layouts  5.74 us (16%)
  waiting for transfers between devices  4.86 us (13%)
  starting transfers between devices  1.29 us (3%)
  between operations  0.66 us (2%)
    all_to_all x1, blocking collectives, body(): got = lax.all_to_all(packed, ('patch', 'sub'), 0, 0, tiled=True)  17.4 us
    unnamed x16, local copies, waits for them, and re-layouts  5.74 us
    pallas_call x1, Pallas kernels, body(): pl.pallas_call(functools.partial(final_kernel, subs), out_shape=[jax.Shap...  5.51 us
    ppermute x1, waiting for transfers between devices, body(): lax.ppermute(strips, 'level', [(source, source - 1) for source in range(1...  4.86 us
    ppermute x1, starting transfers between devices, body(): lax.ppermute(strips, 'level', [(source, source - 1) for source in range(1...  1.29 us
    pallas_call x1, Pallas kernels, body(): pl.pallas_call(functools.partial(strips_kernel, subs), out_shape=jax.Shap...  0.76 us
  transfers between devices with their start and end apart: 1, of which 1 were waited for; matrix products, arithmetic and copies ran while one was open for 0% of the time, Pallas kernels for 0%

profile of v3, /device:TPU:0, one launch (start us, length us, event | category | flops | bytes accessed | tf_op | source)
XLA Modules:
  0.0 36.5 jit_solution(14371925071894320881)
XLA Ops:
  0.6 0.0 copy-start
  0.6 1.2 %copy-done = f32[2,1,128,1024]{3,2,1,0:T(8,128)S(1)} copy-done((f32[2,1,128,1024]{3,2,1,0:T(8,128)S(1)}, f32[2,1,128,1024]{3,2,1,0:T(8,128)}, u32[]{:S(2)}) %copy-start) | copy-done | bytes 1048600
  1.9 0.0 copy-start.1
  1.9 1.0 %copy-done.1 = f32[1,128,1024]{2,1,0:T(8,128)S(1)} copy-done((f32[1,128,1024]{2,1,0:T(8,128)S(1)}, f32[1,128,1024]{2,1,0:T(8,128)}, u32[]{:S(2)}) %copy-start.1) | copy-done | bytes 524312
  2.9 0.0 copy-start.3
  2.9 1.0 %copy-done.3 = f32[1,128,1024]{2,1,0:T(8,128)S(1)} copy-done((f32[1,128,1024]{2,1,0:T(8,128)S(1)}, f32[1,128,1024]{2,1,0:T(8,128)}, u32[]{:S(2)}) %copy-start.3) | copy-done | bytes 524312
  3.9 0.0 copy-start.4
  3.9 1.0 %copy-done.4 = s32[1,128,1024]{2,1,0:T(8,128)S(1)} copy-done((s32[1,128,1024]{2,1,0:T(8,128)S(1)}, s32[1,128,1024]{2,1,0:T(8,128)}, u32[]{:S(2)}) %copy-start.4) | copy-done | bytes 524312
  5.0 0.0 copy-start.5
  5.0 0.7 %copy-done.5 = f32[2,1024]{1,0:T(2,128)S(1)} copy-done((f32[2,1024]{1,0:T(2,128)S(1)}, f32[2,1024]{1,0:T(2,128)}, u32[]{:S(2)}) %copy-start.5) | copy-done | bytes 8216
  5.7 0.0 copy-start.6
  5.7 0.7 %copy-done.6 = s32[2,1024]{1,0:T(2,128)S(1)} copy-done((s32[2,1024]{1,0:T(2,128)S(1)}, s32[2,1024]{1,0:T(2,128)}, u32[]{:S(2)}) %copy-start.6) | copy-done | bytes 8216
  6.4 0.3 pack.1
  6.7 0.0 copy-start.7
  6.7 0.0 copy-start.2
  6.7 17.4 %all_to_all.5.refs_1_.got_ref = f32[8,8,1280]{2,1,0:T(8,128)S(1)} all-to-all(f32[8,8,1280]{2,1,0:T(8,128)S(1)} %pack.1), channel_id=1, replica_groups=mesh['parts'=2,'patch'=4,'level'=2,'sub'=2] {'patch','sub'}, dimensions={0} | all-to-all | bytes 655360 | tf_op jit(solution)/shard_map/all_to_all | solution.py:379
  24.1 0.0 copy-done.7
  24.1 0.8 %strips.1 = f32[2,8,1024]{2,1,0:T(8,128)S(1)} custom-call(s32[1,4,4]{2,1,0:T(4,128)S(1)} %copy-done.7, f32[8,8,1280]{2,1,0:T(8,128)S(1)} %all_to_all.5.refs_1_.got_ref), custom_call_target="tpu_custom_call" | custom-call | tf_op jit(solution)/shard_map/strips/pallas_call | solution.py:384
  24.8 1.3 %collective-permute-start = (f32[2,8,1024]{2,1,0:T(8,128)S(1)}, f32[2,8,1024]{2,1,0:T(8,128)S(1)}, u32[]{:S(2)}, u32[]{:S(2)}) collective-permute-start(f32[2,8,1024]{2,1,0:T(8,128)S(1)} %strips.1), channel_id=1, source_target_pairs={{2,0},{3,1},{6,4},{7,5},{10,8},{11,9},{14,12},{15,13},{18,16},{19,... | collective-permute-start | bytes 196616 | tf_op jit(solution)/shard_map/ppermute | solution.py:393
  26.1 4.9 %collective-permute-done.finer_ref = f32[2,8,1024]{2,1,0:T(8,128)S(1)} collective-permute-done((f32[2,8,1024]{2,1,0:T(8,128)S(1)}, f32[2,8,1024]{2,1,0:T(8,128)S(1)}, u32[]{:S(2)}, u32[]{:S(2)}) %collective-permute-start) | collective-permute-done | bytes 65568 | tf_op jit(solution)/shard_map/ppermute | solution.py:393
  31.0 0.0 copy-done.2
  31.0 5.5 %final.1 = (f32[1,128,1024]{2,1,0:T(8,128)}, f32[2,1,128,1024]{3,2,1,0:T(8,128)}) custom-call(s32[1,4,4]{2,1,0:T(4,128)S(1)} %copy-done.7, f32[8,8,1280]{2,1,0:T(8,128)S(1)} %all_to_all.5.refs_1_.got_ref, f32[2,8,1024]{2,1,0:T(8,128)S(1)} %collective-permute-done.finer_ref, f32[1,128,1024]{2,1,0:T(8,128)S(1)} %copy-done.2, f32[2,1,128,1024]{3,2,1,0:T(8,128)S(1)} %copy-done, ...), custom_call_target="tpu_custom_call" | custom-call | tf_op jit(solution)/shard_map/final/pallas_call | solution.py:395
Async XLA Ops:
  0.6 1.2 %copy-start = (f32[2,1,128,1024]{3,2,1,0:T(8,128)S(1)}, f32[2,1,128,1024]{3,2,1,0:T(8,128)}, u32[]{:S(2)}) copy-start(f32[2,1,128,1024]{3,2,1,0:T(8,128)} %momenta_ref.1) | copy-start | bytes 3145732
  1.9 1.0 %copy-start.1 = (f32[1,128,1024]{2,1,0:T(8,128)S(1)}, f32[1,128,1024]{2,1,0:T(8,128)}, u32[]{:S(2)}) copy-start(f32[1,128,1024]{2,1,0:T(8,128)} %eta_ref.1) | copy-start | bytes 1572868
  2.9 1.0 %copy-start.3 = (f32[1,128,1024]{2,1,0:T(8,128)S(1)}, f32[1,128,1024]{2,1,0:T(8,128)}, u32[]{:S(2)}) copy-start(f32[1,128,1024]{2,1,0:T(8,128)} %depth_ref.1) | copy-start | bytes 1572868
  3.9 1.0 %copy-start.4 = (s32[1,128,1024]{2,1,0:T(8,128)S(1)}, s32[1,128,1024]{2,1,0:T(8,128)}, u32[]{:S(2)}) copy-start(s32[1,128,1024]{2,1,0:T(8,128)} %wet_ref.1) | copy-start | bytes 1572868
  5.0 0.7 %copy-start.5 = (f32[2,1024]{1,0:T(2,128)S(1)}, f32[2,1024]{1,0:T(2,128)}, u32[]{:S(2)}) copy-start(f32[2,1024]{1,0:T(2,128)} %refs_20_.1) | copy-start | bytes 24580
  5.7 0.7 %copy-start.6 = (s32[2,1024]{1,0:T(2,128)S(1)}, s32[2,1024]{1,0:T(2,128)}, u32[]{:S(2)}) copy-start(s32[2,1024]{1,0:T(2,128)} %refs_21_.1) | copy-start | bytes 24580
  6.7 17.4 %copy-start.7 = (s32[1,4,4]{2,1,0:T(4,128)S(1)}, s32[1,4,4]{2,1,0:T(4,128)}, u32[]{:S(2)}) copy-start(s32[1,4,4]{2,1,0:T(4,128)} %links_ref.1) | copy-start | bytes 196
  6.7 24.3 %copy-start.2 = (f32[1,128,1024]{2,1,0:T(8,128)S(1)}, f32[1,128,1024]{2,1,0:T(8,128)}, u32[]{:S(2)}) copy-start(f32[1,128,1024]{2,1,0:T(8,128)} %eta_ref.1) | copy-start | bytes 1572868
  24.8 6.2 %collective-permute-start = (f32[2,8,1024]{2,1,0:T(8,128)S(1)}, f32[2,8,1024]{2,1,0:T(8,128)S(1)}, u32[]{:S(2)}, u32[]{:S(2)}) collective-permute-start(f32[2,8,1024]{2,1,0:T(8,128)S(1)} %strips.1), channel_id=1, source_target_pairs={{2,0},{3,1},{6,4},{7,5},{10,8},{11,9},{14,12},{15,13},{18,16},{19,... | collective-permute-start | bytes 196616 | tf_op jit(solution)/shard_map/ppermute | solution.py:393

commit v4 on v3

v4 whole, which is shorter than its diff:
```python
import functools

import jax
import jax.numpy as jnp
from jax import lax
from jax.experimental import pallas as pl
from jax.experimental.pallas import tpu as pltpu
from jax.sharding import PartitionSpec as P

STEPS = 2
LANES = 128
TILE = 8
VMEM_LIMIT = 48 * 1024 * 1024

courant = 0.45

STRIP_SUM, STRIP, STRIP_DEPTH, GAIN, INDEX, EDGE_FLOW, EDGE_DEPTH, EDGE_SUM = range(8)
(FIRST_ETA, SECOND_ETA, FIRST_ROW, FIRST_COL, FIRST_DEPTH, NEXT_ETA, LAST_ETA, NEXT_ROW,
 LAST_ROW, LAST_COL, NEXT_DEPTH, LAST_DEPTH) = range(12)


def iota(shape, axis):
    return lax.broadcasted_iota(jnp.int32, shape, axis)


def rolled(value, shift, axis):
    return pltpu.roll(value, shift % value.shape[axis], axis)


def wet(depth):
    return (depth > 0).astype(jnp.float32)


def copied(pairs, sems):
    copies = [pltpu.make_async_copy(source, target, sems.at[place]) for place, (source, target) in enumerate(pairs)]
    for copy in copies:
        copy.start()
    return copies


def pack_kernel(eta_ref, momenta_ref, depth_ref, wet_ref, gain_ref, index_ref, out_ref,
                ends, end_wet, sides, side_wet, gains, indices, sems):
    count, _, width = out_ref.shape
    rows, cols = eta_ref.shape[1:]
    fields = eta_ref.at[0], momenta_ref.at[0, 0], momenta_ref.at[1, 0], depth_ref.at[0]
    pairs = []
    for end in range(2):
        tall = pl.ds(end * (rows - TILE), TILE)
        wide = pl.ds(end * (cols - LANES), LANES)
        for place, field in enumerate(fields):
            pairs.append((field.at[tall, :], ends.at[end, place]))
            pairs.append((field.at[:, wide], sides.at[end, place]))
        pairs.append((wet_ref.at[0, tall, :], end_wet.at[end]))
        pairs.append((wet_ref.at[0, :, wide], side_wet.at[end]))
    for copy in copied(pairs + [(gain_ref, gains), (index_ref, indices)], sems):
        copy.wait()
    level = lax.axis_index("level")
    lane = iota((TILE, cols), 1)

    def loaded(end):
        mask = end_wet[end].astype(jnp.float32)
        return ends[end, 0], ends[end, 1], ends[end, 2], mask * ends[end, 3], mask

    eta, row, col, depth, mask = loaded(0)
    east = jnp.where(lane == cols - 1, 0.0, rolled(eta, -1, 1))
    row = mask * (row - courant * (east - eta))
    west = jnp.where(lane == 0, 0.0, rolled(row, 1, 1))
    col = mask * (col - courant * (rolled(eta, -1, 0) - eta))
    strip_sum = mask * eta - courant * depth * (row - west + col)
    out_ref[0, STRIP_SUM:STRIP_SUM + 1, :cols] = strip_sum[:1]
    out_ref[0, STRIP:STRIP + 1, :cols] = eta[:1]
    out_ref[0, STRIP_DEPTH:STRIP_DEPTH + 1, :cols] = depth[:1]
    out_ref[0, GAIN:GAIN + 1, :cols] = gains[pl.ds(level, 1), :]
    out_ref[0, INDEX:INDEX + 1, :cols] = indices[pl.ds(level, 1), :].astype(jnp.float32)

    eta, row, col, depth, mask = loaded(1)
    east = jnp.where(lane == cols - 1, 0.0, rolled(eta, -1, 1))
    row = mask * (row - courant * (east - eta))
    west = jnp.where(lane == 0, 0.0, rolled(row, 1, 1))
    flow = mask * (col + courant * eta)
    above = rolled(flow - courant * mask * rolled(eta, -1, 0), 1, 0)
    edge_sum = mask * eta - courant * depth * (row - west - above)
    out_ref[0, EDGE_FLOW:EDGE_FLOW + 1, :cols] = flow[TILE - 1:]
    out_ref[0, EDGE_DEPTH:EDGE_DEPTH + 1, :cols] = depth[TILE - 1:]
    out_ref[0, EDGE_SUM:EDGE_SUM + 1, :cols] = edge_sum[TILE - 1:]

    lane = iota((rows, LANES), 1)
    columns = jnp.zeros((rows, LANES), jnp.float32)
    depths = [sides[end, 3] * side_wet[end].astype(jnp.float32) for end in range(2)]
    for place, value, at in (
        (FIRST_ETA, sides[0, 0], 0), (SECOND_ETA, sides[0, 0], 1), (FIRST_ROW, sides[0, 1], 0),
        (FIRST_COL, sides[0, 2], 0), (FIRST_DEPTH, depths[0], 0),
        (NEXT_ETA, sides[1, 0], LANES - 2), (LAST_ETA, sides[1, 0], LANES - 1),
        (NEXT_ROW, sides[1, 1], LANES - 2), (LAST_ROW, sides[1, 1], LANES - 1),
        (LAST_COL, sides[1, 2], LANES - 1),
        (NEXT_DEPTH, depths[1], LANES - 2), (LAST_DEPTH, depths[1], LANES - 1),
    ):
        moved = value if place == at else rolled(value, place - at, 1)
        columns = jnp.where(lane == place, moved, columns)
    columns = columns.T
    out_ref[0, :, cols:cols + LANES] = columns[:TILE]
    out_ref[0, :, cols + LANES:] = columns[TILE:2 * TILE]
    packet = out_ref[0]
    for turn in range(1, count):
        out_ref[turn] = packet


def bulk_kernel(eta_ref, momenta_ref, depth_ref, wet_ref, eta_out, momenta_out,
                eta_after, momenta_after, wet_after, depth_after, eta_ends, row_ends, turned,
                eta_pad, col_pad, momenta_in, depth_in, wet_in, eta_left, row_right, sems, out_sems):
    rows, cols = eta_ref.shape[1:]
    parts = sems.shape[0]
    size = rows // parts
    loads = []
    for part in range(parts):
        here = pl.ds(part * size, size)
        loads.append(copied([
            (eta_ref.at[0, here, :], eta_pad.at[pl.ds(TILE + part * size, size), :]),
            (momenta_ref.at[:, 0, here, :], momenta_in.at[:, here, :]),
            (depth_ref.at[0, here, :], depth_in.at[here, :]),
            (wet_ref.at[0, here, :], wet_in.at[here, :]),
        ], sems.at[part]))
    lane = iota((TILE, cols), 1)
    eta_pad[TILE + rows:] = jnp.zeros((TILE, cols), jnp.float32)
    col_pad[:TILE] = jnp.zeros((TILE, cols), jnp.float32)

    def step(number, low):
        chunk, padded = slice(low, low + TILE), slice(TILE + low, 2 * TILE + low)
        eta = eta_pad[padded]
        if number == 0:
            mask = wet_in[chunk].astype(jnp.float32)
            depth = courant * mask * depth_in[chunk]
            wet_after[chunk] = mask
            depth_after[chunk] = depth
            row, col = momenta_in[0, chunk], momenta_in[1, chunk]
        else:
            mask, depth = wet_after[chunk], depth_after[chunk]
            row, col = momenta_after[0, chunk], col_pad[padded]
        east = jnp.where(lane == cols - 1, 0.0, rolled(eta, -1, 1))
        south = eta_pad[TILE + low + 1:2 * TILE + low + 1]
        row = mask * (row - courant * (east - eta))
        col = mask * (col - courant * (south - eta))
        momenta_after[0, chunk] = row
        col_pad[padded] = col
        if number:
            momenta_after[1, chunk] = col
        west = jnp.where(lane == 0, 0.0, rolled(row, 1, 1))
        north = col_pad[TILE + low - 1:2 * TILE + low - 1]
        eta = mask * eta - depth * (row - west + (col - north))
        if number:
            eta_after[chunk] = eta
            return
        eta_pad[padded] = eta
        eta_left[chunk] = eta[:, :LANES]
        row_right[chunk] = row[:, cols - LANES:]
        if low in (0, rows - TILE):
            end = int(low > 0)
            eta_ends[end] = eta
            row_ends[end] = row

    for copy in loads[0]:
        copy.wait()
    stores = []
    for part in range(parts + 1):
        if part + 1 < parts:
            for copy in loads[part + 1]:
                copy.wait()
        if part < parts:
            for low in range(part * size, (part + 1) * size, TILE):
                step(0, low)
        if part:
            for low in range((part - 1) * size, part * size, TILE):
                step(1, low)
            here = pl.ds((part - 1) * size, size)
            stores += copied([
                (eta_after.at[here, :], eta_out.at[0, here, :]),
                (momenta_after.at[:, here, :], momenta_out.at[:, 0, here, :]),
            ], out_sems.at[part - 1])
    right = cols - LANES
    turned[0] = wet_after[:, :LANES].T[:TILE]
    turned[1] = depth_after[:, :LANES].T[:TILE]
    turned[2] = wet_after[:, right:].T[LANES - TILE:]
    turned[3] = depth_after[:, right:].T[LANES - TILE:]
    turned[4] = eta_left[...].T[:TILE]
    turned[5] = row_right[...].T[LANES - TILE:]
    for copy in stores:
        copy.wait()


class Links:
    def __init__(self, links_ref, subs):
        self.links_ref, self.subs = links_ref, subs

    def across(self, segment, way):
        patch = self.links_ref[0, segment // self.subs, way]
        return jnp.maximum(patch, 0), jnp.where(patch >= 0, 1.0, 0.0)

    def north(self, segment):
        patch, there = self.across(segment, 0)
        inside = segment % self.subs > 0
        return jnp.where(inside, segment - 1, patch * self.subs + self.subs - 1), jnp.where(inside, 1.0, there)

    def south(self, segment):
        patch, there = self.across(segment, 1)
        inside = segment % self.subs < self.subs - 1
        return jnp.where(inside, segment + 1, patch * self.subs), jnp.where(inside, 1.0, there)

    def west(self, segment):
        patch, there = self.across(segment, 2)
        return patch * self.subs + segment % self.subs, there

    def east(self, segment):
        patch, there = self.across(segment, 3)
        return patch * self.subs + segment % self.subs, there


def nested(flux, index):
    segments, cols = index.shape
    rows = []
    for low in range(0, segments, TILE):
        tiles = []
        for left in range(0, cols, LANES):
            at = index[low:low + TILE, left:left + LANES]
            lane, tile = at % LANES, at // LANES
            taken = jnp.zeros(at.shape, jnp.float32)
            for source in range(cols // LANES):
                values = flux[low:low + TILE, source * LANES:(source + 1) * LANES]
                found = jnp.take_along_axis(values, lane, axis=1, mode="promise_in_bounds")
                taken = jnp.where(tile == source, found, taken)
            tiles.append(taken)
        rows.append(jnp.concatenate(tiles, axis=1))
    return jnp.concatenate(rows, axis=0) if len(rows) > 1 else rows[0]


def strips_of(links, got_ref, finer, picked_ref, narrow_ref):
    count, _, width = got_ref.shape
    cols = width - 2 * LANES
    lane = iota((count, LANES), 1)
    strip, depth = got_ref[:, STRIP, :cols], got_ref[:, STRIP_DEPTH, :cols]
    mask = wet(depth)
    if finer is None:
        inflow = jnp.zeros_like(strip)
    else:
        gain = got_ref[:, GAIN, :cols]
        index = got_ref[:, INDEX, :cols].astype(jnp.int32)
        inflow = gain * nested(finer[0], index)
    eta = strip + inflow

    narrow_ref[...] = eta[:, :LANES]
    for segment in range(count):
        east, there = links.east(segment)
        picked_ref[segment:segment + 1, :LANES] = narrow_ref[pl.ds(east, 1), :] * there
    east_eta = rolled(picked_ref[:, :LANES], -1, 1)
    after = rolled(inflow, -1, 1)
    after = jnp.concatenate(
        [after[:, :-LANES], jnp.where(lane == LANES - 1, east_eta, after[:, -LANES:])], axis=1)
    more_row = courant * mask * (inflow - after)

    last_eta = got_ref[:, LAST_ETA % TILE, cols:cols + LANES]
    last_row = got_ref[:, LAST_ROW % TILE, cols + LANES:]
    first_of_last = rolled(last_row + courant * last_eta, -1, 1)
    narrow_ref[...] = mask[:, -LANES:] * first_of_last + more_row[:, -LANES:]
    for segment in range(count):
        west, there = links.west(segment)
        picked_ref[segment:segment + 1, :LANES] = narrow_ref[pl.ds(west, 1), :] * there
    west_row = rolled(picked_ref[:, :LANES], 1, 1)
    before = rolled(more_row, 1, 1)
    before = jnp.concatenate([jnp.where(lane == 0, west_row, before[:, :LANES]), before[:, LANES:]], axis=1)

    for segment in range(count):
        north, there = links.north(segment)
        picked_ref[segment:segment + 1, :] = got_ref[pl.ds(north, 1), EDGE_FLOW, :cols] * there
    flow = picked_ref[...]
    for segment in range(count):
        north, there = links.north(segment)
        picked_ref[segment:segment + 1, :] = got_ref[pl.ds(north, 1), EDGE_DEPTH, :cols] * there
    north_col = flow - courant * wet(picked_ref[...]) * eta
    later = (got_ref[:, STRIP_SUM, :cols] + mask * inflow
             - courant * depth * (more_row - before + courant * mask * inflow - north_col))
    if finer is None:
        return eta, later
    return eta, later + gain * nested(finer[1], index)


def strips_kernel(subs, *refs):
    links_ref, got_ref = refs[:2]
    out_ref, rows_ref, picked_ref, narrow_ref = refs[-4:]
    finer = (refs[2][0], refs[2][1]) if len(refs) == 7 else None
    eta, later = strips_of(Links(links_ref, subs), got_ref, finer, picked_ref, narrow_ref)
    out_ref[0] = eta
    out_ref[1] = later
    for segment in range(out_ref.shape[1]):
        rows_ref[segment] = later[segment:segment + 1]


class Packets:
    def __init__(self, got_ref, rows, cols, inflow_ref=None):
        self.got_ref, self.rows, self.cols, self.inflow_ref = got_ref, rows, cols, inflow_ref

    def row(self, segment, row, left=0, size=None):
        size = self.cols if size is None else size
        return self.got_ref[pl.ds(segment, 1), row, left:left + size]

    def column(self, segment, column):
        left = self.cols + column // TILE * LANES
        return self.got_ref[pl.ds(segment, 1), column % TILE, left:left + LANES]

    def field_row(self, segment, row, left=0, size=None):
        return self.row(segment, row, left, size) if self.inflow_ref is None else 0.0

    def field_column(self, segment, column):
        return self.column(segment, column) if self.inflow_ref is None else 0.0

    def inflow(self, step, segment, left=0, size=None):
        size = self.cols if size is None else size
        count = self.got_ref.shape[0]
        return self.inflow_ref[step * count + segment, :, left:left + size]

    def strip_tile(self, segment, left):
        if self.inflow_ref is None:
            return self.row(segment, STRIP, left, LANES)
        return self.inflow(0, segment, left, LANES)

    def at_first(self, step, segment, left, turned):
        if self.inflow_ref is None:
            return 0.0
        tile = self.inflow(step, segment, left, LANES)
        return jnp.where(iota((1, LANES), 1) == 0, rolled(tile, turned, 1) if turned else tile, 0.0)


def beside(links, packets, own):
    lane = iota((1, LANES), 1)
    first, last = lane == 0, lane == LANES - 1
    end = packets.cols - LANES

    def corner_col(segment, eta, left, turned):
        north, beyond = links.north(segment)
        flow = packets.field_row(north, EDGE_FLOW, left, LANES)
        mask = wet(packets.row(north, EDGE_DEPTH, left, LANES))
        if turned:
            flow = rolled(flow, turned, 1) if packets.inflow_ref is None else flow
            mask = rolled(mask, turned, 1)
        return beyond * (flow - courant * mask * eta)

    west, there = links.west(own)
    eta = packets.field_column(west, LAST_ETA) + packets.at_first(0, west, end, 1)
    next_eta = packets.field_column(west, NEXT_ETA) + packets.at_first(0, west, end, 2)
    own_eta = packets.field_column(own, FIRST_ETA) + packets.at_first(0, own, 0, 0)
    depth = packets.column(west, LAST_DEPTH) * there
    mask = wet(depth)
    next_row = wet(packets.column(west, NEXT_DEPTH)) * (
        packets.field_column(west, NEXT_ROW) - courant * (eta - next_eta))
    below, beyond = links.south(west)
    south_eta = jnp.where(last, packets.strip_tile(below, end) * beyond, rolled(eta, -1, 1))
    col = mask * (packets.field_column(west, LAST_COL) - courant * (south_eta - eta))
    north_col = jnp.where(first, corner_col(west, eta, end, 1), rolled(col, 1, 1))
    west_row = mask * (packets.field_column(west, LAST_ROW) - courant * (own_eta - eta))
    west_eta = (mask * eta - courant * depth * (west_row - next_row + col - north_col)
                + packets.at_first(1, west, end, 1))
    west_mask = mask

    east, there = links.east(own)
    eta = there * (packets.field_column(east, FIRST_ETA) + packets.at_first(0, east, 0, 0))
    second_eta = packets.field_column(east, SECOND_ETA) + packets.at_first(0, east, 0, -1)
    depth = packets.column(east, FIRST_DEPTH) * there
    mask = wet(depth)
    row = mask * (packets.field_column(east, FIRST_ROW) - courant * (second_eta - eta))
    below, beyond = links.south(east)
    south_eta = jnp.where(last, rolled(packets.strip_tile(below, 0), -1, 1) * beyond, rolled(eta, -1, 1))
    col = mask * (packets.field_column(east, FIRST_COL) - courant * (south_eta - eta))
    north_col = jnp.where(first, corner_col(east, eta, 0, 0), rolled(col, 1, 1))
    east_sum = (mask * eta - courant * depth * (row + col - north_col)
                + there * packets.at_first(1, east, 0, 0))
    return west_row, west_mask, west_eta, eta, east_sum, courant * depth


def advanced(eta, row, col, mask, depth, east, south, west, north):
    row = mask * (row - courant * (east(eta) - eta))
    col = mask * (col - courant * (south(eta) - eta))
    return mask * eta - depth * (row - west(row) + col - north(col)), row, col


def two_steps(start, mask, depth, sides, base, north=None, south=None, second=None):
    lane, line = iota(mask.shape, 1), iota(mask.shape, 0)
    cols = mask.shape[1]
    west_row, west_mask, west_eta, east_eta, east_sum, east_depth = sides
    state = start, 0.0, 0.0
    flow, beyond = west_row, east_eta
    above = 0.0 if north is None else north[0]
    for number in range(2):
        below = 0.0 if south is None else south[number]
        state = advanced(
            *state, mask, depth,
            lambda eta: jnp.where(lane == cols - 1, beyond, rolled(eta, -1, 1)),
            lambda eta: jnp.where(line == TILE - 1, below, rolled(eta, -1, 0)),
            lambda row: jnp.where(lane == 0, flow, rolled(row, 1, 1)),
            lambda col: jnp.where(line == 0, above, rolled(col, 1, 0)))
        if number:
            return state
        eta, row, col = state
        if second is not None:
            eta = eta + jnp.where(line == 0, second, 0.0)
            state = eta, row, col
        whole_eta, whole_row = (eta, row) if base is None else (eta + base[0], row + base[1])
        flow = west_mask * (west_row - courant * (whole_eta[:, :1] - west_eta))
        beyond = east_sum + east_depth * whole_row[:, cols - 1:]
        if north is not None:
            above = north[1] * (north[0] - courant * (whole_eta[:1] - north[2]))


def north_of(links, packets, own, own_strip):
    cols = packets.cols
    lane = iota((1, LANES), 1)
    north, there = links.north(own)
    depth = packets.row(north, EDGE_DEPTH) * there
    mask = wet(depth)
    if packets.inflow_ref is not None:
        col = -courant * mask * own_strip
        return col, mask, -courant * depth * col
    col = packets.row(north, EDGE_FLOW) * there - courant * mask * own_strip
    north_east, beyond = links.east(north)
    right_eta = beyond * packets.column(north_east, FIRST_ETA)
    north_west, beyond = links.west(north)
    left_row = beyond * wet(packets.column(north_west, LAST_DEPTH)) * (
        packets.column(north_west, LAST_ROW)
        - courant * (packets.column(north, FIRST_ETA) - packets.column(north_west, LAST_ETA)))
    nothing = jnp.zeros((1, cols - LANES), jnp.float32)
    corners = (jnp.concatenate([jnp.where(lane == 0, rolled(left_row, 1, 1), 0.0), nothing], axis=1)
               + jnp.concatenate([nothing, jnp.where(lane == LANES - 1, courant * right_eta, 0.0)], axis=1))
    return col, mask, packets.row(north, EDGE_SUM) + courant * depth * (corners - col)


def as_sublanes(columns):
    rows = columns[0].shape[1]
    count = -len(columns) % TILE
    turned = jnp.concatenate(list(columns) + [jnp.zeros((count, rows), jnp.float32)], axis=0).T
    return [[turned[low:low + TILE, place:place + 1] for place in range(len(columns))]
            for low in (0, rows - TILE)]


def own_segment(subs):
    return lax.axis_index("patch") * subs + lax.axis_index("sub")


def halo_kernel(subs, links_ref, got_ref, later_ref, eta_after, momenta_after, wet_after, depth_after,
                eta_ends, row_ends, turned, eta_hbm, momenta_hbm, eta_out, momenta_out, ends_out,
                left_new, right_new, sems):
    del eta_hbm, momenta_hbm
    rows, cols = eta_after.shape
    right = cols - LANES
    links, own = Links(links_ref, subs), own_segment(subs)
    packets = Packets(got_ref, rows, cols)
    columns = beside(links, packets, own)
    west_row, west_mask, west_eta, east_eta, east_sum, east_depth = columns
    fields = eta_after, momenta_after.at[0], momenta_after.at[1]

    line = iota((TILE, rows), 0)
    lane = iota((TILE, rows), 1)
    nothing = jnp.zeros((TILE, rows), jnp.float32)

    def south(eta):
        return jnp.where(lane == rows - 1, 0.0, rolled(eta, -1, 1))

    def north(col):
        return jnp.where(lane == 0, 0.0, rolled(col, 1, 1))

    def column_steps(mask, depth, east, west):
        state = nothing, nothing, nothing
        for number in range(2):
            state = advanced(
                *state, mask, depth,
                lambda eta: jnp.where(line == TILE - 1, east(number, state), rolled(eta, -1, 0)), south,
                lambda row: jnp.where(line == 0, west(number, state), rolled(row, 1, 0)), north)
        return state

    def west_of(number, state):
        if number == 0:
            return west_row
        whole = state[0][:1] + turned[4, :1]
        return west_mask * (west_row - courant * (whole - west_eta))

    def east_of(number, state):
        if number == 0:
            return east_eta
        return east_sum + east_depth * (state[1][TILE - 1:] + turned[5, TILE - 1:])

    left = column_steps(turned[0], turned[1], lambda number, state: 0.0, west_of)
    last = column_steps(turned[2], turned[3], east_of, lambda number, state: 0.0)
    middle = jnp.zeros((LANES - 2 * TILE, rows), jnp.float32)
    lane = iota((rows, LANES), 1)
    body_rows = slice(TILE, rows - TILE)
    copies = []
    outs = eta_out.at[0], momenta_out.at[0, 0], momenta_out.at[1, 0]
    inner = pl.ds(TILE, rows - 2 * TILE)
    for place, field in enumerate(fields):
        more = jnp.concatenate([left[place], middle, last[place]], axis=0).T[body_rows]
        inside = iota(more.shape, 1)
        left_new[place] = field[body_rows, :LANES] + jnp.where(inside < TILE, more, 0.0)
        right_new[place] = field[body_rows, right:] + jnp.where(inside >= LANES - TILE, more, 0.0)
        copies += copied([
            (left_new.at[place], outs[place].at[inner, pl.ds(0, LANES)]),
            (right_new.at[place], outs[place].at[inner, pl.ds(right, LANES)]),
        ], sems.at[place])

    top_sides, low_sides = as_sublanes(columns)
    nothing = jnp.zeros((TILE, cols), jnp.float32)
    top = two_steps(
        nothing, wet_after[:TILE], depth_after[:TILE], top_sides, (eta_ends[0], row_ends[0]),
        north=north_of(links, packets, own, packets.row(own, STRIP)))
    below, there = links.south(own)
    low = two_steps(
        nothing, wet_after[rows - TILE:], depth_after[rows - TILE:], low_sides, (eta_ends[1], row_ends[1]),
        south=(packets.row(below, STRIP) * there, later_ref[below] * there))
    line, lane = iota((TILE, cols), 0), iota((TILE, cols), 1)
    for place, field in enumerate(fields):
        more = jnp.concatenate([left[place], middle, last[place]], axis=0).T
        gap = jnp.zeros((TILE, cols - 2 * LANES), jnp.float32)
        for end, (low_row, near, found) in enumerate(
                ((0, line < TILE // 2, top), (rows - TILE, line >= TILE // 2, low))):
            tile = more[low_row:low_row + TILE]
            inside = iota(tile.shape, 1)
            wide = jnp.concatenate(
                [jnp.where(inside < TILE, tile, 0.0), gap, jnp.where(inside >= LANES - TILE, tile, 0.0)], axis=1)
            ends_out[place, end] = field[low_row:low_row + TILE] + jnp.where(near, found[place], wide)
    for copy in copies:
        copy.wait()


def inflow_kernel(subs, links_ref, got_ref, finer_ref, wet_after, depth_after, ends_ref, eta_hbm, momenta_hbm,
                  eta_out, momenta_out, inflow_ref, new_ref, sems):
    del eta_hbm, momenta_hbm
    rows, cols = wet_after.shape
    count = got_ref.shape[0]
    links, own = Links(links_ref, subs), own_segment(subs)
    gain = got_ref[:, GAIN, :cols]
    index = got_ref[:, INDEX, :cols].astype(jnp.int32)
    for number in range(2):
        inflow = gain * nested(finer_ref[number], index)
        for segment in range(count):
            inflow_ref[number * count + segment] = inflow[segment:segment + 1]
    packets = Packets(got_ref, rows, cols, inflow_ref)
    columns = beside(links, packets, own)
    top_sides, low_sides = as_sublanes(columns)
    line = iota((TILE, cols), 0)
    strip = packets.inflow(0, own)
    top = two_steps(
        jnp.where(line == 0, strip, 0.0), wet_after[:TILE], depth_after[:TILE], top_sides, None,
        north=north_of(links, packets, own, strip), second=packets.inflow(1, own))

    below, there = links.south(own)
    strip = packets.inflow(0, below) * there
    lane = iota((1, cols), 1)
    depth = packets.row(below, STRIP_DEPTH)
    mask = wet(depth)
    east, beyond = links.east(below)
    last_eta = rolled(packets.inflow(0, east, 0, LANES) * beyond, -1, 1)[:, LANES - 1:]
    after = jnp.where(lane == cols - 1, last_eta, rolled(strip, -1, 1))
    row = courant * mask * (strip - after)
    west, beyond = links.west(below)
    end = cols - LANES
    first_row = rolled(courant * wet(packets.row(west, STRIP_DEPTH, end, LANES)) * beyond * (
        packets.inflow(0, west, end, LANES) - rolled(strip[:, :LANES], -1, 1)), 1, 1)[:, :1]
    before = jnp.where(lane == 0, first_row, rolled(row, 1, 1))
    north, beyond = links.north(below)
    north_col = -courant * wet(packets.row(north, EDGE_DEPTH)) * beyond * strip
    later = there * (mask * strip - courant * depth * (row - before + courant * mask * strip - north_col)
                     + packets.inflow(1, below))
    low = two_steps(
        jnp.zeros((TILE, cols), jnp.float32), wet_after[rows - TILE:], depth_after[rows - TILE:],
        low_sides, None, south=(strip, later))
    copies = []
    outs = eta_out.at[0], momenta_out.at[0, 0], momenta_out.at[1, 0]
    for place, out in enumerate(outs):
        for end, (low_row, near, found) in enumerate(
                ((0, line < TILE // 2, top), (rows - TILE, line >= TILE // 2, low))):
            new_ref[place, end] = ends_ref[place, end] + jnp.where(near, found[place], 0.0)
        copies += copied([
            (new_ref.at[place, end], out.at[pl.ds(end * (rows - TILE), TILE), :]) for end in range(2)
        ], sems.at[place])
    for copy in copies:
        copy.wait()


def body(adjoint_height, adjoint_momenta, depth, wet_mask, adjacency, nest_gain, nest_index):
    rows, cols = adjoint_height.shape[1:]
    levels = lax.axis_size("level")
    subs = lax.axis_size("sub")
    count = lax.axis_size("patch") * subs
    params = pltpu.CompilerParams(vmem_limit_bytes=VMEM_LIMIT)
    vmem = pl.BlockSpec(memory_space=pltpu.VMEM)
    smem = pl.BlockSpec(memory_space=pltpu.SMEM)
    hbm = pl.BlockSpec(memory_space=pltpu.HBM)

    def array(*shape):
        return jax.ShapeDtypeStruct(shape, jnp.float32)

    def scratch(*shape):
        return pltpu.VMEM(shape, jnp.float32)

    fields = [pltpu.with_memory_space_constraint(field, pltpu.HBM)
              for field in (adjoint_height, adjoint_momenta, depth, wet_mask, nest_gain, nest_index)]
    packed = pl.pallas_call(
        pack_kernel,
        out_shape=array(count, 8, cols + 2 * LANES),
        in_specs=[hbm] * 6,
        out_specs=vmem,
        scratch_shapes=[
            scratch(2, 4, TILE, cols), pltpu.VMEM((2, TILE, cols), jnp.int32),
            scratch(2, 4, rows, LANES), pltpu.VMEM((2, rows, LANES), jnp.int32),
            scratch(levels, cols), pltpu.VMEM((levels, cols), jnp.int32),
            pltpu.SemaphoreType.DMA((22,)),
        ],
        compiler_params=params,
        name="pack",
    )(*fields)
    got = lax.all_to_all(packed, ("patch", "sub"), 0, 0, tiled=True)

    parts = 4
    eta_new, momenta_new, *after = pl.pallas_call(
        bulk_kernel,
        out_shape=[
            array(*adjoint_height.shape), array(*adjoint_momenta.shape),
            array(rows, cols), array(2, rows, cols), array(rows, cols), array(rows, cols),
            array(2, TILE, cols), array(2, TILE, cols), array(6, TILE, rows),
        ],
        in_specs=[hbm] * 4,
        out_specs=[hbm] * 2 + [vmem] * 7,
        scratch_shapes=[
            scratch(rows + 2 * TILE, cols), scratch(rows + 2 * TILE, cols),
            scratch(2, rows, cols), scratch(rows, cols), pltpu.VMEM((rows, cols), jnp.int32),
            scratch(rows, LANES), scratch(rows, LANES),
            pltpu.SemaphoreType.DMA((parts, 4)), pltpu.SemaphoreType.DMA((parts, 2)),
        ],
        compiler_params=params,
        name="bulk",
    )(*fields[:4])

    flux = ()
    laters = []
    for turn in range(levels - 1):
        strips, later = pl.pallas_call(
            functools.partial(strips_kernel, subs),
            out_shape=[array(2, count, cols), array(count, 1, cols)],
            in_specs=[smem, vmem] + [vmem] * len(flux),
            out_specs=[vmem, vmem],
            scratch_shapes=[scratch(count, cols), scratch(count, LANES)],
            compiler_params=params,
            name="strips",
        )(adjacency, got, *flux)
        laters.append(later)
        flux = (lax.ppermute(strips, "level", [(source, source - 1) for source in range(1, levels)]),)

    eta_new, momenta_new, ends = pl.pallas_call(
        functools.partial(halo_kernel, subs),
        out_shape=[array(*adjoint_height.shape), array(*adjoint_momenta.shape), array(3, 2, TILE, cols)],
        in_specs=[smem] + [vmem] * 9 + [hbm] * 2,
        out_specs=[hbm, hbm, vmem],
        input_output_aliases={10: 0, 11: 1},
        scratch_shapes=[
            scratch(3, rows - 2 * TILE, LANES), scratch(3, rows - 2 * TILE, LANES), pltpu.SemaphoreType.DMA((3, 2)),
        ],
        compiler_params=params,
        name="halo",
    )(adjacency, got, laters[0], *after, eta_new, momenta_new)

    return pl.pallas_call(
        functools.partial(inflow_kernel, subs),
        out_shape=[array(*adjoint_height.shape), array(*adjoint_momenta.shape)],
        in_specs=[smem] + [vmem] * 5 + [hbm] * 2,
        out_specs=[hbm, hbm],
        input_output_aliases={6: 0, 7: 1},
        scratch_shapes=[
            scratch(2 * count, 1, cols), scratch(3, 2, TILE, cols), pltpu.SemaphoreType.DMA((3, 2)),
        ],
        compiler_params=params,
        name="inflow",
    )(adjacency, got, *flux, after[2], after[3], ends, eta_new, momenta_new)


def solution(mesh):
    in_specs = (
        P(("parts", "level"), ("patch", "sub"), None),
        P(None, ("parts", "level"), ("patch", "sub"), None),
        P("level", ("patch", "sub"), None),
        P("level", ("patch", "sub"), None),
        P("level", None, None),
        P(None, ("patch", "sub")),
        P(None, ("patch", "sub")),
    )
    out_specs = (
        P(("parts", "level"), ("patch", "sub"), None),
        P(None, ("parts", "level"), ("patch", "sub"), None),
    )
    return jax.shard_map(body, mesh=mesh, in_specs=in_specs, out_specs=out_specs, check_vma=False)
```

time: 36.9 us -> 30.9 us (0.84)
  local copies, waits for them, and re-layouts: 5.74 us -> 0.01 us
  Pallas kernels: 6.55 us -> 11.4 us
  waiting for transfers between devices: 4.86 us -> 0.01 us
    unnamed x16 -> x2, local copies, waits for them, and re-layouts: 5.74 us -> 0.01 us
    ppermute x1, waiting for transfers between devices: 4.86 us -> 0.01 us  [body(): lax.ppermute(strips, 'level', [(source, source - 1) for source in range(1...]
    pallas_call x3 -> x5, Pallas kernels: 6.55 us -> 11.4 us  [the longest x1 4.28 us: body(): pl.pallas_call(bulk_kernel, out_shape=[array(*adjoint_height.shape), arra...]
  transfers between devices with their start and end apart: 1 -> 1, of which waited for: 1 -> 0; matrix products, arithmetic and copies ran while one was open for 0% -> 0% of each run, Pallas kernels for 0% -> 21%
where the time goes in v4:
time: 30.9 us; the launch traced here: 30.6 us
  blocking collectives  17.3 us (56%)
  Pallas kernels  11.4 us (37%)
  starting transfers between devices  1.29 us (4%)
  between operations  0.68 us (2%)
    all_to_all x1, blocking collectives, body(): got = lax.all_to_all(packed, ('patch', 'sub'), 0, 0, tiled=True)  17.3 us
    pallas_call x1, Pallas kernels, body(): pl.pallas_call(bulk_kernel, out_shape=[array(*adjoint_height.shape), arra...  4.28 us
    pallas_call x1, Pallas kernels, body(): pl.pallas_call(functools.partial(inflow_kernel, subs), out_shape=[array(*...  2.55 us
    pallas_call x1, Pallas kernels, body(): pl.pallas_call(functools.partial(halo_kernel, subs), out_shape=[array(*ad...  2.07 us
    pallas_call x1, Pallas kernels, body(): pl.pallas_call(pack_kernel, out_shape=array(count, 8, cols + 2 * LANES),...  1.7 us
    ppermute x1, starting transfers between devices, body(): lax.ppermute(strips, 'level', [(source, source - 1) for source in range(1...  1.29 us
    pallas_call x1, Pallas kernels, body(): pl.pallas_call(functools.partial(strips_kernel, subs), out_shape=[array(2...  0.77 us
  transfers between devices with their start and end apart: 1, of which 0 were waited for; matrix products, arithmetic and copies ran while one was open for 0% of the time, Pallas kernels for 21%

profile of v4, /device:TPU:0, one launch (start us, length us, event | category | flops | bytes accessed | tf_op | source)
XLA Modules:
  0.0 30.6 jit_solution(10867036040376539527)
XLA Ops:
  0.6 1.7 %pack.1 = f32[8,8,1280]{2,1,0:T(8,128)S(1)} custom-call(f32[1,128,1024]{2,1,0:T(8,128)} %eta_ref.3, f32[2,1,128,1024]{3,2,1,0:T(8,128)} %momenta_ref.3, f32[1,128,1024]{2,1,0:T(8,128)} %depth_ref.3, s32[1,128,1024]{2,1,0:T(8,128)} %wet_ref.3, f32[2,1024]{1,0:T(2,128)} %gain_ref.1, s32[2,1024]{1,0:T(2,128)} %index_ref.1), custom_call_target="tpu_custom_call" | custom-call | tf_op jit(solution)/shard_map/pack/pallas_call | solution.py:602
  2.3 0.0 copy-start
  2.4 17.3 %all_to_all.5.refs_1_.got_ref = f32[8,8,1280]{2,1,0:T(8,128)S(1)} all-to-all(f32[8,8,1280]{2,1,0:T(8,128)S(1)} %pack.1), channel_id=1, replica_groups=mesh['parts'=2,'patch'=4,'level'=2,'sub'=2] {'patch','sub'}, dimensions={0} | all-to-all | bytes 655360 | tf_op jit(solution)/shard_map/all_to_all | solution.py:616
  19.6 0.0 copy-done
  19.6 0.8 %strips.1 = (f32[2,8,1024]{2,1,0:T(8,128)S(1)}, f32[8,1,1024]{2,1,0:T(1,128)S(1)}) custom-call(s32[1,4,4]{2,1,0:T(4,128)S(1)} %copy-done, f32[8,8,1280]{2,1,0:T(8,128)S(1)} %all_to_all.5.refs_1_.got_ref), custom_call_target="tpu_custom_call" | custom-call | tf_op jit(solution)/shard_map/strips/pallas_call | solution.py:641
  20.4 1.3 %collective-permute-start = (f32[2,8,1024]{2,1,0:T(8,128)S(1)}, f32[2,8,1024]{2,1,0:T(8,128)S(1)}, u32[]{:S(2)}, u32[]{:S(2)}) collective-permute-start(f32[2,8,1024]{2,1,0:T(8,128)S(1)} %get-tuple-element.16), channel_id=1, source_target_pairs={{2,0},{3,1},{6,4},{7,5},{10,8},{11,9},{14,12},{15,13},{18,16},{19,... | collective-permute-start | bytes 196616 | tf_op jit(solution)/shard_map/ppermute | solution.py:651
  21.7 4.3 %bulk.1 = (f32[1,128,1024]{2,1,0:T(8,128)}, f32[2,1,128,1024]{3,2,1,0:T(8,128)}, f32[128,1024]{1,0:T(8,128)S(1)}, f32[2,128,1024]{2,1,0:T(8,128)S(1)}, f32[128,1...) custom-call(f32[1,128,1024]{2,1,0:T(8,128)} %eta_ref.3, ...), custom_call_target="tpu_custom_call" | custom-call | tf_op jit(solution)/shard_map/bulk/pallas_call | solution.py:619
  26.0 2.1 %halo.1 = (f32[1,128,1024]{2,1,0:T(8,128)}, f32[2,1,128,1024]{3,2,1,0:T(8,128)}, f32[3,2,8,1024]{3,2,1,0:T(8,128)S(1)}) custom-call(s32[1,4,4]{2,1,0:T(4,128)S(1)} %copy-done, f32[8,8,1280]{2,1,0:T(8,128)S(1)} %all_to_all.5.refs_1_.got_ref, f32[8,1,1024]{2,1,0:T(1,128)S(1)} %get-tuple-element.19.later_ref, ...), custom_call_target="tpu_custom_call", output_to_operand_aliasing={{0}: (10, {}), {1}: (11, {})} | custom-call | tf_op jit(solution)/shard_map/halo/pallas_call | solution.py:653
  28.1 0.0 collective-permute-done.finer_ref
  28.1 2.6 %inflow.1 = (f32[1,128,1024]{2,1,0:T(8,128)}, f32[2,1,128,1024]{3,2,1,0:T(8,128)}) custom-call(s32[1,4,4]{2,1,0:T(4,128)S(1)} %copy-done, f32[8,8,1280]{2,1,0:T(8,128)S(1)} %all_to_all.5.refs_1_.got_ref, f32[2,8,1024]{2,1,0:T(8,128)S(1)} %collective-permute-done.finer_ref, ...), custom_call_target="tpu_custom_call", output_to_operand_aliasing={{0}: (6, {}), {1}: (7, {})} | custom-call | tf_op jit(solution)/shard_map/inflow/pallas_call | solution.py:666
Async XLA Ops:
  2.3 17.3 %copy-start = (s32[1,4,4]{2,1,0:T(4,128)S(1)}, s32[1,4,4]{2,1,0:T(4,128)}, u32[]{:S(2)}) copy-start(s32[1,4,4]{2,1,0:T(4,128)} %links_ref.3) | copy-start | bytes 196
  20.4 7.7 %collective-permute-start = (f32[2,8,1024]{2,1,0:T(8,128)S(1)}, f32[2,8,1024]{2,1,0:T(8,128)S(1)}, u32[]{:S(2)}, u32[]{:S(2)}) collective-permute-start(f32[2,8,1024]{2,1,0:T(8,128)S(1)} %get-tuple-element.16), channel_id=1, source_target_pairs={{2,0},{3,1},{6,4},{7,5},{10,8},{11,9},{14,12},{15,13},{18,16},{19,... | collective-permute-start | bytes 196616 | tf_op jit(solution)/shard_map/ppermute | solution.py:651

commit v5 on v4

--- a/solution.py
+++ b/solution.py
@@ -15,8 +15,18 @@
 courant = 0.45
 
 STRIP_SUM, STRIP, STRIP_DEPTH, GAIN, INDEX, EDGE_FLOW, EDGE_DEPTH, EDGE_SUM = range(8)
+ROWS = 8
 (FIRST_ETA, SECOND_ETA, FIRST_ROW, FIRST_COL, FIRST_DEPTH, NEXT_ETA, LAST_ETA, NEXT_ROW,
  LAST_ROW, LAST_COL, NEXT_DEPTH, LAST_DEPTH) = range(12)
+COLUMNS = 12
+
+
+def row_at(row, cols, left=0, size=None):
+    return slice(row * cols + left, row * cols + left + (cols if size is None else size))
+
+
+def column_at(column, cols):
+    return slice(ROWS * cols + column * LANES, ROWS * cols + (column + 1) * LANES)
 
 
 def iota(shape, axis):
@@ -40,7 +50,7 @@
 
 def pack_kernel(eta_ref, momenta_ref, depth_ref, wet_ref, gain_ref, index_ref, out_ref,
                 ends, end_wet, sides, side_wet, gains, indices, sems):
-    count, _, width = out_ref.shape
+    count = out_ref.shape[0]
     rows, cols = eta_ref.shape[1:]
     fields = eta_ref.at[0], momenta_ref.at[0, 0], momenta_ref.at[1, 0], depth_ref.at[0]
     pairs = []
@@ -67,11 +77,11 @@
     west = jnp.where(lane == 0, 0.0, rolled(row, 1, 1))
     col = mask * (col - courant * (rolled(eta, -1, 0) - eta))
     strip_sum = mask * eta - courant * depth * (row - west + col)
-    out_ref[0, STRIP_SUM:STRIP_SUM + 1, :cols] = strip_sum[:1]
-    out_ref[0, STRIP:STRIP + 1, :cols] = eta[:1]
-    out_ref[0, STRIP_DEPTH:STRIP_DEPTH + 1, :cols] = depth[:1]
-    out_ref[0, GAIN:GAIN + 1, :cols] = gains[pl.ds(level, 1), :]
-    out_ref[0, INDEX:INDEX + 1, :cols] = indices[pl.ds(level, 1), :].astype(jnp.float32)
+    out_ref[0, :, row_at(STRIP_SUM, cols)] = strip_sum[:1]
+    out_ref[0, :, row_at(STRIP, cols)] = eta[:1]
+    out_ref[0, :, row_at(STRIP_DEPTH, cols)] = depth[:1]
+    out_ref[0, :, row_at(GAIN, cols)] = gains[pl.ds(level, 1), :]
+    out_ref[0, :, row_at(INDEX, cols)] = indices[pl.ds(level, 1), :].astype(jnp.float32)
 
     eta, row, col, depth, mask = loaded(1)
     east = jnp.where(lane == cols - 1, 0.0, rolled(eta, -1, 1))
@@ -80,9 +90,9 @@
     flow = mask * (col + courant * eta)
     above = rolled(flow - courant * mask * rolled(eta, -1, 0), 1, 0)
     edge_sum = mask * eta - courant * depth * (row - west - above)
-    out_ref[0, EDGE_FLOW:EDGE_FLOW + 1, :cols] = flow[TILE - 1:]
-    out_ref[0, EDGE_DEPTH:EDGE_DEPTH + 1, :cols] = depth[TILE - 1:]
-    out_ref[0, EDGE_SUM:EDGE_SUM + 1, :cols] = edge_sum[TILE - 1:]
+    out_ref[0, :, row_at(EDGE_FLOW, cols)] = flow[TILE - 1:]
+    out_ref[0, :, row_at(EDGE_DEPTH, cols)] = depth[TILE - 1:]
+    out_ref[0, :, row_at(EDGE_SUM, cols)] = edge_sum[TILE - 1:]
 
     lane = iota((rows, LANES), 1)
     columns = jnp.zeros((rows, LANES), jnp.float32)
@@ -98,8 +108,8 @@
         moved = value if place == at else rolled(value, place - at, 1)
         columns = jnp.where(lane == place, moved, columns)
     columns = columns.T
-    out_ref[0, :, cols:cols + LANES] = columns[:TILE]
-    out_ref[0, :, cols + LANES:] = columns[TILE:2 * TILE]
+    for place in range(COLUMNS):
+        out_ref[0, :, column_at(place, cols)] = columns[place:place + 1]
     packet = out_ref[0]
     for turn in range(1, count):
         out_ref[turn] = packet
@@ -187,6 +197,10 @@
         copy.wait()
 
 
+def stacked(got_ref, part):
+    return jnp.concatenate([got_ref[segment, :, part] for segment in range(got_ref.shape[0])], axis=0)
+
+
 class Links:
     def __init__(self, links_ref, subs):
         self.links_ref, self.subs = links_ref, subs
@@ -233,16 +247,15 @@
 
 
 def strips_of(links, got_ref, finer, picked_ref, narrow_ref):
-    count, _, width = got_ref.shape
-    cols = width - 2 * LANES
+    count, cols = picked_ref.shape
     lane = iota((count, LANES), 1)
-    strip, depth = got_ref[:, STRIP, :cols], got_ref[:, STRIP_DEPTH, :cols]
+    strip, depth = stacked(got_ref, row_at(STRIP, cols)), stacked(got_ref, row_at(STRIP_DEPTH, cols))
     mask = wet(depth)
     if finer is None:
         inflow = jnp.zeros_like(strip)
     else:
-        gain = got_ref[:, GAIN, :cols]
-        index = got_ref[:, INDEX, :cols].astype(jnp.int32)
+        gain = stacked(got_ref, row_at(GAIN, cols))
+        index = stacked(got_ref, row_at(INDEX, cols)).astype(jnp.int32)
         inflow = gain * nested(finer[0], index)
     eta = strip + inflow
 
@@ -256,8 +269,8 @@
         [after[:, :-LANES], jnp.where(lane == LANES - 1, east_eta, after[:, -LANES:])], axis=1)
     more_row = courant * mask * (inflow - after)
 
-    last_eta = got_ref[:, LAST_ETA % TILE, cols:cols + LANES]
-    last_row = got_ref[:, LAST_ROW % TILE, cols + LANES:]
+    last_eta = stacked(got_ref, column_at(LAST_ETA, cols))
+    last_row = stacked(got_ref, column_at(LAST_ROW, cols))
     first_of_last = rolled(last_row + courant * last_eta, -1, 1)
     narrow_ref[...] = mask[:, -LANES:] * first_of_last + more_row[:, -LANES:]
     for segment in range(count):
@@ -269,13 +282,13 @@
 
     for segment in range(count):
         north, there = links.north(segment)
-        picked_ref[segment:segment + 1, :] = got_ref[pl.ds(north, 1), EDGE_FLOW, :cols] * there
+        picked_ref[segment:segment + 1, :] = got_ref[north, :, row_at(EDGE_FLOW, cols)] * there
     flow = picked_ref[...]
     for segment in range(count):
         north, there = links.north(segment)
-        picked_ref[segment:segment + 1, :] = got_ref[pl.ds(north, 1), EDGE_DEPTH, :cols] * there
+        picked_ref[segment:segment + 1, :] = got_ref[north, :, row_at(EDGE_DEPTH, cols)] * there
     north_col = flow - courant * wet(picked_ref[...]) * eta
-    later = (got_ref[:, STRIP_SUM, :cols] + mask * inflow
+    later = (stacked(got_ref, row_at(STRIP_SUM, cols)) + mask * inflow
              - courant * depth * (more_row - before + courant * mask * inflow - north_col))
     if finer is None:
         return eta, later
@@ -298,12 +311,10 @@
         self.got_ref, self.rows, self.cols, self.inflow_ref = got_ref, rows, cols, inflow_ref
 
     def row(self, segment, row, left=0, size=None):
-        size = self.cols if size is None else size
-        return self.got_ref[pl.ds(segment, 1), row, left:left + size]
+        return self.got_ref[segment, :, row_at(row, self.cols, left, size)]
 
     def column(self, segment, column):
-        left = self.cols + column // TILE * LANES
-        return self.got_ref[pl.ds(segment, 1), column % TILE, left:left + LANES]
+        return self.got_ref[segment, :, column_at(column, self.cols)]
 
     def field_row(self, segment, row, left=0, size=None):
         return self.row(segment, row, left, size) if self.inflow_ref is None else 0.0
@@ -532,8 +543,8 @@
     rows, cols = wet_after.shape
     count = got_ref.shape[0]
     links, own = Links(links_ref, subs), own_segment(subs)
-    gain = got_ref[:, GAIN, :cols]
-    index = got_ref[:, INDEX, :cols].astype(jnp.int32)
+    gain = stacked(got_ref, row_at(GAIN, cols))
+    index = stacked(got_ref, row_at(INDEX, cols)).astype(jnp.int32)
     for number in range(2):
         inflow = gain * nested(finer_ref[number], index)
         for segment in range(count):
@@ -601,7 +612,7 @@
               for field in (adjoint_height, adjoint_momenta, depth, wet_mask, nest_gain, nest_index)]
     packed = pl.pallas_call(
         pack_kernel,
-        out_shape=array(count, 8, cols + 2 * LANES),
+        out_shape=array(count, 1, ROWS * cols + COLUMNS * LANES),
         in_specs=[hbm] * 6,
         out_specs=vmem,
         scratch_shapes=[

time: 30.9 us -> 30.4 us (0.984)
  blocking collectives: 17.3 us -> 16.9 us
    all_to_all x1, blocking collectives: 17.3 us -> 16.9 us  [body(): got = lax.all_to_all(packed, ('patch', 'sub'), 0, 0, tiled=True)]
where the time goes in v5:
time: 30.4 us; the launch traced here: 30.1 us
  blocking collectives  16.9 us (56%)
  Pallas kernels  11.2 us (37%)
  starting transfers between devices  1.29 us (4%)
  between operations  0.68 us (2%)
    all_to_all x1, blocking collectives, body(): got = lax.all_to_all(packed, ('patch', 'sub'), 0, 0, tiled=True)  16.9 us
    pallas_call x1, Pallas kernels, body(): pl.pallas_call(bulk_kernel, out_shape=[array(*adjoint_height.shape), arra...  4.28 us
    pallas_call x1, Pallas kernels, body(): pl.pallas_call(functools.partial(inflow_kernel, subs), out_shape=[array(*...  2.42 us
    pallas_call x1, Pallas kernels, body(): pl.pallas_call(functools.partial(halo_kernel, subs), out_shape=[array(*ad...  2.07 us
    pallas_call x1, Pallas kernels, body(): pl.pallas_call(pack_kernel, out_shape=array(count, 1, ROWS * cols + COLUM...  1.71 us
    ppermute x1, starting transfers between devices, body(): lax.ppermute(strips, 'level', [(source, source - 1) for source in range(1...  1.29 us
    pallas_call x1, Pallas kernels, body(): pl.pallas_call(functools.partial(strips_kernel, subs), out_shape=[array(2...  0.76 us
  transfers between devices with their start and end apart: 1, of which 0 were waited for; matrix products, arithmetic and copies ran while one was open for 0% of the time, Pallas kernels for 21%

profile of v5, /device:TPU:0, one launch (start us, length us, event | category | flops | bytes accessed | tf_op | source)
XLA Modules:
  0.0 30.1 jit_solution(8756185583196071797)
XLA Ops:
  0.6 1.7 %pack.1 = f32[8,1,9728]{2,1,0:T(1,128)S(1)} custom-call(f32[1,128,1024]{2,1,0:T(8,128)} %eta_ref.3, f32[2,1,128,1024]{3,2,1,0:T(8,128)} %momenta_ref.3, f32[1,128,1024]{2,1,0:T(8,128)} %depth_ref.3, s32[1,128,1024]{2,1,0:T(8,128)} %wet_ref.3, f32[2,1024]{1,0:T(2,128)} %gain_ref.1, s32[2,1024]{1,0:T(2,128)} %index_ref.1), custom_call_target="tpu_custom_call" | custom-call | tf_op jit(solution)/shard_map/pack/pallas_call | solution.py:613
  2.3 0.0 copy-start
  2.4 16.9 %all_to_all.5.refs_1_.got_ref = f32[8,1,9728]{2,1,0:T(1,128)S(1)} all-to-all(f32[8,1,9728]{2,1,0:T(1,128)S(1)} %pack.1), channel_id=1, replica_groups=mesh['parts'=2,'patch'=4,'level'=2,'sub'=2] {'patch','sub'}, dimensions={0} | all-to-all | bytes 622592 | tf_op jit(solution)/shard_map/all_to_all | solution.py:627
  19.3 0.0 copy-done
  19.3 0.8 %strips.1 = (f32[2,8,1024]{2,1,0:T(8,128)S(1)}, f32[8,1,1024]{2,1,0:T(1,128)S(1)}) custom-call(s32[1,4,4]{2,1,0:T(4,128)S(1)} %copy-done, f32[8,1,9728]{2,1,0:T(1,128)S(1)} %all_to_all.5.refs_1_.got_ref), custom_call_target="tpu_custom_call" | custom-call | tf_op jit(solution)/shard_map/strips/pallas_call | solution.py:652
  20.0 1.3 %collective-permute-start = (f32[2,8,1024]{2,1,0:T(8,128)S(1)}, f32[2,8,1024]{2,1,0:T(8,128)S(1)}, u32[]{:S(2)}, u32[]{:S(2)}) collective-permute-start(f32[2,8,1024]{2,1,0:T(8,128)S(1)} %get-tuple-element.16), channel_id=1, source_target_pairs={{2,0},{3,1},{6,4},{7,5},{10,8},{11,9},{14,12},{15,13},{18,16},{19,... | collective-permute-start | bytes 196616 | tf_op jit(solution)/shard_map/ppermute | solution.py:662
  21.3 4.3 %bulk.1 = (f32[1,128,1024]{2,1,0:T(8,128)}, f32[2,1,128,1024]{3,2,1,0:T(8,128)}, f32[128,1024]{1,0:T(8,128)S(1)}, f32[2,128,1024]{2,1,0:T(8,128)S(1)}, f32[128,1...) custom-call(f32[1,128,1024]{2,1,0:T(8,128)} %eta_ref.3, ...), custom_call_target="tpu_custom_call" | custom-call | tf_op jit(solution)/shard_map/bulk/pallas_call | solution.py:630
  25.6 2.1 %halo.1 = (f32[1,128,1024]{2,1,0:T(8,128)}, f32[2,1,128,1024]{3,2,1,0:T(8,128)}, f32[3,2,8,1024]{3,2,1,0:T(8,128)S(1)}) custom-call(s32[1,4,4]{2,1,0:T(4,128)S(1)} %copy-done, f32[8,1,9728]{2,1,0:T(1,128)S(1)} %all_to_all.5.refs_1_.got_ref, f32[8,1,1024]{2,1,0:T(1,128)S(1)} %get-tuple-element.19.later_ref, ...), custom_call_target="tpu_custom_call", output_to_operand_aliasing={{0}: (10, {}), {1}: (11, {})} | custom-call | tf_op jit(solution)/shard_map/halo/pallas_call | solution.py:664
  27.7 0.0 collective-permute-done.finer_ref
  27.7 2.4 %inflow.1 = (f32[1,128,1024]{2,1,0:T(8,128)}, f32[2,1,128,1024]{3,2,1,0:T(8,128)}) custom-call(s32[1,4,4]{2,1,0:T(4,128)S(1)} %copy-done, f32[8,1,9728]{2,1,0:T(1,128)S(1)} %all_to_all.5.refs_1_.got_ref, f32[2,8,1024]{2,1,0:T(8,128)S(1)} %collective-permute-done.finer_ref, ...), custom_call_target="tpu_custom_call", output_to_operand_aliasing={{0}: (6, {}), {1}: (7, {})} | custom-call | tf_op jit(solution)/shard_map/inflow/pallas_call | solution.py:677
Async XLA Ops:
  2.3 16.9 %copy-start = (s32[1,4,4]{2,1,0:T(4,128)S(1)}, s32[1,4,4]{2,1,0:T(4,128)}, u32[]{:S(2)}) copy-start(s32[1,4,4]{2,1,0:T(4,128)} %links_ref.3) | copy-start | bytes 196
  20.0 7.7 %collective-permute-start = (f32[2,8,1024]{2,1,0:T(8,128)S(1)}, f32[2,8,1024]{2,1,0:T(8,128)S(1)}, u32[]{:S(2)}, u32[]{:S(2)}) collective-permute-start(f32[2,8,1024]{2,1,0:T(8,128)S(1)} %get-tuple-element.16), channel_id=1, source_target_pairs={{2,0},{3,1},{6,4},{7,5},{10,8},{11,9},{14,12},{15,13},{18,16},{19,... | collective-permute-start | bytes 196616 | tf_op jit(solution)/shard_map/ppermute | solution.py:662

commit v6 on v5

--- a/solution.py
+++ b/solution.py
@@ -296,9 +296,9 @@
 
 
 def strips_kernel(subs, *refs):
-    links_ref, got_ref = refs[:2]
+    links_ref, got_ref, _ = refs[:3]
     out_ref, rows_ref, picked_ref, narrow_ref = refs[-4:]
-    finer = (refs[2][0], refs[2][1]) if len(refs) == 7 else None
+    finer = (refs[3][0], refs[3][1]) if len(refs) == 8 else None
     eta, later = strips_of(Links(links_ref, subs), got_ref, finer, picked_ref, narrow_ref)
     out_ref[0] = eta
     out_ref[1] = later
@@ -652,12 +652,12 @@
         strips, later = pl.pallas_call(
             functools.partial(strips_kernel, subs),
             out_shape=[array(2, count, cols), array(count, 1, cols)],
-            in_specs=[smem, vmem] + [vmem] * len(flux),
+            in_specs=[smem, vmem, vmem] + [vmem] * len(flux),
             out_specs=[vmem, vmem],
             scratch_shapes=[scratch(count, cols), scratch(count, LANES)],
             compiler_params=params,
             name="strips",
-        )(adjacency, got, *flux)
+        )(adjacency, got, after[-1], *flux)
         laters.append(later)
         flux = (lax.ppermute(strips, "level", [(source, source - 1) for source in range(1, levels)]),)
 

time: 30.4 us -> 29.9 us (0.984)
  blocking collectives: 16.9 us -> 0 us
  waiting for transfers between devices: 0.01 us -> 9.4 us
  starting transfers between devices: 1.29 us -> 7.63 us
  Pallas kernels: 11.2 us -> 11.8 us
    all_to_all x1 -> x0, blocking collectives: 16.9 us -> none  [body(): got = lax.all_to_all(packed, ('patch', 'sub'), 0, 0, tiled=True)]
    all_to_all x0 -> x1, waiting for transfers between devices: none -> 6.62 us  [body(): got = lax.all_to_all(packed, ('patch', 'sub'), 0, 0, tiled=True)]
    all_to_all x0 -> x1, starting transfers between devices: none -> 6.34 us  [body(): got = lax.all_to_all(packed, ('patch', 'sub'), 0, 0, tiled=True)]
    ppermute x1, waiting for transfers between devices: 0.01 us -> 2.79 us  [body(): lax.ppermute(strips, 'level', [(source, source - 1) for source in range(1...]
    pallas_call x1, Pallas kernels: 1.71 us -> 2.43 us  [body(): pl.pallas_call(pack_kernel, out_shape=array(count, 1, ROWS * cols + COLUM...]
  transfers between devices with their start and end apart: 1 -> 2, of which waited for: 0 -> 2; matrix products, arithmetic and copies ran while one was open for 0% -> 0% of each run, Pallas kernels for 21% -> 21%
where the time goes in v6:
time: 29.9 us; the launch traced here: 29.5 us
  Pallas kernels  11.8 us (39%)
  waiting for transfers between devices  9.4 us (31%)
  starting transfers between devices  7.63 us (26%)
  between operations  0.67 us (2%)
    all_to_all x1, waiting for transfers between devices, body(): got = lax.all_to_all(packed, ('patch', 'sub'), 0, 0, tiled=True)  6.62 us
    all_to_all x1, starting transfers between devices, body(): got = lax.all_to_all(packed, ('patch', 'sub'), 0, 0, tiled=True)  6.34 us
    pallas_call x1, Pallas kernels, body(): pl.pallas_call(bulk_kernel, out_shape=[array(*adjoint_height.shape), arra...  4.17 us
    ppermute x1, waiting for transfers between devices, body(): lax.ppermute(strips, 'level', [(source, source - 1) for source in range(1...  2.79 us
    pallas_call x1, Pallas kernels, body(): pl.pallas_call(pack_kernel, out_shape=array(count, 1, ROWS * cols + COLUM...  2.43 us
    pallas_call x1, Pallas kernels, body(): pl.pallas_call(functools.partial(inflow_kernel, subs), out_shape=[array(*...  2.41 us
    pallas_call x1, Pallas kernels, body(): pl.pallas_call(functools.partial(halo_kernel, subs), out_shape=[array(*ad...  2.07 us
    ppermute x1, starting transfers between devices, body(): lax.ppermute(strips, 'level', [(source, source - 1) for source in range(1...  1.29 us
  transfers between devices with their start and end apart: 2, of which 2 were waited for; matrix products, arithmetic and copies ran while one was open for 0% of the time, Pallas kernels for 21%

profile of v6, /device:TPU:0, one launch (start us, length us, event | category | flops | bytes accessed | tf_op | source)
XLA Modules:
  0.0 29.5 jit_solution(7352995693303535296)
XLA Ops:
  0.6 2.4 %pack.1 = f32[8,1,9728]{2,1,0:T(1,128)} custom-call(f32[1,128,1024]{2,1,0:T(8,128)} %eta_ref.3, f32[2,1,128,1024]{3,2,1,0:T(8,128)} %momenta_ref.3, f32[1,128,1024]{2,1,0:T(8,128)} %depth_ref.3, s32[1,128,1024]{2,1,0:T(8,128)} %wet_ref.3, f32[2,1024]{1,0:T(2,128)} %gain_ref.1, s32[2,1024]{1,0:T(2,128)} %index_ref.1), custom_call_target="tpu_custom_call" | custom-call | tf_op jit(solution)/shard_map/pack/pallas_call | solution.py:613
  3.1 6.3 %all-to-all-start = ((f32[8,1,9728]{2,1,0:T(1,128)}), f32[8,1,9728]{2,1,0:T(1,128)S(1)}, u32[]{:S(2)}, u32[]{:S(2)}) async-start(f32[8,1,9728]{2,1,0:T(1,128)} %pack.1), calls=%async_computation | async-start | bytes 622592 | tf_op jit(solution)/shard_map/all_to_all | solution.py:627
  9.4 0.0 copy-start
  9.4 4.2 %bulk.1 = (f32[1,128,1024]{2,1,0:T(8,128)}, f32[2,1,128,1024]{3,2,1,0:T(8,128)}, f32[128,1024]{1,0:T(8,128)S(1)}, f32[2,128,1024]{2,1,0:T(8,128)S(1)}, f32[128,1...) custom-call(f32[1,128,1024]{2,1,0:T(8,128)} %eta_ref.3, ...), custom_call_target="tpu_custom_call" | custom-call | tf_op jit(solution)/shard_map/bulk/pallas_call | solution.py:630
  13.6 6.6 %all-to-all-done.refs_1_.got_ref = f32[8,1,9728]{2,1,0:T(1,128)S(1)} async-done(((f32[8,1,9728]{2,1,0:T(1,128)}), f32[8,1,9728]{2,1,0:T(1,128)S(1)}, u32[]{:S(2)}, u32[]{:S(2)}) %all-to-all-start) | async-done | bytes 311328 | tf_op jit(solution)/shard_map/all_to_all | solution.py:627
  20.2 0.0 copy-done
  20.2 0.8 %strips.1 = (f32[2,8,1024]{2,1,0:T(8,128)S(1)}, f32[8,1,1024]{2,1,0:T(1,128)S(1)}) custom-call(s32[1,4,4]{2,1,0:T(4,128)S(1)} %copy-done, f32[8,1,9728]{2,1,0:T(1,128)S(1)} %all-to-all-done.refs_1_.got_ref, f32[6,8,128]{2,1,0:T(8,128)S(1)} %get-tuple-element.16.refs_2_.turned), custom_call_target="tpu_custom_call" | custom-call | tf_op jit(solution)/shard_map/strips/pallas_call | solution.py:652
  21.0 1.3 %collective-permute-start = (f32[2,8,1024]{2,1,0:T(8,128)S(1)}, f32[2,8,1024]{2,1,0:T(8,128)S(1)}, u32[]{:S(2)}, u32[]{:S(2)}) collective-permute-start(f32[2,8,1024]{2,1,0:T(8,128)S(1)} %get-tuple-element.17), channel_id=1, source_target_pairs={{2,0},{3,1},{6,4},{7,5},{10,8},{11,9},{14,12},{15,13},{18,16},{19,... | collective-permute-start | bytes 196616 | tf_op jit(solution)/shard_map/ppermute | solution.py:662
  22.3 2.1 %halo.1 = (f32[1,128,1024]{2,1,0:T(8,128)}, f32[2,1,128,1024]{3,2,1,0:T(8,128)}, f32[3,2,8,1024]{3,2,1,0:T(8,128)S(1)}) custom-call(s32[1,4,4]{2,1,0:T(4,128)S(1)} %copy-done, f32[8,1,9728]{2,1,0:T(1,128)S(1)} %all-to-all-done.refs_1_.got_ref, f32[8,1,1024]{2,1,0:T(1,128)S(1)} %get-tuple-element.20.later_ref, ...), custom_call_target="tpu_custom_call", output_to_operand_aliasing={{0}: (10, {}), {1}: (11, {})} | custom-call | tf_op jit(solution)/shard_map/halo/pallas_call | solution.py:664
  24.3 2.8 %collective-permute-done.finer_ref = f32[2,8,1024]{2,1,0:T(8,128)S(1)} collective-permute-done((f32[2,8,1024]{2,1,0:T(8,128)S(1)}, f32[2,8,1024]{2,1,0:T(8,128)S(1)}, u32[]{:S(2)}, u32[]{:S(2)}) %collective-permute-start) | collective-permute-done | bytes 65568 | tf_op jit(solution)/shard_map/ppermute | solution.py:662
  27.1 2.4 %inflow.1 = (f32[1,128,1024]{2,1,0:T(8,128)}, f32[2,1,128,1024]{3,2,1,0:T(8,128)}) custom-call(s32[1,4,4]{2,1,0:T(4,128)S(1)} %copy-done, f32[8,1,9728]{2,1,0:T(1,128)S(1)} %all-to-all-done.refs_1_.got_ref, f32[2,8,1024]{2,1,0:T(8,128)S(1)} %collective-permute-done.finer_ref, ...), custom_call_target="tpu_custom_call", output_to_operand_aliasing={{0}: (6, {}), {1}: (7, {})} | custom-call | tf_op jit(solution)/shard_map/inflow/pallas_call | solution.py:677
Async XLA Ops:
  3.1 17.1 %all-to-all-start = ((f32[8,1,9728]{2,1,0:T(1,128)}), f32[8,1,9728]{2,1,0:T(1,128)S(1)}, u32[]{:S(2)}, u32[]{:S(2)}) async-start(f32[8,1,9728]{2,1,0:T(1,128)} %pack.1), calls=%async_computation | async-start | bytes 622592 | tf_op jit(solution)/shard_map/all_to_all | solution.py:627
  9.4 10.8 %copy-start = (s32[1,4,4]{2,1,0:T(4,128)S(1)}, s32[1,4,4]{2,1,0:T(4,128)}, u32[]{:S(2)}) copy-start(s32[1,4,4]{2,1,0:T(4,128)} %links_ref.3) | copy-start | bytes 196
  21.0 6.2 %collective-permute-start = (f32[2,8,1024]{2,1,0:T(8,128)S(1)}, f32[2,8,1024]{2,1,0:T(8,128)S(1)}, u32[]{:S(2)}, u32[]{:S(2)}) collective-permute-start(f32[2,8,1024]{2,1,0:T(8,128)S(1)} %get-tuple-element.17), channel_id=1, source_target_pairs={{2,0},{3,1},{6,4},{7,5},{10,8},{11,9},{14,12},{15,13},{18,16},{19,... | collective-permute-start | bytes 196616 | tf_op jit(solution)/shard_map/ppermute | solution.py:662

commit v7 on v6

--- a/solution.py
+++ b/solution.py
@@ -1,5 +1,3 @@
-import functools
-
 import jax
 import jax.numpy as jnp
 from jax import lax
@@ -197,35 +195,91 @@
         copy.wait()
 
 
-def stacked(got_ref, part):
-    return jnp.concatenate([got_ref[segment, :, part] for segment in range(got_ref.shape[0])], axis=0)
+def after_kernel(value_ref, other_ref, out_ref):
+    del value_ref, other_ref, out_ref
+
+
+class Segment:
+    def __init__(self, patch, flipped):
+        self.patch, self.flipped = patch, flipped
+
+    def place(self, patches):
+        return self.flipped * patches + self.patch
 
 
 class Links:
-    def __init__(self, links_ref, subs):
-        self.links_ref, self.subs = links_ref, subs
+    def __init__(self, links_ref, patches):
+        self.links_ref, self.patches = links_ref, patches
+        self.half = lax.axis_index("sub")
+
+    def own(self):
+        return Segment(lax.axis_index("patch"), 0)
+
+    def all(self):
+        return [Segment(patch, flipped) for flipped in range(2) for patch in range(self.patches)]
 
     def across(self, segment, way):
-        patch = self.links_ref[0, segment // self.subs, way]
+        patch = self.links_ref[0, segment.patch, way]
         return jnp.maximum(patch, 0), jnp.where(patch >= 0, 1.0, 0.0)
 
+    def other_half(self, segment, way, inner):
+        patch, there = self.across(segment, way)
+        inside = self.half == (inner ^ segment.flipped)
+        return Segment(jnp.where(inside, segment.patch, patch), 1 - segment.flipped), jnp.where(inside, 1.0, there)
+
     def north(self, segment):
-        patch, there = self.across(segment, 0)
-        inside = segment % self.subs > 0
-        return jnp.where(inside, segment - 1, patch * self.subs + self.subs - 1), jnp.where(inside, 1.0, there)
+        return self.other_half(segment, 0, 1)
 
     def south(self, segment):
-        patch, there = self.across(segment, 1)
-        inside = segment % self.subs < self.subs - 1
-        return jnp.where(inside, segment + 1, patch * self.subs), jnp.where(inside, 1.0, there)
+        return self.other_half(segment, 1, 0)
 
     def west(self, segment):
         patch, there = self.across(segment, 2)
-        return patch * self.subs + segment % self.subs, there
+        return Segment(patch, segment.flipped), there
 
     def east(self, segment):
         patch, there = self.across(segment, 3)
-        return patch * self.subs + segment % self.subs, there
+        return Segment(patch, segment.flipped), there
+
+
+class Packets:
+    def __init__(self, got_refs, rows, cols, inflow_ref=None):
+        self.got_refs, self.rows, self.cols, self.inflow_ref = got_refs, rows, cols, inflow_ref
+        self.patches = got_refs[0].shape[0]
+
+    def row(self, segment, row, left=0, size=None):
+        return self.got_refs[segment.flipped][segment.patch, :, row_at(row, self.cols, left, size)]
+
+    def column(self, segment, column):
+        return self.got_refs[segment.flipped][segment.patch, :, column_at(column, self.cols)]
+
+    def rows_of(self, segments, row):
+        return jnp.concatenate([self.row(segment, row) for segment in segments], axis=0)
+
+    def columns_of(self, segments, column):
+        return jnp.concatenate([self.column(segment, column) for segment in segments], axis=0)
+
+    def field_row(self, segment, row, left=0, size=None):
+        return self.row(segment, row, left, size) if self.inflow_ref is None else 0.0
+
+    def field_column(self, segment, column):
+        return self.column(segment, column) if self.inflow_ref is None else 0.0
+
+    def inflow(self, step, segment, left=0, size=None):
+        size = self.cols if size is None else size
+        place = 2 * self.patches * step + segment.place(self.patches)
+        return self.inflow_ref[place, :, left:left + size]
+
+    def strip_tile(self, segment, left):
+        if self.inflow_ref is None:
+            return self.row(segment, STRIP, left, LANES)
+        return self.inflow(0, segment, left, LANES)
+
+    def at_first(self, step, segment, left, turned):
+        if self.inflow_ref is None:
+            return 0.0
+        tile = self.inflow(step, segment, left, LANES)
+        return jnp.where(iota((1, LANES), 1) == 0, rolled(tile, turned, 1) if turned else tile, 0.0)
 
 
 def nested(flux, index):
@@ -246,97 +300,68 @@
     return jnp.concatenate(rows, axis=0) if len(rows) > 1 else rows[0]
 
 
-def strips_of(links, got_ref, finer, picked_ref, narrow_ref):
+def strips_of(links, packets, finer, picked_ref, narrow_ref):
     count, cols = picked_ref.shape
+    patches = packets.patches
     lane = iota((count, LANES), 1)
-    strip, depth = stacked(got_ref, row_at(STRIP, cols)), stacked(got_ref, row_at(STRIP_DEPTH, cols))
+    every = links.all()
+    strip, depth = packets.rows_of(every, STRIP), packets.rows_of(every, STRIP_DEPTH)
     mask = wet(depth)
     if finer is None:
         inflow = jnp.zeros_like(strip)
     else:
-        gain = stacked(got_ref, row_at(GAIN, cols))
-        index = stacked(got_ref, row_at(INDEX, cols)).astype(jnp.int32)
+        gain = packets.rows_of(every, GAIN)
+        index = packets.rows_of(every, INDEX).astype(jnp.int32)
         inflow = gain * nested(finer[0], index)
     eta = strip + inflow
 
     narrow_ref[...] = eta[:, :LANES]
-    for segment in range(count):
+    for place, segment in enumerate(every):
         east, there = links.east(segment)
-        picked_ref[segment:segment + 1, :LANES] = narrow_ref[pl.ds(east, 1), :] * there
+        picked_ref[place:place + 1, :LANES] = narrow_ref[pl.ds(east.place(patches), 1), :] * there
     east_eta = rolled(picked_ref[:, :LANES], -1, 1)
     after = rolled(inflow, -1, 1)
     after = jnp.concatenate(
         [after[:, :-LANES], jnp.where(lane == LANES - 1, east_eta, after[:, -LANES:])], axis=1)
     more_row = courant * mask * (inflow - after)
 
-    last_eta = stacked(got_ref, column_at(LAST_ETA, cols))
-    last_row = stacked(got_ref, column_at(LAST_ROW, cols))
+    last_eta = packets.columns_of(every, LAST_ETA)
+    last_row = packets.columns_of(every, LAST_ROW)
     first_of_last = rolled(last_row + courant * last_eta, -1, 1)
     narrow_ref[...] = mask[:, -LANES:] * first_of_last + more_row[:, -LANES:]
-    for segment in range(count):
+    for place, segment in enumerate(every):
         west, there = links.west(segment)
-        picked_ref[segment:segment + 1, :LANES] = narrow_ref[pl.ds(west, 1), :] * there
+        picked_ref[place:place + 1, :LANES] = narrow_ref[pl.ds(west.place(patches), 1), :] * there
     west_row = rolled(picked_ref[:, :LANES], 1, 1)
     before = rolled(more_row, 1, 1)
     before = jnp.concatenate([jnp.where(lane == 0, west_row, before[:, :LANES]), before[:, LANES:]], axis=1)
 
-    for segment in range(count):
+    for place, segment in enumerate(every):
         north, there = links.north(segment)
-        picked_ref[segment:segment + 1, :] = got_ref[north, :, row_at(EDGE_FLOW, cols)] * there
+        picked_ref[place:place + 1, :] = packets.row(north, EDGE_FLOW) * there
     flow = picked_ref[...]
-    for segment in range(count):
+    for place, segment in enumerate(every):
         north, there = links.north(segment)
-        picked_ref[segment:segment + 1, :] = got_ref[north, :, row_at(EDGE_DEPTH, cols)] * there
+        picked_ref[place:place + 1, :] = packets.row(north, EDGE_DEPTH) * there
     north_col = flow - courant * wet(picked_ref[...]) * eta
-    later = (stacked(got_ref, row_at(STRIP_SUM, cols)) + mask * inflow
+    later = (packets.rows_of(every, STRIP_SUM) + mask * inflow
              - courant * depth * (more_row - before + courant * mask * inflow - north_col))
     if finer is None:
         return eta, later
     return eta, later + gain * nested(finer[1], index)
 
 
-def strips_kernel(subs, *refs):
-    links_ref, got_ref, _ = refs[:3]
+def strips_kernel(*refs):
+    links_ref, mine_ref, other_ref = refs[:3]
     out_ref, rows_ref, picked_ref, narrow_ref = refs[-4:]
     finer = (refs[3][0], refs[3][1]) if len(refs) == 8 else None
-    eta, later = strips_of(Links(links_ref, subs), got_ref, finer, picked_ref, narrow_ref)
+    links = Links(links_ref, mine_ref.shape[0])
+    packets = Packets((mine_ref, other_ref), None, out_ref.shape[2])
+    eta, later = strips_of(links, packets, finer, picked_ref, narrow_ref)
     out_ref[0] = eta
     out_ref[1] = later
-    for segment in range(out_ref.shape[1]):
-        rows_ref[segment] = later[segment:segment + 1]
-
-
-class Packets:
-    def __init__(self, got_ref, rows, cols, inflow_ref=None):
-        self.got_ref, self.rows, self.cols, self.inflow_ref = got_ref, rows, cols, inflow_ref
-
-    def row(self, segment, row, left=0, size=None):
-        return self.got_ref[segment, :, row_at(row, self.cols, left, size)]
-
-    def column(self, segment, column):
-        return self.got_ref[segment, :, column_at(column, self.cols)]
-
-    def field_row(self, segment, row, left=0, size=None):
-        return self.row(segment, row, left, size) if self.inflow_ref is None else 0.0
-
-    def field_column(self, segment, column):
-        return self.column(segment, column) if self.inflow_ref is None else 0.0
-
-    def inflow(self, step, segment, left=0, size=None):
-        size = self.cols if size is None else size
-        count = self.got_ref.shape[0]
-        return self.inflow_ref[step * count + segment, :, left:left + size]
-
-    def strip_tile(self, segment, left):
-        if self.inflow_ref is None:
-            return self.row(segment, STRIP, left, LANES)
-        return self.inflow(0, segment, left, LANES)
-
-    def at_first(self, step, segment, left, turned):
-        if self.inflow_ref is None:
-            return 0.0
-        tile = self.inflow(step, segment, left, LANES)
-        return jnp.where(iota((1, LANES), 1) == 0, rolled(tile, turned, 1) if turned else tile, 0.0)
+    for place in range(out_ref.shape[1]):
+        rows_ref[place] = later[place:place + 1]
 
 
 def beside(links, packets, own):
@@ -449,18 +474,15 @@
             for low in (0, rows - TILE)]
 
 
-def own_segment(subs):
-    return lax.axis_index("patch") * subs + lax.axis_index("sub")
-
-
-def halo_kernel(subs, links_ref, got_ref, later_ref, eta_after, momenta_after, wet_after, depth_after,
+def halo_kernel(links_ref, mine_ref, other_ref, later_ref, eta_after, momenta_after, wet_after, depth_after,
                 eta_ends, row_ends, turned, eta_hbm, momenta_hbm, eta_out, momenta_out, ends_out,
                 left_new, right_new, sems):
     del eta_hbm, momenta_hbm
     rows, cols = eta_after.shape
     right = cols - LANES
-    links, own = Links(links_ref, subs), own_segment(subs)
-    packets = Packets(got_ref, rows, cols)
+    links = Links(links_ref, mine_ref.shape[0])
+    own = links.own()
+    packets = Packets((mine_ref, other_ref), rows, cols)
     columns = beside(links, packets, own)
     west_row, west_mask, west_eta, east_eta, east_sum, east_depth = columns
     fields = eta_after, momenta_after.at[0], momenta_after.at[1]
@@ -521,7 +543,7 @@
     below, there = links.south(own)
     low = two_steps(
         nothing, wet_after[rows - TILE:], depth_after[rows - TILE:], low_sides, (eta_ends[1], row_ends[1]),
-        south=(packets.row(below, STRIP) * there, later_ref[below] * there))
+        south=(packets.row(below, STRIP) * there, later_ref[below.place(packets.patches)] * there))
     line, lane = iota((TILE, cols), 0), iota((TILE, cols), 1)
     for place, field in enumerate(fields):
         more = jnp.concatenate([left[place], middle, last[place]], axis=0).T
@@ -537,19 +559,19 @@
         copy.wait()
 
 
-def inflow_kernel(subs, links_ref, got_ref, finer_ref, wet_after, depth_after, ends_ref, eta_hbm, momenta_hbm,
+def inflow_kernel(links_ref, mine_ref, other_ref, finer_ref, wet_after, depth_after, ends_ref, eta_hbm, momenta_hbm,
                   eta_out, momenta_out, inflow_ref, new_ref, sems):
     del eta_hbm, momenta_hbm
     rows, cols = wet_after.shape
-    count = got_ref.shape[0]
-    links, own = Links(links_ref, subs), own_segment(subs)
-    gain = stacked(got_ref, row_at(GAIN, cols))
-    index = stacked(got_ref, row_at(INDEX, cols)).astype(jnp.int32)
+    links = Links(links_ref, mine_ref.shape[0])
+    own, every = links.own(), links.all()
+    packets = Packets((mine_ref, other_ref), rows, cols, inflow_ref)
+    gain = packets.rows_of(every, GAIN)
+    index = packets.rows_of(every, INDEX).astype(jnp.int32)
     for number in range(2):
         inflow = gain * nested(finer_ref[number], index)
-        for segment in range(count):
-            inflow_ref[number * count + segment] = inflow[segment:segment + 1]
-    packets = Packets(got_ref, rows, cols, inflow_ref)
+        for place in range(len(every)):
+            inflow_ref[number * len(every) + place] = inflow[place:place + 1]
     columns = beside(links, packets, own)
     top_sides, low_sides = as_sublanes(columns)
     line = iota((TILE, cols), 0)
@@ -595,8 +617,8 @@
 def body(adjoint_height, adjoint_momenta, depth, wet_mask, adjacency, nest_gain, nest_index):
     rows, cols = adjoint_height.shape[1:]
     levels = lax.axis_size("level")
-    subs = lax.axis_size("sub")
-    count = lax.axis_size("patch") * subs
+    patches = lax.axis_size("patch")
+    count = 2 * patches
     params = pltpu.CompilerParams(vmem_limit_bytes=VMEM_LIMIT)
     vmem = pl.BlockSpec(memory_space=pltpu.VMEM)
     smem = pl.BlockSpec(memory_space=pltpu.SMEM)
@@ -612,7 +634,7 @@
               for field in (adjoint_height, adjoint_momenta, depth, wet_mask, nest_gain, nest_index)]
     packed = pl.pallas_call(
         pack_kernel,
-        out_shape=array(count, 1, ROWS * cols + COLUMNS * LANES),
+        out_shape=pltpu.VMEM((patches, 1, ROWS * cols + COLUMNS * LANES), jnp.float32),
         in_specs=[hbm] * 6,
         out_specs=vmem,
         scratch_shapes=[
@@ -624,8 +646,6 @@
         compiler_params=params,
         name="pack",
     )(*fields)
-    got = lax.all_to_all(packed, ("patch", "sub"), 0, 0, tiled=True)
-
     parts = 4
     eta_new, momenta_new, *after = pl.pallas_call(
         bulk_kernel,
@@ -646,46 +666,57 @@
         name="bulk",
     )(*fields[:4])
 
+    mine = pl.pallas_call(
+        after_kernel,
+        out_shape=array(*packed.shape),
+        in_specs=[vmem, vmem],
+        out_specs=vmem,
+        input_output_aliases={0: 0},
+        compiler_params=params,
+        name="after",
+    )(lax.all_to_all(packed, "patch", 0, 0, tiled=True), after[-1])
+    other = lax.ppermute(mine, "sub", [(0, 1), (1, 0)])
+
     flux = ()
     laters = []
     for turn in range(levels - 1):
         strips, later = pl.pallas_call(
-            functools.partial(strips_kernel, subs),
+            strips_kernel,
             out_shape=[array(2, count, cols), array(count, 1, cols)],
-            in_specs=[smem, vmem, vmem] + [vmem] * len(flux),
+            in_specs=[smem] + [vmem] * (2 + len(flux)),
             out_specs=[vmem, vmem],
             scratch_shapes=[scratch(count, cols), scratch(count, LANES)],
             compiler_params=params,
             name="strips",
-        )(adjacency, got, after[-1], *flux)
+        )(adjacency, mine, other, *flux)
         laters.append(later)
         flux = (lax.ppermute(strips, "level", [(source, source - 1) for source in range(1, levels)]),)
 
     eta_new, momenta_new, ends = pl.pallas_call(
-        functools.partial(halo_kernel, subs),
+        halo_kernel,
         out_shape=[array(*adjoint_height.shape), array(*adjoint_momenta.shape), array(3, 2, TILE, cols)],
-        in_specs=[smem] + [vmem] * 9 + [hbm] * 2,
+        in_specs=[smem] + [vmem] * 10 + [hbm] * 2,
         out_specs=[hbm, hbm, vmem],
-        input_output_aliases={10: 0, 11: 1},
+        input_output_aliases={11: 0, 12: 1},
         scratch_shapes=[
             scratch(3, rows - 2 * TILE, LANES), scratch(3, rows - 2 * TILE, LANES), pltpu.SemaphoreType.DMA((3, 2)),
         ],
         compiler_params=params,
         name="halo",
-    )(adjacency, got, laters[0], *after, eta_new, momenta_new)
+    )(adjacency, mine, other, laters[0], *after, eta_new, momenta_new)
 
     return pl.pallas_call(
-        functools.partial(inflow_kernel, subs),
+        inflow_kernel,
         out_shape=[array(*adjoint_height.shape), array(*adjoint_momenta.shape)],
-        in_specs=[smem] + [vmem] * 5 + [hbm] * 2,
+        in_specs=[smem] + [vmem] * 6 + [hbm] * 2,
         out_specs=[hbm, hbm],
-        input_output_aliases={6: 0, 7: 1},
+        input_output_aliases={7: 0, 8: 1},
         scratch_shapes=[
             scratch(2 * count, 1, cols), scratch(3, 2, TILE, cols), pltpu.SemaphoreType.DMA((3, 2)),
         ],
         compiler_params=params,
         name="inflow",
-    )(adjacency, got, *flux, after[2], after[3], ends, eta_new, momenta_new)
+    )(adjacency, mine, other, *flux, after[2], after[3], ends, eta_new, momenta_new)
 
 
 def solution(mesh):

time: 29.9 us -> 26.7 us (0.89)
  waiting for transfers between devices: 9.4 us -> 6.25 us
    all_to_all x1, waiting for transfers between devices: 6.62 us -> 2.07 us  [body(): lax.all_to_all(packed, 'patch', 0, 0, tiled=True)]
    ppermute x0 -> x1, waiting for transfers between devices: none -> 1.38 us  [body(): other = lax.ppermute(mine, 'sub', [(0, 1), (1, 0)])]
    pallas_call x4 -> x5, Pallas kernels: 7.66 us -> 7.58 us  [the longest x1 2.41 us: body(): pl.pallas_call(inflow_kernel, out_shape=[array(*adjoint_height.shape), ar...]
  transfers between devices with their start and end apart: 2 -> 3, of which waited for: 2 -> 3; matrix products, arithmetic and copies ran while one was open for 0% -> 0% of each run, Pallas kernels for 21% -> 24%
where the time goes in v7:
time: 26.7 us; the launch traced here: 26.4 us
  Pallas kernels  11.8 us (44%)
  starting transfers between devices  7.62 us (29%)
  waiting for transfers between devices  6.25 us (23%)
  between operations  0.67 us (3%)
    all_to_all x1, starting transfers between devices, body(): lax.all_to_all(packed, 'patch', 0, 0, tiled=True)  6.33 us
    pallas_call x1, Pallas kernels, body(): pl.pallas_call(bulk_kernel, out_shape=[array(*adjoint_height.shape), arra...  4.26 us
    ppermute x1, waiting for transfers between devices, body(): lax.ppermute(strips, 'level', [(source, source - 1) for source in range(1...  2.8 us
    pallas_call x1, Pallas kernels, body(): pl.pallas_call(inflow_kernel, out_shape=[array(*adjoint_height.shape), ar...  2.41 us
    pallas_call x1, Pallas kernels, body(): pl.pallas_call(pack_kernel, out_shape=pltpu.VMEM((patches, 1, ROWS * cols...  2.36 us
    all_to_all x1, waiting for transfers between devices, body(): lax.all_to_all(packed, 'patch', 0, 0, tiled=True)  2.07 us
    pallas_call x1, Pallas kernels, body(): pl.pallas_call(halo_kernel, out_shape=[array(*adjoint_height.shape), arra...  2.05 us
    ppermute x1, waiting for transfers between devices, body(): other = lax.ppermute(mine, 'sub', [(0, 1), (1, 0)])  1.38 us
  transfers between devices with their start and end apart: 3, of which 3 were waited for; matrix products, arithmetic and copies ran while one was open for 0% of the time, Pallas kernels for 24%

profile of v7, /device:TPU:0, one launch (start us, length us, event | category | flops | bytes accessed | tf_op | source)
XLA Modules:
  0.0 26.4 jit_solution(17432222354741065210)
XLA Ops:
  0.6 2.4 %pack.1 = f32[4,1,9728]{2,1,0:T(1,128)} custom-call(f32[1,128,1024]{2,1,0:T(8,128)} %eta_ref.3, f32[2,1,128,1024]{3,2,1,0:T(8,128)} %momenta_ref.3, f32[1,128,1024]{2,1,0:T(8,128)} %depth_ref.3, s32[1,128,1024]{2,1,0:T(8,128)} %wet_ref.3, f32[2,1024]{1,0:T(2,128)} %gain_ref.1, s32[2,1024]{1,0:T(2,128)} %index_ref.1), custom_call_target="tpu_custom_call" | custom-call | tf_op jit(solution)/shard_map/pack/pallas_call | solution.py:635
  3.0 6.3 %all-to-all-start = ((f32[4,1,9728]{2,1,0:T(1,128)}), f32[4,1,9728]{2,1,0:T(1,128)S(1)}, u32[]{:S(2)}, u32[]{:S(2)}) async-start(f32[4,1,9728]{2,1,0:T(1,128)} %pack.1), calls=%async_computation | async-start | bytes 311296 | tf_op jit(solution)/shard_map/all_to_all | solution.py:677
  9.3 4.3 %bulk.1 = (f32[1,128,1024]{2,1,0:T(8,128)}, f32[2,1,128,1024]{3,2,1,0:T(8,128)}, f32[128,1024]{1,0:T(8,128)S(1)}, f32[2,128,1024]{2,1,0:T(8,128)S(1)}, f32[128,1...) custom-call(f32[1,128,1024]{2,1,0:T(8,128)} %eta_ref.3, ...), custom_call_target="tpu_custom_call" | custom-call | tf_op jit(solution)/shard_map/bulk/pallas_call | solution.py:650
  13.6 2.1 %all-to-all-done.value_ref = f32[4,1,9728]{2,1,0:T(1,128)S(1)} async-done(((f32[4,1,9728]{2,1,0:T(1,128)}), f32[4,1,9728]{2,1,0:T(1,128)S(1)}, u32[]{:S(2)}, u32[]{:S(2)}) %all-to-all-start) | async-done | bytes 155680 | tf_op jit(solution)/shard_map/all_to_all | solution.py:677
  15.7 0.0 copy-start
  15.7 0.0 collective-permute-start
  15.7 1.4 %collective-permute-done.refs_2_.other_ref = f32[4,1,9728]{2,1,0:T(1,128)S(1)} collective-permute-done((f32[4,1,9728]{2,1,0:T(1,128)S(1)}, f32[4,1,9728]{2,1,0:T(1,128)S(1)}, u32[]{:S(2)}, u32[]{:S(2)}) %collective-permute-start) | collective-permute-done | bytes 155680 | tf_op jit(solution)/shard_map/ppermute | solution.py:678
  17.1 0.0 copy-done
  17.1 0.8 %strips.1 = (f32[2,8,1024]{2,1,0:T(8,128)S(1)}, f32[8,1,1024]{2,1,0:T(1,128)S(1)}) custom-call(s32[1,4,4]{2,1,0:T(4,128)S(1)} %copy-done, f32[4,1,9728]{2,1,0:T(1,128)S(1)} %after.1.refs_1_.mine_ref, f32[4,1,9728]{2,1,0:T(1,128)S(1)} %collective-permute-done.refs_2_.other_ref), custom_call_target="tpu_custom_call" | custom-call | tf_op jit(solution)/shard_map/strips/pallas_call | solution.py:683
  17.8 1.3 %collective-permute-start.1 = (f32[2,8,1024]{2,1,0:T(8,128)S(1)}, f32[2,8,1024]{2,1,0:T(8,128)S(1)}, u32[]{:S(2)}, u32[]{:S(2)}) collective-permute-start(f32[2,8,1024]{2,1,0:T(8,128)S(1)} %get-tuple-element.17), channel_id=1, source_target_pairs={{2,0},{3,1},{6,4},{7,5},{10,8},{11,9},{14,12},{15,13},{18,16},{19,... | collective-permute-start | bytes 196616 | tf_op jit(solution)/shard_map/ppermute | solution.py:693
  19.1 2.0 %halo.1 = (f32[1,128,1024]{2,1,0:T(8,128)}, f32[2,1,128,1024]{3,2,1,0:T(8,128)}, f32[3,2,8,1024]{3,2,1,0:T(8,128)S(1)}) custom-call(s32[1,4,4]{2,1,0:T(4,128)S(1)} %copy-done, f32[4,1,9728]{2,1,0:T(1,128)S(1)} %after.1.refs_1_.mine_ref, f32[4,1,9728]{2,1,0:T(1,128)S(1)} %collective-permute-done.refs_2_.other_ref, ...), custom_call_target="tpu_custom_call", output_to_operand_aliasing={{0}: (11, {}), {1}: (12, {})} | custom-call | tf_op jit(solution)/shard_map/halo/pallas_call | solution.py:695
  21.2 2.8 %collective-permute-done.1.finer_ref = f32[2,8,1024]{2,1,0:T(8,128)S(1)} collective-permute-done((f32[2,8,1024]{2,1,0:T(8,128)S(1)}, f32[2,8,1024]{2,1,0:T(8,128)S(1)}, u32[]{:S(2)}, u32[]{:S(2)}) %collective-permute-start.1) | collective-permute-done | bytes 65568 | tf_op jit(solution)/shard_map/ppermute | solution.py:693
  24.0 2.4 %inflow.1 = (f32[1,128,1024]{2,1,0:T(8,128)}, f32[2,1,128,1024]{3,2,1,0:T(8,128)}) custom-call(s32[1,4,4]{2,1,0:T(4,128)S(1)} %copy-done, f32[4,1,9728]{2,1,0:T(1,128)S(1)} %after.1.refs_1_.mine_ref, f32[4,1,9728]{2,1,0:T(1,128)S(1)} %collective-permute-done.refs_2_.other_ref, ...), custom_call_target="tpu_custom_call", output_to_operand_aliasing={{0}: (7, {}), {1}: (8, {})} | custom-call | tf_op jit(solution)/shard_map/inflow/pallas_call | solution.py:708
  (1 shorter events, 0.0 us)
Async XLA Ops:
  3.0 12.7 %all-to-all-start = ((f32[4,1,9728]{2,1,0:T(1,128)}), f32[4,1,9728]{2,1,0:T(1,128)S(1)}, u32[]{:S(2)}, u32[]{:S(2)}) async-start(f32[4,1,9728]{2,1,0:T(1,128)} %pack.1), calls=%async_computation | async-start | bytes 311296 | tf_op jit(solution)/shard_map/all_to_all | solution.py:677
  15.7 1.4 %copy-start = (s32[1,4,4]{2,1,0:T(4,128)S(1)}, s32[1,4,4]{2,1,0:T(4,128)}, u32[]{:S(2)}) copy-start(s32[1,4,4]{2,1,0:T(4,128)} %links_ref.3) | copy-start | bytes 196
  15.7 1.4 %collective-permute-start = (f32[4,1,9728]{2,1,0:T(1,128)S(1)}, f32[4,1,9728]{2,1,0:T(1,128)S(1)}, u32[]{:S(2)}, u32[]{:S(2)}) collective-permute-start(f32[4,1,9728]{2,1,0:T(1,128)S(1)} %after.1.refs_1_.mine_ref), channel_id=1, source_target_pairs={{0,1},{1,0},{2,3},{3,2},{4,5},{5,4},{6,7},{7,6},{8,9},{9,8},{10,11... | collective-permute-start | bytes 466952 | tf_op jit(solution)/shard_map/ppermute | solution.py:678
  17.8 6.2 %collective-permute-start.1 = (f32[2,8,1024]{2,1,0:T(8,128)S(1)}, f32[2,8,1024]{2,1,0:T(8,128)S(1)}, u32[]{:S(2)}, u32[]{:S(2)}) collective-permute-start(f32[2,8,1024]{2,1,0:T(8,128)S(1)} %get-tuple-element.17), channel_id=1, source_target_pairs={{2,0},{3,1},{6,4},{7,5},{10,8},{11,9},{14,12},{15,13},{18,16},{19,... | collective-permute-start | bytes 196616 | tf_op jit(solution)/shard_map/ppermute | solution.py:693

commit v8 on v7

--- a/solution.py
+++ b/solution.py
@@ -13,18 +13,10 @@
 courant = 0.45
 
 STRIP_SUM, STRIP, STRIP_DEPTH, GAIN, INDEX, EDGE_FLOW, EDGE_DEPTH, EDGE_SUM = range(8)
-ROWS = 8
 (FIRST_ETA, SECOND_ETA, FIRST_ROW, FIRST_COL, FIRST_DEPTH, NEXT_ETA, LAST_ETA, NEXT_ROW,
  LAST_ROW, LAST_COL, NEXT_DEPTH, LAST_DEPTH) = range(12)
-COLUMNS = 12
-
-
-def row_at(row, cols, left=0, size=None):
-    return slice(row * cols + left, row * cols + left + (cols if size is None else size))
-
-
-def column_at(column, cols):
-    return slice(ROWS * cols + column * LANES, ROWS * cols + (column + 1) * LANES)
+ROWS, COLUMNS = 8, 16
+LINES = ROWS * TILE + COLUMNS
 
 
 def iota(shape, axis):
@@ -32,6 +24,8 @@
 
 
 def rolled(value, shift, axis):
+    if shift == 0:
+        return value
     return pltpu.roll(value, shift % value.shape[axis], axis)
 
 
@@ -47,20 +41,20 @@
 
 
 def pack_kernel(eta_ref, momenta_ref, depth_ref, wet_ref, gain_ref, index_ref, out_ref,
-                ends, end_wet, sides, side_wet, gains, indices, sems):
-    count = out_ref.shape[0]
+                ends, end_wet, sides, side_wet, gains, indices, packet, sems, out_sems):
     rows, cols = eta_ref.shape[1:]
     fields = eta_ref.at[0], momenta_ref.at[0, 0], momenta_ref.at[1, 0], depth_ref.at[0]
-    pairs = []
+    tall, wide = [], []
     for end in range(2):
-        tall = pl.ds(end * (rows - TILE), TILE)
-        wide = pl.ds(end * (cols - LANES), LANES)
-        for place, field in enumerate(fields):
-            pairs.append((field.at[tall, :], ends.at[end, place]))
-            pairs.append((field.at[:, wide], sides.at[end, place]))
-        pairs.append((wet_ref.at[0, tall, :], end_wet.at[end]))
-        pairs.append((wet_ref.at[0, :, wide], side_wet.at[end]))
-    for copy in copied(pairs + [(gain_ref, gains), (index_ref, indices)], sems):
+        here = pl.ds(end * (rows - TILE), TILE)
+        tall += [(field.at[here, :], ends.at[end, place]) for place, field in enumerate(fields)]
+        tall.append((wet_ref.at[0, here, :], end_wet.at[end]))
+        here = pl.ds(end * (cols - LANES), LANES)
+        wide += [(field.at[:, here], sides.at[end, place]) for place, field in enumerate(fields)]
+        wide.append((wet_ref.at[0, :, here], side_wet.at[end]))
+    tall += [(gain_ref, gains), (index_ref, indices)]
+    copies = copied(tall + wide, sems)
+    for copy in copies[:len(tall)]:
         copy.wait()
     level = lax.axis_index("level")
     lane = iota((TILE, cols), 1)
@@ -68,6 +62,10 @@
     def loaded(end):
         mask = end_wet[end].astype(jnp.float32)
         return ends[end, 0], ends[end, 1], ends[end, 2], mask * ends[end, 3], mask
+
+    def put(row, value):
+        for tile in range(TILE):
+            packet[row * TILE + tile:row * TILE + tile + 1] = value[:, tile * LANES:(tile + 1) * LANES]
 
     eta, row, col, depth, mask = loaded(0)
     east = jnp.where(lane == cols - 1, 0.0, rolled(eta, -1, 1))
@@ -75,11 +73,11 @@
     west = jnp.where(lane == 0, 0.0, rolled(row, 1, 1))
     col = mask * (col - courant * (rolled(eta, -1, 0) - eta))
     strip_sum = mask * eta - courant * depth * (row - west + col)
-    out_ref[0, :, row_at(STRIP_SUM, cols)] = strip_sum[:1]
-    out_ref[0, :, row_at(STRIP, cols)] = eta[:1]
-    out_ref[0, :, row_at(STRIP_DEPTH, cols)] = depth[:1]
-    out_ref[0, :, row_at(GAIN, cols)] = gains[pl.ds(level, 1), :]
-    out_ref[0, :, row_at(INDEX, cols)] = indices[pl.ds(level, 1), :].astype(jnp.float32)
+    put(STRIP_SUM, strip_sum[:1])
+    put(STRIP, eta[:1])
+    put(STRIP_DEPTH, depth[:1])
+    put(GAIN, gains[pl.ds(level, 1), :])
+    put(INDEX, indices[pl.ds(level, 1), :].astype(jnp.float32))
 
     eta, row, col, depth, mask = loaded(1)
     east = jnp.where(lane == cols - 1, 0.0, rolled(eta, -1, 1))
@@ -88,10 +86,15 @@
     flow = mask * (col + courant * eta)
     above = rolled(flow - courant * mask * rolled(eta, -1, 0), 1, 0)
     edge_sum = mask * eta - courant * depth * (row - west - above)
-    out_ref[0, :, row_at(EDGE_FLOW, cols)] = flow[TILE - 1:]
-    out_ref[0, :, row_at(EDGE_DEPTH, cols)] = depth[TILE - 1:]
-    out_ref[0, :, row_at(EDGE_SUM, cols)] = edge_sum[TILE - 1:]
-
+    put(EDGE_FLOW, flow[TILE - 1:])
+    put(EDGE_DEPTH, depth[TILE - 1:])
+    put(EDGE_SUM, edge_sum[TILE - 1:])
+    lines = pl.ds(0, ROWS * TILE)
+    out_copies = copied(
+        [(packet.at[lines], out_ref.at[turn, lines]) for turn in range(out_ref.shape[0])], out_sems.at[0])
+
+    for copy in copies[len(tall):]:
+        copy.wait()
     lane = iota((rows, LANES), 1)
     columns = jnp.zeros((rows, LANES), jnp.float32)
     depths = [sides[end, 3] * side_wet[end].astype(jnp.float32) for end in range(2)]
@@ -105,12 +108,12 @@
     ):
         moved = value if place == at else rolled(value, place - at, 1)
         columns = jnp.where(lane == place, moved, columns)
-    columns = columns.T
-    for place in range(COLUMNS):
-        out_ref[0, :, column_at(place, cols)] = columns[place:place + 1]
-    packet = out_ref[0]
-    for turn in range(1, count):
-        out_ref[turn] = packet
+    packet[ROWS * TILE:] = columns.T[:COLUMNS]
+    lines = pl.ds(ROWS * TILE, COLUMNS)
+    out_copies += copied(
+        [(packet.at[lines], out_ref.at[turn, lines]) for turn in range(out_ref.shape[0])], out_sems.at[1])
+    for copy in out_copies:
+        copy.wait()
 
 
 def bulk_kernel(eta_ref, momenta_ref, depth_ref, wet_ref, eta_out, momenta_out,
@@ -243,170 +246,145 @@
 
 
 class Packets:
-    def __init__(self, got_refs, rows, cols, inflow_ref=None):
-        self.got_refs, self.rows, self.cols, self.inflow_ref = got_refs, rows, cols, inflow_ref
-        self.patches = got_refs[0].shape[0]
-
-    def row(self, segment, row, left=0, size=None):
-        return self.got_refs[segment.flipped][segment.patch, :, row_at(row, self.cols, left, size)]
+    def __init__(self, got_refs):
+        self.got_refs = got_refs
+
+    def tile(self, segment, row):
+        return self.got_refs[segment.flipped][segment.patch, row * TILE:(row + 1) * TILE]
+
+    def line(self, segment, row, line):
+        return self.got_refs[segment.flipped][segment.patch, row * TILE + line:row * TILE + line + 1]
+
+    def row(self, segment, row):
+        return jnp.concatenate([self.line(segment, row, line) for line in range(TILE)], axis=1)
 
     def column(self, segment, column):
-        return self.got_refs[segment.flipped][segment.patch, :, column_at(column, self.cols)]
-
-    def rows_of(self, segments, row):
-        return jnp.concatenate([self.row(segment, row) for segment in segments], axis=0)
-
-    def columns_of(self, segments, column):
-        return jnp.concatenate([self.column(segment, column) for segment in segments], axis=0)
-
-    def field_row(self, segment, row, left=0, size=None):
-        return self.row(segment, row, left, size) if self.inflow_ref is None else 0.0
-
-    def field_column(self, segment, column):
-        return self.column(segment, column) if self.inflow_ref is None else 0.0
-
-    def inflow(self, step, segment, left=0, size=None):
-        size = self.cols if size is None else size
-        place = 2 * self.patches * step + segment.place(self.patches)
-        return self.inflow_ref[place, :, left:left + size]
-
-    def strip_tile(self, segment, left):
-        if self.inflow_ref is None:
-            return self.row(segment, STRIP, left, LANES)
-        return self.inflow(0, segment, left, LANES)
-
-    def at_first(self, step, segment, left, turned):
-        if self.inflow_ref is None:
-            return 0.0
-        tile = self.inflow(step, segment, left, LANES)
-        return jnp.where(iota((1, LANES), 1) == 0, rolled(tile, turned, 1) if turned else tile, 0.0)
+        return self.line(segment, ROWS, column)
+
+
+def is_first(shape=(TILE, LANES)):
+    return (iota(shape, 0) == 0) & (iota(shape, 1) == 0)
+
+
+def is_last(shape=(TILE, LANES)):
+    return (iota(shape, 0) == shape[0] - 1) & (iota(shape, 1) == shape[1] - 1)
+
+
+def next_cells(tile, edge):
+    lane = iota(tile.shape, 1)
+    moved = rolled(tile, -1, 1)
+    moved = jnp.where(lane == LANES - 1, rolled(moved, -1, 0), moved)
+    return jnp.where(is_last(), edge, moved)
+
+
+def last_cells(tile, edge):
+    lane = iota(tile.shape, 1)
+    moved = rolled(tile, 1, 1)
+    moved = jnp.where(lane == 0, rolled(moved, 1, 0), moved)
+    return jnp.where(is_first(), edge, moved)
+
+
+def row_of(ref, place):
+    return jnp.concatenate([ref[place, line:line + 1] for line in range(TILE)], axis=1)
 
 
 def nested(flux, index):
-    segments, cols = index.shape
-    rows = []
-    for low in range(0, segments, TILE):
-        tiles = []
-        for left in range(0, cols, LANES):
-            at = index[low:low + TILE, left:left + LANES]
-            lane, tile = at % LANES, at // LANES
-            taken = jnp.zeros(at.shape, jnp.float32)
-            for source in range(cols // LANES):
-                values = flux[low:low + TILE, source * LANES:(source + 1) * LANES]
-                found = jnp.take_along_axis(values, lane, axis=1, mode="promise_in_bounds")
-                taken = jnp.where(tile == source, found, taken)
-            tiles.append(taken)
-        rows.append(jnp.concatenate(tiles, axis=1))
-    return jnp.concatenate(rows, axis=0) if len(rows) > 1 else rows[0]
-
-
-def strips_of(links, packets, finer, picked_ref, narrow_ref):
-    count, cols = picked_ref.shape
-    patches = packets.patches
-    lane = iota((count, LANES), 1)
-    every = links.all()
-    strip, depth = packets.rows_of(every, STRIP), packets.rows_of(every, STRIP_DEPTH)
-    mask = wet(depth)
-    if finer is None:
-        inflow = jnp.zeros_like(strip)
-    else:
-        gain = packets.rows_of(every, GAIN)
-        index = packets.rows_of(every, INDEX).astype(jnp.int32)
-        inflow = gain * nested(finer[0], index)
-    eta = strip + inflow
-
-    narrow_ref[...] = eta[:, :LANES]
-    for place, segment in enumerate(every):
-        east, there = links.east(segment)
-        picked_ref[place:place + 1, :LANES] = narrow_ref[pl.ds(east.place(patches), 1), :] * there
-    east_eta = rolled(picked_ref[:, :LANES], -1, 1)
-    after = rolled(inflow, -1, 1)
-    after = jnp.concatenate(
-        [after[:, :-LANES], jnp.where(lane == LANES - 1, east_eta, after[:, -LANES:])], axis=1)
-    more_row = courant * mask * (inflow - after)
-
-    last_eta = packets.columns_of(every, LAST_ETA)
-    last_row = packets.columns_of(every, LAST_ROW)
-    first_of_last = rolled(last_row + courant * last_eta, -1, 1)
-    narrow_ref[...] = mask[:, -LANES:] * first_of_last + more_row[:, -LANES:]
-    for place, segment in enumerate(every):
-        west, there = links.west(segment)
-        picked_ref[place:place + 1, :LANES] = narrow_ref[pl.ds(west.place(patches), 1), :] * there
-    west_row = rolled(picked_ref[:, :LANES], 1, 1)
-    before = rolled(more_row, 1, 1)
-    before = jnp.concatenate([jnp.where(lane == 0, west_row, before[:, :LANES]), before[:, LANES:]], axis=1)
-
-    for place, segment in enumerate(every):
-        north, there = links.north(segment)
-        picked_ref[place:place + 1, :] = packets.row(north, EDGE_FLOW) * there
-    flow = picked_ref[...]
-    for place, segment in enumerate(every):
-        north, there = links.north(segment)
-        picked_ref[place:place + 1, :] = packets.row(north, EDGE_DEPTH) * there
-    north_col = flow - courant * wet(picked_ref[...]) * eta
-    later = (packets.rows_of(every, STRIP_SUM) + mask * inflow
-             - courant * depth * (more_row - before + courant * mask * inflow - north_col))
-    if finer is None:
-        return eta, later
-    return eta, later + gain * nested(finer[1], index)
+    lane, line = index % LANES, index // LANES
+    taken = jnp.zeros(index.shape, jnp.float32)
+    for source in range(TILE):
+        values = jnp.broadcast_to(flux[source:source + 1], index.shape)
+        found = jnp.take_along_axis(values, lane, axis=1, mode="promise_in_bounds")
+        taken = jnp.where(line == source, found, taken)
+    return taken
 
 
 def strips_kernel(*refs):
     links_ref, mine_ref, other_ref = refs[:3]
-    out_ref, rows_ref, picked_ref, narrow_ref = refs[-4:]
-    finer = (refs[3][0], refs[3][1]) if len(refs) == 8 else None
+    out_ref = refs[-1]
+    finer_ref = refs[3] if len(refs) == 5 else None
     links = Links(links_ref, mine_ref.shape[0])
-    packets = Packets((mine_ref, other_ref), None, out_ref.shape[2])
-    eta, later = strips_of(links, packets, finer, picked_ref, narrow_ref)
-    out_ref[0] = eta
-    out_ref[1] = later
-    for place in range(out_ref.shape[1]):
-        rows_ref[place] = later[place:place + 1]
-
-
-def beside(links, packets, own):
+    patches, count = links.patches, 2 * links.patches
+    packets = Packets((mine_ref, other_ref))
+    inflows = []
+    for segment in links.all():
+        eta = packets.tile(segment, STRIP)
+        if finer_ref is not None:
+            place = segment.place(patches)
+            gain, index = packets.tile(segment, GAIN), packets.tile(segment, INDEX).astype(jnp.int32)
+            inflow, later = [gain * nested(finer_ref[step * count + place], index) for step in range(2)]
+            inflows.append((inflow, later))
+            eta = eta + inflow
+        out_ref[segment.place(patches)] = eta
+    for segment in links.all():
+        place = segment.place(patches)
+        eta, depth = out_ref[place], packets.tile(segment, STRIP_DEPTH)
+        mask = wet(depth)
+        east, there = links.east(segment)
+        edge = there * rolled(rolled(out_ref[east.place(patches)], -1, 1), -1, 0)
+        if finer_ref is None:
+            row = jnp.where(is_last(), -courant * mask * edge, 0.0)
+        else:
+            inflow, later = inflows[place]
+            row = courant * mask * (inflow - next_cells(inflow, edge))
+        west, there = links.west(segment)
+        west_eta = rolled(rolled(out_ref[west.place(patches)], 1, 1), 1, 0)
+        west_mask = rolled(rolled(wet(packets.tile(west, STRIP_DEPTH)), 1, 1), 1, 0)
+        edge = there * west_mask * (packets.column(west, LAST_ROW) - courant * (eta - west_eta))
+        north, there = links.north(segment)
+        col = there * (packets.tile(north, EDGE_FLOW) - courant * wet(packets.tile(north, EDGE_DEPTH)) * eta)
+        total = packets.tile(segment, STRIP_SUM)
+        if finer_ref is None:
+            total = total - courant * depth * (row - jnp.where(is_first(), edge, 0.0) - col)
+        else:
+            total = (total + mask * inflow + later
+                     - courant * depth * (row - last_cells(row, edge) + courant * mask * inflow - col))
+        out_ref[count + place] = total
+
+
+def beside(links, packets, own, inflow=None):
     lane = iota((1, LANES), 1)
     first, last = lane == 0, lane == LANES - 1
-    end = packets.cols - LANES
-
-    def corner_col(segment, eta, left, turned):
+
+    def field(segment, column):
+        return packets.column(segment, column) if inflow is None else 0.0
+
+    def strip(name, turned):
+        return 0.0 if inflow is None else jnp.where(first, rolled(inflow[name], turned, 1), 0.0)
+
+    def corner_col(segment, eta, line, turned):
         north, beyond = links.north(segment)
-        flow = packets.field_row(north, EDGE_FLOW, left, LANES)
-        mask = wet(packets.row(north, EDGE_DEPTH, left, LANES))
-        if turned:
-            flow = rolled(flow, turned, 1) if packets.inflow_ref is None else flow
-            mask = rolled(mask, turned, 1)
+        mask = rolled(wet(packets.line(north, EDGE_DEPTH, line)), turned, 1)
+        flow = rolled(packets.line(north, EDGE_FLOW, line), turned, 1) if inflow is None else 0.0
         return beyond * (flow - courant * mask * eta)
 
     west, there = links.west(own)
-    eta = packets.field_column(west, LAST_ETA) + packets.at_first(0, west, end, 1)
-    next_eta = packets.field_column(west, NEXT_ETA) + packets.at_first(0, west, end, 2)
-    own_eta = packets.field_column(own, FIRST_ETA) + packets.at_first(0, own, 0, 0)
+    eta = field(west, LAST_ETA) + strip("west", 1)
+    next_eta = field(west, NEXT_ETA) + strip("west", 2)
+    own_eta = field(own, FIRST_ETA) + strip("own", 0)
     depth = packets.column(west, LAST_DEPTH) * there
     mask = wet(depth)
-    next_row = wet(packets.column(west, NEXT_DEPTH)) * (
-        packets.field_column(west, NEXT_ROW) - courant * (eta - next_eta))
+    next_row = wet(packets.column(west, NEXT_DEPTH)) * (field(west, NEXT_ROW) - courant * (eta - next_eta))
     below, beyond = links.south(west)
-    south_eta = jnp.where(last, packets.strip_tile(below, end) * beyond, rolled(eta, -1, 1))
-    col = mask * (packets.field_column(west, LAST_COL) - courant * (south_eta - eta))
-    north_col = jnp.where(first, corner_col(west, eta, end, 1), rolled(col, 1, 1))
-    west_row = mask * (packets.field_column(west, LAST_ROW) - courant * (own_eta - eta))
-    west_eta = (mask * eta - courant * depth * (west_row - next_row + col - north_col)
-                + packets.at_first(1, west, end, 1))
+    corner = packets.line(below, STRIP, TILE - 1) if inflow is None else inflow["south west"]
+    south_eta = jnp.where(last, corner * beyond, rolled(eta, -1, 1))
+    col = mask * (field(west, LAST_COL) - courant * (south_eta - eta))
+    north_col = jnp.where(first, corner_col(west, eta, TILE - 1, 1), rolled(col, 1, 1))
+    west_row = mask * (field(west, LAST_ROW) - courant * (own_eta - eta))
+    west_eta = (mask * eta - courant * depth * (west_row - next_row + col - north_col) + strip("west later", 1))
     west_mask = mask
 
     east, there = links.east(own)
-    eta = there * (packets.field_column(east, FIRST_ETA) + packets.at_first(0, east, 0, 0))
-    second_eta = packets.field_column(east, SECOND_ETA) + packets.at_first(0, east, 0, -1)
+    eta = there * (field(east, FIRST_ETA) + strip("east", 0))
+    second_eta = field(east, SECOND_ETA) + strip("east", -1)
     depth = packets.column(east, FIRST_DEPTH) * there
     mask = wet(depth)
-    row = mask * (packets.field_column(east, FIRST_ROW) - courant * (second_eta - eta))
+    row = mask * (field(east, FIRST_ROW) - courant * (second_eta - eta))
     below, beyond = links.south(east)
-    south_eta = jnp.where(last, rolled(packets.strip_tile(below, 0), -1, 1) * beyond, rolled(eta, -1, 1))
-    col = mask * (packets.field_column(east, FIRST_COL) - courant * (south_eta - eta))
+    corner = packets.line(below, STRIP, 0) if inflow is None else inflow["south east"]
+    south_eta = jnp.where(last, rolled(corner, -1, 1) * beyond, rolled(eta, -1, 1))
+    col = mask * (field(east, FIRST_COL) - courant * (south_eta - eta))
     north_col = jnp.where(first, corner_col(east, eta, 0, 0), rolled(col, 1, 1))
-    east_sum = (mask * eta - courant * depth * (row + col - north_col)
-                + there * packets.at_first(1, east, 0, 0))
+    east_sum = mask * eta - courant * depth * (row + col - north_col) + there * strip("east later", 0)
     return west_row, west_mask, west_eta, eta, east_sum, courant * depth
 
 
@@ -444,13 +422,13 @@
             above = north[1] * (north[0] - courant * (whole_eta[:1] - north[2]))
 
 
-def north_of(links, packets, own, own_strip):
-    cols = packets.cols
+def north_of(links, packets, own, own_strip, inflow=None):
+    cols = own_strip.shape[1]
     lane = iota((1, LANES), 1)
     north, there = links.north(own)
     depth = packets.row(north, EDGE_DEPTH) * there
     mask = wet(depth)
-    if packets.inflow_ref is not None:
+    if inflow is not None:
         col = -courant * mask * own_strip
         return col, mask, -courant * depth * col
     col = packets.row(north, EDGE_FLOW) * there - courant * mask * own_strip
@@ -474,7 +452,7 @@
             for low in (0, rows - TILE)]
 
 
-def halo_kernel(links_ref, mine_ref, other_ref, later_ref, eta_after, momenta_after, wet_after, depth_after,
+def halo_kernel(links_ref, mine_ref, other_ref, strips_ref, eta_after, momenta_after, wet_after, depth_after,
                 eta_ends, row_ends, turned, eta_hbm, momenta_hbm, eta_out, momenta_out, ends_out,
                 left_new, right_new, sems):
     del eta_hbm, momenta_hbm
@@ -482,7 +460,7 @@
     right = cols - LANES
     links = Links(links_ref, mine_ref.shape[0])
     own = links.own()
-    packets = Packets((mine_ref, other_ref), rows, cols)
+    packets = Packets((mine_ref, other_ref))
     columns = beside(links, packets, own)
     west_row, west_mask, west_eta, east_eta, east_sum, east_depth = columns
     fields = eta_after, momenta_after.at[0], momenta_after.at[1]
@@ -543,7 +521,7 @@
     below, there = links.south(own)
     low = two_steps(
         nothing, wet_after[rows - TILE:], depth_after[rows - TILE:], low_sides, (eta_ends[1], row_ends[1]),
-        south=(packets.row(below, STRIP) * there, later_ref[below.place(packets.patches)] * there))
+        south=(packets.row(below, STRIP) * there, row_of(strips_ref, 2 * links.patches + below.place(links.patches)) * there))
     line, lane = iota((TILE, cols), 0), iota((TILE, cols), 1)
     for place, field in enumerate(fields):
         more = jnp.concatenate([left[place], middle, last[place]], axis=0).T
@@ -560,56 +538,79 @@
 
 
 def inflow_kernel(links_ref, mine_ref, other_ref, finer_ref, wet_after, depth_after, ends_ref, eta_hbm, momenta_hbm,
-                  eta_out, momenta_out, inflow_ref, new_ref, sems):
+                  eta_out, momenta_out, rows_ref, new_ref, sems):
     del eta_hbm, momenta_hbm
     rows, cols = wet_after.shape
     links = Links(links_ref, mine_ref.shape[0])
-    own, every = links.own(), links.all()
-    packets = Packets((mine_ref, other_ref), rows, cols, inflow_ref)
-    gain = packets.rows_of(every, GAIN)
-    index = packets.rows_of(every, INDEX).astype(jnp.int32)
-    for number in range(2):
-        inflow = gain * nested(finer_ref[number], index)
-        for place in range(len(every)):
-            inflow_ref[number * len(every) + place] = inflow[place:place + 1]
-    columns = beside(links, packets, own)
+    patches = links.patches
+    own = links.own()
+    packets = Packets((mine_ref, other_ref))
+
+    def flux_place(step, segment):
+        return step * 2 * patches + segment.place(patches)
+
+    def inflows(segment):
+        gain, index = packets.tile(segment, GAIN), packets.tile(segment, INDEX).astype(jnp.int32)
+        return [gain * nested(finer_ref[flux_place(step, segment)], index) for step in range(2)]
+
+    below, there = links.south(own)
+    west, east = links.west(own)[0], links.east(own)[0]
+    below_west, beyond_west = links.west(below)
+    below_east, beyond_east = links.east(below)
+    wanted = (
+        ("west", 0, west, TILE - 1), ("west later", 1, west, TILE - 1), ("east", 0, east, 0),
+        ("east later", 1, east, 0), ("south west", 0, links.south(west)[0], TILE - 1),
+        ("south east", 0, links.south(east)[0], 0), ("below west", 0, below_west, TILE - 1),
+        ("below east", 0, below_east, 0))
+    gain = jnp.concatenate([packets.line(segment, GAIN, line) for _, _, segment, line in wanted], axis=0)
+    index = jnp.concatenate([packets.line(segment, INDEX, line) for _, _, segment, line in wanted], axis=0)
+    index = index.astype(jnp.int32)
+    lane, line = index % LANES, index // LANES
+    taken = jnp.zeros((TILE, LANES), jnp.float32)
+    for source in range(TILE):
+        values = jnp.concatenate(
+            [finer_ref[flux_place(step, segment), source:source + 1] for _, step, segment, _ in wanted], axis=0)
+        found = jnp.take_along_axis(values, lane, axis=1, mode="promise_in_bounds")
+        taken = jnp.where(line == source, found, taken)
+    taken = gain * taken
+    inflow = {name: taken[place:place + 1] for place, (name, _, _, _) in enumerate(wanted)}
+
+    rows_ref[0], rows_ref[1] = inflows(own)
+    strip, later = inflows(below)
+    strip, later = strip * there, later * there
+    inflow["own"] = rows_ref[0, :1]
+
+    depth = packets.tile(below, STRIP_DEPTH)
+    mask = wet(depth)
+    edge = jnp.broadcast_to(rolled(inflow["below east"] * beyond_east, -1, 1), (TILE, LANES))
+    row = courant * mask * (strip - next_cells(strip, edge))
+    west_mask = rolled(wet(packets.line(below_west, STRIP_DEPTH, TILE - 1)), 1, 1)
+    edge = beyond_west * courant * west_mask * (rolled(inflow["below west"], 1, 1) - strip[:1])
+    edge = jnp.broadcast_to(edge, (TILE, LANES))
+    north, beyond = links.north(below)
+    col = -courant * wet(packets.tile(north, EDGE_DEPTH)) * beyond * strip
+    rows_ref[2] = strip
+    rows_ref[3] = there * (
+        mask * strip - courant * depth * (row - last_cells(row, edge) + courant * mask * strip - col) + later)
+
+    columns = beside(links, packets, own, inflow)
     top_sides, low_sides = as_sublanes(columns)
     line = iota((TILE, cols), 0)
-    strip = packets.inflow(0, own)
+    strip = row_of(rows_ref, 0)
     top = two_steps(
         jnp.where(line == 0, strip, 0.0), wet_after[:TILE], depth_after[:TILE], top_sides, None,
-        north=north_of(links, packets, own, strip), second=packets.inflow(1, own))
-
-    below, there = links.south(own)
-    strip = packets.inflow(0, below) * there
-    lane = iota((1, cols), 1)
-    depth = packets.row(below, STRIP_DEPTH)
-    mask = wet(depth)
-    east, beyond = links.east(below)
-    last_eta = rolled(packets.inflow(0, east, 0, LANES) * beyond, -1, 1)[:, LANES - 1:]
-    after = jnp.where(lane == cols - 1, last_eta, rolled(strip, -1, 1))
-    row = courant * mask * (strip - after)
-    west, beyond = links.west(below)
-    end = cols - LANES
-    first_row = rolled(courant * wet(packets.row(west, STRIP_DEPTH, end, LANES)) * beyond * (
-        packets.inflow(0, west, end, LANES) - rolled(strip[:, :LANES], -1, 1)), 1, 1)[:, :1]
-    before = jnp.where(lane == 0, first_row, rolled(row, 1, 1))
-    north, beyond = links.north(below)
-    north_col = -courant * wet(packets.row(north, EDGE_DEPTH)) * beyond * strip
-    later = there * (mask * strip - courant * depth * (row - before + courant * mask * strip - north_col)
-                     + packets.inflow(1, below))
+        north=north_of(links, packets, own, strip, inflow), second=row_of(rows_ref, 1))
     low = two_steps(
         jnp.zeros((TILE, cols), jnp.float32), wet_after[rows - TILE:], depth_after[rows - TILE:],
-        low_sides, None, south=(strip, later))
+        low_sides, None, south=(row_of(rows_ref, 2), row_of(rows_ref, 3)))
     copies = []
     outs = eta_out.at[0], momenta_out.at[0, 0], momenta_out.at[1, 0]
-    for place, out in enumerate(outs):
-        for end, (low_row, near, found) in enumerate(
-                ((0, line < TILE // 2, top), (rows - TILE, line >= TILE // 2, low))):
+    for end, (near, found) in enumerate(((line < TILE // 2, top), (line >= TILE // 2, low))):
+        for place in range(3):
             new_ref[place, end] = ends_ref[place, end] + jnp.where(near, found[place], 0.0)
         copies += copied([
-            (new_ref.at[place, end], out.at[pl.ds(end * (rows - TILE), TILE), :]) for end in range(2)
-        ], sems.at[place])
+            (new_ref.at[place, end], out.at[pl.ds(end * (rows - TILE), TILE), :]) for place, out in enumerate(outs)
+        ], sems.at[end])
     for copy in copies:
         copy.wait()
 
@@ -634,14 +635,14 @@
               for field in (adjoint_height, adjoint_momenta, depth, wet_mask, nest_gain, nest_index)]
     packed = pl.pallas_call(
         pack_kernel,
-        out_shape=pltpu.VMEM((patches, 1, ROWS * cols + COLUMNS * LANES), jnp.float32),
+        out_shape=array(patches, LINES, LANES),
         in_specs=[hbm] * 6,
-        out_specs=vmem,
+        out_specs=hbm,
         scratch_shapes=[
             scratch(2, 4, TILE, cols), pltpu.VMEM((2, TILE, cols), jnp.int32),
             scratch(2, 4, rows, LANES), pltpu.VMEM((2, rows, LANES), jnp.int32),
             scratch(levels, cols), pltpu.VMEM((levels, cols), jnp.int32),
-            pltpu.SemaphoreType.DMA((22,)),
+            scratch(LINES, LANES), pltpu.SemaphoreType.DMA((22,)), pltpu.SemaphoreType.DMA((2, patches)),
         ],
         compiler_params=params,
         name="pack",
@@ -678,19 +679,17 @@
     other = lax.ppermute(mine, "sub", [(0, 1), (1, 0)])
 
     flux = ()
-    laters = []
+    strips = []
     for turn in range(levels - 1):
-        strips, later = pl.pallas_call(
+        strips.append(pl.pallas_call(
             strips_kernel,
-            out_shape=[array(2, count, cols), array(count, 1, cols)],
+            out_shape=array(2 * count, TILE, LANES),
             in_specs=[smem] + [vmem] * (2 + len(flux)),
-            out_specs=[vmem, vmem],
-            scratch_shapes=[scratch(count, cols), scratch(count, LANES)],
+            out_specs=vmem,
             compiler_params=params,
             name="strips",
-        )(adjacency, mine, other, *flux)
-        laters.append(later)
-        flux = (lax.ppermute(strips, "level", [(source, source - 1) for source in range(1, levels)]),)
+        )(adjacency, mine, other, *flux))
+        flux = (lax.ppermute(strips[-1], "level", [(source, source - 1) for source in range(1, levels)]),)
 
     eta_new, momenta_new, ends = pl.pallas_call(
         halo_kernel,
@@ -703,7 +702,7 @@
         ],
         compiler_params=params,
         name="halo",
-    )(adjacency, mine, other, laters[0], *after, eta_new, momenta_new)
+    )(adjacency, mine, other, strips[0], *after, eta_new, momenta_new)
 
     return pl.pallas_call(
         inflow_kernel,
@@ -712,7 +711,7 @@
         out_specs=[hbm, hbm],
         input_output_aliases={7: 0, 8: 1},
         scratch_shapes=[
-            scratch(2 * count, 1, cols), scratch(3, 2, TILE, cols), pltpu.SemaphoreType.DMA((3, 2)),
+            scratch(4, TILE, LANES), scratch(3, 2, TILE, cols), pltpu.SemaphoreType.DMA((2, 3)),
         ],
         compiler_params=params,
         name="inflow",

time: 26.7 us -> 26.9 us (level)
    pallas_call x2, Pallas kernels: 3.12 us -> 3.57 us  [the longest x1 2.38 us: body(): pl.pallas_call(pack_kernel, out_shape=array(patches, LINES, LANES), in_sp...]
    pallas_call x1, Pallas kernels: 2.41 us -> 2.08 us  [body(): pl.pallas_call(inflow_kernel, out_shape=[array(*adjoint_height.shape), ar...]
  transfers between devices with their start and end apart: 3 -> 3, of which waited for: 3 -> 3; matrix products, arithmetic and copies ran while one was open for 0% -> 0% of each run, Pallas kernels for 24% -> 23%
where the time goes in v8:
time: 26.9 us; the launch traced here: 26.6 us
  Pallas kernels  11.9 us (44%)
  starting transfers between devices  7.62 us (28%)
  waiting for transfers between devices  6.46 us (24%)
  between operations  0.67 us (2%)
    all_to_all x1, starting transfers between devices, body(): lax.all_to_all(packed, 'patch', 0, 0, tiled=True)  6.33 us
    pallas_call x1, Pallas kernels, body(): pl.pallas_call(bulk_kernel, out_shape=[array(*adjoint_height.shape), arra...  4.16 us
    ppermute x1, waiting for transfers between devices, body(): lax.ppermute(strips[-1], 'level', [(source, source - 1) for source in ran...  2.8 us
    pallas_call x1, Pallas kernels, body(): pl.pallas_call(pack_kernel, out_shape=array(patches, LINES, LANES), in_sp...  2.38 us
    all_to_all x1, waiting for transfers between devices, body(): lax.all_to_all(packed, 'patch', 0, 0, tiled=True)  2.26 us
    pallas_call x1, Pallas kernels, body(): pl.pallas_call(inflow_kernel, out_shape=[array(*adjoint_height.shape), ar...  2.08 us
    pallas_call x1, Pallas kernels, body(): pl.pallas_call(halo_kernel, out_shape=[array(*adjoint_height.shape), arra...  2.05 us
    ppermute x1, waiting for transfers between devices, body(): other = lax.ppermute(mine, 'sub', [(0, 1), (1, 0)])  1.39 us
  transfers between devices with their start and end apart: 3, of which 3 were waited for; matrix products, arithmetic and copies ran while one was open for 0% of the time, Pallas kernels for 23%

profile of v8, /device:TPU:0, one launch (start us, length us, event | category | flops | bytes accessed | tf_op | source)
XLA Modules:
  0.0 26.6 jit_solution(5194041069868299242)
XLA Ops:
  0.6 2.4 %pack.1 = f32[4,80,128]{2,1,0:T(8,128)} custom-call(f32[1,128,1024]{2,1,0:T(8,128)} %eta_ref.3, f32[2,1,128,1024]{3,2,1,0:T(8,128)} %momenta_ref.3, f32[1,128,1024]{2,1,0:T(8,128)} %depth_ref.3, s32[1,128,1024]{2,1,0:T(8,128)} %wet_ref.3, f32[2,1024]{1,0:T(2,128)} %gain_ref.1, s32[2,1024]{1,0:T(2,128)} %index_ref.1), custom_call_target="tpu_custom_call" | custom-call | tf_op jit(solution)/shard_map/pack/pallas_call | solution.py:636
  3.0 6.3 %all-to-all-start = ((f32[4,80,128]{2,1,0:T(8,128)}), f32[4,80,128]{2,1,0:T(8,128)S(1)}, u32[]{:S(2)}, u32[]{:S(2)}) async-start(f32[4,80,128]{2,1,0:T(8,128)} %pack.1), calls=%async_computation | async-start | bytes 327680 | tf_op jit(solution)/shard_map/all_to_all | solution.py:678
  9.3 4.2 %bulk.1 = (f32[1,128,1024]{2,1,0:T(8,128)}, f32[2,1,128,1024]{3,2,1,0:T(8,128)}, f32[128,1024]{1,0:T(8,128)S(1)}, f32[2,128,1024]{2,1,0:T(8,128)S(1)}, f32[128,1...) custom-call(f32[1,128,1024]{2,1,0:T(8,128)} %eta_ref.3, ...), custom_call_target="tpu_custom_call" | custom-call | tf_op jit(solution)/shard_map/bulk/pallas_call | solution.py:651
  13.5 2.3 %all-to-all-done.value_ref = f32[4,80,128]{2,1,0:T(8,128)S(1)} async-done(((f32[4,80,128]{2,1,0:T(8,128)}), f32[4,80,128]{2,1,0:T(8,128)S(1)}, u32[]{:S(2)}, u32[]{:S(2)}) %all-to-all-start) | async-done | bytes 163872 | tf_op jit(solution)/shard_map/all_to_all | solution.py:678
  15.8 0.0 copy-start
  15.8 0.0 collective-permute-start
  15.8 1.4 %collective-permute-done.refs_2_.other_ref = f32[4,80,128]{2,1,0:T(8,128)S(1)} collective-permute-done((f32[4,80,128]{2,1,0:T(8,128)S(1)}, f32[4,80,128]{2,1,0:T(8,128)S(1)}, u32[]{:S(2)}, u32[]{:S(2)}) %collective-permute-start) | collective-permute-done | bytes 163872 | tf_op jit(solution)/shard_map/ppermute | solution.py:679
  17.2 0.0 copy-done
  17.2 1.2 %strips.1.strips_ref = f32[16,8,128]{2,1,0:T(8,128)S(1)} custom-call(s32[1,4,4]{2,1,0:T(4,128)S(1)} %copy-done, f32[4,80,128]{2,1,0:T(8,128)S(1)} %after.1.refs_1_.mine_ref, f32[4,80,128]{2,1,0:T(8,128)S(1)} %collective-permute-done.refs_2_.other_ref), custom_call_target="tpu_custom_call" | custom-call | tf_op jit(solution)/shard_map/strips/pallas_call | solution.py:684
  18.4 1.3 %collective-permute-start.1 = (f32[16,8,128]{2,1,0:T(8,128)S(1)}, f32[16,8,128]{2,1,0:T(8,128)S(1)}, u32[]{:S(2)}, u32[]{:S(2)}) collective-permute-start(f32[16,8,128]{2,1,0:T(8,128)S(1)} %strips.1.strips_ref), channel_id=1, source_target_pairs={{2,0},{3,1},{6,4},{7,5},{10,8},{11,9},{14,12},{15,13},{18,16},{19,... | collective-permute-start | bytes 196616 | tf_op jit(solution)/shard_map/ppermute | solution.py:692
  19.7 2.0 %halo.1 = (f32[1,128,1024]{2,1,0:T(8,128)}, f32[2,1,128,1024]{3,2,1,0:T(8,128)}, f32[3,2,8,1024]{3,2,1,0:T(8,128)S(1)}) custom-call(s32[1,4,4]{2,1,0:T(4,128)S(1)} %copy-done, f32[4,80,128]{2,1,0:T(8,128)S(1)} %after.1.refs_1_.mine_ref, f32[4,80,128]{2,1,0:T(8,128)S(1)} %collective-permute-done.refs_2_.other_ref, ...), custom_call_target="tpu_custom_call", output_to_operand_aliasing={{0}: (11, {}), {1}: (12, {})} | custom-call | tf_op jit(solution)/shard_map/halo/pallas_call | solution.py:694
  21.7 2.8 %collective-permute-done.1.finer_ref = f32[16,8,128]{2,1,0:T(8,128)S(1)} collective-permute-done((f32[16,8,128]{2,1,0:T(8,128)S(1)}, f32[16,8,128]{2,1,0:T(8,128)S(1)}, u32[]{:S(2)}, u32[]{:S(2)}) %collective-permute-start.1) | collective-permute-done | bytes 65568 | tf_op jit(solution)/shard_map/ppermute | solution.py:692
  24.5 2.1 %inflow.1 = (f32[1,128,1024]{2,1,0:T(8,128)}, f32[2,1,128,1024]{3,2,1,0:T(8,128)}) custom-call(s32[1,4,4]{2,1,0:T(4,128)S(1)} %copy-done, f32[4,80,128]{2,1,0:T(8,128)S(1)} %after.1.refs_1_.mine_ref, f32[4,80,128]{2,1,0:T(8,128)S(1)} %collective-permute-done.refs_2_.other_ref, ...), custom_call_target="tpu_custom_call", output_to_operand_aliasing={{0}: (7, {}), {1}: (8, {})} | custom-call | tf_op jit(solution)/shard_map/inflow/pallas_call | solution.py:707
  (1 shorter events, 0.0 us)
Async XLA Ops:
  3.0 12.8 %all-to-all-start = ((f32[4,80,128]{2,1,0:T(8,128)}), f32[4,80,128]{2,1,0:T(8,128)S(1)}, u32[]{:S(2)}, u32[]{:S(2)}) async-start(f32[4,80,128]{2,1,0:T(8,128)} %pack.1), calls=%async_computation | async-start | bytes 327680 | tf_op jit(solution)/shard_map/all_to_all | solution.py:678
  15.8 1.4 %copy-start = (s32[1,4,4]{2,1,0:T(4,128)S(1)}, s32[1,4,4]{2,1,0:T(4,128)}, u32[]{:S(2)}) copy-start(s32[1,4,4]{2,1,0:T(4,128)} %links_ref.3) | copy-start | bytes 196
  15.8 1.4 %collective-permute-start = (f32[4,80,128]{2,1,0:T(8,128)S(1)}, f32[4,80,128]{2,1,0:T(8,128)S(1)}, u32[]{:S(2)}, u32[]{:S(2)}) collective-permute-start(f32[4,80,128]{2,1,0:T(8,128)S(1)} %after.1.refs_1_.mine_ref), channel_id=1, source_target_pairs={{0,1},{1,0},{2,3},{3,2},{4,5},{5,4},{6,7},{7,6},{8,9},{9,8},{10,11... | collective-permute-start | bytes 491528 | tf_op jit(solution)/shard_map/ppermute | solution.py:679
  18.4 6.2 %collective-permute-start.1 = (f32[16,8,128]{2,1,0:T(8,128)S(1)}, f32[16,8,128]{2,1,0:T(8,128)S(1)}, u32[]{:S(2)}, u32[]{:S(2)}) collective-permute-start(f32[16,8,128]{2,1,0:T(8,128)S(1)} %strips.1.strips_ref), channel_id=1, source_target_pairs={{2,0},{3,1},{6,4},{7,5},{10,8},{11,9},{14,12},{15,13},{18,16},{19,... | collective-permute-start | bytes 196616 | tf_op jit(solution)/shard_map/ppermute | solution.py:692

commit v9 on v8

--- a/solution.py
+++ b/solution.py
@@ -41,7 +41,7 @@
 
 
 def pack_kernel(eta_ref, momenta_ref, depth_ref, wet_ref, gain_ref, index_ref, out_ref,
-                ends, end_wet, sides, side_wet, gains, indices, packet, sems, out_sems):
+                ends, end_wet, sides, side_wet, gains, indices, sems):
     rows, cols = eta_ref.shape[1:]
     fields = eta_ref.at[0], momenta_ref.at[0, 0], momenta_ref.at[1, 0], depth_ref.at[0]
     tall, wide = [], []
@@ -65,7 +65,7 @@
 
     def put(row, value):
         for tile in range(TILE):
-            packet[row * TILE + tile:row * TILE + tile + 1] = value[:, tile * LANES:(tile + 1) * LANES]
+            out_ref[row * TILE + tile:row * TILE + tile + 1] = value[:, tile * LANES:(tile + 1) * LANES]
 
     eta, row, col, depth, mask = loaded(0)
     east = jnp.where(lane == cols - 1, 0.0, rolled(eta, -1, 1))
@@ -89,9 +89,6 @@
     put(EDGE_FLOW, flow[TILE - 1:])
     put(EDGE_DEPTH, depth[TILE - 1:])
     put(EDGE_SUM, edge_sum[TILE - 1:])
-    lines = pl.ds(0, ROWS * TILE)
-    out_copies = copied(
-        [(packet.at[lines], out_ref.at[turn, lines]) for turn in range(out_ref.shape[0])], out_sems.at[0])
 
     for copy in copies[len(tall):]:
         copy.wait()
@@ -108,12 +105,7 @@
     ):
         moved = value if place == at else rolled(value, place - at, 1)
         columns = jnp.where(lane == place, moved, columns)
-    packet[ROWS * TILE:] = columns.T[:COLUMNS]
-    lines = pl.ds(ROWS * TILE, COLUMNS)
-    out_copies += copied(
-        [(packet.at[lines], out_ref.at[turn, lines]) for turn in range(out_ref.shape[0])], out_sems.at[1])
-    for copy in out_copies:
-        copy.wait()
+    out_ref[ROWS * TILE:] = columns.T[:COLUMNS]
 
 
 def bulk_kernel(eta_ref, momenta_ref, depth_ref, wet_ref, eta_out, momenta_out,
@@ -198,8 +190,11 @@
         copy.wait()
 
 
-def after_kernel(value_ref, other_ref, out_ref):
-    del value_ref, other_ref, out_ref
+def gather_kernel(*refs):
+    packets, out_ref = refs[:-2], refs[-1]
+    own = lax.axis_index("patch")
+    for turn, packet in enumerate(packets):
+        out_ref[own ^ turn] = packet[...]
 
 
 class Segment:
@@ -300,34 +295,40 @@
 
 def strips_kernel(*refs):
     links_ref, mine_ref, other_ref = refs[:3]
-    out_ref = refs[-1]
-    finer_ref = refs[3] if len(refs) == 5 else None
+    out_ref, strips_ref = refs[-2:]
+    finer_ref = refs[3] if len(refs) == 6 else None
     links = Links(links_ref, mine_ref.shape[0])
     patches, count = links.patches, 2 * links.patches
     packets = Packets((mine_ref, other_ref))
-    inflows = []
-    for segment in links.all():
-        eta = packets.tile(segment, STRIP)
+    every = links.all()
+    strips, inflows = [], []
+    for segment in every:
+        strip = packets.tile(segment, STRIP)
         if finer_ref is not None:
             place = segment.place(patches)
             gain, index = packets.tile(segment, GAIN), packets.tile(segment, INDEX).astype(jnp.int32)
             inflow, later = [gain * nested(finer_ref[step * count + place], index) for step in range(2)]
             inflows.append((inflow, later))
-            eta = eta + inflow
-        out_ref[segment.place(patches)] = eta
-    for segment in links.all():
-        place = segment.place(patches)
-        eta, depth = out_ref[place], packets.tile(segment, STRIP_DEPTH)
+            strip = strip + inflow
+            strips_ref[place] = strip
+        strips.append(strip)
+
+    def strip_at(segment):
+        return packets.tile(segment, STRIP) if finer_ref is None else strips_ref[segment.place(patches)]
+
+    totals = []
+    for place, segment in enumerate(every):
+        eta, depth = strips[place], packets.tile(segment, STRIP_DEPTH)
         mask = wet(depth)
         east, there = links.east(segment)
-        edge = there * rolled(rolled(out_ref[east.place(patches)], -1, 1), -1, 0)
+        edge = there * rolled(rolled(strip_at(east), -1, 1), -1, 0)
         if finer_ref is None:
             row = jnp.where(is_last(), -courant * mask * edge, 0.0)
         else:
             inflow, later = inflows[place]
             row = courant * mask * (inflow - next_cells(inflow, edge))
         west, there = links.west(segment)
-        west_eta = rolled(rolled(out_ref[west.place(patches)], 1, 1), 1, 0)
+        west_eta = rolled(rolled(strip_at(west), 1, 1), 1, 0)
         west_mask = rolled(rolled(wet(packets.tile(west, STRIP_DEPTH)), 1, 1), 1, 0)
         edge = there * west_mask * (packets.column(west, LAST_ROW) - courant * (eta - west_eta))
         north, there = links.north(segment)
@@ -338,6 +339,9 @@
         else:
             total = (total + mask * inflow + later
                      - courant * depth * (row - last_cells(row, edge) + courant * mask * inflow - col))
+        totals.append(total)
+    for place, (strip, total) in enumerate(zip(strips, totals)):
+        out_ref[place] = strip
         out_ref[count + place] = total
 
 
@@ -635,14 +639,14 @@
               for field in (adjoint_height, adjoint_momenta, depth, wet_mask, nest_gain, nest_index)]
     packed = pl.pallas_call(
         pack_kernel,
-        out_shape=array(patches, LINES, LANES),
+        out_shape=array(LINES, LANES),
         in_specs=[hbm] * 6,
-        out_specs=hbm,
+        out_specs=vmem,
         scratch_shapes=[
             scratch(2, 4, TILE, cols), pltpu.VMEM((2, TILE, cols), jnp.int32),
             scratch(2, 4, rows, LANES), pltpu.VMEM((2, rows, LANES), jnp.int32),
             scratch(levels, cols), pltpu.VMEM((levels, cols), jnp.int32),
-            scratch(LINES, LANES), pltpu.SemaphoreType.DMA((22,)), pltpu.SemaphoreType.DMA((2, patches)),
+            pltpu.SemaphoreType.DMA((22,)),
         ],
         compiler_params=params,
         name="pack",
@@ -667,15 +671,18 @@
         name="bulk",
     )(*fields[:4])
 
+    sent = [packed] + [
+        lax.ppermute(packed, "patch", [(source, source ^ turn) for source in range(patches)])
+        for turn in range(1, patches)
+    ]
     mine = pl.pallas_call(
-        after_kernel,
-        out_shape=array(*packed.shape),
-        in_specs=[vmem, vmem],
+        gather_kernel,
+        out_shape=array(patches, LINES, LANES),
+        in_specs=[vmem] * (patches + 1),
         out_specs=vmem,
-        input_output_aliases={0: 0},
         compiler_params=params,
-        name="after",
-    )(lax.all_to_all(packed, "patch", 0, 0, tiled=True), after[-1])
+        name="gather",
+    )(*sent, after[-1])
     other = lax.ppermute(mine, "sub", [(0, 1), (1, 0)])
 
     flux = ()
@@ -686,6 +693,7 @@
             out_shape=array(2 * count, TILE, LANES),
             in_specs=[smem] + [vmem] * (2 + len(flux)),
             out_specs=vmem,
+            scratch_shapes=[scratch(count, TILE, LANES)],
             compiler_params=params,
             name="strips",
         )(adjacency, mine, other, *flux))

time: 26.9 us -> 23 us (0.86)
  waiting for transfers between devices: 6.46 us -> 4.19 us
  Pallas kernels: 11.9 us -> 10.7 us
  starting transfers between devices: 7.62 us -> 7.12 us
    all_to_all x1 -> x0, starting transfers between devices: 6.33 us -> none  [body(): lax.all_to_all(packed, 'patch', 0, 0, tiled=True)]
    ppermute x0 -> x3, starting transfers between devices: none -> 5.76 us  [body(): lax.ppermute(packed, 'patch', [(source, source ^ turn) for source in rang...]
    all_to_all x1 -> x0, waiting for transfers between devices: 2.26 us -> none  [body(): lax.all_to_all(packed, 'patch', 0, 0, tiled=True)]
    pallas_call x2, Pallas kernels: 2.38 us -> 1.7 us  [the longest x1 1.67 us: body(): pl.pallas_call(pack_kernel, out_shape=array(LINES, LANES), in_specs=[hbm]...]
    pallas_call x1, Pallas kernels: 1.2 us -> 0.67 us  [body(): pl.pallas_call(strips_kernel, out_shape=array(2 * count, TILE, LANES), in...]
  transfers between devices with their start and end apart: 3 -> 5, of which waited for: 3 -> 2; matrix products, arithmetic and copies ran while one was open for 0% -> 0% of each run, Pallas kernels for 23% -> 28%
where the time goes in v9:
time: 23 us; the launch traced here: 22.8 us
  Pallas kernels  10.7 us (47%)
  starting transfers between devices  7.12 us (31%)
  waiting for transfers between devices  4.19 us (18%)
  between operations  0.72 us (3%)
    ppermute x3, starting transfers between devices, body(): lax.ppermute(packed, 'patch', [(source, source ^ turn) for source in rang...  5.76 us
    pallas_call x1, Pallas kernels, body(): pl.pallas_call(bulk_kernel, out_shape=[array(*adjoint_height.shape), arra...  4.24 us
    ppermute x1, waiting for transfers between devices, body(): lax.ppermute(strips[-1], 'level', [(source, source - 1) for source in ran...  2.8 us
    pallas_call x1, Pallas kernels, body(): pl.pallas_call(inflow_kernel, out_shape=[array(*adjoint_height.shape), ar...  2.08 us
    pallas_call x1, Pallas kernels, body(): pl.pallas_call(halo_kernel, out_shape=[array(*adjoint_height.shape), arra...  2.05 us
    pallas_call x1, Pallas kernels, body(): pl.pallas_call(pack_kernel, out_shape=array(LINES, LANES), in_specs=[hbm]...  1.67 us
    ppermute x1, waiting for transfers between devices, body(): other = lax.ppermute(mine, 'sub', [(0, 1), (1, 0)])  1.38 us
    ppermute x1, starting transfers between devices, body(): lax.ppermute(strips[-1], 'level', [(source, source - 1) for source in ran...  1.29 us
  transfers between devices with their start and end apart: 5, of which 2 were waited for; matrix products, arithmetic and copies ran while one was open for 0% of the time, Pallas kernels for 28%

profile of v9, /device:TPU:0, one launch (start us, length us, event | category | flops | bytes accessed | tf_op | source)
XLA Modules:
  0.0 22.8 jit_solution(13616228539060954112)
XLA Ops:
  0.6 1.7 %pack.1.refs_0_ = f32[80,128]{1,0:T(8,128)S(1)} custom-call(f32[1,128,1024]{2,1,0:T(8,128)} %eta_ref.3, f32[2,1,128,1024]{3,2,1,0:T(8,128)} %momenta_ref.3, f32[1,128,1024]{2,1,0:T(8,128)} %depth_ref.3, s32[1,128,1024]{2,1,0:T(8,128)} %wet_ref.3, f32[2,1024]{1,0:T(2,128)} %gain_ref.1, s32[2,1024]{1,0:T(2,128)} %index_ref.1), custom_call_target="tpu_custom_call" | custom-call | tf_op jit(solution)/shard_map/pack/pallas_call | solution.py:640
  2.3 5.1 %collective-permute-start.2 = (f32[80,128]{1,0:T(8,128)S(1)}, f32[80,128]{1,0:T(8,128)S(1)}, u32[]{:S(2)}, u32[]{:S(2)}) collective-permute-start(f32[80,128]{1,0:T(8,128)S(1)} %pack.1.refs_0_), channel_id=1, source_target_pairs={{0,12},{4,8},{8,4},{12,0},{1,13},{5,9},{9,5},{13,1},{2,14},{6,10},... | collective-permute-start | bytes 122888 | tf_op jit(solution)/shard_map/ppermute | solution.py:675
  7.4 0.0 collective-permute-start.1
  7.4 0.6 %collective-permute-start = (f32[80,128]{1,0:T(8,128)S(1)}, f32[80,128]{1,0:T(8,128)S(1)}, u32[]{:S(2)}, u32[]{:S(2)}) collective-permute-start(f32[80,128]{1,0:T(8,128)S(1)} %pack.1.refs_0_), channel_id=1, source_target_pairs={{0,4},{4,0},{8,12},{12,8},{1,5},{5,1},{9,13},{13,9},{2,6},{6,2},{1... | collective-permute-start | bytes 122888 | tf_op jit(solution)/shard_map/ppermute | solution.py:675
  8.1 4.2 %bulk.1 = (f32[1,128,1024]{2,1,0:T(8,128)}, f32[2,1,128,1024]{3,2,1,0:T(8,128)}, f32[128,1024]{1,0:T(8,128)S(1)}, f32[2,128,1024]{2,1,0:T(8,128)S(1)}, f32[128,1...) custom-call(f32[1,128,1024]{2,1,0:T(8,128)} %eta_ref.3, ...), custom_call_target="tpu_custom_call" | custom-call | tf_op jit(solution)/shard_map/bulk/pallas_call | solution.py:655
  12.3 0.0 collective-permute-done.2.refs_3_
  12.3 0.0 collective-permute-done.1.refs_2_
  12.3 0.0 collective-permute-done.refs_1_
  12.4 0.0 copy-start
  12.4 0.1 collective-permute-start.3
  12.5 1.4 %collective-permute-done.3.refs_2_.other_ref = f32[4,80,128]{2,1,0:T(8,128)S(1)} collective-permute-done((f32[4,80,128]{2,1,0:T(8,128)S(1)}, f32[4,80,128]{2,1,0:T(8,128)S(1)}, u32[]{:S(2)}, u32[]{:S(2)}) %collective-permute-start.3) | collective-permute-done | bytes 163872 | tf_op jit(solution)/shard_map/ppermute | solution.py:686
  13.9 0.0 copy-done
  13.9 0.7 %strips.1.strips_ref = f32[16,8,128]{2,1,0:T(8,128)S(1)} custom-call(s32[1,4,4]{2,1,0:T(4,128)S(1)} %copy-done, f32[4,80,128]{2,1,0:T(8,128)S(1)} %gather.1.refs_1_.mine_ref, f32[4,80,128]{2,1,0:T(8,128)S(1)} %collective-permute-done.3.refs_2_.other_ref), custom_call_target="tpu_custom_call" | custom-call | tf_op jit(solution)/shard_map/strips/pallas_call | solution.py:691
  14.5 1.3 %collective-permute-start.4 = (f32[16,8,128]{2,1,0:T(8,128)S(1)}, f32[16,8,128]{2,1,0:T(8,128)S(1)}, u32[]{:S(2)}, u32[]{:S(2)}) collective-permute-start(f32[16,8,128]{2,1,0:T(8,128)S(1)} %strips.1.strips_ref), channel_id=1, source_target_pairs={{2,0},{3,1},{6,4},{7,5},{10,8},{11,9},{14,12},{15,13},{18,16},{19,... | collective-permute-start | bytes 196616 | tf_op jit(solution)/shard_map/ppermute | solution.py:700
  15.8 2.1 %halo.1 = (f32[1,128,1024]{2,1,0:T(8,128)}, f32[2,1,128,1024]{3,2,1,0:T(8,128)}, f32[3,2,8,1024]{3,2,1,0:T(8,128)S(1)}) custom-call(s32[1,4,4]{2,1,0:T(4,128)S(1)} %copy-done, f32[4,80,128]{2,1,0:T(8,128)S(1)} %gather.1.refs_1_.mine_ref, f32[4,80,128]{2,1,0:T(8,128)S(1)} %collective-permute-done.3.refs_2_.other_ref, ...), custom_call_target="tpu_custom_call", output_to_operand_aliasing={{0}: (11, {}), {1}: (12, {})} | custom-call | tf_op jit(solution)/shard_map/halo/pallas_call | solution.py:702
  17.9 2.8 %collective-permute-done.4.finer_ref = f32[16,8,128]{2,1,0:T(8,128)S(1)} collective-permute-done((f32[16,8,128]{2,1,0:T(8,128)S(1)}, f32[16,8,128]{2,1,0:T(8,128)S(1)}, u32[]{:S(2)}, u32[]{:S(2)}) %collective-permute-start.4) | collective-permute-done | bytes 65568 | tf_op jit(solution)/shard_map/ppermute | solution.py:700
  20.7 2.1 %inflow.1 = (f32[1,128,1024]{2,1,0:T(8,128)}, f32[2,1,128,1024]{3,2,1,0:T(8,128)}) custom-call(s32[1,4,4]{2,1,0:T(4,128)S(1)} %copy-done, f32[4,80,128]{2,1,0:T(8,128)S(1)} %gather.1.refs_1_.mine_ref, f32[4,80,128]{2,1,0:T(8,128)S(1)} %collective-permute-done.3.refs_2_.other_ref, ...), custom_call_target="tpu_custom_call", output_to_operand_aliasing={{0}: (7, {}), {1}: (8, {})} | custom-call | tf_op jit(solution)/shard_map/inflow/pallas_call | solution.py:715
  (1 shorter events, 0.0 us)
Async XLA Ops:
  2.3 10.0 %collective-permute-start.2 = (f32[80,128]{1,0:T(8,128)S(1)}, f32[80,128]{1,0:T(8,128)S(1)}, u32[]{:S(2)}, u32[]{:S(2)}) collective-permute-start(f32[80,128]{1,0:T(8,128)S(1)} %pack.1.refs_0_), channel_id=1, source_target_pairs={{0,12},{4,8},{8,4},{12,0},{1,13},{5,9},{9,5},{13,1},{2,14},{6,10},... | collective-permute-start | bytes 122888 | tf_op jit(solution)/shard_map/ppermute | solution.py:675
  7.4 4.9 %collective-permute-start.1 = (f32[80,128]{1,0:T(8,128)S(1)}, f32[80,128]{1,0:T(8,128)S(1)}, u32[]{:S(2)}, u32[]{:S(2)}) collective-permute-start(f32[80,128]{1,0:T(8,128)S(1)} %pack.1.refs_0_), channel_id=1, source_target_pairs={{0,8},{4,12},{8,0},{12,4},{1,9},{5,13},{9,1},{13,5},{2,10},{6,14},... | collective-permute-start | bytes 122888 | tf_op jit(solution)/shard_map/ppermute | solution.py:675
  7.4 4.9 %collective-permute-start = (f32[80,128]{1,0:T(8,128)S(1)}, f32[80,128]{1,0:T(8,128)S(1)}, u32[]{:S(2)}, u32[]{:S(2)}) collective-permute-start(f32[80,128]{1,0:T(8,128)S(1)} %pack.1.refs_0_), channel_id=1, source_target_pairs={{0,4},{4,0},{8,12},{12,8},{1,5},{5,1},{9,13},{13,9},{2,6},{6,2},{1... | collective-permute-start | bytes 122888 | tf_op jit(solution)/shard_map/ppermute | solution.py:675
  12.4 1.5 %copy-start = (s32[1,4,4]{2,1,0:T(4,128)S(1)}, s32[1,4,4]{2,1,0:T(4,128)}, u32[]{:S(2)}) copy-start(s32[1,4,4]{2,1,0:T(4,128)} %links_ref.3) | copy-start | bytes 196
  12.4 1.5 %collective-permute-start.3 = (f32[4,80,128]{2,1,0:T(8,128)S(1)}, f32[4,80,128]{2,1,0:T(8,128)S(1)}, u32[]{:S(2)}, u32[]{:S(2)}) collective-permute-start(f32[4,80,128]{2,1,0:T(8,128)S(1)} %gather.1.refs_1_.mine_ref), channel_id=1, source_target_pairs={{0,1},{1,0},{2,3},{3,2},{4,5},{5,4},{6,7},{7,6},{8,9},{9,8},{10,11... | collective-permute-start | bytes 491528 | tf_op jit(solution)/shard_map/ppermute | solution.py:686
  14.5 6.2 %collective-permute-start.4 = (f32[16,8,128]{2,1,0:T(8,128)S(1)}, f32[16,8,128]{2,1,0:T(8,128)S(1)}, u32[]{:S(2)}, u32[]{:S(2)}) collective-permute-start(f32[16,8,128]{2,1,0:T(8,128)S(1)} %strips.1.strips_ref), channel_id=1, source_target_pairs={{2,0},{3,1},{6,4},{7,5},{10,8},{11,9},{14,12},{15,13},{18,16},{19,... | collective-permute-start | bytes 196616 | tf_op jit(solution)/shard_map/ppermute | solution.py:700

commit v10 on v9

--- a/solution.py
+++ b/solution.py
@@ -108,86 +108,50 @@
     out_ref[ROWS * TILE:] = columns.T[:COLUMNS]
 
 
-def bulk_kernel(eta_ref, momenta_ref, depth_ref, wet_ref, eta_out, momenta_out,
-                eta_after, momenta_after, wet_after, depth_after, eta_ends, row_ends, turned,
-                eta_pad, col_pad, momenta_in, depth_in, wet_in, eta_left, row_right, sems, out_sems):
-    rows, cols = eta_ref.shape[1:]
+def first_kernel(eta_ref, momenta_ref, depth_ref, wet_ref, eta_after, row_after, col_after, wet_after, depth_after,
+                 turned, eta_pad, momenta_in, depth_in, wet_in, sems):
+    rows, cols = row_after.shape
     parts = sems.shape[0]
     size = rows // parts
     loads = []
     for part in range(parts):
         here = pl.ds(part * size, size)
         loads.append(copied([
-            (eta_ref.at[0, here, :], eta_pad.at[pl.ds(TILE + part * size, size), :]),
+            (eta_ref.at[0, here, :], eta_pad.at[here, :]),
             (momenta_ref.at[:, 0, here, :], momenta_in.at[:, here, :]),
             (depth_ref.at[0, here, :], depth_in.at[here, :]),
             (wet_ref.at[0, here, :], wet_in.at[here, :]),
         ], sems.at[part]))
-    lane = iota((TILE, cols), 1)
-    eta_pad[TILE + rows:] = jnp.zeros((TILE, cols), jnp.float32)
-    col_pad[:TILE] = jnp.zeros((TILE, cols), jnp.float32)
-
-    def step(number, low):
-        chunk, padded = slice(low, low + TILE), slice(TILE + low, 2 * TILE + low)
-        eta = eta_pad[padded]
-        if number == 0:
-            mask = wet_in[chunk].astype(jnp.float32)
-            depth = courant * mask * depth_in[chunk]
-            wet_after[chunk] = mask
-            depth_after[chunk] = depth
-            row, col = momenta_in[0, chunk], momenta_in[1, chunk]
-        else:
-            mask, depth = wet_after[chunk], depth_after[chunk]
-            row, col = momenta_after[0, chunk], col_pad[padded]
-        east = jnp.where(lane == cols - 1, 0.0, rolled(eta, -1, 1))
-        south = eta_pad[TILE + low + 1:2 * TILE + low + 1]
-        row = mask * (row - courant * (east - eta))
-        col = mask * (col - courant * (south - eta))
-        momenta_after[0, chunk] = row
-        col_pad[padded] = col
-        if number:
-            momenta_after[1, chunk] = col
-        west = jnp.where(lane == 0, 0.0, rolled(row, 1, 1))
-        north = col_pad[TILE + low - 1:2 * TILE + low - 1]
-        eta = mask * eta - depth * (row - west + (col - north))
-        if number:
-            eta_after[chunk] = eta
-            return
-        eta_pad[padded] = eta
-        eta_left[chunk] = eta[:, :LANES]
-        row_right[chunk] = row[:, cols - LANES:]
-        if low in (0, rows - TILE):
-            end = int(low > 0)
-            eta_ends[end] = eta
-            row_ends[end] = row
-
+    lane, line = iota((TILE, cols), 1), iota((TILE, cols), 0)
+    eta_pad[rows:] = jnp.zeros((TILE, cols), jnp.float32)
+    eta_after[rows:] = jnp.zeros((TILE, cols), jnp.float32)
+    above = jnp.zeros((1, cols), jnp.float32)
     for copy in loads[0]:
         copy.wait()
-    stores = []
-    for part in range(parts + 1):
+    for part in range(parts):
         if part + 1 < parts:
             for copy in loads[part + 1]:
                 copy.wait()
-        if part < parts:
-            for low in range(part * size, (part + 1) * size, TILE):
-                step(0, low)
-        if part:
-            for low in range((part - 1) * size, part * size, TILE):
-                step(1, low)
-            here = pl.ds((part - 1) * size, size)
-            stores += copied([
-                (eta_after.at[here, :], eta_out.at[0, here, :]),
-                (momenta_after.at[:, here, :], momenta_out.at[:, 0, here, :]),
-            ], out_sems.at[part - 1])
+        for low in range(part * size, (part + 1) * size, TILE):
+            chunk = slice(low, low + TILE)
+            mask = wet_in[chunk].astype(jnp.float32)
+            depth = courant * mask * depth_in[chunk]
+            below = eta_pad[low + 1:low + TILE + 1]
+            eta, row, col = advanced(
+                eta_pad[chunk], momenta_in[0, chunk], momenta_in[1, chunk], mask, depth,
+                lambda eta: jnp.where(lane == cols - 1, 0.0, rolled(eta, -1, 1)), lambda eta: below,
+                lambda row: jnp.where(lane == 0, 0.0, rolled(row, 1, 1)),
+                lambda col: jnp.where(line == 0, above, rolled(col, 1, 0)))
+            above = col[TILE - 1:]
+            eta_after[chunk], row_after[chunk], col_after[chunk] = eta, row, col
+            wet_after[chunk], depth_after[chunk] = mask, depth
     right = cols - LANES
     turned[0] = wet_after[:, :LANES].T[:TILE]
     turned[1] = depth_after[:, :LANES].T[:TILE]
     turned[2] = wet_after[:, right:].T[LANES - TILE:]
     turned[3] = depth_after[:, right:].T[LANES - TILE:]
-    turned[4] = eta_left[...].T[:TILE]
-    turned[5] = row_right[...].T[LANES - TILE:]
-    for copy in stores:
-        copy.wait()
+    turned[4] = eta_after[:rows, :LANES].T[:TILE]
+    turned[5] = row_after[:, right:].T[LANES - TILE:]
 
 
 def gather_kernel(*refs):
@@ -203,6 +167,10 @@
 
     def place(self, patches):
         return self.flipped * patches + self.patch
+
+
+def below_finest():
+    return jnp.where(lax.axis_index("level") < lax.axis_size("level") - 1, 1.0, 0.0)
 
 
 class Links:
@@ -306,7 +274,7 @@
         strip = packets.tile(segment, STRIP)
         if finer_ref is not None:
             place = segment.place(patches)
-            gain, index = packets.tile(segment, GAIN), packets.tile(segment, INDEX).astype(jnp.int32)
+            gain, index = packets.tile(segment, GAIN) * below_finest(), packets.tile(segment, INDEX).astype(jnp.int32)
             inflow, later = [gain * nested(finer_ref[step * count + place], index) for step in range(2)]
             inflows.append((inflow, later))
             strip = strip + inflow
@@ -456,36 +424,27 @@
             for low in (0, rows - TILE)]
 
 
-def halo_kernel(links_ref, mine_ref, other_ref, strips_ref, eta_after, momenta_after, wet_after, depth_after,
-                eta_ends, row_ends, turned, eta_hbm, momenta_hbm, eta_out, momenta_out, ends_out,
-                left_new, right_new, sems):
-    del eta_hbm, momenta_hbm
-    rows, cols = eta_after.shape
-    right = cols - LANES
+def second_kernel(links_ref, mine_ref, other_ref, strips_ref, eta_after, row_after, col_after, wet_after,
+                  depth_after, turned, eta_out, momenta_out, ends_out, new_ref, more_ref, sems):
+    rows, cols = row_after.shape
     links = Links(links_ref, mine_ref.shape[0])
     own = links.own()
     packets = Packets((mine_ref, other_ref))
     columns = beside(links, packets, own)
     west_row, west_mask, west_eta, east_eta, east_sum, east_depth = columns
-    fields = eta_after, momenta_after.at[0], momenta_after.at[1]
-
-    line = iota((TILE, rows), 0)
-    lane = iota((TILE, rows), 1)
+
+    line, lane = iota((TILE, rows), 0), iota((TILE, rows), 1)
     nothing = jnp.zeros((TILE, rows), jnp.float32)
-
-    def south(eta):
-        return jnp.where(lane == rows - 1, 0.0, rolled(eta, -1, 1))
-
-    def north(col):
-        return jnp.where(lane == 0, 0.0, rolled(col, 1, 1))
 
     def column_steps(mask, depth, east, west):
         state = nothing, nothing, nothing
         for number in range(2):
             state = advanced(
                 *state, mask, depth,
-                lambda eta: jnp.where(line == TILE - 1, east(number, state), rolled(eta, -1, 0)), south,
-                lambda row: jnp.where(line == 0, west(number, state), rolled(row, 1, 0)), north)
+                lambda eta: jnp.where(line == TILE - 1, east(number, state), rolled(eta, -1, 0)),
+                lambda eta: jnp.where(lane == rows - 1, 0.0, rolled(eta, -1, 1)),
+                lambda row: jnp.where(line == 0, west(number, state), rolled(row, 1, 0)),
+                lambda col: jnp.where(lane == 0, 0.0, rolled(col, 1, 1)))
         return state
 
     def west_of(number, state):
@@ -502,41 +461,54 @@
     left = column_steps(turned[0], turned[1], lambda number, state: 0.0, west_of)
     last = column_steps(turned[2], turned[3], east_of, lambda number, state: 0.0)
     middle = jnp.zeros((LANES - 2 * TILE, rows), jnp.float32)
-    lane = iota((rows, LANES), 1)
-    body_rows = slice(TILE, rows - TILE)
-    copies = []
-    outs = eta_out.at[0], momenta_out.at[0, 0], momenta_out.at[1, 0]
-    inner = pl.ds(TILE, rows - 2 * TILE)
-    for place, field in enumerate(fields):
-        more = jnp.concatenate([left[place], middle, last[place]], axis=0).T[body_rows]
-        inside = iota(more.shape, 1)
-        left_new[place] = field[body_rows, :LANES] + jnp.where(inside < TILE, more, 0.0)
-        right_new[place] = field[body_rows, right:] + jnp.where(inside >= LANES - TILE, more, 0.0)
-        copies += copied([
-            (left_new.at[place], outs[place].at[inner, pl.ds(0, LANES)]),
-            (right_new.at[place], outs[place].at[inner, pl.ds(right, LANES)]),
-        ], sems.at[place])
+    for place in range(3):
+        more_ref[place] = jnp.concatenate([left[place], middle, last[place]], axis=0).T
 
     top_sides, low_sides = as_sublanes(columns)
     nothing = jnp.zeros((TILE, cols), jnp.float32)
+    end = slice(rows - TILE, rows)
     top = two_steps(
-        nothing, wet_after[:TILE], depth_after[:TILE], top_sides, (eta_ends[0], row_ends[0]),
+        nothing, wet_after[:TILE], depth_after[:TILE], top_sides, (eta_after[:TILE], row_after[:TILE]),
         north=north_of(links, packets, own, packets.row(own, STRIP)))
     below, there = links.south(own)
     low = two_steps(
-        nothing, wet_after[rows - TILE:], depth_after[rows - TILE:], low_sides, (eta_ends[1], row_ends[1]),
-        south=(packets.row(below, STRIP) * there, row_of(strips_ref, 2 * links.patches + below.place(links.patches)) * there))
+        nothing, wet_after[end], depth_after[end], low_sides, (eta_after[end], row_after[end]),
+        south=(packets.row(below, STRIP) * there,
+               row_of(strips_ref, 2 * links.patches + below.place(links.patches)) * there))
+
     line, lane = iota((TILE, cols), 0), iota((TILE, cols), 1)
-    for place, field in enumerate(fields):
-        more = jnp.concatenate([left[place], middle, last[place]], axis=0).T
-        gap = jnp.zeros((TILE, cols - 2 * LANES), jnp.float32)
-        for end, (low_row, near, found) in enumerate(
-                ((0, line < TILE // 2, top), (rows - TILE, line >= TILE // 2, low))):
-            tile = more[low_row:low_row + TILE]
-            inside = iota(tile.shape, 1)
-            wide = jnp.concatenate(
-                [jnp.where(inside < TILE, tile, 0.0), gap, jnp.where(inside >= LANES - TILE, tile, 0.0)], axis=1)
-            ends_out[place, end] = field[low_row:low_row + TILE] + jnp.where(near, found[place], wide)
+    inside = iota((TILE, LANES), 1)
+    outs = eta_out.at[0], momenta_out.at[0, 0], momenta_out.at[1, 0]
+    above = jnp.zeros((1, cols), jnp.float32)
+    parts = sems.shape[0]
+    size = (rows - 2 * TILE) // parts
+    copies = []
+    for first in range(0, rows, TILE):
+        chunk = slice(first, first + TILE)
+        south = eta_after[first + 1:first + TILE + 1]
+        fields = advanced(
+            eta_after[chunk], row_after[chunk], col_after[chunk], wet_after[chunk], depth_after[chunk],
+            lambda eta: jnp.where(lane == cols - 1, 0.0, rolled(eta, -1, 1)), lambda eta: south,
+            lambda row: jnp.where(lane == 0, 0.0, rolled(row, 1, 1)),
+            lambda col: jnp.where(line == 0, above, rolled(col, 1, 0)))
+        above = fields[2][TILE - 1:]
+        for place, field in enumerate(fields):
+            more = more_ref[place, chunk]
+            sides = [jnp.where(inside < TILE, more, 0.0), jnp.where(inside >= LANES - TILE, more, 0.0)]
+            if first in (0, rows - TILE):
+                near, found = (line < TILE // 2, top) if first == 0 else (line >= TILE // 2, low)
+                gap = jnp.zeros((TILE, cols - 2 * LANES), jnp.float32)
+                wide = jnp.concatenate([sides[0], gap, sides[1]], axis=1)
+                ends_out[place, int(first > 0)] = field + jnp.where(near, found[place], wide)
+            else:
+                new_ref[place, first - TILE:first] = jnp.concatenate(
+                    [field[:, :LANES] + sides[0], field[:, LANES:cols - LANES], field[:, cols - LANES:] + sides[1]],
+                    axis=1)
+        if first and first % size == 0 and first < rows - TILE:
+            part = first // size - 1
+            here, there = pl.ds(part * size, size), pl.ds(TILE + part * size, size)
+            copies += copied([(new_ref.at[place, here], out.at[there, :]) for place, out in enumerate(outs)],
+                             sems.at[part])
     for copy in copies:
         copy.wait()
 
@@ -549,12 +521,13 @@
     patches = links.patches
     own = links.own()
     packets = Packets((mine_ref, other_ref))
+    some = below_finest()
 
     def flux_place(step, segment):
         return step * 2 * patches + segment.place(patches)
 
     def inflows(segment):
-        gain, index = packets.tile(segment, GAIN), packets.tile(segment, INDEX).astype(jnp.int32)
+        gain, index = packets.tile(segment, GAIN) * some, packets.tile(segment, INDEX).astype(jnp.int32)
         return [gain * nested(finer_ref[flux_place(step, segment)], index) for step in range(2)]
 
     below, there = links.south(own)
@@ -576,7 +549,7 @@
             [finer_ref[flux_place(step, segment), source:source + 1] for _, step, segment, _ in wanted], axis=0)
         found = jnp.take_along_axis(values, lane, axis=1, mode="promise_in_bounds")
         taken = jnp.where(line == source, found, taken)
-    taken = gain * taken
+    taken = some * gain * taken
     inflow = {name: taken[place:place + 1] for place, (name, _, _, _) in enumerate(wanted)}
 
     rows_ref[0], rows_ref[1] = inflows(own)
@@ -652,23 +625,20 @@
         name="pack",
     )(*fields)
     parts = 4
-    eta_new, momenta_new, *after = pl.pallas_call(
-        bulk_kernel,
+    after = pl.pallas_call(
+        first_kernel,
         out_shape=[
-            array(*adjoint_height.shape), array(*adjoint_momenta.shape),
-            array(rows, cols), array(2, rows, cols), array(rows, cols), array(rows, cols),
-            array(2, TILE, cols), array(2, TILE, cols), array(6, TILE, rows),
+            array(rows + TILE, cols), array(rows, cols), array(rows, cols), array(rows, cols), array(rows, cols),
+            array(6, TILE, rows),
         ],
         in_specs=[hbm] * 4,
-        out_specs=[hbm] * 2 + [vmem] * 7,
+        out_specs=[vmem] * 6,
         scratch_shapes=[
-            scratch(rows + 2 * TILE, cols), scratch(rows + 2 * TILE, cols),
-            scratch(2, rows, cols), scratch(rows, cols), pltpu.VMEM((rows, cols), jnp.int32),
-            scratch(rows, LANES), scratch(rows, LANES),
-            pltpu.SemaphoreType.DMA((parts, 4)), pltpu.SemaphoreType.DMA((parts, 2)),
+            scratch(rows + TILE, cols), scratch(2, rows, cols), scratch(rows, cols),
+            pltpu.VMEM((rows, cols), jnp.int32), pltpu.SemaphoreType.DMA((parts, 4)),
         ],
         compiler_params=params,
-        name="bulk",
+        name="first",
     )(*fields[:4])
 
     sent = [packed] + [
@@ -697,20 +667,19 @@
             compiler_params=params,
             name="strips",
         )(adjacency, mine, other, *flux))
-        flux = (lax.ppermute(strips[-1], "level", [(source, source - 1) for source in range(1, levels)]),)
+        flux = (lax.ppermute(strips[-1], "level", [(source, (source - 1) % levels) for source in range(levels)]),)
 
     eta_new, momenta_new, ends = pl.pallas_call(
-        halo_kernel,
+        second_kernel,
         out_shape=[array(*adjoint_height.shape), array(*adjoint_momenta.shape), array(3, 2, TILE, cols)],
-        in_specs=[smem] + [vmem] * 10 + [hbm] * 2,
+        in_specs=[smem] + [vmem] * 9,
         out_specs=[hbm, hbm, vmem],
-        input_output_aliases={11: 0, 12: 1},
         scratch_shapes=[
-            scratch(3, rows - 2 * TILE, LANES), scratch(3, rows - 2 * TILE, LANES), pltpu.SemaphoreType.DMA((3, 2)),
+            scratch(3, rows - 2 * TILE, cols), scratch(3, rows, LANES), pltpu.SemaphoreType.DMA((2, 3)),
         ],
         compiler_params=params,
-        name="halo",
-    )(adjacency, mine, other, strips[0], *after, eta_new, momenta_new)
+        name="second",
+    )(adjacency, mine, other, strips[0], *after)
 
     return pl.pallas_call(
         inflow_kernel,
@@ -723,7 +692,7 @@
         ],
         compiler_params=params,
         name="inflow",
-    )(adjacency, mine, other, *flux, after[2], after[3], ends, eta_new, momenta_new)
+    )(adjacency, mine, other, *flux, after[3], after[4], ends, eta_new, momenta_new)
 
 
 def solution(mesh):

time: 23 us -> 22.9 us (level)
  Pallas kernels: 10.7 us -> 9.94 us
  waiting for transfers between devices: 4.19 us -> 4.7 us
    ppermute x3, waiting for transfers between devices: 0.01 us -> 3.32 us  [body(): lax.ppermute(packed, 'patch', [(source, source ^ turn) for source in rang...]
    ppermute x1, waiting for transfers between devices: 2.8 us -> 0.01 us  [body(): lax.ppermute(strips[-1], 'level', [(source, (source - 1) % levels) for so...]
    pallas_call x2, Pallas kernels: 6.29 us -> 5.48 us  [the longest x1 3.02 us: body(): pl.pallas_call(second_kernel, out_shape=[array(*adjoint_height.shape), ar...]
    ppermute x1, starting transfers between devices: 1.29 us -> 1.56 us  [body(): lax.ppermute(strips[-1], 'level', [(source, (source - 1) % levels) for so...]
  transfers between devices with their start and end apart: 5 -> 5, of which waited for: 2 -> 3; matrix products, arithmetic and copies ran while one was open for 0% -> 0% of each run, Pallas kernels for 28% -> 24%
where the time goes in v10:
time: 22.9 us; the launch traced here: 22.6 us
  Pallas kernels  9.94 us (43%)
  starting transfers between devices  7.31 us (32%)
  waiting for transfers between devices  4.7 us (21%)
  between operations  0.69 us (3%)
    ppermute x3, starting transfers between devices, body(): lax.ppermute(packed, 'patch', [(source, source ^ turn) for source in rang...  5.68 us
    ppermute x3, waiting for transfers between devices, body(): lax.ppermute(packed, 'patch', [(source, source ^ turn) for source in rang...  3.32 us
    pallas_call x1, Pallas kernels, body(): pl.pallas_call(second_kernel, out_shape=[array(*adjoint_height.shape), ar...  3.02 us
    pallas_call x1, Pallas kernels, body(): pl.pallas_call(first_kernel, out_shape=[array(rows + TILE, cols), array(r...  2.46 us
    pallas_call x1, Pallas kernels, body(): pl.pallas_call(inflow_kernel, out_shape=[array(*adjoint_height.shape), ar...  2.09 us
    pallas_call x1, Pallas kernels, body(): pl.pallas_call(pack_kernel, out_shape=array(LINES, LANES), in_specs=[hbm]...  1.67 us
    ppermute x1, starting transfers between devices, body(): lax.ppermute(strips[-1], 'level', [(source, (source - 1) % levels) for so...  1.56 us
    ppermute x1, waiting for transfers between devices, body(): other = lax.ppermute(mine, 'sub', [(0, 1), (1, 0)])  1.38 us
  transfers between devices with their start and end apart: 5, of which 3 were waited for; matrix products, arithmetic and copies ran while one was open for 0% of the time, Pallas kernels for 24%

profile of v10, /device:TPU:0, one launch (start us, length us, event | category | flops | bytes accessed | tf_op | source)
XLA Modules:
  0.0 22.6 jit_solution(1176749011447266142)
XLA Ops:
  0.6 1.7 %pack.1.refs_0_ = f32[80,128]{1,0:T(8,128)S(1)} custom-call(f32[1,128,1024]{2,1,0:T(8,128)} %eta_ref.3, f32[2,1,128,1024]{3,2,1,0:T(8,128)} %momenta_ref.3, f32[1,128,1024]{2,1,0:T(8,128)} %depth_ref.3, s32[1,128,1024]{2,1,0:T(8,128)} %wet_ref.3, f32[2,1024]{1,0:T(2,128)} %gain_ref.1, s32[2,1024]{1,0:T(2,128)} %index_ref.1), custom_call_target="tpu_custom_call" | custom-call | tf_op jit(solution)/shard_map/pack/pallas_call | solution.py:613
  2.3 3.1 %collective-permute-start = (f32[80,128]{1,0:T(8,128)S(1)}, f32[80,128]{1,0:T(8,128)S(1)}, u32[]{:S(2)}, u32[]{:S(2)}) collective-permute-start(f32[80,128]{1,0:T(8,128)S(1)} %pack.1.refs_0_), channel_id=1, source_target_pairs={{0,4},{4,0},{8,12},{12,8},{1,5},{5,1},{9,13},{13,9},{2,6},{6,2},{1... | collective-permute-start | bytes 122888 | tf_op jit(solution)/shard_map/ppermute | solution.py:645
  5.4 2.6 %collective-permute-start.1 = (f32[80,128]{1,0:T(8,128)S(1)}, f32[80,128]{1,0:T(8,128)S(1)}, u32[]{:S(2)}, u32[]{:S(2)}) collective-permute-start(f32[80,128]{1,0:T(8,128)S(1)} %pack.1.refs_0_), channel_id=1, source_target_pairs={{0,8},{4,12},{8,0},{12,4},{1,9},{5,13},{9,1},{13,5},{2,10},{6,14},... | collective-permute-start | bytes 122888 | tf_op jit(solution)/shard_map/ppermute | solution.py:645
  8.0 0.0 collective-permute-start.2
  8.0 2.5 %first.1 = (f32[136,1024]{1,0:T(8,128)S(1)}, f32[128,1024]{1,0:T(8,128)S(1)}, f32[128,1024]{1,0:T(8,128)S(1)}, f32[128,1024]{1,0:T(8,128)S(1)}, f32[128,1024]{1,0:T(8,128)S(1)}, /*index=5*/f32[6,8,128]{2,1,0:T(8,128)S(1)}) custom-call(f32[1,128,1024]{2,1,0:T(8,128)} %eta_ref.3, f32[2,1,128,1024]{3,2,1,0:T(8,128)} %momenta_ref.3, f32[1,128,1024]{2,1,0:T(8,128)} %depth_ref.3, ...), custom_call_target="tpu_custom_call" | custom-call | tf_op jit(solution)/shard_map/first/pallas_call | solution.py:628
  10.5 0.0 collective-permute-done.refs_1_
  10.5 0.6 %collective-permute-done.1.refs_2_ = f32[80,128]{1,0:T(8,128)S(1)} collective-permute-done((f32[80,128]{1,0:T(8,128)S(1)}, f32[80,128]{1,0:T(8,128)S(1)}, u32[]{:S(2)}, u32[]{:S(2)}) %collective-permute-start.1) | collective-permute-done | bytes 40992 | tf_op jit(solution)/shard_map/ppermute | solution.py:645
  11.1 2.7 %collective-permute-done.2.refs_3_ = f32[80,128]{1,0:T(8,128)S(1)} collective-permute-done((f32[80,128]{1,0:T(8,128)S(1)}, f32[80,128]{1,0:T(8,128)S(1)}, u32[]{:S(2)}, u32[]{:S(2)}) %collective-permute-start.2) | collective-permute-done | bytes 40992 | tf_op jit(solution)/shard_map/ppermute | solution.py:645
  13.8 0.0 copy-start
  13.8 0.1 collective-permute-start.3
  13.9 1.4 %collective-permute-done.3.refs_2_.other_ref = f32[4,80,128]{2,1,0:T(8,128)S(1)} collective-permute-done((f32[4,80,128]{2,1,0:T(8,128)S(1)}, f32[4,80,128]{2,1,0:T(8,128)S(1)}, u32[]{:S(2)}, u32[]{:S(2)}) %collective-permute-start.3) | collective-permute-done | bytes 163872 | tf_op jit(solution)/shard_map/ppermute | solution.py:656
  15.3 0.0 copy-done
  15.3 0.7 %strips.1.strips_ref = f32[16,8,128]{2,1,0:T(8,128)S(1)} custom-call(s32[1,4,4]{2,1,0:T(4,128)S(1)} %copy-done, f32[4,80,128]{2,1,0:T(8,128)S(1)} %gather.1.refs_1_.mine_ref, f32[4,80,128]{2,1,0:T(8,128)S(1)} %collective-permute-done.3.refs_2_.other_ref), custom_call_target="tpu_custom_call" | custom-call | tf_op jit(solution)/shard_map/strips/pallas_call | solution.py:661
  16.0 1.6 %collective-permute-start.4 = (f32[16,8,128]{2,1,0:T(8,128)S(1)}, f32[16,8,128]{2,1,0:T(8,128)S(1)}, u32[]{:S(2)}, u32[]{:S(2)}) collective-permute-start(f32[16,8,128]{2,1,0:T(8,128)S(1)} %strips.1.strips_ref), channel_id=1, source_target_pairs={{0,2},{2,0},{1,3},{3,1},{4,6},{6,4},{5,7},{7,5},{8,10},{10,8},{9,1... | collective-permute-start | bytes 196616 | tf_op jit(solution)/shard_map/ppermute | solution.py:670
  17.5 3.0 %second.1 = (f32[1,128,1024]{2,1,0:T(8,128)}, f32[2,1,128,1024]{3,2,1,0:T(8,128)}, f32[3,2,8,1024]{3,2,1,0:T(8,128)S(1)}) custom-call(s32[1,4,4]{2,1,0:T(4,128)S(1)} %copy-done, f32[4,80,128]{2,1,0:T(8,128)S(1)} %gather.1.refs_1_.mine_ref, f32[4,80,128]{2,1,0:T(8,128)S(1)} %collective-permute-done.3.refs_2_.other_ref, f32[16,8,128]{2,1,0:T(8,128)S(1)} %strips.1.strips_ref, ...), custom_call_target="tpu_custom_call" | custom-call | tf_op jit(solution)/shard_map/second/pallas_call | solution.py:672
  20.5 0.0 collective-permute-done.4.finer_ref
  20.6 2.1 %inflow.1 = (f32[1,128,1024]{2,1,0:T(8,128)}, f32[2,1,128,1024]{3,2,1,0:T(8,128)}) custom-call(s32[1,4,4]{2,1,0:T(4,128)S(1)} %copy-done, f32[4,80,128]{2,1,0:T(8,128)S(1)} %gather.1.refs_1_.mine_ref, f32[4,80,128]{2,1,0:T(8,128)S(1)} %collective-permute-done.3.refs_2_.other_ref, ...), custom_call_target="tpu_custom_call", output_to_operand_aliasing={{0}: (7, {}), {1}: (8, {})} | custom-call | tf_op jit(solution)/shard_map/inflow/pallas_call | solution.py:684
  (1 shorter events, 0.0 us)
Async XLA Ops:
  2.3 8.2 %collective-permute-start = (f32[80,128]{1,0:T(8,128)S(1)}, f32[80,128]{1,0:T(8,128)S(1)}, u32[]{:S(2)}, u32[]{:S(2)}) collective-permute-start(f32[80,128]{1,0:T(8,128)S(1)} %pack.1.refs_0_), channel_id=1, source_target_pairs={{0,4},{4,0},{8,12},{12,8},{1,5},{5,1},{9,13},{13,9},{2,6},{6,2},{1... | collective-permute-start | bytes 122888 | tf_op jit(solution)/shard_map/ppermute | solution.py:645
  5.4 5.7 %collective-permute-start.1 = (f32[80,128]{1,0:T(8,128)S(1)}, f32[80,128]{1,0:T(8,128)S(1)}, u32[]{:S(2)}, u32[]{:S(2)}) collective-permute-start(f32[80,128]{1,0:T(8,128)S(1)} %pack.1.refs_0_), channel_id=1, source_target_pairs={{0,8},{4,12},{8,0},{12,4},{1,9},{5,13},{9,1},{13,5},{2,10},{6,14},... | collective-permute-start | bytes 122888 | tf_op jit(solution)/shard_map/ppermute | solution.py:645
  8.0 5.8 %collective-permute-start.2 = (f32[80,128]{1,0:T(8,128)S(1)}, f32[80,128]{1,0:T(8,128)S(1)}, u32[]{:S(2)}, u32[]{:S(2)}) collective-permute-start(f32[80,128]{1,0:T(8,128)S(1)} %pack.1.refs_0_), channel_id=1, source_target_pairs={{0,12},{4,8},{8,4},{12,0},{1,13},{5,9},{9,5},{13,1},{2,14},{6,10},... | collective-permute-start | bytes 122888 | tf_op jit(solution)/shard_map/ppermute | solution.py:645
  13.8 1.5 %copy-start = (s32[1,4,4]{2,1,0:T(4,128)S(1)}, s32[1,4,4]{2,1,0:T(4,128)}, u32[]{:S(2)}) copy-start(s32[1,4,4]{2,1,0:T(4,128)} %links_ref.3) | copy-start | bytes 196
  13.8 1.5 %collective-permute-start.3 = (f32[4,80,128]{2,1,0:T(8,128)S(1)}, f32[4,80,128]{2,1,0:T(8,128)S(1)}, u32[]{:S(2)}, u32[]{:S(2)}) collective-permute-start(f32[4,80,128]{2,1,0:T(8,128)S(1)} %gather.1.refs_1_.mine_ref), channel_id=1, source_target_pairs={{0,1},{1,0},{2,3},{3,2},{4,5},{5,4},{6,7},{7,6},{8,9},{9,8},{10,11... | collective-permute-start | bytes 491528 | tf_op jit(solution)/shard_map/ppermute | solution.py:656
  16.0 4.6 %collective-permute-start.4 = (f32[16,8,128]{2,1,0:T(8,128)S(1)}, f32[16,8,128]{2,1,0:T(8,128)S(1)}, u32[]{:S(2)}, u32[]{:S(2)}) collective-permute-start(f32[16,8,128]{2,1,0:T(8,128)S(1)} %strips.1.strips_ref), channel_id=1, source_target_pairs={{0,2},{2,0},{1,3},{3,1},{4,6},{6,4},{5,7},{7,5},{8,10},{10,8},{9,1... | collective-permute-start | bytes 196616 | tf_op jit(solution)/shard_map/ppermute | solution.py:670

commit v11 on v10

--- a/solution.py
+++ b/solution.py
@@ -17,6 +17,7 @@
  LAST_ROW, LAST_COL, NEXT_DEPTH, LAST_DEPTH) = range(12)
 ROWS, COLUMNS = 8, 16
 LINES = ROWS * TILE + COLUMNS
+TRIMMED, SPARE = LINES - 2 * TILE, 4
 
 
 def iota(shape, axis):
@@ -40,18 +41,19 @@
     return copies
 
 
-def pack_kernel(eta_ref, momenta_ref, depth_ref, wet_ref, gain_ref, index_ref, out_ref,
+def pack_kernel(eta_ref, momenta_ref, depth_ref, wet_ref, gain_ref, index_ref, out_ref, trimmed_ref,
                 ends, end_wet, sides, side_wet, gains, indices, sems):
     rows, cols = eta_ref.shape[1:]
-    fields = eta_ref.at[0], momenta_ref.at[0, 0], momenta_ref.at[1, 0], depth_ref.at[0]
     tall, wide = [], []
     for end in range(2):
         here = pl.ds(end * (rows - TILE), TILE)
-        tall += [(field.at[here, :], ends.at[end, place]) for place, field in enumerate(fields)]
-        tall.append((wet_ref.at[0, here, :], end_wet.at[end]))
+        tall += [
+            (eta_ref.at[0, here, :], ends.at[end, 0]), (momenta_ref.at[:, 0, here, :], ends.at[end, pl.ds(1, 2)]),
+            (depth_ref.at[0, here, :], ends.at[end, 3]), (wet_ref.at[0, here, :], end_wet.at[end])]
         here = pl.ds(end * (cols - LANES), LANES)
-        wide += [(field.at[:, here], sides.at[end, place]) for place, field in enumerate(fields)]
-        wide.append((wet_ref.at[0, :, here], side_wet.at[end]))
+        wide += [
+            (eta_ref.at[0, :, here], sides.at[end, 0]), (momenta_ref.at[:, 0, :, here], sides.at[end, pl.ds(1, 2)]),
+            (depth_ref.at[0, :, here], sides.at[end, 3]), (wet_ref.at[0, :, here], side_wet.at[end])]
     tall += [(gain_ref, gains), (index_ref, indices)]
     copies = copied(tall + wide, sems)
     for copy in copies[:len(tall)]:
@@ -106,6 +108,22 @@
         moved = value if place == at else rolled(value, place - at, 1)
         columns = jnp.where(lane == place, moved, columns)
     out_ref[ROWS * TILE:] = columns.T[:COLUMNS]
+
+    def tile(row):
+        return out_ref[row * TILE:(row + 1) * TILE]
+
+    tables = sends_tables()
+    flow, depth, gain, index = tile(EDGE_FLOW), tile(EDGE_DEPTH), tile(GAIN), tile(INDEX)
+    trimmed_ref[:GAIN * TILE] = out_ref[:GAIN * TILE]
+    trimmed_ref[GAIN * TILE:INDEX * TILE] = jnp.where(tables, gain, flow)
+    trimmed_ref[INDEX * TILE:(INDEX + 1) * TILE] = jnp.where(tables, index, depth)
+    trimmed_ref[(INDEX + 1) * TILE:(INDEX + 2) * TILE] = tile(EDGE_SUM)
+    trimmed_ref[(INDEX + 2) * TILE:] = out_ref[ROWS * TILE:]
+    spare = TRIMMED - SPARE
+    for place, (other, own) in enumerate(((flow, gain), (depth, index))):
+        chosen = jnp.where(tables, other, own)
+        trimmed_ref[spare + 2 * place:spare + 2 * place + 1] = chosen[:1]
+        trimmed_ref[spare + 2 * place + 1:spare + 2 * place + 2] = chosen[TILE - 1:]
 
 
 def first_kernel(eta_ref, momenta_ref, depth_ref, wet_ref, eta_after, row_after, col_after, wet_after, depth_after,
@@ -154,11 +172,39 @@
     turned[5] = row_after[:, right:].T[LANES - TILE:]
 
 
+def sends_tables():
+    return (lax.axis_index("level") == 0) & (lax.axis_index("sub") == 0)
+
+
 def gather_kernel(*refs):
-    packets, out_ref = refs[:-2], refs[-1]
+    first, packets, turns, out_ref = refs[0], refs[1:-2], len(refs) - 2, refs[-1]
     own = lax.axis_index("patch")
-    for turn, packet in enumerate(packets):
-        out_ref[own ^ turn] = packet[...]
+    out_ref[own] = first[...]
+    tables = sends_tables()
+    line = iota((TILE, LANES), 0)
+
+    def ends_of(packet, at):
+        value = jnp.where(line == 0, packet[at:at + 1], 0.0)
+        return jnp.where(line == TILE - 1, packet[at + 1:at + 2], value)
+
+    for place, packet in enumerate(packets):
+        patch = own ^ (turns - 1 - place)
+        if packet.shape[0] == LINES:
+            out_ref[patch] = packet[...]
+            continue
+
+        def put(row, value):
+            out_ref[patch, row * TILE:(row + 1) * TILE] = value
+
+        out_ref[patch, :GAIN * TILE] = packet[:GAIN * TILE]
+        whole = packet[GAIN * TILE:INDEX * TILE], packet[INDEX * TILE:(INDEX + 1) * TILE]
+        ends = ends_of(packet, TRIMMED - SPARE), ends_of(packet, TRIMMED - SPARE + 2)
+        put(GAIN, jnp.where(tables, whole[0], ends[0]))
+        put(INDEX, jnp.where(tables, whole[1], ends[1]))
+        put(EDGE_FLOW, jnp.where(tables, ends[0], whole[0]))
+        put(EDGE_DEPTH, jnp.where(tables, ends[1], whole[1]))
+        put(EDGE_SUM, packet[(INDEX + 1) * TILE:(INDEX + 2) * TILE])
+        out_ref[patch, ROWS * TILE:] = packet[(INDEX + 2) * TILE:]
 
 
 class Segment:
@@ -464,18 +510,6 @@
     for place in range(3):
         more_ref[place] = jnp.concatenate([left[place], middle, last[place]], axis=0).T
 
-    top_sides, low_sides = as_sublanes(columns)
-    nothing = jnp.zeros((TILE, cols), jnp.float32)
-    end = slice(rows - TILE, rows)
-    top = two_steps(
-        nothing, wet_after[:TILE], depth_after[:TILE], top_sides, (eta_after[:TILE], row_after[:TILE]),
-        north=north_of(links, packets, own, packets.row(own, STRIP)))
-    below, there = links.south(own)
-    low = two_steps(
-        nothing, wet_after[end], depth_after[end], low_sides, (eta_after[end], row_after[end]),
-        south=(packets.row(below, STRIP) * there,
-               row_of(strips_ref, 2 * links.patches + below.place(links.patches)) * there))
-
     line, lane = iota((TILE, cols), 0), iota((TILE, cols), 1)
     inside = iota((TILE, LANES), 1)
     outs = eta_out.at[0], momenta_out.at[0, 0], momenta_out.at[1, 0]
@@ -496,10 +530,7 @@
             more = more_ref[place, chunk]
             sides = [jnp.where(inside < TILE, more, 0.0), jnp.where(inside >= LANES - TILE, more, 0.0)]
             if first in (0, rows - TILE):
-                near, found = (line < TILE // 2, top) if first == 0 else (line >= TILE // 2, low)
-                gap = jnp.zeros((TILE, cols - 2 * LANES), jnp.float32)
-                wide = jnp.concatenate([sides[0], gap, sides[1]], axis=1)
-                ends_out[place, int(first > 0)] = field + jnp.where(near, found[place], wide)
+                ends_out[place, int(first > 0)] = field
             else:
                 new_ref[place, first - TILE:first] = jnp.concatenate(
                     [field[:, :LANES] + sides[0], field[:, LANES:cols - LANES], field[:, cols - LANES:] + sides[1]],
@@ -509,6 +540,25 @@
             here, there = pl.ds(part * size, size), pl.ds(TILE + part * size, size)
             copies += copied([(new_ref.at[place, here], out.at[there, :]) for place, out in enumerate(outs)],
                              sems.at[part])
+    top_sides, low_sides = as_sublanes(columns)
+    nothing = jnp.zeros((TILE, cols), jnp.float32)
+    end = slice(rows - TILE, rows)
+    top = two_steps(
+        nothing, wet_after[:TILE], depth_after[:TILE], top_sides, (eta_after[:TILE], row_after[:TILE]),
+        north=north_of(links, packets, own, packets.row(own, STRIP)))
+    below, there = links.south(own)
+    low = two_steps(
+        nothing, wet_after[end], depth_after[end], low_sides, (eta_after[end], row_after[end]),
+        south=(packets.row(below, STRIP) * there,
+               row_of(strips_ref, 2 * links.patches + below.place(links.patches)) * there))
+    gap = jnp.zeros((TILE, cols - 2 * LANES), jnp.float32)
+    for edge, (chunk, near, found) in enumerate(
+            ((slice(0, TILE), line < TILE // 2, top), (end, line >= TILE // 2, low))):
+        for place in range(3):
+            more = more_ref[place, chunk]
+            wide = jnp.concatenate(
+                [jnp.where(inside < TILE, more, 0.0), gap, jnp.where(inside >= LANES - TILE, more, 0.0)], axis=1)
+            ends_out[place, edge] += jnp.where(near, found[place], wide)
     for copy in copies:
         copy.wait()
 
@@ -577,17 +627,21 @@
     top = two_steps(
         jnp.where(line == 0, strip, 0.0), wet_after[:TILE], depth_after[:TILE], top_sides, None,
         north=north_of(links, packets, own, strip, inflow), second=row_of(rows_ref, 1))
+    copies = []
+    outs = eta_out.at[0], momenta_out.at[0, 0], momenta_out.at[1, 0]
+
+    def write(end, near, found):
+        for place in range(3):
+            new_ref[place, end] = ends_ref[place, end] + jnp.where(near, found[place], 0.0)
+        here = pl.ds(end * (rows - TILE), TILE)
+        copies.extend(copied(
+            [(new_ref.at[place, end], out.at[here, :]) for place, out in enumerate(outs)], sems.at[end]))
+
+    write(0, line < TILE // 2, top)
     low = two_steps(
         jnp.zeros((TILE, cols), jnp.float32), wet_after[rows - TILE:], depth_after[rows - TILE:],
         low_sides, None, south=(row_of(rows_ref, 2), row_of(rows_ref, 3)))
-    copies = []
-    outs = eta_out.at[0], momenta_out.at[0, 0], momenta_out.at[1, 0]
-    for end, (near, found) in enumerate(((line < TILE // 2, top), (line >= TILE // 2, low))):
-        for place in range(3):
-            new_ref[place, end] = ends_ref[place, end] + jnp.where(near, found[place], 0.0)
-        copies += copied([
-            (new_ref.at[place, end], out.at[pl.ds(end * (rows - TILE), TILE), :]) for place, out in enumerate(outs)
-        ], sems.at[end])
+    write(1, line >= TILE // 2, low)
     for copy in copies:
         copy.wait()
 
@@ -610,16 +664,16 @@
 
     fields = [pltpu.with_memory_space_constraint(field, pltpu.HBM)
               for field in (adjoint_height, adjoint_momenta, depth, wet_mask, nest_gain, nest_index)]
-    packed = pl.pallas_call(
+    packed, trimmed = pl.pallas_call(
         pack_kernel,
-        out_shape=array(LINES, LANES),
+        out_shape=[array(LINES, LANES), array(TRIMMED, LANES)],
         in_specs=[hbm] * 6,
-        out_specs=vmem,
+        out_specs=[vmem, vmem],
         scratch_shapes=[
             scratch(2, 4, TILE, cols), pltpu.VMEM((2, TILE, cols), jnp.int32),
             scratch(2, 4, rows, LANES), pltpu.VMEM((2, rows, LANES), jnp.int32),
             scratch(levels, cols), pltpu.VMEM((levels, cols), jnp.int32),
-            pltpu.SemaphoreType.DMA((22,)),
+            pltpu.SemaphoreType.DMA((18,)),
         ],
         compiler_params=params,
         name="pack",
@@ -642,8 +696,9 @@
     )(*fields[:4])
 
     sent = [packed] + [
-        lax.ppermute(packed, "patch", [(source, source ^ turn) for source in range(patches)])
-        for turn in range(1, patches)
+        lax.ppermute(trimmed if levels == 2 else packed, "patch",
+                     [(source, source ^ turn) for source in range(patches)])
+        for turn in range(patches - 1, 0, -1)
     ]
     mine = pl.pallas_call(
         gather_kernel,

time: 22.9 us -> 21.3 us (0.930)
  waiting for transfers between devices: 4.7 us -> 3.08 us
    ppermute x3, waiting for transfers between devices: 3.32 us -> 1.69 us  [body(): lax.ppermute(trimmed if levels == 2 else packed, 'patch', [(source, sourc...]
  transfers between devices with their start and end apart: 5 -> 5, of which waited for: 3 -> 2; matrix products, arithmetic and copies ran while one was open for 0% -> 0% of each run, Pallas kernels for 24% -> 26%
where the time goes in v11:
time: 21.3 us; the launch traced here: 21.1 us
  Pallas kernels  9.95 us (47%)
  starting transfers between devices  7.38 us (35%)
  waiting for transfers between devices  3.08 us (14%)
  between operations  0.69 us (3%)
    ppermute x3, starting transfers between devices, body(): lax.ppermute(trimmed if levels == 2 else packed, 'patch', [(source, sourc...  5.76 us
    pallas_call x1, Pallas kernels, body(): pl.pallas_call(second_kernel, out_shape=[array(*adjoint_height.shape), ar...  3.05 us
    pallas_call x1, Pallas kernels, body(): pl.pallas_call(first_kernel, out_shape=[array(rows + TILE, cols), array(r...  2.46 us
    pallas_call x1, Pallas kernels, body(): pl.pallas_call(inflow_kernel, out_shape=[array(*adjoint_height.shape), ar...  2.09 us
    ppermute x3, waiting for transfers between devices, body(): lax.ppermute(trimmed if levels == 2 else packed, 'patch', [(source, sourc...  1.69 us
    pallas_call x1, Pallas kernels, body(): pl.pallas_call(pack_kernel, out_shape=[array(LINES, LANES), array(TRIMMED...  1.65 us
    ppermute x1, starting transfers between devices, body(): lax.ppermute(strips[-1], 'level', [(source, (source - 1) % levels) for so...  1.56 us
    ppermute x1, waiting for transfers between devices, body(): other = lax.ppermute(mine, 'sub', [(0, 1), (1, 0)])  1.38 us
  transfers between devices with their start and end apart: 5, of which 2 were waited for; matrix products, arithmetic and copies ran while one was open for 0% of the time, Pallas kernels for 26%

profile of v11, /device:TPU:0, one launch (start us, length us, event | category | flops | bytes accessed | tf_op | source)
XLA Modules:
  0.0 21.1 jit_solution(18091427185136967557)
XLA Ops:
  0.6 1.6 %pack.1 = (f32[80,128]{1,0:T(8,128)S(1)}, f32[64,128]{1,0:T(8,128)S(1)}) custom-call(f32[1,128,1024]{2,1,0:T(8,128)} %eta_ref.3, f32[2,1,128,1024]{3,2,1,0:T(8,128)} %momenta_ref.3, f32[1,128,1024]{2,1,0:T(8,128)} %depth_ref.3, s32[1,128,1024]{2,1,0:T(8,128)} %wet_ref.3, f32[2,1024]{1,0:T(2,128)} %gain_ref.1, s32[2,1024]{1,0:T(2,128)} %index_ref.1), custom_call_target="tpu_custom_call" | custom-call | tf_op jit(solution)/shard_map/pack/pallas_call | solution.py:667
  2.3 5.1 %collective-permute-start = (f32[64,128]{1,0:T(8,128)S(1)}, f32[64,128]{1,0:T(8,128)S(1)}, u32[]{:S(2)}, u32[]{:S(2)}) collective-permute-start(f32[64,128]{1,0:T(8,128)S(1)} %get-tuple-element.14), channel_id=1, source_target_pairs={{0,12},{4,8},{8,4},{12,0},{1,13},{5,9},{9,5},{13,1},{2,14},{6,10},... | collective-permute-start | bytes 98312 | tf_op jit(solution)/shard_map/ppermute | solution.py:699
  7.4 0.0 collective-permute-start.1
  7.4 0.6 %collective-permute-start.2 = (f32[64,128]{1,0:T(8,128)S(1)}, f32[64,128]{1,0:T(8,128)S(1)}, u32[]{:S(2)}, u32[]{:S(2)}) collective-permute-start(f32[64,128]{1,0:T(8,128)S(1)} %get-tuple-element.14), channel_id=1, source_target_pairs={{0,4},{4,0},{8,12},{12,8},{1,5},{5,1},{9,13},{13,9},{2,6},{6,2},{1... | collective-permute-start | bytes 98312 | tf_op jit(solution)/shard_map/ppermute | solution.py:699
  8.0 2.5 %first.1 = (f32[136,1024]{1,0:T(8,128)S(1)}, f32[128,1024]{1,0:T(8,128)S(1)}, f32[128,1024]{1,0:T(8,128)S(1)}, f32[128,1024]{1,0:T(8,128)S(1)}, f32[128,1024]{1,0:T(8,128)S(1)}, /*index=5*/f32[6,8,128]{2,1,0:T(8,128)S(1)}) custom-call(f32[1,128,1024]{2,1,0:T(8,128)} %eta_ref.3, f32[2,1,128,1024]{3,2,1,0:T(8,128)} %momenta_ref.3, f32[1,128,1024]{2,1,0:T(8,128)} %depth_ref.3, ...), custom_call_target="tpu_custom_call" | custom-call | tf_op jit(solution)/shard_map/first/pallas_call | solution.py:682
  10.5 0.0 collective-permute-done.refs_1_
  10.5 1.7 %collective-permute-done.1.refs_2_ = f32[64,128]{1,0:T(8,128)S(1)} collective-permute-done((f32[64,128]{1,0:T(8,128)S(1)}, f32[64,128]{1,0:T(8,128)S(1)}, u32[]{:S(2)}, u32[]{:S(2)}) %collective-permute-start.1) | collective-permute-done | bytes 32800 | tf_op jit(solution)/shard_map/ppermute | solution.py:699
  12.2 0.0 collective-permute-done.2.refs_3_
  12.2 0.0 copy-start
  12.2 0.1 collective-permute-start.3
  12.3 1.4 %collective-permute-done.3.refs_2_.other_ref = f32[4,80,128]{2,1,0:T(8,128)S(1)} collective-permute-done((f32[4,80,128]{2,1,0:T(8,128)S(1)}, f32[4,80,128]{2,1,0:T(8,128)S(1)}, u32[]{:S(2)}, u32[]{:S(2)}) %collective-permute-start.3) | collective-permute-done | bytes 163872 | tf_op jit(solution)/shard_map/ppermute | solution.py:711
  13.7 0.0 copy-done
  13.7 0.7 %strips.1.strips_ref = f32[16,8,128]{2,1,0:T(8,128)S(1)} custom-call(s32[1,4,4]{2,1,0:T(4,128)S(1)} %copy-done, f32[4,80,128]{2,1,0:T(8,128)S(1)} %gather.1.refs_1_.mine_ref, f32[4,80,128]{2,1,0:T(8,128)S(1)} %collective-permute-done.3.refs_2_.other_ref), custom_call_target="tpu_custom_call" | custom-call | tf_op jit(solution)/shard_map/strips/pallas_call | solution.py:716
  14.4 1.6 %collective-permute-start.4 = (f32[16,8,128]{2,1,0:T(8,128)S(1)}, f32[16,8,128]{2,1,0:T(8,128)S(1)}, u32[]{:S(2)}, u32[]{:S(2)}) collective-permute-start(f32[16,8,128]{2,1,0:T(8,128)S(1)} %strips.1.strips_ref), channel_id=1, source_target_pairs={{0,2},{2,0},{1,3},{3,1},{4,6},{6,4},{5,7},{7,5},{8,10},{10,8},{9,1... | collective-permute-start | bytes 196616 | tf_op jit(solution)/shard_map/ppermute | solution.py:725
  15.9 3.0 %second.1 = (f32[1,128,1024]{2,1,0:T(8,128)}, f32[2,1,128,1024]{3,2,1,0:T(8,128)}, f32[3,2,8,1024]{3,2,1,0:T(8,128)S(1)}) custom-call(s32[1,4,4]{2,1,0:T(4,128)S(1)} %copy-done, f32[4,80,128]{2,1,0:T(8,128)S(1)} %gather.1.refs_1_.mine_ref, f32[4,80,128]{2,1,0:T(8,128)S(1)} %collective-permute-done.3.refs_2_.other_ref, f32[16,8,128]{2,1,0:T(8,128)S(1)} %strips.1.strips_ref, ...), custom_call_target="tpu_custom_call" | custom-call | tf_op jit(solution)/shard_map/second/pallas_call | solution.py:727
  19.0 0.0 collective-permute-done.4.finer_ref
  19.0 2.1 %inflow.1 = (f32[1,128,1024]{2,1,0:T(8,128)}, f32[2,1,128,1024]{3,2,1,0:T(8,128)}) custom-call(s32[1,4,4]{2,1,0:T(4,128)S(1)} %copy-done, f32[4,80,128]{2,1,0:T(8,128)S(1)} %gather.1.refs_1_.mine_ref, f32[4,80,128]{2,1,0:T(8,128)S(1)} %collective-permute-done.3.refs_2_.other_ref, ...), custom_call_target="tpu_custom_call", output_to_operand_aliasing={{0}: (7, {}), {1}: (8, {})} | custom-call | tf_op jit(solution)/shard_map/inflow/pallas_call | solution.py:739
  (1 shorter events, 0.0 us)
Async XLA Ops:
  2.3 8.2 %collective-permute-start = (f32[64,128]{1,0:T(8,128)S(1)}, f32[64,128]{1,0:T(8,128)S(1)}, u32[]{:S(2)}, u32[]{:S(2)}) collective-permute-start(f32[64,128]{1,0:T(8,128)S(1)} %get-tuple-element.14), channel_id=1, source_target_pairs={{0,12},{4,8},{8,4},{12,0},{1,13},{5,9},{9,5},{13,1},{2,14},{6,10},... | collective-permute-start | bytes 98312 | tf_op jit(solution)/shard_map/ppermute | solution.py:699
  7.4 4.8 %collective-permute-start.1 = (f32[64,128]{1,0:T(8,128)S(1)}, f32[64,128]{1,0:T(8,128)S(1)}, u32[]{:S(2)}, u32[]{:S(2)}) collective-permute-start(f32[64,128]{1,0:T(8,128)S(1)} %get-tuple-element.14), channel_id=1, source_target_pairs={{0,8},{4,12},{8,0},{12,4},{1,9},{5,13},{9,1},{13,5},{2,10},{6,14},... | collective-permute-start | bytes 98312 | tf_op jit(solution)/shard_map/ppermute | solution.py:699
  7.4 4.8 %collective-permute-start.2 = (f32[64,128]{1,0:T(8,128)S(1)}, f32[64,128]{1,0:T(8,128)S(1)}, u32[]{:S(2)}, u32[]{:S(2)}) collective-permute-start(f32[64,128]{1,0:T(8,128)S(1)} %get-tuple-element.14), channel_id=1, source_target_pairs={{0,4},{4,0},{8,12},{12,8},{1,5},{5,1},{9,13},{13,9},{2,6},{6,2},{1... | collective-permute-start | bytes 98312 | tf_op jit(solution)/shard_map/ppermute | solution.py:699
  12.2 1.5 %copy-start = (s32[1,4,4]{2,1,0:T(4,128)S(1)}, s32[1,4,4]{2,1,0:T(4,128)}, u32[]{:S(2)}) copy-start(s32[1,4,4]{2,1,0:T(4,128)} %links_ref.3) | copy-start | bytes 196
  12.2 1.5 %collective-permute-start.3 = (f32[4,80,128]{2,1,0:T(8,128)S(1)}, f32[4,80,128]{2,1,0:T(8,128)S(1)}, u32[]{:S(2)}, u32[]{:S(2)}) collective-permute-start(f32[4,80,128]{2,1,0:T(8,128)S(1)} %gather.1.refs_1_.mine_ref), channel_id=1, source_target_pairs={{0,1},{1,0},{2,3},{3,2},{4,5},{5,4},{6,7},{7,6},{8,9},{9,8},{10,11... | collective-permute-start | bytes 491528 | tf_op jit(solution)/shard_map/ppermute | solution.py:711
  14.4 4.6 %collective-permute-start.4 = (f32[16,8,128]{2,1,0:T(8,128)S(1)}, f32[16,8,128]{2,1,0:T(8,128)S(1)}, u32[]{:S(2)}, u32[]{:S(2)}) collective-permute-start(f32[16,8,128]{2,1,0:T(8,128)S(1)} %strips.1.strips_ref), channel_id=1, source_target_pairs={{0,2},{2,0},{1,3},{3,1},{4,6},{6,4},{5,7},{7,5},{8,10},{10,8},{9,1... | collective-permute-start | bytes 196616 | tf_op jit(solution)/shard_map/ppermute | solution.py:725

commit v12 on v11

--- a/solution.py
+++ b/solution.py
@@ -126,50 +126,77 @@
         trimmed_ref[spare + 2 * place + 1:spare + 2 * place + 2] = chosen[TILE - 1:]
 
 
-def first_kernel(eta_ref, momenta_ref, depth_ref, wet_ref, eta_after, row_after, col_after, wet_after, depth_after,
-                 turned, eta_pad, momenta_in, depth_in, wet_in, sems):
-    rows, cols = row_after.shape
+def bulk_kernel(eta_ref, momenta_ref, depth_ref, wet_ref, eta_after, momenta_after, wet_after, depth_after,
+                eta_ends, row_ends, turned, eta_pad, col_pad, momenta_in, depth_in, wet_in, eta_left, row_right, sems):
+    rows, cols = eta_ref.shape[1:]
     parts = sems.shape[0]
     size = rows // parts
     loads = []
     for part in range(parts):
         here = pl.ds(part * size, size)
         loads.append(copied([
-            (eta_ref.at[0, here, :], eta_pad.at[here, :]),
+            (eta_ref.at[0, here, :], eta_pad.at[pl.ds(TILE + part * size, size), :]),
             (momenta_ref.at[:, 0, here, :], momenta_in.at[:, here, :]),
             (depth_ref.at[0, here, :], depth_in.at[here, :]),
             (wet_ref.at[0, here, :], wet_in.at[here, :]),
         ], sems.at[part]))
-    lane, line = iota((TILE, cols), 1), iota((TILE, cols), 0)
-    eta_pad[rows:] = jnp.zeros((TILE, cols), jnp.float32)
-    eta_after[rows:] = jnp.zeros((TILE, cols), jnp.float32)
-    above = jnp.zeros((1, cols), jnp.float32)
+    lane = iota((TILE, cols), 1)
+    eta_pad[TILE + rows:] = jnp.zeros((TILE, cols), jnp.float32)
+    col_pad[:TILE] = jnp.zeros((TILE, cols), jnp.float32)
+
+    def step(number, low):
+        chunk, padded = slice(low, low + TILE), slice(TILE + low, 2 * TILE + low)
+        eta = eta_pad[padded]
+        if number == 0:
+            mask = wet_in[chunk].astype(jnp.float32)
+            depth = courant * mask * depth_in[chunk]
+            wet_after[chunk] = mask
+            depth_after[chunk] = depth
+            row, col = momenta_in[0, chunk], momenta_in[1, chunk]
+        else:
+            mask, depth = wet_after[chunk], depth_after[chunk]
+            row, col = momenta_after[0, chunk], col_pad[padded]
+        east = jnp.where(lane == cols - 1, 0.0, rolled(eta, -1, 1))
+        south = eta_pad[TILE + low + 1:2 * TILE + low + 1]
+        row = mask * (row - courant * (east - eta))
+        col = mask * (col - courant * (south - eta))
+        momenta_after[0, chunk] = row
+        col_pad[padded] = col
+        if number:
+            momenta_after[1, chunk] = col
+        west = jnp.where(lane == 0, 0.0, rolled(row, 1, 1))
+        north = col_pad[TILE + low - 1:2 * TILE + low - 1]
+        eta = mask * eta - depth * (row - west + (col - north))
+        if number:
+            eta_after[chunk] = eta
+            return
+        eta_pad[padded] = eta
+        eta_left[chunk] = eta[:, :LANES]
+        row_right[chunk] = row[:, cols - LANES:]
+        if low in (0, rows - TILE):
+            end = int(low > 0)
+            eta_ends[end] = eta
+            row_ends[end] = row
+
     for copy in loads[0]:
         copy.wait()
-    for part in range(parts):
+    for part in range(parts + 1):
         if part + 1 < parts:
             for copy in loads[part + 1]:
                 copy.wait()
-        for low in range(part * size, (part + 1) * size, TILE):
-            chunk = slice(low, low + TILE)
-            mask = wet_in[chunk].astype(jnp.float32)
-            depth = courant * mask * depth_in[chunk]
-            below = eta_pad[low + 1:low + TILE + 1]
-            eta, row, col = advanced(
-                eta_pad[chunk], momenta_in[0, chunk], momenta_in[1, chunk], mask, depth,
-                lambda eta: jnp.where(lane == cols - 1, 0.0, rolled(eta, -1, 1)), lambda eta: below,
-                lambda row: jnp.where(lane == 0, 0.0, rolled(row, 1, 1)),
-                lambda col: jnp.where(line == 0, above, rolled(col, 1, 0)))
-            above = col[TILE - 1:]
-            eta_after[chunk], row_after[chunk], col_after[chunk] = eta, row, col
-            wet_after[chunk], depth_after[chunk] = mask, depth
+        if part < parts:
+            for low in range(part * size, (part + 1) * size, TILE):
+                step(0, low)
+        if part:
+            for low in range((part - 1) * size, part * size, TILE):
+                step(1, low)
     right = cols - LANES
     turned[0] = wet_after[:, :LANES].T[:TILE]
     turned[1] = depth_after[:, :LANES].T[:TILE]
     turned[2] = wet_after[:, right:].T[LANES - TILE:]
     turned[3] = depth_after[:, right:].T[LANES - TILE:]
-    turned[4] = eta_after[:rows, :LANES].T[:TILE]
-    turned[5] = row_after[:, right:].T[LANES - TILE:]
+    turned[4] = eta_left[...].T[:TILE]
+    turned[5] = row_right[...].T[LANES - TILE:]
 
 
 def sends_tables():
@@ -470,9 +497,14 @@
             for low in (0, rows - TILE)]
 
 
-def second_kernel(links_ref, mine_ref, other_ref, strips_ref, eta_after, row_after, col_after, wet_after,
-                  depth_after, turned, eta_out, momenta_out, ends_out, new_ref, more_ref, sems):
-    rows, cols = row_after.shape
+def halo_kernel(links_ref, mine_ref, other_ref, strips_ref, eta_after, momenta_after, wet_after, depth_after,
+                eta_ends, row_ends, turned, eta_out, momenta_out, ends_out, sides_new, more_ref, sems):
+    rows, cols = eta_after.shape
+    fields = eta_after, momenta_after.at[0], momenta_after.at[1]
+    outs = eta_out.at[0], momenta_out.at[0, 0], momenta_out.at[1, 0]
+    inner, between = pl.ds(TILE, rows - 2 * TILE), pl.ds(LANES, cols - 2 * LANES)
+    copies = copied(
+        [(field.at[inner, between], out.at[inner, between]) for field, out in zip(fields, outs)], sems.at[0])
     links = Links(links_ref, mine_ref.shape[0])
     own = links.own()
     packets = Packets((mine_ref, other_ref))
@@ -507,50 +539,31 @@
     left = column_steps(turned[0], turned[1], lambda number, state: 0.0, west_of)
     last = column_steps(turned[2], turned[3], east_of, lambda number, state: 0.0)
     middle = jnp.zeros((LANES - 2 * TILE, rows), jnp.float32)
-    for place in range(3):
+    body_rows = slice(TILE, rows - TILE)
+    inside = iota((rows - 2 * TILE, LANES), 1)
+    wides = slice(0, LANES), slice(cols - LANES, cols)
+    for place, field in enumerate(fields):
         more_ref[place] = jnp.concatenate([left[place], middle, last[place]], axis=0).T
-
-    line, lane = iota((TILE, cols), 0), iota((TILE, cols), 1)
-    inside = iota((TILE, LANES), 1)
-    outs = eta_out.at[0], momenta_out.at[0, 0], momenta_out.at[1, 0]
-    above = jnp.zeros((1, cols), jnp.float32)
-    parts = sems.shape[0]
-    size = (rows - 2 * TILE) // parts
-    copies = []
-    for first in range(0, rows, TILE):
-        chunk = slice(first, first + TILE)
-        south = eta_after[first + 1:first + TILE + 1]
-        fields = advanced(
-            eta_after[chunk], row_after[chunk], col_after[chunk], wet_after[chunk], depth_after[chunk],
-            lambda eta: jnp.where(lane == cols - 1, 0.0, rolled(eta, -1, 1)), lambda eta: south,
-            lambda row: jnp.where(lane == 0, 0.0, rolled(row, 1, 1)),
-            lambda col: jnp.where(line == 0, above, rolled(col, 1, 0)))
-        above = fields[2][TILE - 1:]
-        for place, field in enumerate(fields):
-            more = more_ref[place, chunk]
-            sides = [jnp.where(inside < TILE, more, 0.0), jnp.where(inside >= LANES - TILE, more, 0.0)]
-            if first in (0, rows - TILE):
-                ends_out[place, int(first > 0)] = field
-            else:
-                new_ref[place, first - TILE:first] = jnp.concatenate(
-                    [field[:, :LANES] + sides[0], field[:, LANES:cols - LANES], field[:, cols - LANES:] + sides[1]],
-                    axis=1)
-        if first and first % size == 0 and first < rows - TILE:
-            part = first // size - 1
-            here, there = pl.ds(part * size, size), pl.ds(TILE + part * size, size)
-            copies += copied([(new_ref.at[place, here], out.at[there, :]) for place, out in enumerate(outs)],
-                             sems.at[part])
+        more = more_ref[place, body_rows]
+        sides_new[0, place] = field[body_rows, wides[0]] + jnp.where(inside < TILE, more, 0.0)
+        sides_new[1, place] = field[body_rows, wides[1]] + jnp.where(inside >= LANES - TILE, more, 0.0)
+    for side, wide in enumerate(wides):
+        copies += copied(
+            [(sides_new.at[side, place], out.at[inner, pl.ds(wide.start, LANES)]) for place, out in enumerate(outs)],
+            sems.at[1 + side])
+
     top_sides, low_sides = as_sublanes(columns)
     nothing = jnp.zeros((TILE, cols), jnp.float32)
     end = slice(rows - TILE, rows)
     top = two_steps(
-        nothing, wet_after[:TILE], depth_after[:TILE], top_sides, (eta_after[:TILE], row_after[:TILE]),
+        nothing, wet_after[:TILE], depth_after[:TILE], top_sides, (eta_ends[0], row_ends[0]),
         north=north_of(links, packets, own, packets.row(own, STRIP)))
     below, there = links.south(own)
     low = two_steps(
-        nothing, wet_after[end], depth_after[end], low_sides, (eta_after[end], row_after[end]),
+        nothing, wet_after[end], depth_after[end], low_sides, (eta_ends[1], row_ends[1]),
         south=(packets.row(below, STRIP) * there,
                row_of(strips_ref, 2 * links.patches + below.place(links.patches)) * there))
+    line, inside = iota((TILE, cols), 0), iota((TILE, LANES), 1)
     gap = jnp.zeros((TILE, cols - 2 * LANES), jnp.float32)
     for edge, (chunk, near, found) in enumerate(
             ((slice(0, TILE), line < TILE // 2, top), (end, line >= TILE // 2, low))):
@@ -558,7 +571,7 @@
             more = more_ref[place, chunk]
             wide = jnp.concatenate(
                 [jnp.where(inside < TILE, more, 0.0), gap, jnp.where(inside >= LANES - TILE, more, 0.0)], axis=1)
-            ends_out[place, edge] += jnp.where(near, found[place], wide)
+            ends_out[place, edge] = fields[place][chunk] + jnp.where(near, found[place], wide)
     for copy in copies:
         copy.wait()
 
@@ -680,19 +693,20 @@
     )(*fields)
     parts = 4
     after = pl.pallas_call(
-        first_kernel,
+        bulk_kernel,
         out_shape=[
-            array(rows + TILE, cols), array(rows, cols), array(rows, cols), array(rows, cols), array(rows, cols),
-            array(6, TILE, rows),
+            array(rows, cols), array(2, rows, cols), array(rows, cols), array(rows, cols),
+            array(2, TILE, cols), array(2, TILE, cols), array(6, TILE, rows),
         ],
         in_specs=[hbm] * 4,
-        out_specs=[vmem] * 6,
+        out_specs=[vmem] * 7,
         scratch_shapes=[
-            scratch(rows + TILE, cols), scratch(2, rows, cols), scratch(rows, cols),
-            pltpu.VMEM((rows, cols), jnp.int32), pltpu.SemaphoreType.DMA((parts, 4)),
+            scratch(rows + 2 * TILE, cols), scratch(rows + 2 * TILE, cols),
+            scratch(2, rows, cols), scratch(rows, cols), pltpu.VMEM((rows, cols), jnp.int32),
+            scratch(rows, LANES), scratch(rows, LANES), pltpu.SemaphoreType.DMA((parts, 4)),
         ],
         compiler_params=params,
-        name="first",
+        name="bulk",
     )(*fields[:4])
 
     sent = [packed] + [
@@ -725,15 +739,15 @@
         flux = (lax.ppermute(strips[-1], "level", [(source, (source - 1) % levels) for source in range(levels)]),)
 
     eta_new, momenta_new, ends = pl.pallas_call(
-        second_kernel,
+        halo_kernel,
         out_shape=[array(*adjoint_height.shape), array(*adjoint_momenta.shape), array(3, 2, TILE, cols)],
-        in_specs=[smem] + [vmem] * 9,
+        in_specs=[smem] + [vmem] * 10,
         out_specs=[hbm, hbm, vmem],
         scratch_shapes=[
-            scratch(3, rows - 2 * TILE, cols), scratch(3, rows, LANES), pltpu.SemaphoreType.DMA((2, 3)),
+            scratch(2, 3, rows - 2 * TILE, LANES), scratch(3, rows, LANES), pltpu.SemaphoreType.DMA((3, 3)),
         ],
         compiler_params=params,
-        name="second",
+        name="halo",
     )(adjacency, mine, other, strips[0], *after)
 
     return pl.pallas_call(
@@ -747,7 +761,7 @@
         ],
         compiler_params=params,
         name="inflow",
-    )(adjacency, mine, other, *flux, after[3], after[4], ends, eta_new, momenta_new)
+    )(adjacency, mine, other, *flux, after[2], after[3], ends, eta_new, momenta_new)
 
 
 def solution(mesh):

time: 21.3 us -> 22.4 us (1.052)
  waiting for transfers between devices: 3.08 us -> 3.95 us
  Pallas kernels: 9.95 us -> 10.3 us
    ppermute x3, waiting for transfers between devices: 1.69 us -> 2.16 us  [body(): lax.ppermute(trimmed if levels == 2 else packed, 'patch', [(source, sourc...]
    ppermute x1, waiting for transfers between devices: 0.01 us -> 0.42 us  [body(): lax.ppermute(strips[-1], 'level', [(source, (source - 1) % levels) for so...]
    pallas_call x2, Pallas kernels: 5.51 us -> 5.88 us  [the longest x1 3.53 us: body(): pl.pallas_call(bulk_kernel, out_shape=[array(rows, cols), array(2, rows,...]
  transfers between devices with their start and end apart: 5 -> 5, of which waited for: 2 -> 3; matrix products, arithmetic and copies ran while one was open for 0% -> 0% of each run, Pallas kernels for 26% -> 26%
where the time goes in v12:
time: 22.4 us; the launch traced here: 22.3 us
  Pallas kernels  10.3 us (46%)
  starting transfers between devices  7.31 us (33%)
  waiting for transfers between devices  3.95 us (18%)
  between operations  0.69 us (3%)
    ppermute x3, starting transfers between devices, body(): lax.ppermute(trimmed if levels == 2 else packed, 'patch', [(source, sourc...  5.68 us
    pallas_call x1, Pallas kernels, body(): pl.pallas_call(bulk_kernel, out_shape=[array(rows, cols), array(2, rows,...  3.53 us
    pallas_call x1, Pallas kernels, body(): pl.pallas_call(halo_kernel, out_shape=[array(*adjoint_height.shape), arra...  2.35 us
    ppermute x3, waiting for transfers between devices, body(): lax.ppermute(trimmed if levels == 2 else packed, 'patch', [(source, sourc...  2.16 us
    pallas_call x1, Pallas kernels, body(): pl.pallas_call(inflow_kernel, out_shape=[array(*adjoint_height.shape), ar...  2.08 us
    pallas_call x1, Pallas kernels, body(): pl.pallas_call(pack_kernel, out_shape=[array(LINES, LANES), array(TRIMMED...  1.65 us
    ppermute x1, starting transfers between devices, body(): lax.ppermute(strips[-1], 'level', [(source, (source - 1) % levels) for so...  1.56 us
    ppermute x1, waiting for transfers between devices, body(): other = lax.ppermute(mine, 'sub', [(0, 1), (1, 0)])  1.38 us
  transfers between devices with their start and end apart: 5, of which 3 were waited for; matrix products, arithmetic and copies ran while one was open for 0% of the time, Pallas kernels for 26%

profile of v12, /device:TPU:0, one launch (start us, length us, event | category | flops | bytes accessed | tf_op | source)
XLA Modules:
  0.0 22.3 jit_solution(332721211590637325)
XLA Ops:
  0.6 1.6 %pack.1 = (f32[80,128]{1,0:T(8,128)S(1)}, f32[64,128]{1,0:T(8,128)S(1)}) custom-call(f32[1,128,1024]{2,1,0:T(8,128)} %eta_ref.3, f32[2,1,128,1024]{3,2,1,0:T(8,128)} %momenta_ref.3, f32[1,128,1024]{2,1,0:T(8,128)} %depth_ref.3, s32[1,128,1024]{2,1,0:T(8,128)} %wet_ref.3, f32[2,1024]{1,0:T(2,128)} %gain_ref.1, s32[2,1024]{1,0:T(2,128)} %index_ref.1), custom_call_target="tpu_custom_call" | custom-call | tf_op jit(solution)/shard_map/pack/pallas_call | solution.py:680
  2.3 3.1 %collective-permute-start.2 = (f32[64,128]{1,0:T(8,128)S(1)}, f32[64,128]{1,0:T(8,128)S(1)}, u32[]{:S(2)}, u32[]{:S(2)}) collective-permute-start(f32[64,128]{1,0:T(8,128)S(1)} %get-tuple-element.15), channel_id=1, source_target_pairs={{0,4},{4,0},{8,12},{12,8},{1,5},{5,1},{9,13},{13,9},{2,6},{6,2},{1... | collective-permute-start | bytes 98312 | tf_op jit(solution)/shard_map/ppermute | solution.py:713
  5.4 2.6 %collective-permute-start.1 = (f32[64,128]{1,0:T(8,128)S(1)}, f32[64,128]{1,0:T(8,128)S(1)}, u32[]{:S(2)}, u32[]{:S(2)}) collective-permute-start(f32[64,128]{1,0:T(8,128)S(1)} %get-tuple-element.15), channel_id=1, source_target_pairs={{0,8},{4,12},{8,0},{12,4},{1,9},{5,13},{9,1},{13,5},{2,10},{6,14},... | collective-permute-start | bytes 98312 | tf_op jit(solution)/shard_map/ppermute | solution.py:713
  8.0 0.0 collective-permute-start
  8.0 3.5 %bulk.1 = (f32[128,1024]{1,0:T(8,128)S(1)}, f32[2,128,1024]{2,1,0:T(8,128)S(1)}, f32[128,1024]{1,0:T(8,128)S(1)}, f32[128,1024]{1,0:T(8,128)S(1)}, f32[2,8,1024]...) custom-call(f32[1,128,1024]{2,1,0:T(8,128)} %eta_ref.3, f32[2,1,128,1024]{3,2,1,0:T(8,128)} %momenta_ref.3, ...), custom_call_target="tpu_custom_call" | custom-call | tf_op jit(solution)/shard_map/bulk/pallas_call | solution.py:695
  11.5 0.0 collective-permute-done.2.refs_3_
  11.5 0.0 collective-permute-done.1.refs_2_
  11.5 2.2 %collective-permute-done.refs_1_ = f32[64,128]{1,0:T(8,128)S(1)} collective-permute-done((f32[64,128]{1,0:T(8,128)S(1)}, f32[64,128]{1,0:T(8,128)S(1)}, u32[]{:S(2)}, u32[]{:S(2)}) %collective-permute-start) | collective-permute-done | bytes 32800 | tf_op jit(solution)/shard_map/ppermute | solution.py:713
  13.7 0.0 copy-start
  13.7 0.1 collective-permute-start.3
  13.8 1.4 %collective-permute-done.3.refs_2_.other_ref = f32[4,80,128]{2,1,0:T(8,128)S(1)} collective-permute-done((f32[4,80,128]{2,1,0:T(8,128)S(1)}, f32[4,80,128]{2,1,0:T(8,128)S(1)}, u32[]{:S(2)}, u32[]{:S(2)}) %collective-permute-start.3) | collective-permute-done | bytes 163872 | tf_op jit(solution)/shard_map/ppermute | solution.py:725
  15.2 0.0 copy-done
  15.2 0.7 %strips.1.strips_ref = f32[16,8,128]{2,1,0:T(8,128)S(1)} custom-call(s32[1,4,4]{2,1,0:T(4,128)S(1)} %copy-done, f32[4,80,128]{2,1,0:T(8,128)S(1)} %gather.1.refs_1_.mine_ref, f32[4,80,128]{2,1,0:T(8,128)S(1)} %collective-permute-done.3.refs_2_.other_ref), custom_call_target="tpu_custom_call" | custom-call | tf_op jit(solution)/shard_map/strips/pallas_call | solution.py:730
  15.8 1.6 %collective-permute-start.4 = (f32[16,8,128]{2,1,0:T(8,128)S(1)}, f32[16,8,128]{2,1,0:T(8,128)S(1)}, u32[]{:S(2)}, u32[]{:S(2)}) collective-permute-start(f32[16,8,128]{2,1,0:T(8,128)S(1)} %strips.1.strips_ref), channel_id=1, source_target_pairs={{0,2},{2,0},{1,3},{3,1},{4,6},{6,4},{5,7},{7,5},{8,10},{10,8},{9,1... | collective-permute-start | bytes 196616 | tf_op jit(solution)/shard_map/ppermute | solution.py:739
  17.4 2.4 %halo.1 = (f32[1,128,1024]{2,1,0:T(8,128)}, f32[2,1,128,1024]{3,2,1,0:T(8,128)}, f32[3,2,8,1024]{3,2,1,0:T(8,128)S(1)}) custom-call(s32[1,4,4]{2,1,0:T(4,128)S(1)} %copy-done, f32[4,80,128]{2,1,0:T(8,128)S(1)} %gather.1.refs_1_.mine_ref, f32[4,80,128]{2,1,0:T(8,128)S(1)} %collective-permute-done.3.refs_2_.other_ref, f32[16,8,128]{2,1,0:T(8,128)S(1)} %strips.1.strips_ref, ...), custom_call_target="tpu_custom_call" | custom-call | tf_op jit(solution)/shard_map/halo/pallas_call | solution.py:741
  19.8 0.4 %collective-permute-done.4.finer_ref = f32[16,8,128]{2,1,0:T(8,128)S(1)} collective-permute-done((f32[16,8,128]{2,1,0:T(8,128)S(1)}, f32[16,8,128]{2,1,0:T(8,128)S(1)}, u32[]{:S(2)}, u32[]{:S(2)}) %collective-permute-start.4) | collective-permute-done | bytes 65568 | tf_op jit(solution)/shard_map/ppermute | solution.py:739
  20.2 2.1 %inflow.1 = (f32[1,128,1024]{2,1,0:T(8,128)}, f32[2,1,128,1024]{3,2,1,0:T(8,128)}) custom-call(s32[1,4,4]{2,1,0:T(4,128)S(1)} %copy-done, f32[4,80,128]{2,1,0:T(8,128)S(1)} %gather.1.refs_1_.mine_ref, f32[4,80,128]{2,1,0:T(8,128)S(1)} %collective-permute-done.3.refs_2_.other_ref, ...), custom_call_target="tpu_custom_call", output_to_operand_aliasing={{0}: (7, {}), {1}: (8, {})} | custom-call | tf_op jit(solution)/shard_map/inflow/pallas_call | solution.py:753
  (1 shorter events, 0.0 us)
Async XLA Ops:
  2.3 9.2 %collective-permute-start.2 = (f32[64,128]{1,0:T(8,128)S(1)}, f32[64,128]{1,0:T(8,128)S(1)}, u32[]{:S(2)}, u32[]{:S(2)}) collective-permute-start(f32[64,128]{1,0:T(8,128)S(1)} %get-tuple-element.15), channel_id=1, source_target_pairs={{0,4},{4,0},{8,12},{12,8},{1,5},{5,1},{9,13},{13,9},{2,6},{6,2},{1... | collective-permute-start | bytes 98312 | tf_op jit(solution)/shard_map/ppermute | solution.py:713
  5.4 6.1 %collective-permute-start.1 = (f32[64,128]{1,0:T(8,128)S(1)}, f32[64,128]{1,0:T(8,128)S(1)}, u32[]{:S(2)}, u32[]{:S(2)}) collective-permute-start(f32[64,128]{1,0:T(8,128)S(1)} %get-tuple-element.15), channel_id=1, source_target_pairs={{0,8},{4,12},{8,0},{12,4},{1,9},{5,13},{9,1},{13,5},{2,10},{6,14},... | collective-permute-start | bytes 98312 | tf_op jit(solution)/shard_map/ppermute | solution.py:713
  8.0 5.7 %collective-permute-start = (f32[64,128]{1,0:T(8,128)S(1)}, f32[64,128]{1,0:T(8,128)S(1)}, u32[]{:S(2)}, u32[]{:S(2)}) collective-permute-start(f32[64,128]{1,0:T(8,128)S(1)} %get-tuple-element.15), channel_id=1, source_target_pairs={{0,12},{4,8},{8,4},{12,0},{1,13},{5,9},{9,5},{13,1},{2,14},{6,10},... | collective-permute-start | bytes 98312 | tf_op jit(solution)/shard_map/ppermute | solution.py:713
  13.7 1.5 %copy-start = (s32[1,4,4]{2,1,0:T(4,128)S(1)}, s32[1,4,4]{2,1,0:T(4,128)}, u32[]{:S(2)}) copy-start(s32[1,4,4]{2,1,0:T(4,128)} %links_ref.3) | copy-start | bytes 196
  13.7 1.5 %collective-permute-start.3 = (f32[4,80,128]{2,1,0:T(8,128)S(1)}, f32[4,80,128]{2,1,0:T(8,128)S(1)}, u32[]{:S(2)}, u32[]{:S(2)}) collective-permute-start(f32[4,80,128]{2,1,0:T(8,128)S(1)} %gather.1.refs_1_.mine_ref), channel_id=1, source_target_pairs={{0,1},{1,0},{2,3},{3,2},{4,5},{5,4},{6,7},{7,6},{8,9},{9,8},{10,11... | collective-permute-start | bytes 491528 | tf_op jit(solution)/shard_map/ppermute | solution.py:725
  15.8 4.3 %collective-permute-start.4 = (f32[16,8,128]{2,1,0:T(8,128)S(1)}, f32[16,8,128]{2,1,0:T(8,128)S(1)}, u32[]{:S(2)}, u32[]{:S(2)}) collective-permute-start(f32[16,8,128]{2,1,0:T(8,128)S(1)} %strips.1.strips_ref), channel_id=1, source_target_pairs={{0,2},{2,0},{1,3},{3,1},{4,6},{6,4},{5,7},{7,5},{8,10},{10,8},{9,1... | collective-permute-start | bytes 196616 | tf_op jit(solution)/shard_map/ppermute | solution.py:739

commit v13 on v12

--- a/solution.py
+++ b/solution.py
@@ -204,7 +204,7 @@
 
 
 def gather_kernel(*refs):
-    first, packets, turns, out_ref = refs[0], refs[1:-2], len(refs) - 2, refs[-1]
+    first, packets, out_ref = refs[0], refs[1:-2], refs[-1]
     own = lax.axis_index("patch")
     out_ref[own] = first[...]
     tables = sends_tables()
@@ -215,7 +215,7 @@
         return jnp.where(line == TILE - 1, packet[at + 1:at + 2], value)
 
     for place, packet in enumerate(packets):
-        patch = own ^ (turns - 1 - place)
+        patch = own ^ (place + 1)
         if packet.shape[0] == LINES:
             out_ref[patch] = packet[...]
             continue
@@ -712,7 +712,7 @@
     sent = [packed] + [
         lax.ppermute(trimmed if levels == 2 else packed, "patch",
                      [(source, source ^ turn) for source in range(patches)])
-        for turn in range(patches - 1, 0, -1)
+        for turn in range(1, patches)
     ]
     mine = pl.pallas_call(
         gather_kernel,

time: 22.4 us -> 21 us (0.938)
  waiting for transfers between devices: 3.95 us -> 2.43 us
    ppermute x3, waiting for transfers between devices: 2.16 us -> 0.63 us  [body(): lax.ppermute(trimmed if levels == 2 else packed, 'patch', [(source, sourc...]
  transfers between devices with their start and end apart: 5 -> 5, of which waited for: 3 -> 3; matrix products, arithmetic and copies ran while one was open for 0% -> 0% of each run, Pallas kernels for 26% -> 28%
where the time goes in v13:
time: 21 us; the launch traced here: 20.8 us
  Pallas kernels  10.3 us (49%)
  starting transfers between devices  7.38 us (35%)
  waiting for transfers between devices  2.43 us (12%)
  between operations  0.68 us (3%)
    ppermute x3, starting transfers between devices, body(): lax.ppermute(trimmed if levels == 2 else packed, 'patch', [(source, sourc...  5.76 us
    pallas_call x1, Pallas kernels, body(): pl.pallas_call(bulk_kernel, out_shape=[array(rows, cols), array(2, rows,...  3.53 us
    pallas_call x1, Pallas kernels, body(): pl.pallas_call(halo_kernel, out_shape=[array(*adjoint_height.shape), arra...  2.35 us
    pallas_call x1, Pallas kernels, body(): pl.pallas_call(inflow_kernel, out_shape=[array(*adjoint_height.shape), ar...  2.08 us
    pallas_call x1, Pallas kernels, body(): pl.pallas_call(pack_kernel, out_shape=[array(LINES, LANES), array(TRIMMED...  1.65 us
    ppermute x1, starting transfers between devices, body(): lax.ppermute(strips[-1], 'level', [(source, (source - 1) % levels) for so...  1.56 us
    ppermute x1, waiting for transfers between devices, body(): other = lax.ppermute(mine, 'sub', [(0, 1), (1, 0)])  1.38 us
    pallas_call x1, Pallas kernels, body(): pl.pallas_call(strips_kernel, out_shape=array(2 * count, TILE, LANES), in...  0.67 us
  transfers between devices with their start and end apart: 5, of which 3 were waited for; matrix products, arithmetic and copies ran while one was open for 0% of the time, Pallas kernels for 28%

profile of v13, /device:TPU:0, one launch (start us, length us, event | category | flops | bytes accessed | tf_op | source)
XLA Modules:
  0.0 20.8 jit_solution(15157769577412414071)
XLA Ops:
  0.6 1.6 %pack.1 = (f32[80,128]{1,0:T(8,128)S(1)}, f32[64,128]{1,0:T(8,128)S(1)}) custom-call(f32[1,128,1024]{2,1,0:T(8,128)} %eta_ref.3, f32[2,1,128,1024]{3,2,1,0:T(8,128)} %momenta_ref.3, f32[1,128,1024]{2,1,0:T(8,128)} %depth_ref.3, s32[1,128,1024]{2,1,0:T(8,128)} %wet_ref.3, f32[2,1024]{1,0:T(2,128)} %gain_ref.1, s32[2,1024]{1,0:T(2,128)} %index_ref.1), custom_call_target="tpu_custom_call" | custom-call | tf_op jit(solution)/shard_map/pack/pallas_call | solution.py:680
  2.3 5.1 %collective-permute-start.2 = (f32[64,128]{1,0:T(8,128)S(1)}, f32[64,128]{1,0:T(8,128)S(1)}, u32[]{:S(2)}, u32[]{:S(2)}) collective-permute-start(f32[64,128]{1,0:T(8,128)S(1)} %get-tuple-element.15), channel_id=1, source_target_pairs={{0,12},{4,8},{8,4},{12,0},{1,13},{5,9},{9,5},{13,1},{2,14},{6,10},... | collective-permute-start | bytes 98312 | tf_op jit(solution)/shard_map/ppermute | solution.py:713
  7.4 0.0 collective-permute-start.1
  7.4 0.6 %collective-permute-start = (f32[64,128]{1,0:T(8,128)S(1)}, f32[64,128]{1,0:T(8,128)S(1)}, u32[]{:S(2)}, u32[]{:S(2)}) collective-permute-start(f32[64,128]{1,0:T(8,128)S(1)} %get-tuple-element.15), channel_id=1, source_target_pairs={{0,4},{4,0},{8,12},{12,8},{1,5},{5,1},{9,13},{13,9},{2,6},{6,2},{1... | collective-permute-start | bytes 98312 | tf_op jit(solution)/shard_map/ppermute | solution.py:713
  8.0 3.5 %bulk.1 = (f32[128,1024]{1,0:T(8,128)S(1)}, f32[2,128,1024]{2,1,0:T(8,128)S(1)}, f32[128,1024]{1,0:T(8,128)S(1)}, f32[128,1024]{1,0:T(8,128)S(1)}, f32[2,8,1024]...) custom-call(f32[1,128,1024]{2,1,0:T(8,128)} %eta_ref.3, f32[2,1,128,1024]{3,2,1,0:T(8,128)} %momenta_ref.3, ...), custom_call_target="tpu_custom_call" | custom-call | tf_op jit(solution)/shard_map/bulk/pallas_call | solution.py:695
  11.6 0.0 collective-permute-done.2.refs_3_
  11.6 0.6 %collective-permute-done.1.refs_2_ = f32[64,128]{1,0:T(8,128)S(1)} collective-permute-done((f32[64,128]{1,0:T(8,128)S(1)}, f32[64,128]{1,0:T(8,128)S(1)}, u32[]{:S(2)}, u32[]{:S(2)}) %collective-permute-start.1) | collective-permute-done | bytes 32800 | tf_op jit(solution)/shard_map/ppermute | solution.py:713
  12.2 0.0 collective-permute-done.refs_1_
  12.2 0.0 copy-start
  12.2 0.1 collective-permute-start.3
  12.3 1.4 %collective-permute-done.3.refs_2_.other_ref = f32[4,80,128]{2,1,0:T(8,128)S(1)} collective-permute-done((f32[4,80,128]{2,1,0:T(8,128)S(1)}, f32[4,80,128]{2,1,0:T(8,128)S(1)}, u32[]{:S(2)}, u32[]{:S(2)}) %collective-permute-start.3) | collective-permute-done | bytes 163872 | tf_op jit(solution)/shard_map/ppermute | solution.py:725
  13.7 0.0 copy-done
  13.7 0.7 %strips.1.strips_ref = f32[16,8,128]{2,1,0:T(8,128)S(1)} custom-call(s32[1,4,4]{2,1,0:T(4,128)S(1)} %copy-done, f32[4,80,128]{2,1,0:T(8,128)S(1)} %gather.1.refs_1_.mine_ref, f32[4,80,128]{2,1,0:T(8,128)S(1)} %collective-permute-done.3.refs_2_.other_ref), custom_call_target="tpu_custom_call" | custom-call | tf_op jit(solution)/shard_map/strips/pallas_call | solution.py:730
  14.4 1.6 %collective-permute-start.4 = (f32[16,8,128]{2,1,0:T(8,128)S(1)}, f32[16,8,128]{2,1,0:T(8,128)S(1)}, u32[]{:S(2)}, u32[]{:S(2)}) collective-permute-start(f32[16,8,128]{2,1,0:T(8,128)S(1)} %strips.1.strips_ref), channel_id=1, source_target_pairs={{0,2},{2,0},{1,3},{3,1},{4,6},{6,4},{5,7},{7,5},{8,10},{10,8},{9,1... | collective-permute-start | bytes 196616 | tf_op jit(solution)/shard_map/ppermute | solution.py:739
  15.9 2.4 %halo.1 = (f32[1,128,1024]{2,1,0:T(8,128)}, f32[2,1,128,1024]{3,2,1,0:T(8,128)}, f32[3,2,8,1024]{3,2,1,0:T(8,128)S(1)}) custom-call(s32[1,4,4]{2,1,0:T(4,128)S(1)} %copy-done, f32[4,80,128]{2,1,0:T(8,128)S(1)} %gather.1.refs_1_.mine_ref, f32[4,80,128]{2,1,0:T(8,128)S(1)} %collective-permute-done.3.refs_2_.other_ref, f32[16,8,128]{2,1,0:T(8,128)S(1)} %strips.1.strips_ref, ...), custom_call_target="tpu_custom_call" | custom-call | tf_op jit(solution)/shard_map/halo/pallas_call | solution.py:741
  18.3 0.4 %collective-permute-done.4.finer_ref = f32[16,8,128]{2,1,0:T(8,128)S(1)} collective-permute-done((f32[16,8,128]{2,1,0:T(8,128)S(1)}, f32[16,8,128]{2,1,0:T(8,128)S(1)}, u32[]{:S(2)}, u32[]{:S(2)}) %collective-permute-start.4) | collective-permute-done | bytes 65568 | tf_op jit(solution)/shard_map/ppermute | solution.py:739
  18.7 2.1 %inflow.1 = (f32[1,128,1024]{2,1,0:T(8,128)}, f32[2,1,128,1024]{3,2,1,0:T(8,128)}) custom-call(s32[1,4,4]{2,1,0:T(4,128)S(1)} %copy-done, f32[4,80,128]{2,1,0:T(8,128)S(1)} %gather.1.refs_1_.mine_ref, f32[4,80,128]{2,1,0:T(8,128)S(1)} %collective-permute-done.3.refs_2_.other_ref, ...), custom_call_target="tpu_custom_call", output_to_operand_aliasing={{0}: (7, {}), {1}: (8, {})} | custom-call | tf_op jit(solution)/shard_map/inflow/pallas_call | solution.py:753
  (1 shorter events, 0.0 us)
Async XLA Ops:
  2.3 9.3 %collective-permute-start.2 = (f32[64,128]{1,0:T(8,128)S(1)}, f32[64,128]{1,0:T(8,128)S(1)}, u32[]{:S(2)}, u32[]{:S(2)}) collective-permute-start(f32[64,128]{1,0:T(8,128)S(1)} %get-tuple-element.15), channel_id=1, source_target_pairs={{0,12},{4,8},{8,4},{12,0},{1,13},{5,9},{9,5},{13,1},{2,14},{6,10},... | collective-permute-start | bytes 98312 | tf_op jit(solution)/shard_map/ppermute | solution.py:713
  7.4 4.8 %collective-permute-start.1 = (f32[64,128]{1,0:T(8,128)S(1)}, f32[64,128]{1,0:T(8,128)S(1)}, u32[]{:S(2)}, u32[]{:S(2)}) collective-permute-start(f32[64,128]{1,0:T(8,128)S(1)} %get-tuple-element.15), channel_id=1, source_target_pairs={{0,8},{4,12},{8,0},{12,4},{1,9},{5,13},{9,1},{13,5},{2,10},{6,14},... | collective-permute-start | bytes 98312 | tf_op jit(solution)/shard_map/ppermute | solution.py:713
  7.4 4.8 %collective-permute-start = (f32[64,128]{1,0:T(8,128)S(1)}, f32[64,128]{1,0:T(8,128)S(1)}, u32[]{:S(2)}, u32[]{:S(2)}) collective-permute-start(f32[64,128]{1,0:T(8,128)S(1)} %get-tuple-element.15), channel_id=1, source_target_pairs={{0,4},{4,0},{8,12},{12,8},{1,5},{5,1},{9,13},{13,9},{2,6},{6,2},{1... | collective-permute-start | bytes 98312 | tf_op jit(solution)/shard_map/ppermute | solution.py:713
  12.2 1.5 %copy-start = (s32[1,4,4]{2,1,0:T(4,128)S(1)}, s32[1,4,4]{2,1,0:T(4,128)}, u32[]{:S(2)}) copy-start(s32[1,4,4]{2,1,0:T(4,128)} %links_ref.3) | copy-start | bytes 196
  12.2 1.5 %collective-permute-start.3 = (f32[4,80,128]{2,1,0:T(8,128)S(1)}, f32[4,80,128]{2,1,0:T(8,128)S(1)}, u32[]{:S(2)}, u32[]{:S(2)}) collective-permute-start(f32[4,80,128]{2,1,0:T(8,128)S(1)} %gather.1.refs_1_.mine_ref), channel_id=1, source_target_pairs={{0,1},{1,0},{2,3},{3,2},{4,5},{5,4},{6,7},{7,6},{8,9},{9,8},{10,11... | collective-permute-start | bytes 491528 | tf_op jit(solution)/shard_map/ppermute | solution.py:725
  14.4 4.3 %collective-permute-start.4 = (f32[16,8,128]{2,1,0:T(8,128)S(1)}, f32[16,8,128]{2,1,0:T(8,128)S(1)}, u32[]{:S(2)}, u32[]{:S(2)}) collective-permute-start(f32[16,8,128]{2,1,0:T(8,128)S(1)} %strips.1.strips_ref), channel_id=1, source_target_pairs={{0,2},{2,0},{1,3},{3,1},{4,6},{6,4},{5,7},{7,5},{8,10},{10,8},{9,1... | collective-permute-start | bytes 196616 | tf_op jit(solution)/shard_map/ppermute | solution.py:739

commit v14 on v13

--- a/solution.py
+++ b/solution.py
@@ -8,6 +8,7 @@
 STEPS = 2
 LANES = 128
 TILE = 8
+LANE_BITS = LANES.bit_length() - 1
 VMEM_LIMIT = 48 * 1024 * 1024
 
 courant = 0.45
@@ -250,6 +251,7 @@
     def __init__(self, links_ref, patches):
         self.links_ref, self.patches = links_ref, patches
         self.half = lax.axis_index("sub")
+        self.known = {}
 
     def own(self):
         return Segment(lax.axis_index("patch"), 0)
@@ -258,8 +260,11 @@
         return [Segment(patch, flipped) for flipped in range(2) for patch in range(self.patches)]
 
     def across(self, segment, way):
-        patch = self.links_ref[0, segment.patch, way]
-        return jnp.maximum(patch, 0), jnp.where(patch >= 0, 1.0, 0.0)
+        key = id(segment.patch) if isinstance(segment.patch, jax.Array) else segment.patch, way
+        if key not in self.known:
+            patch = self.links_ref[0, segment.patch, way]
+            self.known[key] = segment.patch, jnp.maximum(patch, 0), jnp.where(patch >= 0, 1.0, 0.0)
+        return self.known[key][1:]
 
     def other_half(self, segment, way, inner):
         patch, there = self.across(segment, way)
@@ -324,11 +329,15 @@
     return jnp.concatenate([ref[place, line:line + 1] for line in range(TILE)], axis=1)
 
 
-def nested(flux, index):
-    lane, line = index % LANES, index // LANES
-    taken = jnp.zeros(index.shape, jnp.float32)
+def split_index(index):
+    index = index.astype(jnp.int32)
+    return index & (LANES - 1), index >> LANE_BITS
+
+
+def nested(flux, lane, line):
+    taken = jnp.zeros(lane.shape, jnp.float32)
     for source in range(TILE):
-        values = jnp.broadcast_to(flux[source:source + 1], index.shape)
+        values = jnp.broadcast_to(flux[source:source + 1], lane.shape)
         found = jnp.take_along_axis(values, lane, axis=1, mode="promise_in_bounds")
         taken = jnp.where(line == source, found, taken)
     return taken
@@ -347,8 +356,8 @@
         strip = packets.tile(segment, STRIP)
         if finer_ref is not None:
             place = segment.place(patches)
-            gain, index = packets.tile(segment, GAIN) * below_finest(), packets.tile(segment, INDEX).astype(jnp.int32)
-            inflow, later = [gain * nested(finer_ref[step * count + place], index) for step in range(2)]
+            gain, cells = packets.tile(segment, GAIN) * below_finest(), split_index(packets.tile(segment, INDEX))
+            inflow, later = [gain * nested(finer_ref[step * count + place], *cells) for step in range(2)]
             inflows.append((inflow, later))
             strip = strip + inflow
             strips_ref[place] = strip
@@ -590,8 +599,8 @@
         return step * 2 * patches + segment.place(patches)
 
     def inflows(segment):
-        gain, index = packets.tile(segment, GAIN) * some, packets.tile(segment, INDEX).astype(jnp.int32)
-        return [gain * nested(finer_ref[flux_place(step, segment)], index) for step in range(2)]
+        gain, cells = packets.tile(segment, GAIN) * some, split_index(packets.tile(segment, INDEX))
+        return [gain * nested(finer_ref[flux_place(step, segment)], *cells) for step in range(2)]
 
     below, there = links.south(own)
     west, east = links.west(own)[0], links.east(own)[0]
@@ -604,8 +613,7 @@
         ("below east", 0, below_east, 0))
     gain = jnp.concatenate([packets.line(segment, GAIN, line) for _, _, segment, line in wanted], axis=0)
     index = jnp.concatenate([packets.line(segment, INDEX, line) for _, _, segment, line in wanted], axis=0)
-    index = index.astype(jnp.int32)
-    lane, line = index % LANES, index // LANES
+    lane, line = split_index(index)
     taken = jnp.zeros((TILE, LANES), jnp.float32)
     for source in range(TILE):
         values = jnp.concatenate(

time: 21 us -> 21 us (level)
  no operation moved by 1% of the time
where the time goes in v14:
time: 21 us; the launch traced here: 20.8 us
  Pallas kernels  10.3 us (49%)
  starting transfers between devices  7.38 us (35%)
  waiting for transfers between devices  2.43 us (12%)
  between operations  0.68 us (3%)
    ppermute x3, starting transfers between devices, body(): lax.ppermute(trimmed if levels == 2 else packed, 'patch', [(source, sourc...  5.76 us
    pallas_call x1, Pallas kernels, body(): pl.pallas_call(bulk_kernel, out_shape=[array(rows, cols), array(2, rows,...  3.53 us
    pallas_call x1, Pallas kernels, body(): pl.pallas_call(halo_kernel, out_shape=[array(*adjoint_height.shape), arra...  2.35 us
    pallas_call x1, Pallas kernels, body(): pl.pallas_call(inflow_kernel, out_shape=[array(*adjoint_height.shape), ar...  2.08 us
    pallas_call x1, Pallas kernels, body(): pl.pallas_call(pack_kernel, out_shape=[array(LINES, LANES), array(TRIMMED...  1.65 us
    ppermute x1, starting transfers between devices, body(): lax.ppermute(strips[-1], 'level', [(source, (source - 1) % levels) for so...  1.56 us
    ppermute x1, waiting for transfers between devices, body(): other = lax.ppermute(mine, 'sub', [(0, 1), (1, 0)])  1.38 us
    pallas_call x1, Pallas kernels, body(): pl.pallas_call(strips_kernel, out_shape=array(2 * count, TILE, LANES), in...  0.67 us
  transfers between devices with their start and end apart: 5, of which 3 were waited for; matrix products, arithmetic and copies ran while one was open for 0% of the time, Pallas kernels for 28%

profile of v14, /device:TPU:0, one launch (start us, length us, event | category | flops | bytes accessed | tf_op | source)
XLA Modules:
  0.0 20.8 jit_solution(14487218986543285768)
XLA Ops:
  0.6 1.6 %pack.1 = (f32[80,128]{1,0:T(8,128)S(1)}, f32[64,128]{1,0:T(8,128)S(1)}) custom-call(f32[1,128,1024]{2,1,0:T(8,128)} %eta_ref.3, f32[2,1,128,1024]{3,2,1,0:T(8,128)} %momenta_ref.3, f32[1,128,1024]{2,1,0:T(8,128)} %depth_ref.3, s32[1,128,1024]{2,1,0:T(8,128)} %wet_ref.3, f32[2,1024]{1,0:T(2,128)} %gain_ref.1, s32[2,1024]{1,0:T(2,128)} %index_ref.1), custom_call_target="tpu_custom_call" | custom-call | tf_op jit(solution)/shard_map/pack/pallas_call | solution.py:688
  2.3 5.1 %collective-permute-start.2 = (f32[64,128]{1,0:T(8,128)S(1)}, f32[64,128]{1,0:T(8,128)S(1)}, u32[]{:S(2)}, u32[]{:S(2)}) collective-permute-start(f32[64,128]{1,0:T(8,128)S(1)} %get-tuple-element.15), channel_id=1, source_target_pairs={{0,12},{4,8},{8,4},{12,0},{1,13},{5,9},{9,5},{13,1},{2,14},{6,10},... | collective-permute-start | bytes 98312 | tf_op jit(solution)/shard_map/ppermute | solution.py:721
  7.4 0.0 collective-permute-start.1
  7.4 0.6 %collective-permute-start = (f32[64,128]{1,0:T(8,128)S(1)}, f32[64,128]{1,0:T(8,128)S(1)}, u32[]{:S(2)}, u32[]{:S(2)}) collective-permute-start(f32[64,128]{1,0:T(8,128)S(1)} %get-tuple-element.15), channel_id=1, source_target_pairs={{0,4},{4,0},{8,12},{12,8},{1,5},{5,1},{9,13},{13,9},{2,6},{6,2},{1... | collective-permute-start | bytes 98312 | tf_op jit(solution)/shard_map/ppermute | solution.py:721
  8.0 3.5 %bulk.1 = (f32[128,1024]{1,0:T(8,128)S(1)}, f32[2,128,1024]{2,1,0:T(8,128)S(1)}, f32[128,1024]{1,0:T(8,128)S(1)}, f32[128,1024]{1,0:T(8,128)S(1)}, f32[2,8,1024]...) custom-call(f32[1,128,1024]{2,1,0:T(8,128)} %eta_ref.3, f32[2,1,128,1024]{3,2,1,0:T(8,128)} %momenta_ref.3, ...), custom_call_target="tpu_custom_call" | custom-call | tf_op jit(solution)/shard_map/bulk/pallas_call | solution.py:703
  11.6 0.0 collective-permute-done.2.refs_3_
  11.6 0.6 %collective-permute-done.1.refs_2_ = f32[64,128]{1,0:T(8,128)S(1)} collective-permute-done((f32[64,128]{1,0:T(8,128)S(1)}, f32[64,128]{1,0:T(8,128)S(1)}, u32[]{:S(2)}, u32[]{:S(2)}) %collective-permute-start.1) | collective-permute-done | bytes 32800 | tf_op jit(solution)/shard_map/ppermute | solution.py:721
  12.2 0.0 collective-permute-done.refs_1_
  12.2 0.0 copy-start
  12.2 0.1 collective-permute-start.3
  12.3 1.4 %collective-permute-done.3.refs_2_.other_ref = f32[4,80,128]{2,1,0:T(8,128)S(1)} collective-permute-done((f32[4,80,128]{2,1,0:T(8,128)S(1)}, f32[4,80,128]{2,1,0:T(8,128)S(1)}, u32[]{:S(2)}, u32[]{:S(2)}) %collective-permute-start.3) | collective-permute-done | bytes 163872 | tf_op jit(solution)/shard_map/ppermute | solution.py:733
  13.7 0.0 copy-done
  13.7 0.7 %strips.1.strips_ref = f32[16,8,128]{2,1,0:T(8,128)S(1)} custom-call(s32[1,4,4]{2,1,0:T(4,128)S(1)} %copy-done, f32[4,80,128]{2,1,0:T(8,128)S(1)} %gather.1.refs_1_.mine_ref, f32[4,80,128]{2,1,0:T(8,128)S(1)} %collective-permute-done.3.refs_2_.other_ref), custom_call_target="tpu_custom_call" | custom-call | tf_op jit(solution)/shard_map/strips/pallas_call | solution.py:738
  14.4 1.6 %collective-permute-start.4 = (f32[16,8,128]{2,1,0:T(8,128)S(1)}, f32[16,8,128]{2,1,0:T(8,128)S(1)}, u32[]{:S(2)}, u32[]{:S(2)}) collective-permute-start(f32[16,8,128]{2,1,0:T(8,128)S(1)} %strips.1.strips_ref), channel_id=1, source_target_pairs={{0,2},{2,0},{1,3},{3,1},{4,6},{6,4},{5,7},{7,5},{8,10},{10,8},{9,1... | collective-permute-start | bytes 196616 | tf_op jit(solution)/shard_map/ppermute | solution.py:747
  15.9 2.4 %halo.1 = (f32[1,128,1024]{2,1,0:T(8,128)}, f32[2,1,128,1024]{3,2,1,0:T(8,128)}, f32[3,2,8,1024]{3,2,1,0:T(8,128)S(1)}) custom-call(s32[1,4,4]{2,1,0:T(4,128)S(1)} %copy-done, f32[4,80,128]{2,1,0:T(8,128)S(1)} %gather.1.refs_1_.mine_ref, f32[4,80,128]{2,1,0:T(8,128)S(1)} %collective-permute-done.3.refs_2_.other_ref, f32[16,8,128]{2,1,0:T(8,128)S(1)} %strips.1.strips_ref, ...), custom_call_target="tpu_custom_call" | custom-call | tf_op jit(solution)/shard_map/halo/pallas_call | solution.py:749
  18.3 0.4 %collective-permute-done.4.finer_ref = f32[16,8,128]{2,1,0:T(8,128)S(1)} collective-permute-done((f32[16,8,128]{2,1,0:T(8,128)S(1)}, f32[16,8,128]{2,1,0:T(8,128)S(1)}, u32[]{:S(2)}, u32[]{:S(2)}) %collective-permute-start.4) | collective-permute-done | bytes 65568 | tf_op jit(solution)/shard_map/ppermute | solution.py:747
  18.7 2.1 %inflow.1 = (f32[1,128,1024]{2,1,0:T(8,128)}, f32[2,1,128,1024]{3,2,1,0:T(8,128)}) custom-call(s32[1,4,4]{2,1,0:T(4,128)S(1)} %copy-done, f32[4,80,128]{2,1,0:T(8,128)S(1)} %gather.1.refs_1_.mine_ref, f32[4,80,128]{2,1,0:T(8,128)S(1)} %collective-permute-done.3.refs_2_.other_ref, ...), custom_call_target="tpu_custom_call", output_to_operand_aliasing={{0}: (7, {}), {1}: (8, {})} | custom-call | tf_op jit(solution)/shard_map/inflow/pallas_call | solution.py:761
  (1 shorter events, 0.0 us)
Async XLA Ops:
  2.3 9.3 %collective-permute-start.2 = (f32[64,128]{1,0:T(8,128)S(1)}, f32[64,128]{1,0:T(8,128)S(1)}, u32[]{:S(2)}, u32[]{:S(2)}) collective-permute-start(f32[64,128]{1,0:T(8,128)S(1)} %get-tuple-element.15), channel_id=1, source_target_pairs={{0,12},{4,8},{8,4},{12,0},{1,13},{5,9},{9,5},{13,1},{2,14},{6,10},... | collective-permute-start | bytes 98312 | tf_op jit(solution)/shard_map/ppermute | solution.py:721
  7.4 4.8 %collective-permute-start.1 = (f32[64,128]{1,0:T(8,128)S(1)}, f32[64,128]{1,0:T(8,128)S(1)}, u32[]{:S(2)}, u32[]{:S(2)}) collective-permute-start(f32[64,128]{1,0:T(8,128)S(1)} %get-tuple-element.15), channel_id=1, source_target_pairs={{0,8},{4,12},{8,0},{12,4},{1,9},{5,13},{9,1},{13,5},{2,10},{6,14},... | collective-permute-start | bytes 98312 | tf_op jit(solution)/shard_map/ppermute | solution.py:721
  7.4 4.8 %collective-permute-start = (f32[64,128]{1,0:T(8,128)S(1)}, f32[64,128]{1,0:T(8,128)S(1)}, u32[]{:S(2)}, u32[]{:S(2)}) collective-permute-start(f32[64,128]{1,0:T(8,128)S(1)} %get-tuple-element.15), channel_id=1, source_target_pairs={{0,4},{4,0},{8,12},{12,8},{1,5},{5,1},{9,13},{13,9},{2,6},{6,2},{1... | collective-permute-start | bytes 98312 | tf_op jit(solution)/shard_map/ppermute | solution.py:721
  12.2 1.5 %copy-start = (s32[1,4,4]{2,1,0:T(4,128)S(1)}, s32[1,4,4]{2,1,0:T(4,128)}, u32[]{:S(2)}) copy-start(s32[1,4,4]{2,1,0:T(4,128)} %links_ref.3) | copy-start | bytes 196
  12.2 1.5 %collective-permute-start.3 = (f32[4,80,128]{2,1,0:T(8,128)S(1)}, f32[4,80,128]{2,1,0:T(8,128)S(1)}, u32[]{:S(2)}, u32[]{:S(2)}) collective-permute-start(f32[4,80,128]{2,1,0:T(8,128)S(1)} %gather.1.refs_1_.mine_ref), channel_id=1, source_target_pairs={{0,1},{1,0},{2,3},{3,2},{4,5},{5,4},{6,7},{7,6},{8,9},{9,8},{10,11... | collective-permute-start | bytes 491528 | tf_op jit(solution)/shard_map/ppermute | solution.py:733
  14.4 4.3 %collective-permute-start.4 = (f32[16,8,128]{2,1,0:T(8,128)S(1)}, f32[16,8,128]{2,1,0:T(8,128)S(1)}, u32[]{:S(2)}, u32[]{:S(2)}) collective-permute-start(f32[16,8,128]{2,1,0:T(8,128)S(1)} %strips.1.strips_ref), channel_id=1, source_target_pairs={{0,2},{2,0},{1,3},{3,1},{4,6},{6,4},{5,7},{7,5},{8,10},{10,8},{9,1... | collective-permute-start | bytes 196616 | tf_op jit(solution)/shard_map/ppermute | solution.py:747

commit v15 on v13

--- a/solution.py
+++ b/solution.py
@@ -336,12 +336,27 @@
 
 def strips_kernel(*refs):
     links_ref, mine_ref, other_ref = refs[:3]
-    out_ref, strips_ref = refs[-2:]
-    finer_ref = refs[3] if len(refs) == 6 else None
-    links = Links(links_ref, mine_ref.shape[0])
-    patches, count = links.patches, 2 * links.patches
+    out_ref = refs[-1]
+    finer_ref = refs[3] if len(refs) == 5 else None
+    patches = mine_ref.shape[0]
+    count = 2 * patches
     packets = Packets((mine_ref, other_ref))
-    every = links.all()
+    links = links_ref[0]
+    lower = [lax.axis_index("sub") == 1 ^ flipped for flipped in range(2)]
+    every = [Segment(patch, flipped) for flipped in range(2) for patch in range(patches)]
+
+    def matching(patch, way):
+        link = jnp.broadcast_to(links[patch:patch + 1, way:way + 1], (TILE, LANES))
+        return [link == other for other in range(patches)]
+
+    norths, wests, easts = [[matching(patch, way) for patch in range(patches)] for way in (0, 2, 3)]
+
+    def picked(matches, values):
+        total = jnp.zeros((TILE, LANES), jnp.float32)
+        for match, value in zip(matches, values):
+            total = jnp.where(match, value, total)
+        return total
+
     strips, inflows = [], []
     for segment in every:
         strip = packets.tile(segment, STRIP)
@@ -351,38 +366,37 @@
             inflow, later = [gain * nested(finer_ref[step * count + place], index) for step in range(2)]
             inflows.append((inflow, later))
             strip = strip + inflow
-            strips_ref[place] = strip
         strips.append(strip)
-
-    def strip_at(segment):
-        return packets.tile(segment, STRIP) if finer_ref is None else strips_ref[segment.place(patches)]
-
-    totals = []
+    masks = [wet(packets.tile(segment, STRIP_DEPTH)) for segment in every]
+    flows = [packets.tile(segment, EDGE_FLOW) for segment in every]
+    edges = [wet(packets.tile(segment, EDGE_DEPTH)) for segment in every]
+    firsts = [rolled(rolled(strip, -1, 1), -1, 0) for strip in strips]
+    last_masks = [rolled(rolled(mask, 1, 1), 1, 0) for mask in masks]
+    last_rows = [
+        last * (packets.column(segment, LAST_ROW) + courant * rolled(rolled(strip, 1, 1), 1, 0))
+        for last, segment, strip in zip(last_masks, every, strips)]
     for place, segment in enumerate(every):
-        eta, depth = strips[place], packets.tile(segment, STRIP_DEPTH)
-        mask = wet(depth)
-        east, there = links.east(segment)
-        edge = there * rolled(rolled(strip_at(east), -1, 1), -1, 0)
+        flipped, patch = segment.flipped, segment.patch
+        half = slice(flipped * patches, (flipped + 1) * patches)
+        other = slice((1 - flipped) * patches, (2 - flipped) * patches)
+        eta, mask, depth = strips[place], masks[place], packets.tile(segment, STRIP_DEPTH)
+        edge = picked(easts[patch], firsts[half])
         if finer_ref is None:
             row = jnp.where(is_last(), -courant * mask * edge, 0.0)
         else:
             inflow, later = inflows[place]
             row = courant * mask * (inflow - next_cells(inflow, edge))
-        west, there = links.west(segment)
-        west_eta = rolled(rolled(strip_at(west), 1, 1), 1, 0)
-        west_mask = rolled(rolled(wet(packets.tile(west, STRIP_DEPTH)), 1, 1), 1, 0)
-        edge = there * west_mask * (packets.column(west, LAST_ROW) - courant * (eta - west_eta))
-        north, there = links.north(segment)
-        col = there * (packets.tile(north, EDGE_FLOW) - courant * wet(packets.tile(north, EDGE_DEPTH)) * eta)
+        edge = picked(wests[patch], last_rows[half]) - courant * picked(wests[patch], last_masks[half]) * eta
+        flow = jnp.where(lower[flipped], flows[other][patch], picked(norths[patch], flows[other]))
+        above = jnp.where(lower[flipped], edges[other][patch], picked(norths[patch], edges[other]))
+        col = flow - courant * above * eta
         total = packets.tile(segment, STRIP_SUM)
         if finer_ref is None:
             total = total - courant * depth * (row - jnp.where(is_first(), edge, 0.0) - col)
         else:
             total = (total + mask * inflow + later
                      - courant * depth * (row - last_cells(row, edge) + courant * mask * inflow - col))
-        totals.append(total)
-    for place, (strip, total) in enumerate(zip(strips, totals)):
-        out_ref[place] = strip
+        out_ref[place] = eta
         out_ref[count + place] = total
 
 
@@ -730,9 +744,8 @@
         strips.append(pl.pallas_call(
             strips_kernel,
             out_shape=array(2 * count, TILE, LANES),
-            in_specs=[smem] + [vmem] * (2 + len(flux)),
+            in_specs=[vmem] * (3 + len(flux)),
             out_specs=vmem,
-            scratch_shapes=[scratch(count, TILE, LANES)],
             compiler_params=params,
             name="strips",
         )(adjacency, mine, other, *flux))

time: 21 us -> 20.4 us (0.971)
  Pallas kernels: 10.3 us -> 9.77 us
    pallas_call x1, Pallas kernels: 0.67 us -> 0.14 us  [body(): pl.pallas_call(strips_kernel, out_shape=array(2 * count, TILE, LANES), in...]
  transfers between devices with their start and end apart: 5 -> 5, of which waited for: 3 -> 3; matrix products, arithmetic and copies ran while one was open for 0% -> 0% of each run, Pallas kernels for 28% -> 29%
where the time goes in v15:
time: 20.4 us; the launch traced here: 20.3 us
  Pallas kernels  9.77 us (48%)
  starting transfers between devices  7.38 us (36%)
  waiting for transfers between devices  2.43 us (12%)
  between operations  0.69 us (3%)
    ppermute x3, starting transfers between devices, body(): lax.ppermute(trimmed if levels == 2 else packed, 'patch', [(source, sourc...  5.76 us
    pallas_call x1, Pallas kernels, body(): pl.pallas_call(bulk_kernel, out_shape=[array(rows, cols), array(2, rows,...  3.53 us
    pallas_call x1, Pallas kernels, body(): pl.pallas_call(halo_kernel, out_shape=[array(*adjoint_height.shape), arra...  2.35 us
    pallas_call x1, Pallas kernels, body(): pl.pallas_call(inflow_kernel, out_shape=[array(*adjoint_height.shape), ar...  2.08 us
    pallas_call x1, Pallas kernels, body(): pl.pallas_call(pack_kernel, out_shape=[array(LINES, LANES), array(TRIMMED...  1.65 us
    ppermute x1, starting transfers between devices, body(): lax.ppermute(strips[-1], 'level', [(source, (source - 1) % levels) for so...  1.56 us
    ppermute x1, waiting for transfers between devices, body(): other = lax.ppermute(mine, 'sub', [(0, 1), (1, 0)])  1.38 us
    ppermute x3, waiting for transfers between devices, body(): lax.ppermute(trimmed if levels == 2 else packed, 'patch', [(source, sourc...  0.63 us
  transfers between devices with their start and end apart: 5, of which 3 were waited for; matrix products, arithmetic and copies ran while one was open for 0% of the time, Pallas kernels for 29%

profile of v15, /device:TPU:0, one launch (start us, length us, event | category | flops | bytes accessed | tf_op | source)
XLA Modules:
  0.0 20.3 jit_solution(15178725883732964635)
XLA Ops:
  0.6 1.6 %pack.1 = (f32[80,128]{1,0:T(8,128)S(1)}, f32[64,128]{1,0:T(8,128)S(1)}) custom-call(f32[1,128,1024]{2,1,0:T(8,128)} %eta_ref.3, f32[2,1,128,1024]{3,2,1,0:T(8,128)} %momenta_ref.3, f32[1,128,1024]{2,1,0:T(8,128)} %depth_ref.3, s32[1,128,1024]{2,1,0:T(8,128)} %wet_ref.3, f32[2,1024]{1,0:T(2,128)} %gain_ref.1, s32[2,1024]{1,0:T(2,128)} %index_ref.1), custom_call_target="tpu_custom_call" | custom-call | tf_op jit(solution)/shard_map/pack/pallas_call | solution.py:694
  2.3 5.1 %collective-permute-start.2 = (f32[64,128]{1,0:T(8,128)S(1)}, f32[64,128]{1,0:T(8,128)S(1)}, u32[]{:S(2)}, u32[]{:S(2)}) collective-permute-start(f32[64,128]{1,0:T(8,128)S(1)} %get-tuple-element.15), channel_id=1, source_target_pairs={{0,12},{4,8},{8,4},{12,0},{1,13},{5,9},{9,5},{13,1},{2,14},{6,10},... | collective-permute-start | bytes 98312 | tf_op jit(solution)/shard_map/ppermute | solution.py:727
  7.4 0.0 collective-permute-start.1
  7.4 0.6 %collective-permute-start = (f32[64,128]{1,0:T(8,128)S(1)}, f32[64,128]{1,0:T(8,128)S(1)}, u32[]{:S(2)}, u32[]{:S(2)}) collective-permute-start(f32[64,128]{1,0:T(8,128)S(1)} %get-tuple-element.15), channel_id=1, source_target_pairs={{0,4},{4,0},{8,12},{12,8},{1,5},{5,1},{9,13},{13,9},{2,6},{6,2},{1... | collective-permute-start | bytes 98312 | tf_op jit(solution)/shard_map/ppermute | solution.py:727
  8.0 3.5 %bulk.1 = (f32[128,1024]{1,0:T(8,128)S(1)}, f32[2,128,1024]{2,1,0:T(8,128)S(1)}, f32[128,1024]{1,0:T(8,128)S(1)}, f32[128,1024]{1,0:T(8,128)S(1)}, f32[2,8,1024]...) custom-call(f32[1,128,1024]{2,1,0:T(8,128)} %eta_ref.3, f32[2,1,128,1024]{3,2,1,0:T(8,128)} %momenta_ref.3, ...), custom_call_target="tpu_custom_call" | custom-call | tf_op jit(solution)/shard_map/bulk/pallas_call | solution.py:709
  11.6 0.0 collective-permute-done.2.refs_3_
  11.6 0.6 %collective-permute-done.1.refs_2_ = f32[64,128]{1,0:T(8,128)S(1)} collective-permute-done((f32[64,128]{1,0:T(8,128)S(1)}, f32[64,128]{1,0:T(8,128)S(1)}, u32[]{:S(2)}, u32[]{:S(2)}) %collective-permute-start.1) | collective-permute-done | bytes 32800 | tf_op jit(solution)/shard_map/ppermute | solution.py:727
  12.2 0.0 collective-permute-done.refs_1_
  12.2 0.0 copy-start
  12.2 0.1 collective-permute-start.3
  12.3 1.4 %collective-permute-done.3.refs_2_.other_ref = f32[4,80,128]{2,1,0:T(8,128)S(1)} collective-permute-done((f32[4,80,128]{2,1,0:T(8,128)S(1)}, f32[4,80,128]{2,1,0:T(8,128)S(1)}, u32[]{:S(2)}, u32[]{:S(2)}) %collective-permute-start.3) | collective-permute-done | bytes 163872 | tf_op jit(solution)/shard_map/ppermute | solution.py:739
  13.7 0.0 copy-done
  13.7 0.1 strips.1.strips_ref
  13.9 1.6 %collective-permute-start.4 = (f32[16,8,128]{2,1,0:T(8,128)S(1)}, f32[16,8,128]{2,1,0:T(8,128)S(1)}, u32[]{:S(2)}, u32[]{:S(2)}) collective-permute-start(f32[16,8,128]{2,1,0:T(8,128)S(1)} %strips.1.strips_ref), channel_id=1, source_target_pairs={{0,2},{2,0},{1,3},{3,1},{4,6},{6,4},{5,7},{7,5},{8,10},{10,8},{9,1... | collective-permute-start | bytes 196616 | tf_op jit(solution)/shard_map/ppermute | solution.py:752
  15.4 2.4 %halo.1 = (f32[1,128,1024]{2,1,0:T(8,128)}, f32[2,1,128,1024]{3,2,1,0:T(8,128)}, f32[3,2,8,1024]{3,2,1,0:T(8,128)S(1)}) custom-call(s32[1,4,4]{2,1,0:T(4,128)S(1)} %copy-done, f32[4,80,128]{2,1,0:T(8,128)S(1)} %gather.1.refs_1_.mine_ref, f32[4,80,128]{2,1,0:T(8,128)S(1)} %collective-permute-done.3.refs_2_.other_ref, f32[16,8,128]{2,1,0:T(8,128)S(1)} %strips.1.strips_ref, ...), custom_call_target="tpu_custom_call" | custom-call | tf_op jit(solution)/shard_map/halo/pallas_call | solution.py:754
  17.8 0.4 %collective-permute-done.4.finer_ref = f32[16,8,128]{2,1,0:T(8,128)S(1)} collective-permute-done((f32[16,8,128]{2,1,0:T(8,128)S(1)}, f32[16,8,128]{2,1,0:T(8,128)S(1)}, u32[]{:S(2)}, u32[]{:S(2)}) %collective-permute-start.4) | collective-permute-done | bytes 65568 | tf_op jit(solution)/shard_map/ppermute | solution.py:752
  18.2 2.1 %inflow.1 = (f32[1,128,1024]{2,1,0:T(8,128)}, f32[2,1,128,1024]{3,2,1,0:T(8,128)}) custom-call(s32[1,4,4]{2,1,0:T(4,128)S(1)} %copy-done, f32[4,80,128]{2,1,0:T(8,128)S(1)} %gather.1.refs_1_.mine_ref, f32[4,80,128]{2,1,0:T(8,128)S(1)} %collective-permute-done.3.refs_2_.other_ref, ...), custom_call_target="tpu_custom_call", output_to_operand_aliasing={{0}: (7, {}), {1}: (8, {})} | custom-call | tf_op jit(solution)/shard_map/inflow/pallas_call | solution.py:766
  (1 shorter events, 0.0 us)
Async XLA Ops:
  2.3 9.3 %collective-permute-start.2 = (f32[64,128]{1,0:T(8,128)S(1)}, f32[64,128]{1,0:T(8,128)S(1)}, u32[]{:S(2)}, u32[]{:S(2)}) collective-permute-start(f32[64,128]{1,0:T(8,128)S(1)} %get-tuple-element.15), channel_id=1, source_target_pairs={{0,12},{4,8},{8,4},{12,0},{1,13},{5,9},{9,5},{13,1},{2,14},{6,10},... | collective-permute-start | bytes 98312 | tf_op jit(solution)/shard_map/ppermute | solution.py:727
  7.4 4.8 %collective-permute-start.1 = (f32[64,128]{1,0:T(8,128)S(1)}, f32[64,128]{1,0:T(8,128)S(1)}, u32[]{:S(2)}, u32[]{:S(2)}) collective-permute-start(f32[64,128]{1,0:T(8,128)S(1)} %get-tuple-element.15), channel_id=1, source_target_pairs={{0,8},{4,12},{8,0},{12,4},{1,9},{5,13},{9,1},{13,5},{2,10},{6,14},... | collective-permute-start | bytes 98312 | tf_op jit(solution)/shard_map/ppermute | solution.py:727
  7.4 4.8 %collective-permute-start = (f32[64,128]{1,0:T(8,128)S(1)}, f32[64,128]{1,0:T(8,128)S(1)}, u32[]{:S(2)}, u32[]{:S(2)}) collective-permute-start(f32[64,128]{1,0:T(8,128)S(1)} %get-tuple-element.15), channel_id=1, source_target_pairs={{0,4},{4,0},{8,12},{12,8},{1,5},{5,1},{9,13},{13,9},{2,6},{6,2},{1... | collective-permute-start | bytes 98312 | tf_op jit(solution)/shard_map/ppermute | solution.py:727
  12.2 1.5 %copy-start = (s32[1,4,4]{2,1,0:T(4,128)S(1)}, s32[1,4,4]{2,1,0:T(4,128)}, u32[]{:S(2)}) copy-start(s32[1,4,4]{2,1,0:T(4,128)} %links_ref.3) | copy-start | bytes 196
  12.2 1.5 %collective-permute-start.3 = (f32[4,80,128]{2,1,0:T(8,128)S(1)}, f32[4,80,128]{2,1,0:T(8,128)S(1)}, u32[]{:S(2)}, u32[]{:S(2)}) collective-permute-start(f32[4,80,128]{2,1,0:T(8,128)S(1)} %gather.1.refs_1_.mine_ref), channel_id=1, source_target_pairs={{0,1},{1,0},{2,3},{3,2},{4,5},{5,4},{6,7},{7,6},{8,9},{9,8},{10,11... | collective-permute-start | bytes 491528 | tf_op jit(solution)/shard_map/ppermute | solution.py:739
  13.9 4.3 %collective-permute-start.4 = (f32[16,8,128]{2,1,0:T(8,128)S(1)}, f32[16,8,128]{2,1,0:T(8,128)S(1)}, u32[]{:S(2)}, u32[]{:S(2)}) collective-permute-start(f32[16,8,128]{2,1,0:T(8,128)S(1)} %strips.1.strips_ref), channel_id=1, source_target_pairs={{0,2},{2,0},{1,3},{3,1},{4,6},{6,4},{5,7},{7,5},{8,10},{10,8},{9,1... | collective-permute-start | bytes 196616 | tf_op jit(solution)/shard_map/ppermute | solution.py:752

commit v16 on v15

--- a/solution.py
+++ b/solution.py
@@ -18,6 +18,7 @@
 ROWS, COLUMNS = 8, 16
 LINES = ROWS * TILE + COLUMNS
 TRIMMED, SPARE = LINES - 2 * TILE, 4
+SAVED = 96
 
 
 def iota(shape, axis):
@@ -215,7 +216,7 @@
         return jnp.where(line == TILE - 1, packet[at + 1:at + 2], value)
 
     for place, packet in enumerate(packets):
-        patch = own ^ (place + 1)
+        patch = own ^ (len(packets) - place)
         if packet.shape[0] == LINES:
             out_ref[patch] = packet[...]
             continue
@@ -296,6 +297,87 @@
 
     def column(self, segment, column):
         return self.line(segment, ROWS, column)
+
+
+class Saver:
+    def __init__(self, ref):
+        self.ref, self.count = ref, 0
+
+    def put(self, value):
+        self.ref[self.count, :value.shape[0]] = value
+        self.count += 1
+
+    def take(self, lines=TILE):
+        self.count += 1
+        return self.ref[self.count - 1, :lines]
+
+
+class SavingLinks:
+    def __init__(self, links, saver):
+        self.links, self.saver = links, saver
+
+    def saved(self, found):
+        segment, there = found
+        self.saver.put(jnp.full((TILE, LANES), there))
+        self.saver.put(jnp.full((TILE, LANES), segment.patch).astype(jnp.float32))
+        return found
+
+    def north(self, segment):
+        return self.saved(self.links.north(segment))
+
+    def south(self, segment):
+        return self.saved(self.links.south(segment))
+
+    def west(self, segment):
+        return self.saved(self.links.west(segment))
+
+    def east(self, segment):
+        return self.saved(self.links.east(segment))
+
+
+class SavingPackets(Packets):
+    def __init__(self, got_refs, saver):
+        self.got_refs, self.saver = got_refs, saver
+
+    def tile(self, segment, row):
+        value = Packets.tile(self, segment, row)
+        self.saver.put(value)
+        return value
+
+    def line(self, segment, row, line):
+        value = Packets.line(self, segment, row, line)
+        self.saver.put(value)
+        return value
+
+
+class SavedLinks:
+    def __init__(self, saver):
+        self.saver = saver
+
+    def found(self, flipped):
+        there = self.saver.take()[:1, :1]
+        return Segment(self.saver.take(), flipped), there
+
+    def north(self, segment):
+        return self.found(1 - segment.flipped)
+
+    south = north
+
+    def west(self, segment):
+        return self.found(segment.flipped)
+
+    east = west
+
+
+class SavedPackets(Packets):
+    def __init__(self, saver):
+        self.saver = saver
+
+    def tile(self, segment, row):
+        return self.saver.take()
+
+    def line(self, segment, row, line):
+        return self.saver.take(1)
 
 
 def is_first(shape=(TILE, LANES)):
@@ -512,7 +594,8 @@
 
 
 def halo_kernel(links_ref, mine_ref, other_ref, strips_ref, eta_after, momenta_after, wet_after, depth_after,
-                eta_ends, row_ends, turned, eta_out, momenta_out, ends_out, sides_new, more_ref, sems):
+                eta_ends, row_ends, turned, eta_out, momenta_out, ends_out, saved_ref,
+                sides_new, more_ref, rows_ref, sems):
     rows, cols = eta_after.shape
     fields = eta_after, momenta_after.at[0], momenta_after.at[1]
     outs = eta_out.at[0], momenta_out.at[0, 0], momenta_out.at[1, 0]
@@ -586,26 +669,20 @@
             wide = jnp.concatenate(
                 [jnp.where(inside < TILE, more, 0.0), gap, jnp.where(inside >= LANES - TILE, more, 0.0)], axis=1)
             ends_out[place, edge] = fields[place][chunk] + jnp.where(near, found[place], wide)
+    saver = Saver(saved_ref)
+    inflow_sides(SavingLinks(links, saver), SavingPackets((mine_ref, other_ref), saver), own,
+                 lambda step, segment: jnp.zeros((TILE, LANES), jnp.float32), rows_ref)
+    assert saver.count <= SAVED
     for copy in copies:
         copy.wait()
 
 
-def inflow_kernel(links_ref, mine_ref, other_ref, finer_ref, wet_after, depth_after, ends_ref, eta_hbm, momenta_hbm,
-                  eta_out, momenta_out, rows_ref, new_ref, sems):
-    del eta_hbm, momenta_hbm
-    rows, cols = wet_after.shape
-    links = Links(links_ref, mine_ref.shape[0])
-    patches = links.patches
-    own = links.own()
-    packets = Packets((mine_ref, other_ref))
+def inflow_sides(links, packets, own, flux_of, rows_ref):
     some = below_finest()
-
-    def flux_place(step, segment):
-        return step * 2 * patches + segment.place(patches)
 
     def inflows(segment):
         gain, index = packets.tile(segment, GAIN) * some, packets.tile(segment, INDEX).astype(jnp.int32)
-        return [gain * nested(finer_ref[flux_place(step, segment)], index) for step in range(2)]
+        return [gain * nested(flux_of(step, segment), index) for step in range(2)]
 
     below, there = links.south(own)
     west, east = links.west(own)[0], links.east(own)[0]
@@ -620,10 +697,10 @@
     index = jnp.concatenate([packets.line(segment, INDEX, line) for _, _, segment, line in wanted], axis=0)
     index = index.astype(jnp.int32)
     lane, line = index % LANES, index // LANES
+    fluxes = [flux_of(step, segment) for _, step, segment, _ in wanted]
     taken = jnp.zeros((TILE, LANES), jnp.float32)
     for source in range(TILE):
-        values = jnp.concatenate(
-            [finer_ref[flux_place(step, segment), source:source + 1] for _, step, segment, _ in wanted], axis=0)
+        values = jnp.concatenate([tile[source:source + 1] for tile in fluxes], axis=0)
         found = jnp.take_along_axis(values, lane, axis=1, mode="promise_in_bounds")
         taken = jnp.where(line == source, found, taken)
     taken = some * gain * taken
@@ -648,12 +725,33 @@
         mask * strip - courant * depth * (row - last_cells(row, edge) + courant * mask * strip - col) + later)
 
     columns = beside(links, packets, own, inflow)
+    return columns, north_of(links, packets, own, row_of(rows_ref, 0), inflow)
+
+
+def inflow_kernel(mine_ref, finer_ref, saved_ref, wet_after, depth_after, ends_ref, eta_hbm, momenta_hbm,
+                  eta_out, momenta_out, rows_ref, new_ref, sems):
+    del eta_hbm, momenta_hbm
+    rows, cols = wet_after.shape
+    patches = mine_ref.shape[0]
+    saver = Saver(saved_ref)
+
+    def flux_of(step, segment):
+        first = (2 * step + segment.flipped) * patches
+        if segment is own:
+            return finer_ref[first + own.patch]
+        flux = jnp.zeros((TILE, LANES), jnp.float32)
+        for patch in range(patches):
+            flux = jnp.where(segment.patch == patch, finer_ref[first + patch], flux)
+        return flux
+
+    own = Segment(lax.axis_index("patch"), 0)
+    columns, north = inflow_sides(SavedLinks(saver), SavedPackets(saver), own, flux_of, rows_ref)
     top_sides, low_sides = as_sublanes(columns)
     line = iota((TILE, cols), 0)
     strip = row_of(rows_ref, 0)
     top = two_steps(
         jnp.where(line == 0, strip, 0.0), wet_after[:TILE], depth_after[:TILE], top_sides, None,
-        north=north_of(links, packets, own, strip, inflow), second=row_of(rows_ref, 1))
+        north=north, second=row_of(rows_ref, 1))
     copies = []
     outs = eta_out.at[0], momenta_out.at[0, 0], momenta_out.at[1, 0]
 
@@ -726,7 +824,7 @@
     sent = [packed] + [
         lax.ppermute(trimmed if levels == 2 else packed, "patch",
                      [(source, source ^ turn) for source in range(patches)])
-        for turn in range(1, patches)
+        for turn in range(patches - 1, 0, -1)
     ]
     mine = pl.pallas_call(
         gather_kernel,
@@ -751,13 +849,17 @@
         )(adjacency, mine, other, *flux))
         flux = (lax.ppermute(strips[-1], "level", [(source, (source - 1) % levels) for source in range(levels)]),)
 
-    eta_new, momenta_new, ends = pl.pallas_call(
+    eta_new, momenta_new, ends, saved = pl.pallas_call(
         halo_kernel,
-        out_shape=[array(*adjoint_height.shape), array(*adjoint_momenta.shape), array(3, 2, TILE, cols)],
+        out_shape=[
+            array(*adjoint_height.shape), array(*adjoint_momenta.shape), array(3, 2, TILE, cols),
+            array(SAVED, TILE, LANES),
+        ],
         in_specs=[smem] + [vmem] * 10,
-        out_specs=[hbm, hbm, vmem],
+        out_specs=[hbm, hbm, vmem, vmem],
         scratch_shapes=[
-            scratch(2, 3, rows - 2 * TILE, LANES), scratch(3, rows, LANES), pltpu.SemaphoreType.DMA((3, 3)),
+            scratch(2, 3, rows - 2 * TILE, LANES), scratch(3, rows, LANES), scratch(4, TILE, LANES),
+            pltpu.SemaphoreType.DMA((3, 3)),
         ],
         compiler_params=params,
         name="halo",
@@ -766,15 +868,15 @@
     return pl.pallas_call(
         inflow_kernel,
         out_shape=[array(*adjoint_height.shape), array(*adjoint_momenta.shape)],
-        in_specs=[smem] + [vmem] * 6 + [hbm] * 2,
+        in_specs=[vmem] * 6 + [hbm] * 2,
         out_specs=[hbm, hbm],
-        input_output_aliases={7: 0, 8: 1},
+        input_output_aliases={6: 0, 7: 1},
         scratch_shapes=[
             scratch(4, TILE, LANES), scratch(3, 2, TILE, cols), pltpu.SemaphoreType.DMA((2, 3)),
         ],
         compiler_params=params,
         name="inflow",
-    )(adjacency, mine, other, *flux, after[2], after[3], ends, eta_new, momenta_new)
+    )(mine, *flux, saved, after[2], after[3], ends, eta_new, momenta_new)
 
 
 def solution(mesh):

time: 20.4 us -> 19.8 us (0.971)
  Pallas kernels: 9.77 us -> 9.17 us
    pallas_call x1, Pallas kernels: 2.08 us -> 1.48 us  [body(): pl.pallas_call(inflow_kernel, out_shape=[array(*adjoint_height.shape), ar...]
  transfers between devices with their start and end apart: 5 -> 5, of which waited for: 3 -> 3; matrix products, arithmetic and copies ran while one was open for 0% -> 0% of each run, Pallas kernels for 29% -> 30%
where the time goes in v16:
time: 19.8 us; the launch traced here: 19.7 us
  Pallas kernels  9.17 us (46%)
  starting transfers between devices  7.38 us (37%)
  waiting for transfers between devices  2.43 us (12%)
  between operations  0.69 us (3%)
    ppermute x3, starting transfers between devices, body(): lax.ppermute(trimmed if levels == 2 else packed, 'patch', [(source, sourc...  5.76 us
    pallas_call x1, Pallas kernels, body(): pl.pallas_call(bulk_kernel, out_shape=[array(rows, cols), array(2, rows,...  3.5 us
    pallas_call x1, Pallas kernels, body(): pl.pallas_call(halo_kernel, out_shape=[array(*adjoint_height.shape), arra...  2.38 us
    pallas_call x1, Pallas kernels, body(): pl.pallas_call(pack_kernel, out_shape=[array(LINES, LANES), array(TRIMMED...  1.65 us
    ppermute x1, starting transfers between devices, body(): lax.ppermute(strips[-1], 'level', [(source, (source - 1) % levels) for so...  1.56 us
    pallas_call x1, Pallas kernels, body(): pl.pallas_call(inflow_kernel, out_shape=[array(*adjoint_height.shape), ar...  1.48 us
    ppermute x1, waiting for transfers between devices, body(): other = lax.ppermute(mine, 'sub', [(0, 1), (1, 0)])  1.38 us
    ppermute x3, waiting for transfers between devices, body(): lax.ppermute(trimmed if levels == 2 else packed, 'patch', [(source, sourc...  0.66 us
  transfers between devices with their start and end apart: 5, of which 3 were waited for; matrix products, arithmetic and copies ran while one was open for 0% of the time, Pallas kernels for 30%

profile of v16, /device:TPU:0, one launch (start us, length us, event | category | flops | bytes accessed | tf_op | source)
XLA Modules:
  0.0 19.7 jit_solution(12759164636294406558)
XLA Ops:
  0.6 1.6 %pack.1 = (f32[80,128]{1,0:T(8,128)S(1)}, f32[64,128]{1,0:T(8,128)S(1)}) custom-call(f32[1,128,1024]{2,1,0:T(8,128)} %eta_ref.3, f32[2,1,128,1024]{3,2,1,0:T(8,128)} %momenta_ref.3, f32[1,128,1024]{2,1,0:T(8,128)} %depth_ref.3, s32[1,128,1024]{2,1,0:T(8,128)} %wet_ref.3, f32[2,1024]{1,0:T(2,128)} %gain_ref.1, s32[2,1024]{1,0:T(2,128)} %index_ref.1), custom_call_target="tpu_custom_call" | custom-call | tf_op jit(solution)/shard_map/pack/pallas_call | solution.py:792
  2.3 5.1 %collective-permute-start = (f32[64,128]{1,0:T(8,128)S(1)}, f32[64,128]{1,0:T(8,128)S(1)}, u32[]{:S(2)}, u32[]{:S(2)}) collective-permute-start(f32[64,128]{1,0:T(8,128)S(1)} %get-tuple-element.16), channel_id=1, source_target_pairs={{0,12},{4,8},{8,4},{12,0},{1,13},{5,9},{9,5},{13,1},{2,14},{6,10},... | collective-permute-start | bytes 98312 | tf_op jit(solution)/shard_map/ppermute | solution.py:825
  7.4 0.0 collective-permute-start.1
  7.4 0.6 %collective-permute-start.2 = (f32[64,128]{1,0:T(8,128)S(1)}, f32[64,128]{1,0:T(8,128)S(1)}, u32[]{:S(2)}, u32[]{:S(2)}) collective-permute-start(f32[64,128]{1,0:T(8,128)S(1)} %get-tuple-element.16), channel_id=1, source_target_pairs={{0,4},{4,0},{8,12},{12,8},{1,5},{5,1},{9,13},{13,9},{2,6},{6,2},{1... | collective-permute-start | bytes 98312 | tf_op jit(solution)/shard_map/ppermute | solution.py:825
  8.0 3.5 %bulk.1 = (f32[128,1024]{1,0:T(8,128)S(1)}, f32[2,128,1024]{2,1,0:T(8,128)S(1)}, f32[128,1024]{1,0:T(8,128)S(1)}, f32[128,1024]{1,0:T(8,128)S(1)}, f32[2,8,1024]...) custom-call(f32[1,128,1024]{2,1,0:T(8,128)} %eta_ref.3, f32[2,1,128,1024]{3,2,1,0:T(8,128)} %momenta_ref.3, ...), custom_call_target="tpu_custom_call" | custom-call | tf_op jit(solution)/shard_map/bulk/pallas_call | solution.py:807
  11.6 0.0 collective-permute-done.refs_1_
  11.6 0.7 %collective-permute-done.1.refs_2_ = f32[64,128]{1,0:T(8,128)S(1)} collective-permute-done((f32[64,128]{1,0:T(8,128)S(1)}, f32[64,128]{1,0:T(8,128)S(1)}, u32[]{:S(2)}, u32[]{:S(2)}) %collective-permute-start.1) | collective-permute-done | bytes 32800 | tf_op jit(solution)/shard_map/ppermute | solution.py:825
  12.2 0.0 collective-permute-done.2.refs_3_
  12.2 0.0 copy-start
  12.2 0.1 collective-permute-start.3
  12.3 1.4 %collective-permute-done.3.refs_2_.other_ref = f32[4,80,128]{2,1,0:T(8,128)S(1)} collective-permute-done((f32[4,80,128]{2,1,0:T(8,128)S(1)}, f32[4,80,128]{2,1,0:T(8,128)S(1)}, u32[]{:S(2)}, u32[]{:S(2)}) %collective-permute-start.3) | collective-permute-done | bytes 163872 | tf_op jit(solution)/shard_map/ppermute | solution.py:837
  13.7 0.0 copy-done
  13.7 0.1 strips.1.strips_ref
  13.9 1.6 %collective-permute-start.4 = (f32[16,8,128]{2,1,0:T(8,128)S(1)}, f32[16,8,128]{2,1,0:T(8,128)S(1)}, u32[]{:S(2)}, u32[]{:S(2)}) collective-permute-start(f32[16,8,128]{2,1,0:T(8,128)S(1)} %strips.1.strips_ref), channel_id=1, source_target_pairs={{0,2},{2,0},{1,3},{3,1},{4,6},{6,4},{5,7},{7,5},{8,10},{10,8},{9,1... | collective-permute-start | bytes 196616 | tf_op jit(solution)/shard_map/ppermute | solution.py:850
  15.4 2.4 %halo.1 = (f32[1,128,1024]{2,1,0:T(8,128)}, f32[2,1,128,1024]{3,2,1,0:T(8,128)}, f32[3,2,8,1024]{3,2,1,0:T(8,128)S(1)}, f32[96,8,128]{2,1,0:T(8,128)S(1)}) custom-call(s32[1,4,4]{2,1,0:T(4,128)S(1)} %copy-done, f32[4,80,128]{2,1,0:T(8,128)S(1)} %gather.1.refs_1_.mine_ref, f32[4,80,128]{2,1,0:T(8,128)S(1)} %collective-permute-done.3.refs_2_.other_ref, ...), custom_call_target="tpu_custom_call" | custom-call | tf_op jit(solution)/shard_map/halo/pallas_call | solution.py:852
  17.8 0.4 %collective-permute-done.4.finer_ref = f32[16,8,128]{2,1,0:T(8,128)S(1)} collective-permute-done((f32[16,8,128]{2,1,0:T(8,128)S(1)}, f32[16,8,128]{2,1,0:T(8,128)S(1)}, u32[]{:S(2)}, u32[]{:S(2)}) %collective-permute-start.4) | collective-permute-done | bytes 65568 | tf_op jit(solution)/shard_map/ppermute | solution.py:850
  18.2 1.5 %inflow.1 = (f32[1,128,1024]{2,1,0:T(8,128)}, f32[2,1,128,1024]{3,2,1,0:T(8,128)}) custom-call(f32[4,80,128]{2,1,0:T(8,128)S(1)} %gather.1.refs_1_.mine_ref, f32[16,8,128]{2,1,0:T(8,128)S(1)} %collective-permute-done.4.finer_ref, f32[96,8,128]{2,1,0:T(8,128)S(1)} %get-tuple-element.24.saved_ref, ...), custom_call_target="tpu_custom_call", output_to_operand_aliasing={{0}: (6, {}), {1}: (7, {})} | custom-call | tf_op jit(solution)/shard_map/inflow/pallas_call | solution.py:868
  (1 shorter events, 0.0 us)
Async XLA Ops:
  2.3 9.3 %collective-permute-start = (f32[64,128]{1,0:T(8,128)S(1)}, f32[64,128]{1,0:T(8,128)S(1)}, u32[]{:S(2)}, u32[]{:S(2)}) collective-permute-start(f32[64,128]{1,0:T(8,128)S(1)} %get-tuple-element.16), channel_id=1, source_target_pairs={{0,12},{4,8},{8,4},{12,0},{1,13},{5,9},{9,5},{13,1},{2,14},{6,10},... | collective-permute-start | bytes 98312 | tf_op jit(solution)/shard_map/ppermute | solution.py:825
  7.4 4.8 %collective-permute-start.1 = (f32[64,128]{1,0:T(8,128)S(1)}, f32[64,128]{1,0:T(8,128)S(1)}, u32[]{:S(2)}, u32[]{:S(2)}) collective-permute-start(f32[64,128]{1,0:T(8,128)S(1)} %get-tuple-element.16), channel_id=1, source_target_pairs={{0,8},{4,12},{8,0},{12,4},{1,9},{5,13},{9,1},{13,5},{2,10},{6,14},... | collective-permute-start | bytes 98312 | tf_op jit(solution)/shard_map/ppermute | solution.py:825
  7.4 4.8 %collective-permute-start.2 = (f32[64,128]{1,0:T(8,128)S(1)}, f32[64,128]{1,0:T(8,128)S(1)}, u32[]{:S(2)}, u32[]{:S(2)}) collective-permute-start(f32[64,128]{1,0:T(8,128)S(1)} %get-tuple-element.16), channel_id=1, source_target_pairs={{0,4},{4,0},{8,12},{12,8},{1,5},{5,1},{9,13},{13,9},{2,6},{6,2},{1... | collective-permute-start | bytes 98312 | tf_op jit(solution)/shard_map/ppermute | solution.py:825
  12.2 1.5 %copy-start = (s32[1,4,4]{2,1,0:T(4,128)S(1)}, s32[1,4,4]{2,1,0:T(4,128)}, u32[]{:S(2)}) copy-start(s32[1,4,4]{2,1,0:T(4,128)} %links_ref.1) | copy-start | bytes 196
  12.2 1.5 %collective-permute-start.3 = (f32[4,80,128]{2,1,0:T(8,128)S(1)}, f32[4,80,128]{2,1,0:T(8,128)S(1)}, u32[]{:S(2)}, u32[]{:S(2)}) collective-permute-start(f32[4,80,128]{2,1,0:T(8,128)S(1)} %gather.1.refs_1_.mine_ref), channel_id=1, source_target_pairs={{0,1},{1,0},{2,3},{3,2},{4,5},{5,4},{6,7},{7,6},{8,9},{9,8},{10,11... | collective-permute-start | bytes 491528 | tf_op jit(solution)/shard_map/ppermute | solution.py:837
  13.9 4.3 %collective-permute-start.4 = (f32[16,8,128]{2,1,0:T(8,128)S(1)}, f32[16,8,128]{2,1,0:T(8,128)S(1)}, u32[]{:S(2)}, u32[]{:S(2)}) collective-permute-start(f32[16,8,128]{2,1,0:T(8,128)S(1)} %strips.1.strips_ref), channel_id=1, source_target_pairs={{0,2},{2,0},{1,3},{3,1},{4,6},{6,4},{5,7},{7,5},{8,10},{10,8},{9,1... | collective-permute-start | bytes 196616 | tf_op jit(solution)/shard_map/ppermute | solution.py:850

commit v17 on v16

--- a/solution.py
+++ b/solution.py
@@ -37,8 +37,8 @@
 
 def copied(pairs, sems):
     copies = [pltpu.make_async_copy(source, target, sems.at[place]) for place, (source, target) in enumerate(pairs)]
-    for copy in copies:
-        copy.start()
+    for place, copy in enumerate(copies):
+        copy.start(priority=place % 2)
     return copies
 
 

time: 19.8 us -> 19.9 us (level)
  Pallas kernels: 9.17 us -> 9.43 us
  waiting for transfers between devices: 2.43 us -> 2.21 us
    pallas_call x1, Pallas kernels: 3.5 us -> 3.72 us  [body(): pl.pallas_call(bulk_kernel, out_shape=[array(rows, cols), array(2, rows,...]
    ppermute x3, waiting for transfers between devices: 0.66 us -> 0.44 us  [body(): lax.ppermute(trimmed if levels == 2 else packed, 'patch', [(source, sourc...]
  transfers between devices with their start and end apart: 5 -> 5, of which waited for: 3 -> 3; matrix products, arithmetic and copies ran while one was open for 0% -> 0% of each run, Pallas kernels for 30% -> 31%
where the time goes in v17:
time: 19.9 us; the launch traced here: 19.7 us
  Pallas kernels  9.43 us (47%)
  starting transfers between devices  7.38 us (37%)
  waiting for transfers between devices  2.21 us (11%)
  between operations  0.69 us (3%)
    ppermute x3, starting transfers between devices, body(): lax.ppermute(trimmed if levels == 2 else packed, 'patch', [(source, sourc...  5.76 us
    pallas_call x1, Pallas kernels, body(): pl.pallas_call(bulk_kernel, out_shape=[array(rows, cols), array(2, rows,...  3.72 us
    pallas_call x1, Pallas kernels, body(): pl.pallas_call(halo_kernel, out_shape=[array(*adjoint_height.shape), arra...  2.38 us
    pallas_call x1, Pallas kernels, body(): pl.pallas_call(pack_kernel, out_shape=[array(LINES, LANES), array(TRIMMED...  1.69 us
    ppermute x1, starting transfers between devices, body(): lax.ppermute(strips[-1], 'level', [(source, (source - 1) % levels) for so...  1.56 us
    pallas_call x1, Pallas kernels, body(): pl.pallas_call(inflow_kernel, out_shape=[array(*adjoint_height.shape), ar...  1.48 us
    ppermute x1, waiting for transfers between devices, body(): other = lax.ppermute(mine, 'sub', [(0, 1), (1, 0)])  1.38 us
    ppermute x3, waiting for transfers between devices, body(): lax.ppermute(trimmed if levels == 2 else packed, 'patch', [(source, sourc...  0.44 us
  transfers between devices with their start and end apart: 5, of which 3 were waited for; matrix products, arithmetic and copies ran while one was open for 0% of the time, Pallas kernels for 31%

profile of v17, /device:TPU:0, one launch (start us, length us, event | category | flops | bytes accessed | tf_op | source)
XLA Modules:
  0.0 19.7 jit_solution(2767799725008095969)
XLA Ops:
  0.6 1.7 %pack.1 = (f32[80,128]{1,0:T(8,128)S(1)}, f32[64,128]{1,0:T(8,128)S(1)}) custom-call(f32[1,128,1024]{2,1,0:T(8,128)} %eta_ref.3, f32[2,1,128,1024]{3,2,1,0:T(8,128)} %momenta_ref.3, f32[1,128,1024]{2,1,0:T(8,128)} %depth_ref.3, s32[1,128,1024]{2,1,0:T(8,128)} %wet_ref.3, f32[2,1024]{1,0:T(2,128)} %gain_ref.1, s32[2,1024]{1,0:T(2,128)} %index_ref.1), custom_call_target="tpu_custom_call" | custom-call | tf_op jit(solution)/shard_map/pack/pallas_call | solution.py:792
  2.3 5.1 %collective-permute-start = (f32[64,128]{1,0:T(8,128)S(1)}, f32[64,128]{1,0:T(8,128)S(1)}, u32[]{:S(2)}, u32[]{:S(2)}) collective-permute-start(f32[64,128]{1,0:T(8,128)S(1)} %get-tuple-element.16), channel_id=1, source_target_pairs={{0,12},{4,8},{8,4},{12,0},{1,13},{5,9},{9,5},{13,1},{2,14},{6,10},... | collective-permute-start | bytes 98312 | tf_op jit(solution)/shard_map/ppermute | solution.py:825
  7.4 0.0 collective-permute-start.1
  7.4 0.6 %collective-permute-start.2 = (f32[64,128]{1,0:T(8,128)S(1)}, f32[64,128]{1,0:T(8,128)S(1)}, u32[]{:S(2)}, u32[]{:S(2)}) collective-permute-start(f32[64,128]{1,0:T(8,128)S(1)} %get-tuple-element.16), channel_id=1, source_target_pairs={{0,4},{4,0},{8,12},{12,8},{1,5},{5,1},{9,13},{13,9},{2,6},{6,2},{1... | collective-permute-start | bytes 98312 | tf_op jit(solution)/shard_map/ppermute | solution.py:825
  8.1 3.7 %bulk.1 = (f32[128,1024]{1,0:T(8,128)S(1)}, f32[2,128,1024]{2,1,0:T(8,128)S(1)}, f32[128,1024]{1,0:T(8,128)S(1)}, f32[128,1024]{1,0:T(8,128)S(1)}, f32[2,8,1024]...) custom-call(f32[1,128,1024]{2,1,0:T(8,128)} %eta_ref.3, f32[2,1,128,1024]{3,2,1,0:T(8,128)} %momenta_ref.3, ...), custom_call_target="tpu_custom_call" | custom-call | tf_op jit(solution)/shard_map/bulk/pallas_call | solution.py:807
  11.8 0.0 collective-permute-done.refs_1_
  11.8 0.4 %collective-permute-done.1.refs_2_ = f32[64,128]{1,0:T(8,128)S(1)} collective-permute-done((f32[64,128]{1,0:T(8,128)S(1)}, f32[64,128]{1,0:T(8,128)S(1)}, u32[]{:S(2)}, u32[]{:S(2)}) %collective-permute-start.1) | collective-permute-done | bytes 32800 | tf_op jit(solution)/shard_map/ppermute | solution.py:825
  12.3 0.0 collective-permute-done.2.refs_3_
  12.3 0.0 copy-start
  12.3 0.1 collective-permute-start.3
  12.4 1.4 %collective-permute-done.3.refs_2_.other_ref = f32[4,80,128]{2,1,0:T(8,128)S(1)} collective-permute-done((f32[4,80,128]{2,1,0:T(8,128)S(1)}, f32[4,80,128]{2,1,0:T(8,128)S(1)}, u32[]{:S(2)}, u32[]{:S(2)}) %collective-permute-start.3) | collective-permute-done | bytes 163872 | tf_op jit(solution)/shard_map/ppermute | solution.py:837
  13.7 0.0 copy-done
  13.8 0.1 strips.1.strips_ref
  13.9 1.6 %collective-permute-start.4 = (f32[16,8,128]{2,1,0:T(8,128)S(1)}, f32[16,8,128]{2,1,0:T(8,128)S(1)}, u32[]{:S(2)}, u32[]{:S(2)}) collective-permute-start(f32[16,8,128]{2,1,0:T(8,128)S(1)} %strips.1.strips_ref), channel_id=1, source_target_pairs={{0,2},{2,0},{1,3},{3,1},{4,6},{6,4},{5,7},{7,5},{8,10},{10,8},{9,1... | collective-permute-start | bytes 196616 | tf_op jit(solution)/shard_map/ppermute | solution.py:850
  15.5 2.4 %halo.1 = (f32[1,128,1024]{2,1,0:T(8,128)}, f32[2,1,128,1024]{3,2,1,0:T(8,128)}, f32[3,2,8,1024]{3,2,1,0:T(8,128)S(1)}, f32[96,8,128]{2,1,0:T(8,128)S(1)}) custom-call(s32[1,4,4]{2,1,0:T(4,128)S(1)} %copy-done, f32[4,80,128]{2,1,0:T(8,128)S(1)} %gather.1.refs_1_.mine_ref, f32[4,80,128]{2,1,0:T(8,128)S(1)} %collective-permute-done.3.refs_2_.other_ref, ...), custom_call_target="tpu_custom_call" | custom-call | tf_op jit(solution)/shard_map/halo/pallas_call | solution.py:852
  17.8 0.4 %collective-permute-done.4.finer_ref = f32[16,8,128]{2,1,0:T(8,128)S(1)} collective-permute-done((f32[16,8,128]{2,1,0:T(8,128)S(1)}, f32[16,8,128]{2,1,0:T(8,128)S(1)}, u32[]{:S(2)}, u32[]{:S(2)}) %collective-permute-start.4) | collective-permute-done | bytes 65568 | tf_op jit(solution)/shard_map/ppermute | solution.py:850
  18.2 1.5 %inflow.1 = (f32[1,128,1024]{2,1,0:T(8,128)}, f32[2,1,128,1024]{3,2,1,0:T(8,128)}) custom-call(f32[4,80,128]{2,1,0:T(8,128)S(1)} %gather.1.refs_1_.mine_ref, f32[16,8,128]{2,1,0:T(8,128)S(1)} %collective-permute-done.4.finer_ref, f32[96,8,128]{2,1,0:T(8,128)S(1)} %get-tuple-element.24.saved_ref, ...), custom_call_target="tpu_custom_call", output_to_operand_aliasing={{0}: (6, {}), {1}: (7, {})} | custom-call | tf_op jit(solution)/shard_map/inflow/pallas_call | solution.py:868
  (1 shorter events, 0.0 us)
Async XLA Ops:
  2.3 9.5 %collective-permute-start = (f32[64,128]{1,0:T(8,128)S(1)}, f32[64,128]{1,0:T(8,128)S(1)}, u32[]{:S(2)}, u32[]{:S(2)}) collective-permute-start(f32[64,128]{1,0:T(8,128)S(1)} %get-tuple-element.16), channel_id=1, source_target_pairs={{0,12},{4,8},{8,4},{12,0},{1,13},{5,9},{9,5},{13,1},{2,14},{6,10},... | collective-permute-start | bytes 98312 | tf_op jit(solution)/shard_map/ppermute | solution.py:825
  7.4 4.8 %collective-permute-start.1 = (f32[64,128]{1,0:T(8,128)S(1)}, f32[64,128]{1,0:T(8,128)S(1)}, u32[]{:S(2)}, u32[]{:S(2)}) collective-permute-start(f32[64,128]{1,0:T(8,128)S(1)} %get-tuple-element.16), channel_id=1, source_target_pairs={{0,8},{4,12},{8,0},{12,4},{1,9},{5,13},{9,1},{13,5},{2,10},{6,14},... | collective-permute-start | bytes 98312 | tf_op jit(solution)/shard_map/ppermute | solution.py:825
  7.4 4.8 %collective-permute-start.2 = (f32[64,128]{1,0:T(8,128)S(1)}, f32[64,128]{1,0:T(8,128)S(1)}, u32[]{:S(2)}, u32[]{:S(2)}) collective-permute-start(f32[64,128]{1,0:T(8,128)S(1)} %get-tuple-element.16), channel_id=1, source_target_pairs={{0,4},{4,0},{8,12},{12,8},{1,5},{5,1},{9,13},{13,9},{2,6},{6,2},{1... | collective-permute-start | bytes 98312 | tf_op jit(solution)/shard_map/ppermute | solution.py:825
  12.3 1.5 %copy-start = (s32[1,4,4]{2,1,0:T(4,128)S(1)}, s32[1,4,4]{2,1,0:T(4,128)}, u32[]{:S(2)}) copy-start(s32[1,4,4]{2,1,0:T(4,128)} %links_ref.1) | copy-start | bytes 196
  12.3 1.5 %collective-permute-start.3 = (f32[4,80,128]{2,1,0:T(8,128)S(1)}, f32[4,80,128]{2,1,0:T(8,128)S(1)}, u32[]{:S(2)}, u32[]{:S(2)}) collective-permute-start(f32[4,80,128]{2,1,0:T(8,128)S(1)} %gather.1.refs_1_.mine_ref), channel_id=1, source_target_pairs={{0,1},{1,0},{2,3},{3,2},{4,5},{5,4},{6,7},{7,6},{8,9},{9,8},{10,11... | collective-permute-start | bytes 491528 | tf_op jit(solution)/shard_map/ppermute | solution.py:837
  13.9 4.3 %collective-permute-start.4 = (f32[16,8,128]{2,1,0:T(8,128)S(1)}, f32[16,8,128]{2,1,0:T(8,128)S(1)}, u32[]{:S(2)}, u32[]{:S(2)}) collective-permute-start(f32[16,8,128]{2,1,0:T(8,128)S(1)} %strips.1.strips_ref), channel_id=1, source_target_pairs={{0,2},{2,0},{1,3},{3,1},{4,6},{6,4},{5,7},{7,5},{8,10},{10,8},{9,1... | collective-permute-start | bytes 196616 | tf_op jit(solution)/shard_map/ppermute | solution.py:850

commit v18 on v16

--- a/solution.py
+++ b/solution.py
@@ -204,6 +204,10 @@
     return (lax.axis_index("level") == 0) & (lax.axis_index("sub") == 0)
 
 
+def send_order(patches):
+    return sorted(range(1, patches), key=lambda turn: (turn < patches // 2, turn))
+
+
 def gather_kernel(*refs):
     first, packets, out_ref = refs[0], refs[1:-2], refs[-1]
     own = lax.axis_index("patch")
@@ -216,7 +220,7 @@
         return jnp.where(line == TILE - 1, packet[at + 1:at + 2], value)
 
     for place, packet in enumerate(packets):
-        patch = own ^ (len(packets) - place)
+        patch = own ^ send_order(len(packets) + 1)[place]
         if packet.shape[0] == LINES:
             out_ref[patch] = packet[...]
             continue
@@ -824,7 +828,7 @@
     sent = [packed] + [
         lax.ppermute(trimmed if levels == 2 else packed, "patch",
                      [(source, source ^ turn) for source in range(patches)])
-        for turn in range(patches - 1, 0, -1)
+        for turn in send_order(patches)
     ]
     mine = pl.pallas_call(
         gather_kernel,

time: 19.8 us -> 19.7 us (level)
  no operation moved by 1% of the time
where the time goes in v18:
time: 19.7 us; the launch traced here: 19.6 us
  Pallas kernels  9.17 us (47%)
  starting transfers between devices  7.31 us (37%)
  waiting for transfers between devices  2.39 us (12%)
  between operations  0.69 us (4%)
    ppermute x3, starting transfers between devices, body(): lax.ppermute(trimmed if levels == 2 else packed, 'patch', [(source, sourc...  5.68 us
    pallas_call x1, Pallas kernels, body(): pl.pallas_call(bulk_kernel, out_shape=[array(rows, cols), array(2, rows,...  3.5 us
    pallas_call x1, Pallas kernels, body(): pl.pallas_call(halo_kernel, out_shape=[array(*adjoint_height.shape), arra...  2.38 us
    pallas_call x1, Pallas kernels, body(): pl.pallas_call(pack_kernel, out_shape=[array(LINES, LANES), array(TRIMMED...  1.65 us
    ppermute x1, starting transfers between devices, body(): lax.ppermute(strips[-1], 'level', [(source, (source - 1) % levels) for so...  1.56 us
    pallas_call x1, Pallas kernels, body(): pl.pallas_call(inflow_kernel, out_shape=[array(*adjoint_height.shape), ar...  1.48 us
    ppermute x1, waiting for transfers between devices, body(): other = lax.ppermute(mine, 'sub', [(0, 1), (1, 0)])  1.38 us
    ppermute x3, waiting for transfers between devices, body(): lax.ppermute(trimmed if levels == 2 else packed, 'patch', [(source, sourc...  0.62 us
  transfers between devices with their start and end apart: 5, of which 3 were waited for; matrix products, arithmetic and copies ran while one was open for 0% of the time, Pallas kernels for 30%

profile of v18, /device:TPU:0, one launch (start us, length us, event | category | flops | bytes accessed | tf_op | source)
XLA Modules:
  0.0 19.6 jit_solution(12807705617670718618)
XLA Ops:
  0.6 1.6 %pack.1 = (f32[80,128]{1,0:T(8,128)S(1)}, f32[64,128]{1,0:T(8,128)S(1)}) custom-call(f32[1,128,1024]{2,1,0:T(8,128)} %eta_ref.3, f32[2,1,128,1024]{3,2,1,0:T(8,128)} %momenta_ref.3, f32[1,128,1024]{2,1,0:T(8,128)} %depth_ref.3, s32[1,128,1024]{2,1,0:T(8,128)} %wet_ref.3, f32[2,1024]{1,0:T(2,128)} %gain_ref.1, s32[2,1024]{1,0:T(2,128)} %index_ref.1), custom_call_target="tpu_custom_call" | custom-call | tf_op jit(solution)/shard_map/pack/pallas_call | solution.py:796
  2.3 4.1 %collective-permute-start = (f32[64,128]{1,0:T(8,128)S(1)}, f32[64,128]{1,0:T(8,128)S(1)}, u32[]{:S(2)}, u32[]{:S(2)}) collective-permute-start(f32[64,128]{1,0:T(8,128)S(1)} %get-tuple-element.16), channel_id=1, source_target_pairs={{0,8},{4,12},{8,0},{12,4},{1,9},{5,13},{9,1},{13,5},{2,10},{6,14},... | collective-permute-start | bytes 98312 | tf_op jit(solution)/shard_map/ppermute | solution.py:829
  6.4 1.3 %collective-permute-start.1 = (f32[64,128]{1,0:T(8,128)S(1)}, f32[64,128]{1,0:T(8,128)S(1)}, u32[]{:S(2)}, u32[]{:S(2)}) collective-permute-start(f32[64,128]{1,0:T(8,128)S(1)} %get-tuple-element.16), channel_id=1, source_target_pairs={{0,12},{4,8},{8,4},{12,0},{1,13},{5,9},{9,5},{13,1},{2,14},{6,10},... | collective-permute-start | bytes 98312 | tf_op jit(solution)/shard_map/ppermute | solution.py:829
  7.7 0.2 %collective-permute-start.2 = (f32[64,128]{1,0:T(8,128)S(1)}, f32[64,128]{1,0:T(8,128)S(1)}, u32[]{:S(2)}, u32[]{:S(2)}) collective-permute-start(f32[64,128]{1,0:T(8,128)S(1)} %get-tuple-element.16), channel_id=1, source_target_pairs={{0,4},{4,0},{8,12},{12,8},{1,5},{5,1},{9,13},{13,9},{2,6},{6,2},{1... | collective-permute-start | bytes 98312 | tf_op jit(solution)/shard_map/ppermute | solution.py:829
  8.0 3.5 %bulk.1 = (f32[128,1024]{1,0:T(8,128)S(1)}, f32[2,128,1024]{2,1,0:T(8,128)S(1)}, f32[128,1024]{1,0:T(8,128)S(1)}, f32[128,1024]{1,0:T(8,128)S(1)}, f32[2,8,1024]...) custom-call(f32[1,128,1024]{2,1,0:T(8,128)} %eta_ref.3, f32[2,1,128,1024]{3,2,1,0:T(8,128)} %momenta_ref.3, ...), custom_call_target="tpu_custom_call" | custom-call | tf_op jit(solution)/shard_map/bulk/pallas_call | solution.py:811
  11.5 0.0 collective-permute-done.refs_1_
  11.5 0.6 %collective-permute-done.1.refs_2_ = f32[64,128]{1,0:T(8,128)S(1)} collective-permute-done((f32[64,128]{1,0:T(8,128)S(1)}, f32[64,128]{1,0:T(8,128)S(1)}, u32[]{:S(2)}, u32[]{:S(2)}) %collective-permute-start.1) | collective-permute-done | bytes 32800 | tf_op jit(solution)/shard_map/ppermute | solution.py:829
  12.1 0.0 collective-permute-done.2.refs_3_
  12.1 0.0 copy-start
  12.1 0.1 collective-permute-start.3
  12.2 1.4 %collective-permute-done.3.refs_2_.other_ref = f32[4,80,128]{2,1,0:T(8,128)S(1)} collective-permute-done((f32[4,80,128]{2,1,0:T(8,128)S(1)}, f32[4,80,128]{2,1,0:T(8,128)S(1)}, u32[]{:S(2)}, u32[]{:S(2)}) %collective-permute-start.3) | collective-permute-done | bytes 163872 | tf_op jit(solution)/shard_map/ppermute | solution.py:841
  13.6 0.0 copy-done
  13.6 0.1 strips.1.strips_ref
  13.7 1.6 %collective-permute-start.4 = (f32[16,8,128]{2,1,0:T(8,128)S(1)}, f32[16,8,128]{2,1,0:T(8,128)S(1)}, u32[]{:S(2)}, u32[]{:S(2)}) collective-permute-start(f32[16,8,128]{2,1,0:T(8,128)S(1)} %strips.1.strips_ref), channel_id=1, source_target_pairs={{0,2},{2,0},{1,3},{3,1},{4,6},{6,4},{5,7},{7,5},{8,10},{10,8},{9,1... | collective-permute-start | bytes 196616 | tf_op jit(solution)/shard_map/ppermute | solution.py:854
  15.3 2.4 %halo.1 = (f32[1,128,1024]{2,1,0:T(8,128)}, f32[2,1,128,1024]{3,2,1,0:T(8,128)}, f32[3,2,8,1024]{3,2,1,0:T(8,128)S(1)}, f32[96,8,128]{2,1,0:T(8,128)S(1)}) custom-call(s32[1,4,4]{2,1,0:T(4,128)S(1)} %copy-done, f32[4,80,128]{2,1,0:T(8,128)S(1)} %gather.1.refs_1_.mine_ref, f32[4,80,128]{2,1,0:T(8,128)S(1)} %collective-permute-done.3.refs_2_.other_ref, ...), custom_call_target="tpu_custom_call" | custom-call | tf_op jit(solution)/shard_map/halo/pallas_call | solution.py:856
  17.7 0.4 %collective-permute-done.4.finer_ref = f32[16,8,128]{2,1,0:T(8,128)S(1)} collective-permute-done((f32[16,8,128]{2,1,0:T(8,128)S(1)}, f32[16,8,128]{2,1,0:T(8,128)S(1)}, u32[]{:S(2)}, u32[]{:S(2)}) %collective-permute-start.4) | collective-permute-done | bytes 65568 | tf_op jit(solution)/shard_map/ppermute | solution.py:854
  18.1 1.5 %inflow.1 = (f32[1,128,1024]{2,1,0:T(8,128)}, f32[2,1,128,1024]{3,2,1,0:T(8,128)}) custom-call(f32[4,80,128]{2,1,0:T(8,128)S(1)} %gather.1.refs_1_.mine_ref, f32[16,8,128]{2,1,0:T(8,128)S(1)} %collective-permute-done.4.finer_ref, f32[96,8,128]{2,1,0:T(8,128)S(1)} %get-tuple-element.24.saved_ref, ...), custom_call_target="tpu_custom_call", output_to_operand_aliasing={{0}: (6, {}), {1}: (7, {})} | custom-call | tf_op jit(solution)/shard_map/inflow/pallas_call | solution.py:872
  (1 shorter events, 0.0 us)
Async XLA Ops:
  2.3 9.2 %collective-permute-start = (f32[64,128]{1,0:T(8,128)S(1)}, f32[64,128]{1,0:T(8,128)S(1)}, u32[]{:S(2)}, u32[]{:S(2)}) collective-permute-start(f32[64,128]{1,0:T(8,128)S(1)} %get-tuple-element.16), channel_id=1, source_target_pairs={{0,8},{4,12},{8,0},{12,4},{1,9},{5,13},{9,1},{13,5},{2,10},{6,14},... | collective-permute-start | bytes 98312 | tf_op jit(solution)/shard_map/ppermute | solution.py:829
  6.4 5.7 %collective-permute-start.1 = (f32[64,128]{1,0:T(8,128)S(1)}, f32[64,128]{1,0:T(8,128)S(1)}, u32[]{:S(2)}, u32[]{:S(2)}) collective-permute-start(f32[64,128]{1,0:T(8,128)S(1)} %get-tuple-element.16), channel_id=1, source_target_pairs={{0,12},{4,8},{8,4},{12,0},{1,13},{5,9},{9,5},{13,1},{2,14},{6,10},... | collective-permute-start | bytes 98312 | tf_op jit(solution)/shard_map/ppermute | solution.py:829
  7.7 4.4 %collective-permute-start.2 = (f32[64,128]{1,0:T(8,128)S(1)}, f32[64,128]{1,0:T(8,128)S(1)}, u32[]{:S(2)}, u32[]{:S(2)}) collective-permute-start(f32[64,128]{1,0:T(8,128)S(1)} %get-tuple-element.16), channel_id=1, source_target_pairs={{0,4},{4,0},{8,12},{12,8},{1,5},{5,1},{9,13},{13,9},{2,6},{6,2},{1... | collective-permute-start | bytes 98312 | tf_op jit(solution)/shard_map/ppermute | solution.py:829
  12.1 1.5 %copy-start = (s32[1,4,4]{2,1,0:T(4,128)S(1)}, s32[1,4,4]{2,1,0:T(4,128)}, u32[]{:S(2)}) copy-start(s32[1,4,4]{2,1,0:T(4,128)} %links_ref.1) | copy-start | bytes 196
  12.1 1.5 %collective-permute-start.3 = (f32[4,80,128]{2,1,0:T(8,128)S(1)}, f32[4,80,128]{2,1,0:T(8,128)S(1)}, u32[]{:S(2)}, u32[]{:S(2)}) collective-permute-start(f32[4,80,128]{2,1,0:T(8,128)S(1)} %gather.1.refs_1_.mine_ref), channel_id=1, source_target_pairs={{0,1},{1,0},{2,3},{3,2},{4,5},{5,4},{6,7},{7,6},{8,9},{9,8},{10,11... | collective-permute-start | bytes 491528 | tf_op jit(solution)/shard_map/ppermute | solution.py:841
  13.7 4.3 %collective-permute-start.4 = (f32[16,8,128]{2,1,0:T(8,128)S(1)}, f32[16,8,128]{2,1,0:T(8,128)S(1)}, u32[]{:S(2)}, u32[]{:S(2)}) collective-permute-start(f32[16,8,128]{2,1,0:T(8,128)S(1)} %strips.1.strips_ref), channel_id=1, source_target_pairs={{0,2},{2,0},{1,3},{3,1},{4,6},{6,4},{5,7},{7,5},{8,10},{10,8},{9,1... | collective-permute-start | bytes 196616 | tf_op jit(solution)/shard_map/ppermute | solution.py:854
